TPU v7x, 32 devices: a whole 2x2x4 slice. The times are simulated.
32 devices in a mesh: grp: 2 (over y), row: 8 (over z, core), ch: 2 (over x), sub: 1.
Axes of the slice: x: 2, y: 2, z: 4, core: 2. Of those that a mesh axis runs over, the one named last changes fastest.
Arguments:
- pair: float32 [256, 128, 128], P(('grp', 'row'), 'sub'), parts along dimension 0, may hold values from -50 to 50
- pair_mask: int32 [256, 128], P(('grp', 'row'), 'sub'), parts along dimension 0, may hold values 0 or 1
- w_proj: float32 [4, 128, 128], P(None, None, 'ch'), may hold values from -0.5 to 0.5
- w_gate: float32 [128, 128], replicated, may hold values from -0.5 to 0.5
- w_out: float32 [128, 128], P('ch'), may hold values from -0.5 to 0.5
- cotangent: float32 [256, 128, 128], P(('grp', 'row'), 'sub'), parts along dimension 0, may hold values from -6 to 6
Outputs:
- update: float32 [256, 128, 128], P(('grp', 'row'), 'sub'), parts along dimension 0
- d_pair: float32 [256, 128, 128], P(('grp', 'row'), 'sub'), parts along dimension 0
There are 2 independent parts, one for each index of `grp`. A program takes and returns all parts, laid end to end along the dimension named above; an argument that names none is the same for every part. Nothing has to cross between parts.
All inputs are finite; a program needn't handle non-finite values. No bound on the sum of `pair_mask` on one device may be relied on, other than what follows from the above.
Results may differ from a plain program's by a relative error of at most 0.0001.
Values sent between devices are 32-bit elements; how exact they have to be, the bound alone decides.
No kernel may reach another device: no remote copies, remote signals or barrier semaphores. Data moves between devices by JAX's collectives and lax.ppermute only.
A program may use at most 64 MiB of HBM per device.

v0:
```python
import jax
import jax.numpy as jnp
from jax import lax
from jax.sharding import PartitionSpec as P

C = 128


def passed_along(block, axis, distance):
    devices = range(lax.axis_size(axis))
    route = [((i - distance) % len(devices), i) for i in devices]
    return lax.ppermute(block, axis, route)


def normalize(values):
    mean = jnp.mean(values, axis=-1, keepdims=True)
    centered = values - mean
    variance = jnp.mean(centered * centered, axis=-1, keepdims=True)
    scale = lax.rsqrt(variance + 1e-05)
    return (centered * scale, scale)


def on_device(pair, pair_mask, w_proj, w_gate, w_out, cotangent):
    highest = lax.Precision.HIGHEST
    normed, pair_scale = normalize(pair)
    proj = jnp.einsum("rqz,pzc->pcrq", normed, w_proj, precision=highest)
    keep = pair_mask.astype(jnp.float32)
    sig_left = jax.nn.sigmoid(proj[1])
    sig_right = jax.nn.sigmoid(proj[3])
    left = keep * sig_left * proj[0]
    right = keep * sig_right * proj[2]
    chans, rows, cols = left.shape
    count = lax.axis_size("row")
    here = lax.axis_index("row")

    def visit(step, carry):
        block, store, partial_value = carry
        source = (here - step) % count
        store = lax.dynamic_update_slice_in_dim(store, block, source * rows, 1)
        product = jnp.einsum("cik,cjk->cij", left, block, precision=highest)
        partial_value = lax.dynamic_update_slice_in_dim(partial_value, product, source * rows, 2)
        block = passed_along(block, "row", 1)
        return (block, store, partial_value)

    store = jnp.zeros((chans, rows * count, cols), jnp.float32)
    partial_value = jnp.zeros((chans, rows, rows * count), jnp.float32)
    block, store, partial_value = lax.fori_loop(0, count - 1, visit, (right, store, partial_value))
    source = (here + 1) % count
    right_all = lax.dynamic_update_slice_in_dim(store, block, source * rows, 1)
    product = jnp.einsum("cik,cjk->cij", left, block, precision=highest)
    partial_value = lax.dynamic_update_slice_in_dim(partial_value, product, source * rows, 2)
    mixed = lax.psum_scatter(partial_value, "sub", scatter_dimension=2, tiled=True)
    first = jnp.sum(mixed, axis=0)
    second = jnp.sum(mixed * mixed, axis=0)
    projected = jnp.einsum("crq,cd->rqd", mixed, w_out, precision=highest)
    col_total = jnp.sum(w_out, axis=0)
    projected, first, second, col_total = lax.psum((projected, first, second, col_total), "ch")
    center = first / C
    spread = lax.rsqrt(second / C - center * center + 1e-05)
    outgoing = (projected - center[..., None] * col_total) * spread[..., None]
    gate = jax.nn.sigmoid(jnp.einsum("rqz,zd->rqd", normed, w_gate, precision=highest))
    update = gate * outgoing
    d_outgoing = cotangent * gate
    d_gate_pre = cotangent * outgoing * gate * (1.0 - gate)
    d_mixed_norm = jnp.einsum("rqd,cd->crq", d_outgoing, w_out, precision=highest)
    mean_one = jnp.sum(d_outgoing * col_total, axis=-1) / C
    mean_two = jnp.sum(d_outgoing * outgoing, axis=-1) / C
    mixed_norm = (mixed - center) * spread
    d_mixed = (d_mixed_norm - mean_one - mixed_norm * mean_two) * spread
    d_mixed_full = lax.all_gather(d_mixed, "sub", axis=2, tiled=True)
    d_left = jnp.einsum("cij,cjk->cik", d_mixed_full, right_all, precision=highest)
    d_right = jnp.transpose(
        lax.psum_scatter(
            jnp.einsum("cij,cik->jck", d_mixed_full, left, precision=highest),
            "row",
            scatter_dimension=0,
            tiled=True,
        ),
        (1, 0, 2),
    )
    d_proj = jnp.stack(
        [
            d_left * keep * sig_left,
            d_left * keep * proj[0] * sig_left * (1.0 - sig_left),
            d_right * keep * sig_right,
            d_right * keep * proj[2] * sig_right * (1.0 - sig_right),
        ]
    )
    d_normed_part = jnp.einsum("pcrq,pzc->rqz", d_proj, w_proj, precision=highest)
    d_normed = lax.psum(d_normed_part, "ch")
    d_normed = d_normed + jnp.einsum("rqd,zd->rqz", d_gate_pre, w_gate, precision=highest)
    mean_grad = jnp.mean(d_normed, axis=-1, keepdims=True)
    mean_cross = jnp.mean(d_normed * normed, axis=-1, keepdims=True)
    d_pair = (d_normed - mean_grad - normed * mean_cross) * pair_scale
    return (update, d_pair)


def solution(mesh):
    return jax.shard_map(
        on_device,
        mesh=mesh,
        in_specs=(
            P(("grp", "row"), "sub", None),
            P(("grp", "row"), "sub"),
            P(None, None, "ch"),
            P(),
            P("ch", None),
            P(("grp", "row"), "sub", None),
        ),
        out_specs=(P(("grp", "row"), "sub", None), P(("grp", "row"), "sub", None)),
        check_vma=False,
    )
```

profile of v0, /device:TPU:0, one launch (start us, length us, event | category | flops | bytes accessed | tf_op | source)
XLA Modules:
  0.0 267.7 jit_solution(10483086999852491645)
XLA Ops:
  7.2 0.7 convert_element_type.3
  7.9 1.6 reduce_sum.81
  9.5 1.9 multiply_reduce_fusion.3
  11.4 3.6 %convolution_bitcast_fusion = f32[4,64,16,128]{3,1,0,2:T(8,128)S(1)} fusion(f32[16,128,128]{2,1,0:T(8,128)} %param.8, f32[16,128]{1,0:T(8,128)S(1)} %add_rsqrt_fusion.1, f32[16,128]{1,0:T(8,128)S(1)} %broadcast_multiply_fusion.5, f32[4,128,64]{1,2,0:T(8,128)S(1)} %copy-done), kind=kOutput, calls=%fused_computation.9 | convolution fusion | flops 805830656 | bytes 3293184 | tf_op jit(solution)/shard_map/rqz,pzc->pcrq/dot_general | solution.py:26
  15.0 0.3 multiply_multiply_fusion
  15.3 0.3 copy.12
  15.6 0.7 copy-done.2
  16.4 0.3 copy.13
  16.7 2.5 broadcast_in_dim.4
  19.2 74.4 %while.19 = (s32[]{:T(128)}, f32[64,16,128]{2,1,0:T(8,128)S(1)}, f32[64,128,128]{2,1,0:T(8,128)}, f32[64,16,128]{2,0,1:T(8,128)S(1)}, s32[]{:T(128)}, /*index=5*...) while((s32[]{:T(128)}, f32[64,16,128]{2,1,0:T(8,128)S(1)}, ...), condition=%wide.region_3.4_spmd, body=%wide.region_2.3_spmd.sunk | while | flops 25165840 | bytes 5570892 | solution.py:47
  19.3 0.5 collective-permute-start
  19.8 0.9 fusion.75
  20.7 0.2 copy.67
  20.9 1.0 dynamic_update_slice.33
  21.9 0.9 constant_dynamic-update-slice_fusion.3
  22.8 7.8 %collective-permute-done = f32[64,16,128]{2,1,0:T(8,128)S(1)} collective-permute-done((f32[64,16,128]{2,1,0:T(8,128)S(1)}, f32[64,16,128]{2,1,0:T(8,128)S(1)}, u32[]{:S(2)}, u32[]{:S(2)}) %collective-permute-start) | collective-permute-done | bytes 524320 | tf_op jit(solution)/shard_map/while/body/eval_jaxpr/ppermute | solution.py:12
  30.8 0.9 fusion.75
  31.7 0.2 copy.67
  31.9 3.6 %dynamic_update_slice.33 = f32[64,16,128]{2,0,1:T(8,128)S(1)} dynamic-update-slice(f32[64,16,128]{2,0,1:T(8,128)S(1)} %get-tuple-element.258, f32[64,16,16]{2,0,1:T(8,128)S(1)} %copy.67, s32[]{:T(128)} %constant.100.clone.1..sunk, s32[]{:T(128)} %constant.100.clone.1..sunk, s32[]{:T(128)S(6)} %select_n.44) | dynamic-update-slice | bytes 131076 | tf_op jit(solution)/shard_map/while/body/eval_jaxpr/dynamic_update_slice | solution.py:41
  35.5 0.9 constant_dynamic-update-slice_fusion.3
  36.4 4.8 %collective-permute-done = f32[64,16,128]{2,1,0:T(8,128)S(1)} collective-permute-done((f32[64,16,128]{2,1,0:T(8,128)S(1)}, f32[64,16,128]{2,1,0:T(8,128)S(1)}, u32[]{:S(2)}, u32[]{:S(2)}) %collective-permute-start) | collective-permute-done | bytes 524320 | tf_op jit(solution)/shard_map/while/body/eval_jaxpr/ppermute | solution.py:12
  41.3 0.9 fusion.75
  42.2 0.2 copy.67
  42.4 3.6 %dynamic_update_slice.33 = f32[64,16,128]{2,0,1:T(8,128)S(1)} dynamic-update-slice(f32[64,16,128]{2,0,1:T(8,128)S(1)} %get-tuple-element.258, f32[64,16,16]{2,0,1:T(8,128)S(1)} %copy.67, s32[]{:T(128)} %constant.100.clone.1..sunk, s32[]{:T(128)} %constant.100.clone.1..sunk, s32[]{:T(128)S(6)} %select_n.44) | dynamic-update-slice | bytes 131076 | tf_op jit(solution)/shard_map/while/body/eval_jaxpr/dynamic_update_slice | solution.py:41
  46.0 0.9 constant_dynamic-update-slice_fusion.3
  46.9 4.7 %collective-permute-done = f32[64,16,128]{2,1,0:T(8,128)S(1)} collective-permute-done((f32[64,16,128]{2,1,0:T(8,128)S(1)}, f32[64,16,128]{2,1,0:T(8,128)S(1)}, u32[]{:S(2)}, u32[]{:S(2)}) %collective-permute-start) | collective-permute-done | bytes 524320 | tf_op jit(solution)/shard_map/while/body/eval_jaxpr/ppermute | solution.py:12
  51.8 0.9 fusion.75
  52.7 0.2 copy.67
  52.9 3.6 %dynamic_update_slice.33 = f32[64,16,128]{2,0,1:T(8,128)S(1)} dynamic-update-slice(f32[64,16,128]{2,0,1:T(8,128)S(1)} %get-tuple-element.258, f32[64,16,16]{2,0,1:T(8,128)S(1)} %copy.67, s32[]{:T(128)} %constant.100.clone.1..sunk, s32[]{:T(128)} %constant.100.clone.1..sunk, s32[]{:T(128)S(6)} %select_n.44) | dynamic-update-slice | bytes 131076 | tf_op jit(solution)/shard_map/while/body/eval_jaxpr/dynamic_update_slice | solution.py:41
  56.5 0.9 constant_dynamic-update-slice_fusion.3
  57.4 4.8 %collective-permute-done = f32[64,16,128]{2,1,0:T(8,128)S(1)} collective-permute-done((f32[64,16,128]{2,1,0:T(8,128)S(1)}, f32[64,16,128]{2,1,0:T(8,128)S(1)}, u32[]{:S(2)}, u32[]{:S(2)}) %collective-permute-start) | collective-permute-done | bytes 524320 | tf_op jit(solution)/shard_map/while/body/eval_jaxpr/ppermute | solution.py:12
  62.3 0.9 fusion.75
  63.2 0.2 copy.67
  63.4 3.6 %dynamic_update_slice.33 = f32[64,16,128]{2,0,1:T(8,128)S(1)} dynamic-update-slice(f32[64,16,128]{2,0,1:T(8,128)S(1)} %get-tuple-element.258, f32[64,16,16]{2,0,1:T(8,128)S(1)} %copy.67, s32[]{:T(128)} %constant.100.clone.1..sunk, s32[]{:T(128)} %constant.100.clone.1..sunk, s32[]{:T(128)S(6)} %select_n.44) | dynamic-update-slice | bytes 131076 | tf_op jit(solution)/shard_map/while/body/eval_jaxpr/dynamic_update_slice | solution.py:41
  67.0 0.9 constant_dynamic-update-slice_fusion.3
  67.9 4.8 %collective-permute-done = f32[64,16,128]{2,1,0:T(8,128)S(1)} collective-permute-done((f32[64,16,128]{2,1,0:T(8,128)S(1)}, f32[64,16,128]{2,1,0:T(8,128)S(1)}, u32[]{:S(2)}, u32[]{:S(2)}) %collective-permute-start) | collective-permute-done | bytes 524320 | tf_op jit(solution)/shard_map/while/body/eval_jaxpr/ppermute | solution.py:12
  72.8 0.9 fusion.75
  73.9 3.6 %dynamic_update_slice.33 = f32[64,16,128]{2,0,1:T(8,128)S(1)} dynamic-update-slice(f32[64,16,128]{2,0,1:T(8,128)S(1)} %get-tuple-element.258, f32[64,16,16]{2,0,1:T(8,128)S(1)} %copy.67, s32[]{:T(128)} %constant.100.clone.1..sunk, s32[]{:T(128)} %constant.100.clone.1..sunk, s32[]{:T(128)S(6)} %select_n.44) | dynamic-update-slice | bytes 131076 | tf_op jit(solution)/shard_map/while/body/eval_jaxpr/dynamic_update_slice | solution.py:41
  77.5 0.9 constant_dynamic-update-slice_fusion.3
  78.3 4.8 %collective-permute-done = f32[64,16,128]{2,1,0:T(8,128)S(1)} collective-permute-done((f32[64,16,128]{2,1,0:T(8,128)S(1)}, f32[64,16,128]{2,1,0:T(8,128)S(1)}, u32[]{:S(2)}, u32[]{:S(2)}) %collective-permute-start) | collective-permute-done | bytes 524320 | tf_op jit(solution)/shard_map/while/body/eval_jaxpr/ppermute | solution.py:12
  83.3 0.9 fusion.75
  84.4 3.6 %dynamic_update_slice.33 = f32[64,16,128]{2,0,1:T(8,128)S(1)} dynamic-update-slice(f32[64,16,128]{2,0,1:T(8,128)S(1)} %get-tuple-element.258, f32[64,16,16]{2,0,1:T(8,128)S(1)} %copy.67, s32[]{:T(128)} %constant.100.clone.1..sunk, s32[]{:T(128)} %constant.100.clone.1..sunk, s32[]{:T(128)S(6)} %select_n.44) | dynamic-update-slice | bytes 131076 | tf_op jit(solution)/shard_map/while/body/eval_jaxpr/dynamic_update_slice | solution.py:41
  88.0 0.9 constant_dynamic-update-slice_fusion.3
  88.9 4.8 %collective-permute-done = f32[64,16,128]{2,1,0:T(8,128)S(1)} collective-permute-done((f32[64,16,128]{2,1,0:T(8,128)S(1)}, f32[64,16,128]{2,1,0:T(8,128)S(1)}, u32[]{:S(2)}, u32[]{:S(2)}) %collective-permute-start) | collective-permute-done | bytes 524320 | tf_op jit(solution)/shard_map/while/body/eval_jaxpr/ppermute | solution.py:12
  93.6 1.2 fusion.59
  95.0 3.6 %dynamic_update_slice.26 = f32[64,16,128]{2,0,1:T(8,128)S(1)} dynamic-update-slice(f32[64,16,128]{2,0,1:T(8,128)S(1)} %get-tuple-element.159, f32[64,16,16]{2,0,1:T(8,128)S(1)} %copy.16, s32[]{:T(128)} %constant.100.clone.1, s32[]{:T(128)} %constant.100.clone.1, s32[]{:T(128)S(6)} %select_n.40) | dynamic-update-slice | bytes 131076 | tf_op jit(solution)/shard_map/dynamic_update_slice | solution.py:51
  98.6 2.0 fusion.54
  100.7 1.6 copy.18
  102.4 9.2 %all-reduce = (f32[16,128]{1,0:T(8,128)S(1)}, f32[16,128]{1,0:T(8,128)S(1)}, f32[128]{0:T(128)S(1)}) all-reduce(f32[16,128]{1,0:T(8,128)S(1)} %get-tuple-element.175, f32[16,128]{1,0:T(8,128)S(1)} %get-tuple-element.174, f32[128]{0:T(128)S(1)} %reduce_sum.84), channel_id=1, replica_groups=mesh['grp'=2,'row'=8,'ch'=2,'sub'=1] {'ch'}, use_global_device_ids=true, to_apply=%region_10.11 | all-reduce | flops 4224 | bytes 33792 | tf_op jit(solution)/shard_map/psum | solution.py:57
  111.6 27.9 %all-reduce.4.cloned.1.call-done = f32[16,128,128]{1,2,0:T(8,128)} async-done(((f32[16,128,128]{1,2,0:T(8,128)}), f32[16,128,128]{1,2,0:T(8,128)}) %all-reduce.4.cloned.1.call-update) | async-done | bytes 1048592 | tf_op jit(solution)/shard_map/psum | solution.py:57
  139.6 4.0 %multiply_reduce_fusion.2 = (f32[16,128]{1,0:T(8,128)S(1)}, f32[16,128]{1,0:T(8,128)S(1)}, f32[16,128,128]{1,2,0:T(8,128)}, f32[16,128,128]{1,2,0:T(8,128)S(1)}) fusion(f32[128]{0:T(128)S(1)} %get-tuple-element.190, f32[16,128,128]{1,2,0:T(8,128)S(1)} %copy.18, f32[16,128]{1,0:T(8,128)S(1)} %get-tuple-element.201, ...), kind=kOutput, calls=%fused_computation.28 | convolution fusion | flops 406319104 | bytes 5358080 | tf_op jit(solution)/shard_map/rqz,zd->rqd/dot_general | solution.py:61
  143.6 1.6 fusion.16
  145.2 9.2 %fusion.45 = f32[64,128,128]{2,1,0:T(8,128)} fusion(f32[64,16,128]{2,0,1:T(8,128)} %fusion.16, f32[64,16,128]{2,0,1:T(8,128)S(1)} %copy-done.7), kind=kOutput, calls=%fused_computation.67 | convolution fusion | flops 201326592 | bytes 5242880 | tf_op jit(solution)/shard_map/cij,cik->jck/dot_general | solution.py:74
  154.4 5.4 %copy.24 = f32[64,128,128]{1,0,2:T(8,128)} copy(f32[64,128,128]{2,1,0:T(8,128)} %fusion.45) | data formatting | bytes 8388608 | tf_op jit(solution)/shard_map/cij,cik->jck/dot_general | solution.py:74
  159.8 0.3 all-reduce.6.cloned.1.call-start
  160.1 0.9 constant_dynamic-update-slice_fusion.1
  161.0 7.2 %fusion.47 = f32[64,16,128]{2,1,0:T(8,128)} fusion(f32[64,128,128]{2,1,0:T(8,128)} %constant_dynamic-update-slice_fusion.1, f32[64,16,128]{2,0,1:T(8,128)} %fusion.16), kind=kOutput, calls=%fused_computation.69 | convolution fusion | flops 201326592 | bytes 5242880 | tf_op jit(solution)/shard_map/cij,cjk->cik/dot_general | solution.py:71
  168.2 41.8 %reduce-scatter.2.cloned.1.call-done = f32[16,64,128]{2,1,0:T(8,128)} async-done(((f32[128,64,128]{2,1,0:T(8,128)}), f32[16,64,128]{2,1,0:T(8,128)}) %reduce-scatter.2.cloned.1.call-update) | async-done | bytes 524304 | tf_op jit(solution)/shard_map/reduce_scatter | solution.py:73
  210.0 1.6 multiply_bitcast_fusion.1
  211.7 4.6 %fusion.8 = f32[16,128,128]{2,1,0:T(8,128)} fusion(f32[1,64,16,128]{3,1,2,0:T(8,128)S(1)} %get-tuple-element.196, f32[1,64,16,128]{3,1,2,0:T(8,128)S(1)} %get-tuple-element.197, f32[1,64,16,128]{3,1,2,0:T(8,128)S(1)} %get-tuple-element.192, f32[1,64,16,128]{3,1,2,0:T(8,128)S(1)} %get-tuple-element.191, f32[4,128,64]{1,2,0:T(8,128)S(1)} %copy-done), kind=kOutput, calls=%fused_computation.10 | convolution fusion | flops 806879232 | bytes 3276800 | tf_op jit(solution)/shard_map/pcrq,pzc->rqz/dot_general | solution.py:89
  216.3 2.5 copy.29
  218.8 35.8 %all-reduce.6.cloned.1.call-done = f32[16,128,128]{2,1,0:T(8,128)} async-done(((f32[16,128,128]{2,1,0:T(8,128)}), f32[16,128,128]{2,1,0:T(8,128)}) %all-reduce.6.cloned.1.call-update) | async-done | bytes 1048592 | tf_op jit(solution)/shard_map/psum | solution.py:90
  254.6 4.4 %fusion.62 = (f32[16,128]{1,0:T(8,128)S(1)}, f32[16,128]{1,0:T(8,128)S(1)}, f32[16,128,128]{2,1,0:T(8,128)S(1)}) fusion(f32[16,128]{1,0:T(8,128)S(1)} %add_rsqrt_fusion.1, f32[16,128,128]{2,1,0:T(8,128)S(1)} %copy-done.1, f32[16,128]{1,0:T(8,128)S(1)} %broadcast_multiply_fusion.5, f32[16,128,128]{2,1,0:T(8,128)} %all-reduce.6.cloned.1.call-done, ...), kind=kOutput, calls=%fused_computation.93 | convolution fusion | flops 406056960 | bytes 6406656 | tf_op jit(solution)/shard_map/rqd,zd->rqz/dot_general | solution.py:91
  259.1 2.0 subtract_multiply_fusion
  (53 shorter events, 1.5 us)
Async XLA Ops:
  7.2 4.2 %copy-start = (f32[4,128,64]{1,2,0:T(8,128)S(1)}, f32[4,128,64]{1,2,0:T(8,128)}, u32[]{:S(2)}) copy-start(f32[4,128,64]{1,2,0:T(8,128)} %param.10) | copy-start | bytes 393220
  7.2 132.4 %all-reduce.4.cloned.1.call-start = ((), (), s32[]{:S(2)}) async-start(), calls=%async_computation.1 | async-start | bytes 2097152 | tf_op jit(solution)/shard_map/psum | solution.py:57
  15.0 1.4 copy-start.2
  15.3 78.3 %copy-start.6 = (f32[64,16,128]{2,0,1:T(8,128)}, f32[64,16,128]{2,0,1:T(8,128)S(1)}, u32[]{:S(2)}) copy-start(f32[64,16,128]{2,0,1:T(8,128)S(1)} %get-tuple-element.198) | copy-start | bytes 1572868
  19.2 79.4 %copy-start.10 = (f32[64,128]{1,0:T(8,128)S(1)}, f32[64,128]{1,0:T(8,128)}, u32[]{:S(2)}) copy-start(f32[64,128]{1,0:T(8,128)} %param.12) | copy-start | bytes 98308
  19.3 11.4 %collective-permute-start = (f32[64,16,128]{2,1,0:T(8,128)S(1)}, f32[64,16,128]{2,1,0:T(8,128)S(1)}, u32[]{:S(2)}, u32[]{:S(2)}) collective-permute-start(f32[64,16,128]{2,1,0:T(8,128)S(1)} %copy.75), channel_id=1, source_target_pairs={{14,0},{0,2},{2,4},{4,6},{6,8},{8,10},{10,12},{12,14},{15,1},{1,3}... | collective-permute-start | bytes 1572872 | tf_op jit(solution)/shard_map/while/body/eval_jaxpr/ppermute | solution.py:12
  30.7 10.5 %collective-permute-start = (f32[64,16,128]{2,1,0:T(8,128)S(1)}, f32[64,16,128]{2,1,0:T(8,128)S(1)}, u32[]{:S(2)}, u32[]{:S(2)}) collective-permute-start(f32[64,16,128]{2,1,0:T(8,128)S(1)} %copy.75), channel_id=1, source_target_pairs={{14,0},{0,2},{2,4},{4,6},{6,8},{8,10},{10,12},{12,14},{15,1},{1,3}... | collective-permute-start | bytes 1572872 | tf_op jit(solution)/shard_map/while/body/eval_jaxpr/ppermute | solution.py:12
  41.2 10.5 %collective-permute-start = (f32[64,16,128]{2,1,0:T(8,128)S(1)}, f32[64,16,128]{2,1,0:T(8,128)S(1)}, u32[]{:S(2)}, u32[]{:S(2)}) collective-permute-start(f32[64,16,128]{2,1,0:T(8,128)S(1)} %copy.75), channel_id=1, source_target_pairs={{14,0},{0,2},{2,4},{4,6},{6,8},{8,10},{10,12},{12,14},{15,1},{1,3}... | collective-permute-start | bytes 1572872 | tf_op jit(solution)/shard_map/while/body/eval_jaxpr/ppermute | solution.py:12
  51.7 10.5 %collective-permute-start = (f32[64,16,128]{2,1,0:T(8,128)S(1)}, f32[64,16,128]{2,1,0:T(8,128)S(1)}, u32[]{:S(2)}, u32[]{:S(2)}) collective-permute-start(f32[64,16,128]{2,1,0:T(8,128)S(1)} %copy.75), channel_id=1, source_target_pairs={{14,0},{0,2},{2,4},{4,6},{6,8},{8,10},{10,12},{12,14},{15,1},{1,3}... | collective-permute-start | bytes 1572872 | tf_op jit(solution)/shard_map/while/body/eval_jaxpr/ppermute | solution.py:12
  62.2 10.5 %collective-permute-start = (f32[64,16,128]{2,1,0:T(8,128)S(1)}, f32[64,16,128]{2,1,0:T(8,128)S(1)}, u32[]{:S(2)}, u32[]{:S(2)}) collective-permute-start(f32[64,16,128]{2,1,0:T(8,128)S(1)} %copy.75), channel_id=1, source_target_pairs={{14,0},{0,2},{2,4},{4,6},{6,8},{8,10},{10,12},{12,14},{15,1},{1,3}... | collective-permute-start | bytes 1572872 | tf_op jit(solution)/shard_map/while/body/eval_jaxpr/ppermute | solution.py:12
  72.7 10.5 %collective-permute-start = (f32[64,16,128]{2,1,0:T(8,128)S(1)}, f32[64,16,128]{2,1,0:T(8,128)S(1)}, u32[]{:S(2)}, u32[]{:S(2)}) collective-permute-start(f32[64,16,128]{2,1,0:T(8,128)S(1)} %copy.75), channel_id=1, source_target_pairs={{14,0},{0,2},{2,4},{4,6},{6,8},{8,10},{10,12},{12,14},{15,1},{1,3}... | collective-permute-start | bytes 1572872 | tf_op jit(solution)/shard_map/while/body/eval_jaxpr/ppermute | solution.py:12
  83.2 10.5 %collective-permute-start = (f32[64,16,128]{2,1,0:T(8,128)S(1)}, f32[64,16,128]{2,1,0:T(8,128)S(1)}, u32[]{:S(2)}, u32[]{:S(2)}) collective-permute-start(f32[64,16,128]{2,1,0:T(8,128)S(1)} %copy.75), channel_id=1, source_target_pairs={{14,0},{0,2},{2,4},{4,6},{6,8},{8,10},{10,12},{12,14},{15,1},{1,3}... | collective-permute-start | bytes 1572872 | tf_op jit(solution)/shard_map/while/body/eval_jaxpr/ppermute | solution.py:12
  93.6 45.9 %copy-start.1 = (f32[16,128,128]{2,1,0:T(8,128)S(1)}, f32[16,128,128]{2,1,0:T(8,128)}, u32[]{:S(2)}) copy-start(f32[16,128,128]{2,1,0:T(8,128)} %param.8) | copy-start | bytes 3145732
  93.6 45.9 %copy-start.11 = (f32[128,128]{1,0:T(8,128)S(1)}, f32[128,128]{1,0:T(8,128)}, u32[]{:S(2)}) copy-start(f32[128,128]{1,0:T(8,128)} %param.11) | copy-start | bytes 196612
  100.6 109.3 %reduce-scatter.2.cloned.1.call-start = ((), (), s32[]{:S(2)}) async-start(), calls=%async_computation.2 | async-start | bytes 4718592 | tf_op jit(solution)/shard_map/reduce_scatter | solution.py:73
  102.3 42.9 %copy-start.4 = (f32[16,128,128]{1,2,0:T(8,128)}, f32[16,128,128]{1,2,0:T(8,128)S(1)}, u32[]{:S(2)}) copy-start(f32[16,128,128]{1,2,0:T(8,128)S(1)} %copy.18) | copy-start | bytes 3145732
  139.6 5.7 %copy-start.7 = (f32[64,16,128]{2,0,1:T(8,128)S(1)}, f32[64,16,128]{2,0,1:T(8,128)}, u32[]{:S(2)}) copy-start(f32[64,16,128]{2,0,1:T(8,128)} %copy-done.6) | copy-start | bytes 1572868
  143.6 1.6 copy-start.8
  159.8 94.8 %all-reduce.6.cloned.1.call-start = ((), (), s32[]{:S(2)}) async-start(), calls=%async_computation.3 | async-start | bytes 2097152 | tf_op jit(solution)/shard_map/psum | solution.py:90
  161.0 49.0 %copy-start.3 = (f32[4,64,16,128]{3,1,0,2:T(8,128)S(1)}, f32[4,64,16,128]{3,1,0,2:T(8,128)}, u32[]{:S(2)}) copy-start(f32[4,64,16,128]{3,1,0,2:T(8,128)} %copy-done.2) | copy-start | bytes 6291460
  211.6 43.0 %copy-start.5 = (f32[16,128,128]{1,2,0:T(8,128)S(1)}, f32[16,128,128]{1,2,0:T(8,128)}, u32[]{:S(2)}) copy-start(f32[16,128,128]{1,2,0:T(8,128)} %copy-done.4) | copy-start | bytes 3145732
  211.7 43.0 %copy-start.9 = (f32[16,128,128]{1,2,0:T(8,128)S(1)}, f32[16,128,128]{1,2,0:T(8,128)}, u32[]{:S(2)}) copy-start(f32[16,128,128]{1,2,0:T(8,128)} %copy-done.8) | copy-start | bytes 3145732
Sparse Core Ops, SparseCore 0:
  100.8 38.7 all-reduce.3
  160.0 49.9 reduce-scatter.1
  216.4 38.1 all-reduce.5
where the time goes:
time: 268 us
  waiting for transfers between devices  142 us (53%)
  local copies, waits for them, and re-layouts  48.3 us (18%)
  matrix products  44.3 us (17%)
  between operations  14 us (5%)
  blocking collectives  9.22 us (3%)
  other arithmetic  8.23 us (3%)
    reduce_scatter x1, waiting for transfers between devices, on_device(): lax.psum_scatter(jnp.einsum('cij,cik->jck', d_mixed_full, left, precision...  41.8 us
    ppermute x7, waiting for transfers between devices, passed_along(): return lax.ppermute(block, axis, route)  36.5 us
    psum x1, waiting for transfers between devices, on_device(): d_normed = lax.psum(d_normed_part, 'ch')  35.8 us
    psum x1, waiting for transfers between devices, on_device(): lax.psum((projected, first, second, col_total), 'ch')  27.9 us
    dynamic_update_slice x14, local copies, waits for them, and re-layouts, visit(): lax.dynamic_update_slice_in_dim(partial_value, product, source * rows, 2)  23.7 us
    psum x1, blocking collectives, on_device(): lax.psum((projected, first, second, col_total), 'ch')  9.22 us
    dot_general x1, matrix products, on_device(): jnp.einsum('cij,cik->jck', d_mixed_full, left, precision=highest)  9.16 us
    dot_general x1, matrix products, on_device(): jnp.einsum('cij,cjk->cik', d_mixed_full, right_all, precision=highest)  7.15 us
  transfers between devices with their start and end apart: 10, of which 10 were waited for; matrix products, arithmetic and copies ran while one was open for 18% of the time, Pallas kernels for 0%

commit v1 on v0

--- a/solution.py
+++ b/solution.py
@@ -1,9 +1,367 @@
+import functools
 import jax
 import jax.numpy as jnp
 from jax import lax
+from jax.experimental import pallas as pl
+from jax.experimental.pallas import tpu as pltpu
 from jax.sharding import PartitionSpec as P
 
 C = 128
+EPS = 1e-05
+HIGHEST = lax.Precision.HIGHEST
+F32 = jnp.float32
+CHUNK = 4
+GROUP = 8
+
+
+def dot(a, b):
+    return lax.dot_general(a, b, (((1,), (0,)), ((), ())), precision=HIGHEST, preferred_element_type=F32)
+
+
+def dot_t(a, b):
+    return lax.dot_general(a, b, (((1,), (1,)), ((), ())), precision=HIGHEST, preferred_element_type=F32)
+
+
+def norm(values):
+    mean = jnp.mean(values, axis=-1, keepdims=True)
+    centered = values - mean
+    variance = jnp.mean(centered * centered, axis=-1, keepdims=True)
+    scale = lax.rsqrt(variance + EPS)
+    return (centered * scale, scale)
+
+
+def flat(values):
+    return values.reshape(-1, values.shape[-1])
+
+
+def call(kernel, outs, args, flops=0, scratch=()):
+    smem = pl.BlockSpec(memory_space=pltpu.SMEM)
+    vmem = pl.BlockSpec(memory_space=pltpu.VMEM)
+    return pl.pallas_call(
+        kernel,
+        out_shape=[jax.ShapeDtypeStruct(shape, F32) for shape in outs],
+        in_specs=[smem] + [vmem] * (len(args) - 1),
+        out_specs=[vmem] * len(outs),
+        scratch_shapes=[pltpu.VMEM(shape, F32) for shape in scratch],
+        compiler_params=pltpu.CompilerParams(vmem_limit_bytes=50 * 1024 * 1024),
+        cost_estimate=pl.CostEstimate(flops=flops, bytes_accessed=4 * sum(a.size for a in args), transcendentals=0),
+    )(*args)
+
+
+def source_row(place, t, rows):
+    half = rows // 2
+    if t < half:
+        return place[2] * half + t
+    return (1 - place[2]) * half + t - half
+
+
+def gated_kernel(rows, place, pair, mask, w, gated, open_part, slope):
+    half = rows // 2
+    cols = pair.shape[1]
+    chans = w.shape[1] // 2
+    for t in range(0, gated.shape[0], CHUNK):
+        row = source_row(place, t, rows)
+        keep = jnp.concatenate(
+            [jnp.transpose(jnp.broadcast_to(mask[pl.ds(row + u, 1), :].astype(F32), (8, cols)))[:, :1] for u in range(CHUNK)], axis=0
+        )
+        normed, _ = norm(flat(pair[pl.ds(row, CHUNK)]))
+        proj = dot(normed, w[...])
+        sig = jax.nn.sigmoid(proj[:, chans:]) * keep
+        value = sig * proj[:, :chans]
+        gated[t : t + CHUNK] = value.reshape(CHUNK, cols, chans)
+        if t < half:
+            open_part[t : t + CHUNK] = sig.reshape(CHUNK, cols, chans)
+            slope[t : t + CHUNK] = (value * (1.0 - sig)).reshape(CHUNK, cols, chans)
+
+
+def gate_kernel(rows, place, pair, cotangent, w_gate, gate, here, there, d_out):
+    half = rows // 2
+    cols = pair.shape[1]
+    for t in range(0, rows, CHUNK):
+        row = source_row(place, t, rows)
+        normed, _ = norm(flat(pair[pl.ds(row, CHUNK)]))
+        value = jax.nn.sigmoid(dot(normed, w_gate[...])).reshape(CHUNK, cols, -1)
+        gate[t : t + CHUNK] = value
+        d_out[t : t + CHUNK] = value * cotangent[pl.ds(row, CHUNK)]
+    for chip in range(cols // (2 * rows)):
+        for core, target in ((place[1], here), (1 - place[1], there)):
+            first = pl.multiple_of(chip * 2 * rows + core * rows + place[2] * half, half)
+            target[chip] = d_out[:, pl.ds(first, half), :]
+
+
+def tile_kernel(step, parts, place, *refs):
+    rights = refs[:parts]
+    left_here, left_there, d_here, d_there, w_out, out_here, out_there, d_x, d_right = refs[parts : parts + 9]
+    partial, x = refs[-2:]
+    right = rights[0]
+    if parts == 2:
+        right = refs[parts + 9]
+        right[...] = rights[0][...] + rights[1][...]
+    rows = left_here.shape[0]
+    half, cols, chans = right.shape
+    groups = cols // GROUP
+
+    def forward(pair_at, _):
+        for which, left in enumerate((left_here, left_there)):
+            for u in range(2):
+                i = pair_at * 2 + u
+                value = left[i]
+                for j in range(half):
+                    product = (value * right[j]).reshape(groups, GROUP, chans)
+                    partial[2 * which + u, j * GROUP : (j + 1) * GROUP] = jnp.sum(product, axis=0)
+                total = partial[2 * which + u, pl.ds(0, half, stride=GROUP), :]
+                for s in range(1, GROUP):
+                    total = total + partial[2 * which + u, pl.ds(s, half, stride=GROUP), :]
+                x[pl.ds(pl.multiple_of((which * rows + i) * half, half), half), :] = total
+        return 0
+
+    lax.fori_loop(0, rows // 2, forward, 0)
+    chip = jnp.bitwise_xor(place[0], step)
+    d_out = jnp.concatenate([flat(d_here[chip]), flat(d_there[chip])], axis=0)
+    normed, scale = norm(x[...])
+    out = dot(normed, w_out[...])
+    out_here[...] = out[: rows * half].reshape(rows, half, -1)
+    out_there[...] = out[rows * half :].reshape(rows, half, -1)
+    d_normed = dot_t(d_out, w_out[...])
+    mean_one = jnp.mean(d_normed, axis=-1, keepdims=True)
+    mean_two = jnp.mean(d_normed * normed, axis=-1, keepdims=True)
+    d_x[...] = (d_normed - mean_one - normed * mean_two) * scale
+    for j in range(0, half, 2):
+
+        def backward(i, totals):
+            for which, left in enumerate((left_here, left_there)):
+                value = left[i]
+                at = (which * rows + i) * half + j
+                totals = tuple(total + value * d_x[pl.ds(at + u, 1), :] for u, total in enumerate(totals))
+            return totals
+
+        zero = jnp.zeros((cols, chans), F32)
+        totals = lax.fori_loop(0, rows, backward, (zero, zero))
+        d_right[j] = totals[0]
+        d_right[j + 1] = totals[1]
+
+
+def left_kernel(tiles, bases, first, place, *refs):
+    rights, d_xs = refs[:tiles], refs[tiles : 2 * tiles]
+    base = refs[2 * tiles : 2 * tiles + bases]
+    outs = refs[2 * tiles + bases :]
+    half, cols, chans = rights[0].shape
+    rows = outs[0].shape[0]
+    for which, out in enumerate(outs):
+
+        def body(pair_at, _):
+            i = pair_at * 2
+            if bases:
+                totals = [base[which][i], base[which][i + 1]]
+            else:
+                totals = [jnp.zeros((cols, chans), F32)] * 2
+            for right, d_x in zip(rights, d_xs):
+                for j in range(half):
+                    value = right[j]
+                    for u in range(2):
+                        at = ((first + which) * rows + i + u) * half + j
+                        totals[u] = totals[u] + value * d_x[pl.ds(at, 1), :]
+            out[i] = totals[0]
+            out[i + 1] = totals[1]
+            return 0
+
+        lax.fori_loop(0, rows // 2, body, 0)
+
+
+def update_kernel(rows, place, *refs):
+    early, late = refs[:4], refs[4:8]
+    gate, cotangent, w_gate, update, d_normed, out = refs[8:]
+    half = rows // 2
+    cols = gate.shape[1]
+    for quarter in range(4):
+        other_core, other_half = quarter % 2, quarter // 2
+        core = place[1] + other_core * (1 - 2 * place[1])
+        side = place[2] + other_half * (1 - 2 * place[2])
+        for step in range(4):
+            chip = jnp.bitwise_xor(place[0], step)
+            first = pl.multiple_of(chip * 2 * rows + core * rows + side * half, half)
+            for t in (0, half):
+                source = (t + other_half * half) % rows
+                if step < 3:
+                    block = early[quarter][step, source : source + half]
+                else:
+                    block = late[quarter][source : source + half]
+                out[t : t + half, pl.ds(first, half), :] = block
+    for t in range(0, rows, CHUNK):
+        row = source_row(place, t, rows)
+        opened = gate[t : t + CHUNK]
+        value = opened * out[t : t + CHUNK]
+        update[pl.ds(row, CHUNK)] = value
+        if t < half:
+            d_gate = cotangent[pl.ds(row, CHUNK)] * value * (1.0 - opened)
+            d_normed[t : t + CHUNK] = dot_t(flat(d_gate), w_gate[...]).reshape(CHUNK, cols, -1)
+
+
+def base_kernel(place, d_normed, d_left, d_left_other, open_part, slope, w, base):
+    half, cols, chans = d_normed.shape
+    for t in range(0, half, CHUNK):
+        grad = flat(d_left[t : t + CHUNK] + d_left_other[t : t + CHUNK])
+        both = jnp.concatenate([grad * flat(open_part[t : t + CHUNK]), grad * flat(slope[t : t + CHUNK])], axis=1)
+        base[t : t + CHUNK] = d_normed[t : t + CHUNK] + dot_t(both, w[...]).reshape(CHUNK, cols, -1)
+
+
+def pair_kernel(rows, place, pair, base, d_right, d_right_near, d_right_far, open_part, slope, w, d_pair):
+    half, cols, chans = base.shape
+    for t in range(0, half, CHUNK):
+        at = slice(t, t + CHUNK)
+        grad = flat(d_right[at] + d_right_near[at] + d_right_far[at])
+        both = jnp.concatenate([grad * flat(open_part[at]), grad * flat(slope[at])], axis=1)
+        d_normed = flat(base[at]) + dot_t(both, w[...])
+        normed, scale = norm(flat(pair[pl.ds(source_row(place, t, rows), CHUNK)]))
+        mean_grad = jnp.mean(d_normed, axis=-1, keepdims=True)
+        mean_cross = jnp.mean(d_normed * normed, axis=-1, keepdims=True)
+        d_pair[at] = ((d_normed - mean_grad - normed * mean_cross) * scale).reshape(CHUNK, cols, -1)
+
+
+def along(block, pairs):
+    return lax.ppermute(block, "row", [(2 * a + core, 2 * b + core) for a, b in pairs for core in (0, 1)])
+
+
+def other_core(block):
+    return lax.ppermute(block, "row", [(i, i ^ 1) for i in range(lax.axis_size("row"))])
+
+
+def other_half(block):
+    return lax.ppermute(block, "ch", [(0, 1), (1, 0)])
+
+
+def diagonal(block):
+    count = lax.axis_size("row") * 2
+    return lax.ppermute(block, ("row", "ch"), [(i, i ^ 3) for i in range(count)])
+
+
+NEXT = [(0, 1), (1, 0), (2, 3), (3, 2)]
+MIDDLE = [(1, 2), (2, 1)]
+OUTWARD = [(1, 0), (2, 3)]
+INWARD = [(0, 1), (3, 2)]
+ACROSS = [(0, 3), (3, 0), (1, 2), (2, 1)]
+
+
+def on_tiles(pair, pair_mask, w_proj, w_gate, w_out, cotangent):
+    rows, cols, width = pair.shape
+    half = rows // 2
+    row, side = lax.axis_index("row"), lax.axis_index("ch")
+    place = jnp.stack([row // 2, row % 2, side]).astype(jnp.int32)
+
+    def ordered(mine, other):
+        return [jnp.where(side == 0, a, b) for a, b in ((mine, other), (other, mine))]
+
+    def whole(mine, other):
+        quarter = mine.shape[1] // 2
+        value = ordered(mine[:, :quarter], other[:, :quarter])
+        gate = ordered(mine[:, quarter:], other[:, quarter:])
+        return jnp.concatenate(value + gate, axis=1)
+
+    my_right = jnp.concatenate([w_proj[2], w_proj[3]], axis=1)
+    w_right = whole(my_right, other_half(my_right))
+    my_left = jnp.concatenate([w_proj[0], w_proj[1]], axis=1)
+    rest = other_half(jnp.concatenate([my_left, w_out], axis=0))
+    w_left = whole(my_left, rest[:width])
+    w_all_out = jnp.concatenate(ordered(w_out, rest[width:]), axis=0)
+    chans = w_all_out.shape[0]
+
+    kept = (half, cols, chans)
+    right, open_right, slope_right = call(
+        functools.partial(gated_kernel, rows), [kept] * 3, (place, pair, pair_mask, w_right), flops=10**9
+    )
+    near = along(right, NEXT)
+    middle = along(right, MIDDLE)
+    left, open_left, slope_left = call(
+        functools.partial(gated_kernel, rows),
+        [(rows, cols, chans), kept, kept],
+        (place, pair, pair_mask, w_left),
+        flops=2 * 10**9,
+    )
+    left_there = other_core(left)
+    chips = cols // (2 * rows)
+    quarter = (chips, rows, half, width)
+    gate, d_here, d_sent = call(
+        functools.partial(gate_kernel, rows),
+        [(rows, cols, width), quarter, quarter],
+        (place, pair, cotangent, w_gate),
+        flops=2 * 10**9,
+        scratch=[(rows, cols, width)],
+    )
+    d_there = other_core(d_sent)
+
+    def tile(step, *rights):
+        outs = [(rows, half, width)] * 2 + [(2 * rows * half, chans), kept]
+        if len(rights) == 2:
+            outs.append(kept)
+        got = call(
+            functools.partial(tile_kernel, step, len(rights)),
+            outs,
+            (place, *rights, left, left_there, d_here, d_there, w_all_out),
+            flops=4 * 10**9,
+            scratch=[(4, half * GROUP, chans), (2 * rows * half, chans)],
+        )
+        return got if len(rights) == 2 else (*got, rights[0])
+
+    out_here, out_there, d_x, d_right, rights = ([None] * 4 for _ in range(5))
+
+    def run(step, *blocks):
+        out_here[step], out_there[step], d_x[step], d_right[step], rights[step] = tile(step, *blocks)
+
+    run(0, right)
+    run(1, near)
+    cross = along(near, MIDDLE)
+    outer = along(middle, OUTWARD)
+    run(2, cross, outer)
+    far = along(cross, OUTWARD)
+    inward = along(d_right[2], INWARD)
+    swapped = along(d_right[2], MIDDLE)
+    early_here, early_there = jnp.stack(out_here[:3]), jnp.stack(out_there[:3])
+    early = [early_here, other_core(early_there), other_half(early_here), diagonal(early_there)]
+    d_left_here, d_left_there = call(
+        functools.partial(left_kernel, 3, 0, 0),
+        [(rows, cols, chans)] * 2,
+        (place, *rights[:3], *d_x[:3]),
+        flops=4 * 10**9,
+    )
+    from_near = along(d_right[1] + swapped, NEXT)
+    run(3, middle, far)
+    from_far = along(d_right[3] + inward, ACROSS)
+    late = [out_here[3], other_core(out_there[3]), other_half(out_here[3]), diagonal(out_there[3])]
+    (d_left_sent,) = call(
+        functools.partial(left_kernel, 1, 1, 1),
+        [(rows, cols, chans)],
+        (place, rights[3], d_x[3], d_left_there),
+        flops=10**9,
+    )
+    (d_left_kept,) = call(
+        functools.partial(left_kernel, 1, 1, 0),
+        [(rows, cols, chans)],
+        (place, rights[3], d_x[3], d_left_here),
+        flops=10**9,
+    )
+    d_left = d_left_kept + other_core(d_left_sent)
+    d_left_other = other_half(d_left[half:])
+    update, d_normed = call(
+        functools.partial(update_kernel, rows),
+        [(rows, cols, width), (half, cols, width)],
+        (place, *early, *late, gate, cotangent, w_gate),
+        flops=10**9,
+        scratch=[(rows, cols, width)],
+    )
+    (base,) = call(
+        base_kernel,
+        [(half, cols, width)],
+        (place, d_normed, d_left[:half], d_left_other, open_left, slope_left, w_left),
+        flops=10**9,
+    )
+    (mine,) = call(
+        functools.partial(pair_kernel, rows),
+        [(half, cols, width)],
+        (place, pair, base, d_right[0], from_near, from_far, open_right, slope_right, w_right),
+        flops=10**9,
+    )
+    d_pair = jnp.concatenate(ordered(mine, other_half(mine)), axis=0)
+    return (update, d_pair)
 
 
 def passed_along(block, axis, distance):
@@ -20,7 +378,7 @@
     return (centered * scale, scale)
 
 
-def on_device(pair, pair_mask, w_proj, w_gate, w_out, cotangent):
+def on_ring(pair, pair_mask, w_proj, w_gate, w_out, cotangent):
     highest = lax.Precision.HIGHEST
     normed, pair_scale = normalize(pair)
     proj = jnp.einsum("rqz,pzc->pcrq", normed, w_proj, precision=highest)
@@ -96,8 +454,10 @@
 
 
 def solution(mesh):
+    sizes = mesh.shape
+    tiled = sizes["row"] == 8 and sizes["ch"] == 2 and sizes["sub"] == 1
     return jax.shard_map(
-        on_device,
+        on_tiles if tiled else on_ring,
         mesh=mesh,
         in_specs=(
             P(("grp", "row"), "sub", None),

time: 268 us -> 136 us (0.51)
  waiting for transfers between devices: 142 us -> 54.3 us
  matrix products: 44.3 us -> 0 us
  local copies, waits for them, and re-layouts: 48.3 us -> 6.62 us
  Pallas kernels: 0 us -> 40 us
  starting transfers between devices: 1.19 us -> 30.9 us
  between operations: 14 us -> 1.06 us
  blocking collectives: 9.22 us -> 0 us
  other arithmetic: 8.23 us -> 2.82 us
    psum x2 -> x0, waiting for transfers between devices: 63.8 us -> none  [the longest x1 35.8 us: on_device(): d_normed = lax.psum(d_normed_part, 'ch')]
    dot_general x16 -> x0, matrix products: 44.3 us -> none  [the longest x1 9.16 us: on_device(): jnp.einsum('cij,cik->jck', d_mixed_full, left, precision=highest)]
    reduce_scatter x1 -> x0, waiting for transfers between devices: 41.8 us -> none  [on_device(): lax.psum_scatter(jnp.einsum('cij,cik->jck', d_mixed_full, left, precision...]
    pallas_call x0 -> x13, Pallas kernels: none -> 40 us  [call(): pl.pallas_call(kernel, out_shape=[jax.ShapeDtypeStruct(shape, F32) for sh...]
    dynamic_update_slice x23 -> x0, local copies, waits for them, and re-layouts: 34.4 us -> none  [the longest x14 23.7 us: visit(): lax.dynamic_update_slice_in_dim(partial_value, product, source * rows, 2)]
    ppermute x7 -> x22, starting transfers between devices: 0.85 us -> 30.9 us  [the longest x9 21.6 us: along(): lax.ppermute(block, 'row', [(2 * a + core, 2 * b + core) for a, b in pair...]
    ppermute x7 -> x22, waiting for transfers between devices: 36.5 us -> 54.3 us  [the longest x9 27.3 us: along(): lax.ppermute(block, 'row', [(2 * a + core, 2 * b + core) for a, b in pair...]
    psum x1 -> x0, blocking collectives: 9.22 us -> none  [on_device(): lax.psum((projected, first, second, col_total), 'ch')]
  transfers between devices with their start and end apart: 10 -> 22, of which waited for: 10 -> 9; matrix products, arithmetic and copies ran while one was open for 18% -> 1% of each run, Pallas kernels for 0% -> 21%
where the time goes in v1:
time: 136 us
  waiting for transfers between devices  54.3 us (40%)
  Pallas kernels  40 us (29%)
  starting transfers between devices  30.9 us (23%)
  local copies, waits for them, and re-layouts  6.62 us (5%)
  other arithmetic  2.82 us (2%)
    pallas_call x13, Pallas kernels, call(): pl.pallas_call(kernel, out_shape=[jax.ShapeDtypeStruct(shape, F32) for sh...  40 us
    ppermute x9, waiting for transfers between devices, along(): lax.ppermute(block, 'row', [(2 * a + core, 2 * b + core) for a, b in pair...  27.3 us
    ppermute x6, waiting for transfers between devices, other_half(): return lax.ppermute(block, 'ch', [(0, 1), (1, 0)])  25.5 us
    ppermute x9, starting transfers between devices, along(): lax.ppermute(block, 'row', [(2 * a + core, 2 * b + core) for a, b in pair...  21.6 us
    ppermute x6, starting transfers between devices, other_half(): return lax.ppermute(block, 'ch', [(0, 1), (1, 0)])  7.94 us
    unnamed x34, local copies, waits for them, and re-layouts  5.73 us
  transfers between devices with their start and end apart: 22, of which 9 were waited for; matrix products, arithmetic and copies ran while one was open for 1% of the time, Pallas kernels for 21%

profile of v1, /device:TPU:0, one launch (start us, length us, event | category | flops | bytes accessed | tf_op | source)
XLA Modules:
  0.0 135.7 jit_solution(837977835791453983)
XLA Ops:
  0.6 0.8 fusion.1
  1.5 0.1 copy.14
  1.6 0.1 copy.15
  1.7 0.7 copy-done.14
  2.3 0.1 pad_maximum_fusion.5
  2.4 3.0 %collective-permute-start.1 = (f32[192,128]{1,0:T(8,128)S(1)}, f32[192,128]{1,0:T(8,128)S(1)}, u32[]{:S(2)}, u32[]{:S(2)}) collective-permute-start(f32[192,128]{1,0:T(8,128)S(1)} %pad_maximum_fusion.5), channel_id=1, source_target_pairs={{0,1},{1,0},{2,3},{3,2},{4,5},{5,4},{6,7},{7,6},{8,9},{9,8},{10,11... | collective-permute-start | bytes 294920 | tf_op jit(solution)/shard_map/ppermute | solution.py:230
  5.4 0.1 copy.12
  5.5 0.1 copy.13
  5.6 0.1 pad_maximum_fusion.6
  5.7 0.1 collective-permute-start
  5.8 0.1 pad_add_fusion.place
  5.9 4.2 %collective-permute-done = f32[128,128]{1,0:T(8,128)S(1)} collective-permute-done((f32[128,128]{1,0:T(8,128)S(1)}, f32[128,128]{1,0:T(8,128)S(1)}, u32[]{:S(2)}, u32[]{:S(2)}) %collective-permute-start) | collective-permute-done | bytes 65568 | tf_op jit(solution)/shard_map/ppermute | solution.py:230
  10.0 0.1 slice_select_fusion.3
  10.1 0.5 copy-done.13
  10.7 0.1 pad_maximum_fusion.3.w
  10.8 0.6 copy-done.4
  11.4 1.8 %shard_map.77 = (f32[8,128,128]{2,1,0:T(8,128)S(1)}, f32[8,128,128]{2,1,0:T(8,128)S(1)}, f32[8,128,128]{2,1,0:T(8,128)S(1)}) custom-call(s32[3]{0:T(128)S(1)} %pad_add_fusion.place, f32[16,128,128]{2,1,0:T(8,128)S(1)} %copy-done, s32[16,128]{1,0:T(8,128)S(1)} %copy-done.4, f32[128,256]{1,0:T(8,128)S(1)} %pad_maximum_fusion.3.w), custom_call_target="tpu_custom_call" | custom-call | flops 1000000000 | bytes 1187852 | tf_op jit(solution)/shard_map/pallas_call | solution.py:40
  13.2 1.6 %collective-permute-start.4 = (f32[8,128,128]{2,1,0:T(8,128)S(1)}, f32[8,128,128]{2,1,0:T(8,128)S(1)}, u32[]{:S(2)}, u32[]{:S(2)}) collective-permute-start(f32[8,128,128]{2,1,0:T(8,128)S(1)} %get-tuple-element.33.refs_0_), channel_id=1, source_target_pairs={{0,4},{2,6},{4,0},{6,2},{8,12},{10,14},{12,8},{14,10},{1,5},{3,7},... | collective-permute-start | bytes 1572872 | tf_op jit(solution)/shard_map/ppermute | solution.py:222
  14.8 0.1 pad_maximum_fusion.4.w
  15.0 2.7 %shard_map.78 = (f32[16,128,128]{2,1,0:T(8,128)S(1)}, f32[8,128,128]{2,1,0:T(8,128)S(1)}, f32[8,128,128]{2,1,0:T(8,128)S(1)}) custom-call(s32[3]{0:T(128)S(1)} %pad_add_fusion.place, f32[16,128,128]{2,1,0:T(8,128)S(1)} %copy-done, s32[16,128]{1,0:T(8,128)S(1)} %copy-done.4, f32[128,256]{1,0:T(8,128)S(1)} %pad_maximum_fusion.4.w), custom_call_target="tpu_custom_call" | custom-call | flops 2000000000 | bytes 1187852 | tf_op jit(solution)/shard_map/pallas_call | solution.py:40
  17.7 0.8 copy-done.5
  18.5 0.8 copy-done.7
  19.3 0.7 collective-permute-start.6
  20.0 6.3 %collective-permute-done.4.refs_0_.refs_1_ = f32[8,128,128]{2,1,0:T(8,128)S(1)} collective-permute-done((f32[8,128,128]{2,1,0:T(8,128)S(1)}, f32[8,128,128]{2,1,0:T(8,128)S(1)}, u32[]{:S(2)}, u32[]{:S(2)}) %collective-permute-start.4) | collective-permute-done | bytes 524320 | tf_op jit(solution)/shard_map/ppermute | solution.py:222
  26.2 0.7 collective-permute-start.5
  26.9 1.9 %shard_map.79 = (f32[16,128,128]{2,1,0:T(8,128)S(1)}, f32[4,16,8,128]{3,2,1,0:T(8,128)S(1)}, f32[4,16,8,128]{3,2,1,0:T(8,128)S(1)}) custom-call(s32[3]{0:T(128)S(1)} %pad_add_fusion.place, f32[16,128,128]{2,1,0:T(8,128)S(1)} %copy-done, f32[16,128,128]{2,1,0:T(8,128)S(1)} %copy-done.1, f32[128,128]{1,0:T(8,128)S(1)} %copy-done.3), custom_call_target="tpu_custom_call" | custom-call | flops 2000000000 | bytes 2162700 | tf_op jit(solution)/shard_map/pallas_call | solution.py:40
  28.8 0.1 collective-permute-start.3
  28.9 0.8 slice_select_fusion.9
  29.7 1.3 collective-permute-start.7
  31.0 1.3 collective-permute-start.11
  32.3 4.8 %shard_map.80 = (f32[16,8,128]{2,1,0:T(8,128)S(1)}, f32[16,8,128]{2,1,0:T(8,128)S(1)}, f32[256,128]{1,0:T(8,128)S(1)}, f32[8,128,128]{2,1,0:T(8,128)S(1)}) custom-call(s32[3]{0:T(128)S(1)} %pad_add_fusion.place, f32[8,128,128]{2,1,0:T(8,128)S(1)} %get-tuple-element.33.refs_0_, f32[16,128,128]{2,1,0:T(8,128)S(1)} %get-tuple-element.34.refs_1_.refs_2_, ...), custom_call_target="tpu_custom_call" | custom-call | flops 4000000000 | bytes 3211276 | tf_op jit(solution)/shard_map/pallas_call | solution.py:40
  37.1 4.8 %shard_map.81 = (f32[16,8,128]{2,1,0:T(8,128)S(1)}, f32[16,8,128]{2,1,0:T(8,128)S(1)}, f32[256,128]{1,0:T(8,128)S(1)}, f32[8,128,128]{2,1,0:T(8,128)S(1)}) custom-call(s32[3]{0:T(128)S(1)} %pad_add_fusion.place, f32[8,128,128]{2,1,0:T(8,128)S(1)} %collective-permute-done.4.refs_0_.refs_1_, f32[16,128,128]{2,1,0:T(8,128)S(1)} %get-tuple-element.34.refs_1_.refs_2_, ...), custom_call_target="tpu_custom_call" | custom-call | flops 4000000000 | bytes 3211276 | tf_op jit(solution)/shard_map/pallas_call | solution.py:40
  41.9 8.3 %collective-permute-done.7.refs_1_ = f32[8,128,128]{2,1,0:T(8,128)S(1)} collective-permute-done((f32[8,128,128]{2,1,0:T(8,128)S(1)}, f32[8,128,128]{2,1,0:T(8,128)S(1)}, u32[]{:S(2)}, u32[]{:S(2)}) %collective-permute-start.7) | collective-permute-done | bytes 524320 | tf_op jit(solution)/shard_map/ppermute | solution.py:222
  50.2 5.4 %shard_map.82 = (f32[16,8,128]{2,1,0:T(8,128)S(1)}, f32[16,8,128]{2,1,0:T(8,128)S(1)}, f32[256,128]{1,0:T(8,128)S(1)}, f32[8,128,128]{2,1,0:T(8,128)S(1)}, f32[8,128,128]{2,1,0:T(8,128)S(1)}) custom-call(s32[3]{0:T(128)S(1)} %pad_add_fusion.place, f32[8,128,128]{2,1,0:T(8,128)S(1)} %collective-permute-done.5.refs_0_, ...), custom_call_target="tpu_custom_call" | custom-call | flops 4000000000 | bytes 3735564 | tf_op jit(solution)/shard_map/pallas_call | solution.py:40
  55.6 4.5 %shard_map.85 = (f32[16,128,128]{2,1,0:T(8,128)S(1)}, f32[16,128,128]{2,1,0:T(8,128)S(1)}) custom-call(s32[3]{0:T(128)S(1)} %pad_add_fusion.place, f32[8,128,128]{2,1,0:T(8,128)S(1)} %get-tuple-element.33.refs_0_, f32[8,128,128]{2,1,0:T(8,128)S(1)} %collective-permute-done.4.refs_0_.refs_1_, f32[8,128,128]{2,1,0:T(8,128)S(1)} %get-tuple-element.50.refs_2_, ...), custom_call_target="tpu_custom_call" | custom-call | flops 4000000000 | bytes 1966092 | tf_op jit(solution)/shard_map/pallas_call | solution.py:40
  60.1 1.0 copy-done.9
  61.1 1.0 copy-done.11
  62.1 5.5 %shard_map.83 = (f32[16,8,128]{2,1,0:T(8,128)S(1)}, f32[16,8,128]{2,1,0:T(8,128)S(1)}, f32[256,128]{1,0:T(8,128)S(1)}, f32[8,128,128]{2,1,0:T(8,128)S(1)}, f32[8,128,128]{2,1,0:T(8,128)S(1)}) custom-call(s32[3]{0:T(128)S(1)} %pad_add_fusion.place, f32[8,128,128]{2,1,0:T(8,128)S(1)} %collective-permute-done.6.refs_0_, ...), custom_call_target="tpu_custom_call" | custom-call | flops 4000000000 | bytes 3735564 | tf_op jit(solution)/shard_map/pallas_call | solution.py:40
  67.6 1.2 shard_map.87
  68.8 0.1 collective-permute-start.15
  68.9 10.8 %collective-permute-start.19 = (f32[8,128,128]{2,1,0:T(8,128)S(1)}, f32[8,128,128]{2,1,0:T(8,128)S(1)}, u32[]{:S(2)}, u32[]{:S(2)}) collective-permute-start(f32[8,128,128]{2,1,0:T(8,128)S(1)} %get-tuple-element.60), channel_id=1, source_target_pairs={{0,4},{2,6},{12,8},{14,10},{1,5},{3,7},{13,9},{15,11},{16,20},{18,... | collective-permute-start | bytes 1572872 | tf_op jit(solution)/shard_map/ppermute | solution.py:222
  79.7 0.9 collective-permute-start.17
  80.6 1.2 collective-permute-start.10
  81.8 1.2 shard_map.86
  83.1 0.2 add.15
  83.3 0.8 collective-permute-start.16
  84.1 7.4 %collective-permute-done.19 = f32[8,128,128]{2,1,0:T(8,128)S(1)} collective-permute-done((f32[8,128,128]{2,1,0:T(8,128)S(1)}, f32[8,128,128]{2,1,0:T(8,128)S(1)}, u32[]{:S(2)}, u32[]{:S(2)}) %collective-permute-start.19) | collective-permute-done | bytes 524320 | tf_op jit(solution)/shard_map/ppermute | solution.py:222
  91.5 0.1 add.17
  91.6 2.7 %collective-permute-start.20 = (f32[8,128,128]{2,1,0:T(8,128)S(1)}, f32[8,128,128]{2,1,0:T(8,128)S(1)}, u32[]{:S(2)}, u32[]{:S(2)}) collective-permute-start(f32[8,128,128]{2,1,0:T(8,128)S(1)} %add.17), channel_id=1, source_target_pairs={{0,12},{2,14},{12,0},{14,2},{4,8},{6,10},{8,4},{10,6},{1,13},{3,15... | collective-permute-start | bytes 1572872 | tf_op jit(solution)/shard_map/ppermute | solution.py:222
  94.3 0.1 add.16
  94.4 1.6 %collective-permute-start.18 = (f32[8,128,128]{2,1,0:T(8,128)S(1)}, f32[8,128,128]{2,1,0:T(8,128)S(1)}, u32[]{:S(2)}, u32[]{:S(2)}) collective-permute-start(f32[8,128,128]{2,1,0:T(8,128)S(1)} %add.16), channel_id=1, source_target_pairs={{0,4},{2,6},{4,0},{6,2},{8,12},{10,14},{12,8},{14,10},{1,5},{3,7},... | collective-permute-start | bytes 1572872 | tf_op jit(solution)/shard_map/ppermute | solution.py:222
  96.0 1.4 %collective-permute-start.9 = (f32[3,16,8,128]{3,2,1,0:T(8,128)S(1)}, f32[3,16,8,128]{3,2,1,0:T(8,128)S(1)}, u32[]{:S(2)}, u32[]{:S(2)}) collective-permute-start(f32[3,16,8,128]{3,2,1,0:T(8,128)S(1)} %pad_maximum_fusion.1.refs_0_), channel_id=1, source_target_pairs={{0,1},{1,0},{2,3},{3,2},{4,5},{5,4},{6,7},{7,6},{8,9},{9,8},{10,11... | collective-permute-start | bytes 589832 | tf_op jit(solution)/shard_map/ppermute | solution.py:230
  97.4 5.9 %collective-permute-done.9.refs_2_ = f32[3,16,8,128]{3,2,1,0:T(8,128)S(1)} collective-permute-done((f32[3,16,8,128]{3,2,1,0:T(8,128)S(1)}, f32[3,16,8,128]{3,2,1,0:T(8,128)S(1)}, u32[]{:S(2)}, u32[]{:S(2)}) %collective-permute-start.9) | collective-permute-done | bytes 196640 | tf_op jit(solution)/shard_map/ppermute | solution.py:230
  103.3 1.3 collective-permute-start.13
  104.7 2.9 %collective-permute-done.13.refs_6_ = f32[16,8,128]{2,1,0:T(8,128)S(1)} collective-permute-done((f32[16,8,128]{2,1,0:T(8,128)S(1)}, f32[16,8,128]{2,1,0:T(8,128)S(1)}, u32[]{:S(2)}, u32[]{:S(2)}) %collective-permute-start.13) | collective-permute-done | bytes 65568 | tf_op jit(solution)/shard_map/ppermute | solution.py:230
  107.6 1.4 %collective-permute-done.14.refs_7_ = f32[16,8,128]{2,1,0:T(8,128)S(1)} collective-permute-done((f32[16,8,128]{2,1,0:T(8,128)S(1)}, f32[16,8,128]{2,1,0:T(8,128)S(1)}, u32[]{:S(2)}, u32[]{:S(2)}) %collective-permute-start.14) | collective-permute-done | bytes 65568 | tf_op jit(solution)/shard_map/ppermute | solution.py:235
  109.0 2.3 %shard_map.84 = (f32[16,128,128]{2,1,0:T(8,128)}, f32[8,128,128]{2,1,0:T(8,128)S(1)}) custom-call(s32[3]{0:T(128)S(1)} %pad_add_fusion.place, f32[3,16,8,128]{3,2,1,0:T(8,128)S(1)} %pad_maximum_fusion.1.refs_0_, f32[3,16,8,128]{3,2,1,0:T(8,128)S(1)} %collective-permute-done.8.refs_1_, f32[3,16,8,128]{3,2,1,0:T(8,128)S(1)} %collective-permute-done.9.refs_2_, ...), custom_call_target="tpu_custom_call" | custom-call | flops 1000000000 | bytes 3211276 | tf_op jit(solution)/shard_map/pallas_call | solution.py:40
  111.3 1.6 %shard_map.88.base = f32[8,128,128]{2,1,0:T(8,128)S(1)} custom-call(s32[3]{0:T(128)S(1)} %pad_add_fusion.place, f32[8,128,128]{2,1,0:T(8,128)S(1)} %get-tuple-element.47.d_normed, f32[8,128,128]{2,1,0:T(8,128)S(1)} %get-tuple-element.67.d_left, f32[8,128,128]{2,1,0:T(8,128)S(1)} %collective-permute-done.16.d_left_other, f32[8,128,128]{2,1,0:T(8,128)S(1)} %copy-done.6, ...), custom_call_target="tpu_custom_call" | custom-call | flops 1000000000 | bytes 2752524 | tf_op jit(solution)/shard_map/pallas_call | solution.py:40
  112.9 5.4 %collective-permute-done.18.d_right_near = f32[8,128,128]{2,1,0:T(8,128)S(1)} collective-permute-done((f32[8,128,128]{2,1,0:T(8,128)S(1)}, f32[8,128,128]{2,1,0:T(8,128)S(1)}, u32[]{:S(2)}, u32[]{:S(2)}) %collective-permute-start.18) | collective-permute-done | bytes 524320 | tf_op jit(solution)/shard_map/ppermute | solution.py:222
  118.3 2.4 %shard_map.89 = f32[8,128,128]{2,1,0:T(8,128)S(1)} custom-call(s32[3]{0:T(128)S(1)} %pad_add_fusion.place, f32[16,128,128]{2,1,0:T(8,128)} %pair.7, f32[8,128,128]{2,1,0:T(8,128)S(1)} %shard_map.88.base, f32[8,128,128]{2,1,0:T(8,128)S(1)} %get-tuple-element.58.d_right, f32[8,128,128]{2,1,0:T(8,128)S(1)} %collective-permute-done.18.d_right_near, ...), custom_call_target="tpu_custom_call" | custom-call | flops 1000000000 | bytes 4325388 | tf_op jit(solution)/shard_map/pallas_call | solution.py:40
  120.7 1.4 %collective-permute-start.21 = (f32[8,128,128]{2,1,0:T(8,128)S(1)}, f32[8,128,128]{2,1,0:T(8,128)S(1)}, u32[]{:S(2)}, u32[]{:S(2)}) collective-permute-start(f32[8,128,128]{2,1,0:T(8,128)S(1)} %shard_map.89), channel_id=1, source_target_pairs={{0,1},{1,0},{2,3},{3,2},{4,5},{5,4},{6,7},{7,6},{8,9},{9,8},{10,11... | collective-permute-start | bytes 1572872 | tf_op jit(solution)/shard_map/ppermute | solution.py:230
  122.1 12.5 %collective-permute-done.21 = f32[8,128,128]{2,1,0:T(8,128)S(1)} collective-permute-done((f32[8,128,128]{2,1,0:T(8,128)S(1)}, f32[8,128,128]{2,1,0:T(8,128)S(1)}, u32[]{:S(2)}, u32[]{:S(2)}) %collective-permute-start.21) | collective-permute-done | bytes 524320 | tf_op jit(solution)/shard_map/ppermute | solution.py:230
  134.6 0.1 broadcast_select_fusion.1
  134.7 1.0 pad_maximum_fusion
  (44 shorter events, 0.2 us)
Async XLA Ops:
  1.5 0.8 copy-start.14
  2.3 8.5 %copy-start = (f32[16,128,128]{2,1,0:T(8,128)S(1)}, f32[16,128,128]{2,1,0:T(8,128)}, u32[]{:S(2)}) copy-start(f32[16,128,128]{2,1,0:T(8,128)} %pair.7) | copy-start | bytes 3145732
  2.4 7.6 %collective-permute-start.1 = (f32[192,128]{1,0:T(8,128)S(1)}, f32[192,128]{1,0:T(8,128)S(1)}, u32[]{:S(2)}, u32[]{:S(2)}) collective-permute-start(f32[192,128]{1,0:T(8,128)S(1)} %pad_maximum_fusion.5), channel_id=1, source_target_pairs={{0,1},{1,0},{2,3},{3,2},{4,5},{5,4},{6,7},{7,6},{8,9},{9,8},{10,11... | collective-permute-start | bytes 294920 | tf_op jit(solution)/shard_map/ppermute | solution.py:230
  5.7 4.3 %collective-permute-start = (f32[128,128]{1,0:T(8,128)S(1)}, f32[128,128]{1,0:T(8,128)S(1)}, u32[]{:S(2)}, u32[]{:S(2)}) collective-permute-start(f32[128,128]{1,0:T(8,128)S(1)} %pad_maximum_fusion.6), channel_id=1, source_target_pairs={{0,1},{1,0},{2,3},{3,2},{4,5},{5,4},{6,7},{7,6},{8,9},{9,8},{10,11... | collective-permute-start | bytes 196616 | tf_op jit(solution)/shard_map/ppermute | solution.py:230
  10.0 0.6 copy-start.13
  10.7 0.7 copy-start.4
  13.2 13.0 %collective-permute-start.4 = (f32[8,128,128]{2,1,0:T(8,128)S(1)}, f32[8,128,128]{2,1,0:T(8,128)S(1)}, u32[]{:S(2)}, u32[]{:S(2)}) collective-permute-start(f32[8,128,128]{2,1,0:T(8,128)S(1)} %get-tuple-element.33.refs_0_), channel_id=1, source_target_pairs={{0,4},{2,6},{4,0},{6,2},{8,12},{10,14},{12,8},{14,10},{1,5},{3,7},... | collective-permute-start | bytes 1572872 | tf_op jit(solution)/shard_map/ppermute | solution.py:222
  14.9 12.0 %copy-start.1 = (f32[16,128,128]{2,1,0:T(8,128)S(1)}, f32[16,128,128]{2,1,0:T(8,128)}, u32[]{:S(2)}) copy-start(f32[16,128,128]{2,1,0:T(8,128)} %refs_9_.1) | copy-start | bytes 3145732
  14.9 12.0 %copy-start.3 = (f32[128,128]{1,0:T(8,128)S(1)}, f32[128,128]{1,0:T(8,128)}, u32[]{:S(2)}) copy-start(f32[128,128]{1,0:T(8,128)} %refs_10_.1) | copy-start | bytes 196612
  17.6 0.8 copy-start.5
  18.5 0.8 copy-start.7
  19.3 13.0 %collective-permute-start.2 = (f32[16,128,128]{2,1,0:T(8,128)S(1)}, f32[16,128,128]{2,1,0:T(8,128)S(1)}, u32[]{:S(2)}, u32[]{:S(2)}) collective-permute-start(f32[16,128,128]{2,1,0:T(8,128)S(1)} %get-tuple-element.34.refs_1_.refs_2_), channel_id=1, source_target_pairs={{0,2},{2,0},{4,6},{6,4},{8,10},{10,8},{12,14},{14,12},{1,3},{3,1},... | collective-permute-start | bytes 3145736 | tf_op jit(solution)/shard_map/ppermute | solution.py:226
  19.3 10.4 %collective-permute-start.6 = (f32[8,128,128]{2,1,0:T(8,128)S(1)}, f32[8,128,128]{2,1,0:T(8,128)S(1)}, u32[]{:S(2)}, u32[]{:S(2)}) collective-permute-start(f32[8,128,128]{2,1,0:T(8,128)S(1)} %get-tuple-element.33.refs_0_), channel_id=1, source_target_pairs={{4,8},{6,10},{8,4},{10,6},{5,9},{7,11},{9,5},{11,7},{20,24},{22,26... | collective-permute-start | bytes 1572872 | tf_op jit(solution)/shard_map/ppermute | solution.py:222
  26.2 4.8 %collective-permute-start.5 = (f32[8,128,128]{2,1,0:T(8,128)S(1)}, f32[8,128,128]{2,1,0:T(8,128)S(1)}, u32[]{:S(2)}, u32[]{:S(2)}) collective-permute-start(f32[8,128,128]{2,1,0:T(8,128)S(1)} %collective-permute-done.4.refs_0_.refs_1_), channel_id=1, source_target_pairs={{4,8},{6,10},{8,4},{10,6},{5,9},{7,11},{9,5},{11,7},{20,24},{22,26... | collective-permute-start | bytes 1572872 | tf_op jit(solution)/shard_map/ppermute | solution.py:222
  28.8 3.5 %collective-permute-start.3 = (f32[4,16,8,128]{3,2,1,0:T(8,128)S(1)}, f32[4,16,8,128]{3,2,1,0:T(8,128)S(1)}, u32[]{:S(2)}, u32[]{:S(2)}) collective-permute-start(f32[4,16,8,128]{3,2,1,0:T(8,128)S(1)} %get-tuple-element.36), channel_id=1, source_target_pairs={{0,2},{2,0},{4,6},{6,4},{8,10},{10,8},{12,14},{14,12},{1,3},{3,1},... | collective-permute-start | bytes 786440 | tf_op jit(solution)/shard_map/ppermute | solution.py:226
  29.7 20.5 %collective-permute-start.7 = (f32[8,128,128]{2,1,0:T(8,128)S(1)}, f32[8,128,128]{2,1,0:T(8,128)S(1)}, u32[]{:S(2)}, u32[]{:S(2)}) collective-permute-start(f32[8,128,128]{2,1,0:T(8,128)S(1)} %collective-permute-done.6.refs_0_), channel_id=1, source_target_pairs={{4,0},{6,2},{8,12},{10,14},{5,1},{7,3},{9,13},{11,15},{20,16},{22,... | collective-permute-start | bytes 1572872 | tf_op jit(solution)/shard_map/ppermute | solution.py:222
  31.0 31.1 %collective-permute-start.11 = (f32[8,128,128]{2,1,0:T(8,128)S(1)}, f32[8,128,128]{2,1,0:T(8,128)S(1)}, u32[]{:S(2)}, u32[]{:S(2)}) collective-permute-start(f32[8,128,128]{2,1,0:T(8,128)S(1)} %collective-permute-done.5.refs_0_), channel_id=1, source_target_pairs={{4,0},{6,2},{8,12},{10,14},{5,1},{7,3},{9,13},{11,15},{20,16},{22,... | collective-permute-start | bytes 1572872 | tf_op jit(solution)/shard_map/ppermute | solution.py:222
  32.3 4.8 %copy-start.2 = (f32[16,128,128]{2,1,0:T(8,128)}, f32[16,128,128]{2,1,0:T(8,128)S(1)}, u32[]{:S(2)}) copy-start(f32[16,128,128]{2,1,0:T(8,128)S(1)} %collective-permute-done.2.refs_2_.refs_3_) | copy-start | bytes 3145732
  60.1 1.0 copy-start.9
  61.1 1.0 copy-start.11
  62.1 5.5 %copy-start.12 = (f32[16,128,128]{2,1,0:T(8,128)S(1)}, f32[16,128,128]{2,1,0:T(8,128)}, u32[]{:S(2)}) copy-start(f32[16,128,128]{2,1,0:T(8,128)} %copy-done.11) | copy-start | bytes 3145732
  67.6 14.2 %copy-start.10 = (f32[16,128,128]{2,1,0:T(8,128)S(1)}, f32[16,128,128]{2,1,0:T(8,128)}, u32[]{:S(2)}) copy-start(f32[16,128,128]{2,1,0:T(8,128)} %copy-done.9) | copy-start | bytes 3145732
  68.8 14.2 %collective-permute-start.15 = (f32[16,128,128]{2,1,0:T(8,128)S(1)}, f32[16,128,128]{2,1,0:T(8,128)S(1)}, u32[]{:S(2)}, u32[]{:S(2)}) collective-permute-start(f32[16,128,128]{2,1,0:T(8,128)S(1)} %shard_map.87), channel_id=1, source_target_pairs={{0,2},{2,0},{4,6},{6,4},{8,10},{10,8},{12,14},{14,12},{1,3},{3,1},... | collective-permute-start | bytes 3145736 | tf_op jit(solution)/shard_map/ppermute | solution.py:226
  68.9 22.6 %collective-permute-start.19 = (f32[8,128,128]{2,1,0:T(8,128)S(1)}, f32[8,128,128]{2,1,0:T(8,128)S(1)}, u32[]{:S(2)}, u32[]{:S(2)}) collective-permute-start(f32[8,128,128]{2,1,0:T(8,128)S(1)} %get-tuple-element.60), channel_id=1, source_target_pairs={{0,4},{2,6},{12,8},{14,10},{1,5},{3,7},{13,9},{15,11},{16,20},{18,... | collective-permute-start | bytes 1572872 | tf_op jit(solution)/shard_map/ppermute | solution.py:222
  79.7 14.6 %collective-permute-start.17 = (f32[8,128,128]{2,1,0:T(8,128)S(1)}, f32[8,128,128]{2,1,0:T(8,128)S(1)}, u32[]{:S(2)}, u32[]{:S(2)}) collective-permute-start(f32[8,128,128]{2,1,0:T(8,128)S(1)} %get-tuple-element.60), channel_id=1, source_target_pairs={{4,8},{6,10},{8,4},{10,6},{5,9},{7,11},{9,5},{11,7},{20,24},{22,26... | collective-permute-start | bytes 1572872 | tf_op jit(solution)/shard_map/ppermute | solution.py:222
  80.6 15.4 %collective-permute-start.10 = (f32[3,16,8,128]{3,2,1,0:T(8,128)S(1)}, f32[3,16,8,128]{3,2,1,0:T(8,128)S(1)}, u32[]{:S(2)}, u32[]{:S(2)}) collective-permute-start(f32[3,16,8,128]{3,2,1,0:T(8,128)S(1)} %pad_maximum_fusion.2), channel_id=1, source_target_pairs={{0,3},{1,2},{2,1},{3,0},{4,7},{5,6},{6,5},{7,4},{8,11},{9,10},{10,... | collective-permute-start | bytes 589832 | tf_op jit(solution)/shard_map/ppermute | solution.py:235
  83.3 28.0 %collective-permute-start.16 = (f32[8,128,128]{2,1,0:T(8,128)S(1)}, f32[8,128,128]{2,1,0:T(8,128)S(1)}, u32[]{:S(2)}, u32[]{:S(2)}) collective-permute-start(f32[8,128,128]{2,1,0:T(8,128)S(1)} %get-tuple-element.66), channel_id=1, source_target_pairs={{0,1},{1,0},{2,3},{3,2},{4,5},{5,4},{6,7},{7,6},{8,9},{9,8},{10,11... | collective-permute-start | bytes 1572872 | tf_op jit(solution)/shard_map/ppermute | solution.py:230
  84.1 13.4 %collective-permute-start.8 = (f32[3,16,8,128]{3,2,1,0:T(8,128)S(1)}, f32[3,16,8,128]{3,2,1,0:T(8,128)S(1)}, u32[]{:S(2)}, u32[]{:S(2)}) collective-permute-start(f32[3,16,8,128]{3,2,1,0:T(8,128)S(1)} %pad_maximum_fusion.2), channel_id=1, source_target_pairs={{0,2},{2,0},{4,6},{6,4},{8,10},{10,8},{12,14},{14,12},{1,3},{3,1},... | collective-permute-start | bytes 589832 | tf_op jit(solution)/shard_map/ppermute | solution.py:226
  91.6 21.3 %collective-permute-start.20 = (f32[8,128,128]{2,1,0:T(8,128)S(1)}, f32[8,128,128]{2,1,0:T(8,128)S(1)}, u32[]{:S(2)}, u32[]{:S(2)}) collective-permute-start(f32[8,128,128]{2,1,0:T(8,128)S(1)} %add.17), channel_id=1, source_target_pairs={{0,12},{2,14},{12,0},{14,2},{4,8},{6,10},{8,4},{10,6},{1,13},{3,15... | collective-permute-start | bytes 1572872 | tf_op jit(solution)/shard_map/ppermute | solution.py:222
  94.4 23.9 %collective-permute-start.18 = (f32[8,128,128]{2,1,0:T(8,128)S(1)}, f32[8,128,128]{2,1,0:T(8,128)S(1)}, u32[]{:S(2)}, u32[]{:S(2)}) collective-permute-start(f32[8,128,128]{2,1,0:T(8,128)S(1)} %add.16), channel_id=1, source_target_pairs={{0,4},{2,6},{4,0},{6,2},{8,12},{10,14},{12,8},{14,10},{1,5},{3,7},... | collective-permute-start | bytes 1572872 | tf_op jit(solution)/shard_map/ppermute | solution.py:222
  96.0 7.3 %collective-permute-start.9 = (f32[3,16,8,128]{3,2,1,0:T(8,128)S(1)}, f32[3,16,8,128]{3,2,1,0:T(8,128)S(1)}, u32[]{:S(2)}, u32[]{:S(2)}) collective-permute-start(f32[3,16,8,128]{3,2,1,0:T(8,128)S(1)} %pad_maximum_fusion.1.refs_0_), channel_id=1, source_target_pairs={{0,1},{1,0},{2,3},{3,2},{4,5},{5,4},{6,7},{7,6},{8,9},{9,8},{10,11... | collective-permute-start | bytes 589832 | tf_op jit(solution)/shard_map/ppermute | solution.py:230
  97.4 7.2 %collective-permute-start.12 = (f32[16,8,128]{2,1,0:T(8,128)S(1)}, f32[16,8,128]{2,1,0:T(8,128)S(1)}, u32[]{:S(2)}, u32[]{:S(2)}) collective-permute-start(f32[16,8,128]{2,1,0:T(8,128)S(1)} %get-tuple-element.44), channel_id=1, source_target_pairs={{0,2},{2,0},{4,6},{6,4},{8,10},{10,8},{12,14},{14,12},{1,3},{3,1},... | collective-permute-start | bytes 196616 | tf_op jit(solution)/shard_map/ppermute | solution.py:226
  103.3 4.3 %collective-permute-start.13 = (f32[16,8,128]{2,1,0:T(8,128)S(1)}, f32[16,8,128]{2,1,0:T(8,128)S(1)}, u32[]{:S(2)}, u32[]{:S(2)}) collective-permute-start(f32[16,8,128]{2,1,0:T(8,128)S(1)} %get-tuple-element.43.refs_4_), channel_id=1, source_target_pairs={{0,1},{1,0},{2,3},{3,2},{4,5},{5,4},{6,7},{7,6},{8,9},{9,8},{10,11... | collective-permute-start | bytes 196616 | tf_op jit(solution)/shard_map/ppermute | solution.py:230
  104.7 4.3 %collective-permute-start.14 = (f32[16,8,128]{2,1,0:T(8,128)S(1)}, f32[16,8,128]{2,1,0:T(8,128)S(1)}, u32[]{:S(2)}, u32[]{:S(2)}) collective-permute-start(f32[16,8,128]{2,1,0:T(8,128)S(1)} %get-tuple-element.44), channel_id=1, source_target_pairs={{0,3},{1,2},{2,1},{3,0},{4,7},{5,6},{6,5},{7,4},{8,11},{9,10},{10,... | collective-permute-start | bytes 196616 | tf_op jit(solution)/shard_map/ppermute | solution.py:235
  109.0 2.3 %copy-start.6 = (f32[8,128,128]{2,1,0:T(8,128)S(1)}, f32[8,128,128]{2,1,0:T(8,128)}, u32[]{:S(2)}) copy-start(f32[8,128,128]{2,1,0:T(8,128)} %copy-done.5) | copy-start | bytes 1572868
  109.0 2.3 %copy-start.8 = (f32[8,128,128]{2,1,0:T(8,128)S(1)}, f32[8,128,128]{2,1,0:T(8,128)}, u32[]{:S(2)}) copy-start(f32[8,128,128]{2,1,0:T(8,128)} %copy-done.7) | copy-start | bytes 1572868
  120.7 13.9 %collective-permute-start.21 = (f32[8,128,128]{2,1,0:T(8,128)S(1)}, f32[8,128,128]{2,1,0:T(8,128)S(1)}, u32[]{:S(2)}, u32[]{:S(2)}) collective-permute-start(f32[8,128,128]{2,1,0:T(8,128)S(1)} %shard_map.89), channel_id=1, source_target_pairs={{0,1},{1,0},{2,3},{3,2},{4,5},{5,4},{6,7},{7,6},{8,9},{9,8},{10,11... | collective-permute-start | bytes 1572872 | tf_op jit(solution)/shard_map/ppermute | solution.py:230

commit v2 on v0

--- a/solution.py
+++ b/solution.py
@@ -1,9 +1,444 @@
+import functools
 import jax
 import jax.numpy as jnp
 from jax import lax
+from jax.experimental import pallas as pl
+from jax.experimental.pallas import tpu as pltpu
 from jax.sharding import PartitionSpec as P
 
 C = 128
+EPS = 1e-05
+HIGHEST = lax.Precision.HIGHEST
+F32 = jnp.float32
+CHUNK = 4
+GROUP = 8
+
+
+def dot(a, b):
+    return lax.dot_general(a, b, (((1,), (0,)), ((), ())), precision=HIGHEST, preferred_element_type=F32)
+
+
+def dot_t(a, b):
+    return lax.dot_general(a, b, (((1,), (1,)), ((), ())), precision=HIGHEST, preferred_element_type=F32)
+
+
+def norm(values):
+    mean = jnp.mean(values, axis=-1, keepdims=True)
+    centered = values - mean
+    variance = jnp.mean(centered * centered, axis=-1, keepdims=True)
+    scale = lax.rsqrt(variance + EPS)
+    return (centered * scale, scale)
+
+
+def flat(values):
+    return values.reshape(-1, values.shape[-1])
+
+
+def call(kernel, outs, args, scratch=(), flops=1000):
+    smem = pl.BlockSpec(memory_space=pltpu.SMEM)
+    vmem = pl.BlockSpec(memory_space=pltpu.VMEM)
+    return pl.pallas_call(
+        kernel,
+        out_shape=[jax.ShapeDtypeStruct(shape, F32) for shape in outs],
+        in_specs=[smem] + [vmem] * (len(args) - 1),
+        out_specs=[vmem] * len(outs),
+        scratch_shapes=[pltpu.VMEM(shape, F32) for shape in scratch],
+        compiler_params=pltpu.CompilerParams(vmem_limit_bytes=50 * 1024 * 1024),
+        cost_estimate=pl.CostEstimate(flops=flops, bytes_accessed=flops, transcendentals=0),
+    )(*args)
+
+
+def source_row(place, t, rows):
+    half = rows // 2
+    if t < half:
+        return place[2] * half + t
+    return (1 - place[2]) * half + t - half
+
+
+def first_col(place, chip, core, rows):
+    half = rows // 2
+    return pl.multiple_of(chip * 2 * rows + core * rows + place[2] * half, half)
+
+
+def rows_kernel(place, pair, mask, cotangent, packed):
+    rows, cols, width = pair.shape
+    half = rows // 2
+    packed[:rows] = pair[...]
+    for chip in range(cols // (2 * rows)):
+        block = cotangent[:, pl.ds(first_col(place, chip, 1 - place[1], rows), half), :]
+        packed[rows + chip] = flat(block)
+    packed[packed.shape[0] - 1, :rows] = mask[...].astype(F32)
+
+
+def both_halves(place, mine, other):
+    first = place[2] == 0
+    a, b = jnp.where(first, mine, other), jnp.where(first, other, mine)
+    return jnp.concatenate([a, b], axis=0)
+
+
+def gated_weights(place, mine, other, which):
+    return jnp.concatenate([both_halves(place, mine[p], other[p]) for p in (which, which + 1)], axis=0)
+
+
+def gated(normed, keep_rows, w):
+    count, cols = keep_rows.shape
+    chans = w.shape[0] // 2
+    spread = jnp.transpose(jnp.concatenate([keep_rows] * (8 // count), axis=0))
+    keep = jnp.concatenate([spread[:, u : u + 1] for u in range(count)], axis=0)
+    proj = dot_t(normed, w)
+    sig = jax.nn.sigmoid(proj[:, chans:]) * keep
+    return sig * proj[:, :chans], sig
+
+
+def right_kernel(rows, place, pair, mask, mine, other, right, open_part, slope):
+    half, cols, chans = right.shape
+    w = gated_weights(place, mine, other, 2)
+    for t in range(0, half, CHUNK):
+        row = source_row(place, t, rows)
+        normed, _ = norm(flat(pair[pl.ds(row, CHUNK)]))
+        value, sig = gated(normed, mask[pl.ds(row, CHUNK), :].astype(F32), w)
+        shape = (CHUNK, cols, chans)
+        right[t : t + CHUNK] = value.reshape(shape)
+        open_part[t : t + CHUNK] = sig.reshape(shape)
+        slope[t : t + CHUNK] = (value * (1.0 - sig)).reshape(shape)
+
+
+def prepare_kernel(rows, place, pair, mask, cotangent, there, mine, other, w_gate, mine_out, other_out, *refs):
+    left_here, left_there, open_part, slope, gate, d_here, d_there, w_out, normed_rows = refs
+    half, cols, chans = open_part.shape
+    chips = cols // (2 * rows)
+    shape = (CHUNK, cols, chans)
+    w = gated_weights(place, mine, other, 0)
+    w_out[...] = both_halves(place, mine_out[...], other_out[...])
+    for t in range(0, rows, CHUNK):
+        row = source_row(place, t, rows)
+        at = slice(t, t + CHUNK)
+        normed, _ = norm(flat(pair[pl.ds(row, CHUNK)]))
+        value, sig = gated(normed, mask[pl.ds(row, CHUNK), :].astype(F32), w)
+        left_here[at] = value.reshape(shape)
+        if t < half:
+            open_part[at] = sig.reshape(shape)
+            slope[at] = (value * (1.0 - sig)).reshape(shape)
+        gate[at] = jax.nn.sigmoid(dot(normed, w_gate[...])).reshape(CHUNK, cols, -1)
+        for chip in range(chips):
+            near = pl.ds(first_col(place, chip, place[1], rows), half)
+            d_here[chip, at] = gate[at, near, :] * cotangent[pl.ds(row, CHUNK), near, :]
+        normed, _ = norm(flat(there[pl.ds(row, CHUNK)]))
+        value, _ = gated(normed, there[there.shape[0] - 1, pl.ds(row, CHUNK), :], w)
+        left_there[at] = value.reshape(shape)
+        normed_rows[...] = normed.reshape(CHUNK, cols, -1)
+        picked = [
+            normed_rows[:, pl.ds(first_col(place, chip, place[1], rows), half), :] for chip in range(chips)
+        ]
+        opened = jax.nn.sigmoid(dot(flat(jnp.stack(picked)), w_gate[...])).reshape(chips, CHUNK, half, -1)
+        for chip in range(chips):
+            d_out = there[rows + chip, pl.ds(row * half, CHUNK * half), :].reshape(CHUNK, half, -1)
+            d_there[chip, at] = opened[chip] * d_out
+
+
+def tile_body(step, place, right, left_here, left_there, d_here, d_there, w_out, out_here, out_there, d_x, d_right, partial, x):
+    rows = left_here.shape[0]
+    half, cols, chans = right.shape
+    groups = cols // GROUP
+
+    def forward(pair_at, _):
+        for which, left in enumerate((left_here, left_there)):
+            i = pair_at * 2
+            value = [left[i], left[i + 1]]
+            for j in range(half):
+                block = right[j]
+                for u in range(2):
+                    product = (value[u] * block).reshape(groups, GROUP, chans)
+                    partial[2 * which + u, j * GROUP : (j + 1) * GROUP] = jnp.sum(product, axis=0)
+            for u in range(2):
+                total = partial[2 * which + u, pl.ds(0, half, stride=GROUP), :]
+                for s in range(1, GROUP):
+                    total = total + partial[2 * which + u, pl.ds(s, half, stride=GROUP), :]
+                x[pl.ds(pl.multiple_of((which * rows + i + u) * half, half), half), :] = total
+        return 0
+
+    lax.fori_loop(0, rows // 2, forward, 0)
+    chip = jnp.bitwise_xor(place[0], step)
+    d_out = jnp.concatenate([flat(d_here[chip]), flat(d_there[chip])], axis=0)
+    normed, scale = norm(x[...])
+    out = dot(normed, w_out[...])
+    out_here[...] = out[: rows * half].reshape(rows, half, -1)
+    out_there[...] = out[rows * half :].reshape(rows, half, -1)
+    d_normed = dot_t(d_out, w_out[...])
+    mean_one = jnp.mean(d_normed, axis=-1, keepdims=True)
+    mean_two = jnp.mean(d_normed * normed, axis=-1, keepdims=True)
+    d_x[...] = (d_normed - mean_one - normed * mean_two) * scale
+    wide = 2 * GROUP
+
+    def backward(at, _):
+        here = pl.ds(pl.multiple_of(at * wide, wide), wide)
+
+        def add(block, totals):
+            totals = list(totals)
+            for u in range(GROUP):
+                for which, left in enumerate((left_here, left_there)):
+                    i = block * GROUP + u
+                    value = left[i, here, :]
+                    for j in range(half):
+                        totals[j] = totals[j] + value * d_x[pl.ds((which * rows + i) * half + j, 1), :]
+            return tuple(totals)
+
+        totals = lax.fori_loop(0, rows // GROUP, add, (jnp.zeros((wide, chans), F32),) * half)
+        for j in range(half):
+            d_right[j, here, :] = totals[j]
+        return 0
+
+    lax.fori_loop(0, cols // wide, backward, 0)
+
+
+def tile_kernel(step, parts, place, *refs):
+    rights, rest = refs[:parts], refs[parts:]
+    if parts == 2:
+        sum_out = rest[9]
+        sum_out[...] = rights[0][...] + rights[1][...]
+        tile_body(step, place, sum_out, *rest[:9], *rest[10:])
+    else:
+        tile_body(step, place, rights[0], *rest)
+
+
+def left_kernel(tiles, bases, place, *refs):
+    rights, d_xs = refs[:tiles], refs[tiles : 2 * tiles]
+    base = refs[2 * tiles : 2 * tiles + bases]
+    outs = refs[2 * tiles + bases :]
+    half, cols, chans = rights[0].shape
+    rows = outs[0].shape[0]
+    for which, out in enumerate(outs):
+
+        def body(pair_at, _):
+            i = pair_at * 2
+            if bases:
+                totals = [base[which][i], base[which][i + 1]]
+            else:
+                totals = [jnp.zeros((cols, chans), F32)] * 2
+            for right, d_x in zip(rights, d_xs):
+                for j in range(half):
+                    value = right[j]
+                    for u in range(2):
+                        at = (which * rows + i + u) * half + j
+                        totals[u] = totals[u] + value * d_x[pl.ds(at, 1), :]
+            out[i] = totals[0]
+            out[i + 1] = totals[1]
+            return 0
+
+        lax.fori_loop(0, rows // 2, body, 0)
+    for plane in range(2, bases):
+        outs[1][rows + plane - 2] = flat(base[plane][...])
+
+
+def share_kernel(place, kept, received, out_here, out_next, d_left, packed, packed_next, rest):
+    half = d_left.shape[0]
+    block = half * half
+    d_left[...] = kept[:half] + received[:half]
+    part = half // 2
+    packed[:part] = kept[half : half + part] + received[half : half + part]
+    packed_next[:part] = kept[half + part :] + received[half + part : 2 * half]
+    for step, out in enumerate((out_here, out_next)):
+        at = slice(step * block, (step + 1) * block)
+        plane = 2 * half + step
+        packed[part, at] = flat(out[half:])
+        packed_next[part, at] = received[plane, block:]
+        rest[0, at] = flat(out[:half])
+        rest[1, at] = received[plane, :block]
+
+
+def gather_out(place, rows, t, out, here, early_other, early_far, received, far):
+    half = rows // 2
+    block = half * half
+    for far_half in (0, 1):
+        source = (t + far_half * half) % rows
+        at, wide = slice(source, source + half), slice(source * half, source * half + block)
+        for far_core in (0, 1):
+            core = place[1] + far_core * (1 - 2 * place[1])
+            side = place[2] + far_half * (1 - 2 * place[2])
+            for step in range(4):
+                chip = jnp.bitwise_xor(place[0], step)
+                first = pl.multiple_of(chip * 2 * rows + core * rows + side * half, half)
+                if far_half:
+                    if step < 2:
+                        value = early_far[far_core, step, at]
+                    else:
+                        ref, plane = far[far_core]
+                        value = ref[plane, (step - 2) * block : (step - 1) * block].reshape(half, half, -1)
+                elif far_core:
+                    if step < 2:
+                        value = early_other[step, at]
+                    else:
+                        value = received[rows + step - 2, wide].reshape(half, half, -1)
+                else:
+                    value = here[step][at]
+                out[t : t + half, pl.ds(first, half), :] = value
+
+
+def update_kernel(rows, place, *refs):
+    here, early_other, early_far, received, far, far_next, rest, gate, update, out = refs[:4], *refs[4:]
+    half = rows // 2
+    part = half // 2
+    gather_out(place, rows, 0, out, here, early_other, early_far, received, ((far, part), (far_next, part)))
+    gather_out(place, rows, half, out, here, early_other, early_far, received, ((rest, 0), (rest, 1)))
+    for t in range(0, rows, CHUNK):
+        update[pl.ds(source_row(place, t, rows), CHUNK)] = gate[t : t + CHUNK] * out[t : t + CHUNK]
+
+
+def base_kernel(rows, place, *refs):
+    here, early_other, early_far, received, far, far_next = refs[:4], *refs[4:9]
+    gate, cotangent, w_gate, d_left, open_part, slope, mine, other, base, out = refs[9:]
+    half, cols, chans = base.shape
+    part = half // 2
+    gather_out(place, rows, 0, out, here, early_other, early_far, received, ((far, part), (far_next, part)))
+    w = gated_weights(place, mine, other, 0)
+    for t in range(0, half, CHUNK):
+        at = slice(t, t + CHUNK)
+        opened = gate[at]
+        d_gate = cotangent[pl.ds(source_row(place, t, rows), CHUNK)] * (opened * out[at]) * (1.0 - opened)
+        from_other = (far if t < part else far_next)[t % part : t % part + CHUNK]
+        grad = flat(d_left[at] + from_other)
+        both = jnp.concatenate([grad * flat(open_part[at]), grad * flat(slope[at])], axis=1)
+        base[at] = (dot_t(flat(d_gate), w_gate[...]) + dot(both, w)).reshape(CHUNK, cols, -1)
+
+
+def pair_kernel(rows, place, pair, base, d_right, d_right_near, d_right_middle, d_right_far, open_part, slope, mine, other, d_mine, d_pair):
+    half, cols, chans = base.shape
+    w = gated_weights(place, mine, other, 2)
+    for t in range(0, half, CHUNK):
+        at = slice(t, t + CHUNK)
+        grad = flat(d_right[at] + d_right_near[at] + (d_right_middle[at] + d_right_far[at]))
+        both = jnp.concatenate([grad * flat(open_part[at]), grad * flat(slope[at])], axis=1)
+        d_normed = flat(base[at]) + dot(both, w)
+        normed, scale = norm(flat(pair[pl.ds(source_row(place, t, rows), CHUNK)]))
+        mean_grad = jnp.mean(d_normed, axis=-1, keepdims=True)
+        mean_cross = jnp.mean(d_normed * normed, axis=-1, keepdims=True)
+        d_mine[at] = ((d_normed - mean_grad - normed * mean_cross) * scale).reshape(CHUNK, cols, -1)
+        d_pair[pl.ds(source_row(place, t, rows), CHUNK)] = d_mine[at]
+
+
+def along(block, pairs):
+    return lax.ppermute(block, "row", [(2 * a + core, 2 * b + core) for a, b in pairs for core in (0, 1)])
+
+
+def other_core(block):
+    return lax.ppermute(block, "row", [(i, i ^ 1) for i in range(lax.axis_size("row"))])
+
+
+def other_half(block):
+    return lax.ppermute(block, "ch", [(0, 1), (1, 0)])
+
+
+NEXT = [(0, 1), (1, 0), (2, 3), (3, 2)]
+MIDDLE = [(1, 2), (2, 1)]
+OUTWARD = [(1, 0), (2, 3)]
+INWARD = [(0, 1), (3, 2)]
+ENDS = [(0, 3), (3, 0)]
+
+
+def on_tiles(pair, pair_mask, w_proj, w_gate, w_out, cotangent):
+    rows, cols, width = pair.shape
+    half = rows // 2
+    chips = cols // (2 * rows)
+    chans = 2 * w_out.shape[0]
+    row, side = lax.axis_index("row"), lax.axis_index("ch")
+    place = jnp.stack([row // 2, row % 2, side]).astype(jnp.int32)
+
+    mine = jnp.swapaxes(w_proj, 1, 2)
+    other = other_half(flat(mine)).reshape(mine.shape)
+    other_out = other_half(w_out)
+    (sent,) = call(rows_kernel, [(rows + chips + 1, cols, width)], (place, pair, pair_mask, cotangent), flops=10**9)
+    there = other_core(sent)
+
+    kept = (half, cols, chans)
+    right, open_right, slope_right = call(
+        functools.partial(right_kernel, rows), [kept] * 3, (place, pair, pair_mask, mine, other)
+    )
+    near = along(right, NEXT)
+    middle = along(right, MIDDLE)
+    quarter = (chips, rows, half, width)
+    tile_outs = [(rows, half, width)] * 2 + [(2 * rows * half, chans), kept]
+    tile_scratch = [(4, half * GROUP, chans), (2 * rows * half, chans)]
+    out_here, out_there, d_x, d_right, rights = ([None] * 4 for _ in range(5))
+    rights[0] = right
+    left, left_there, open_left, slope_left, gate, d_here, d_there, w_all_out = call(
+        functools.partial(prepare_kernel, rows),
+        [(rows, cols, chans)] * 2 + [kept] * 2 + [(rows, cols, width), quarter, quarter, (chans, width)],
+        (place, pair, pair_mask, cotangent, there, mine, other, w_gate, w_out, other_out),
+        scratch=[(CHUNK, cols, width)],
+    )
+
+    def tile(step, *blocks):
+        got = call(
+            functools.partial(tile_kernel, step, len(blocks)),
+            tile_outs + ([kept] if len(blocks) == 2 else []),
+            (place, *blocks, left, left_there, d_here, d_there, w_all_out),
+            scratch=tile_scratch,
+        )
+        out_here[step], out_there[step], d_x[step], d_right[step] = got[:4]
+        rights[step] = got[4] if len(blocks) == 2 else blocks[0]
+
+    near, middle, d_here = lax.optimization_barrier((near, middle, d_here))
+    cross = along(near, MIDDLE)
+    outer = along(middle, OUTWARD)
+    tile(0, right)
+    tile(1, near)
+    early_other = other_core(jnp.stack(out_there[:2]))
+    d_left_here, d_left_there = call(
+        functools.partial(left_kernel, 2, 0),
+        [(rows, cols, chans)] * 2,
+        (place, *rights[:2], *d_x[:2]),
+    )
+    cross, outer, early_other, d_left_here = lax.optimization_barrier((cross, outer, early_other, d_left_here))
+    far = along(cross, OUTWARD)
+    early_far = other_half(jnp.stack([jnp.stack(out_here[:2]), early_other]))
+    tile(2, cross, outer)
+    inward = along(d_right[2], INWARD)
+    swapped = along(d_right[2], MIDDLE)
+    far, d_x[2] = lax.optimization_barrier((far, d_x[2]))
+    tile(3, middle, far)
+    from_far = along(d_right[3], ENDS)
+    inward, swapped, early_far, d_x[3] = lax.optimization_barrier((inward, swapped, early_far, d_x[3]))
+    d_left_kept, d_left_sent = call(
+        functools.partial(left_kernel, 2, 4),
+        [(rows, cols, chans), (rows + 2, cols, chans)],
+        (place, *rights[2:], *d_x[2:], d_left_here, d_left_there, out_there[2], out_there[3]),
+    )
+    received = other_core(d_left_sent)
+    from_near = along(d_right[1] + swapped, NEXT)
+    from_middle = along(d_right[3] + inward, MIDDLE)
+    packed_shape = (half // 2 + 1, cols, chans)
+    d_left, shared, shared_next, rest = call(
+        share_kernel,
+        [kept, packed_shape, packed_shape, (2, cols, chans)],
+        (place, d_left_kept, received, out_here[2], out_here[3]),
+    )
+    shared_other = other_half(shared)
+    shared_other_next = other_half(shared_next)
+    rest_other = other_half(rest)
+    outs = (*out_here, early_other, early_far, received, shared_other, shared_other_next)
+    (base,) = call(
+        functools.partial(base_kernel, rows),
+        [(half, cols, width)],
+        (place, *outs, gate, cotangent, w_gate, d_left, open_left, slope_left, mine, other),
+        scratch=[(half, cols, width)],
+    )
+    base, rest_other = lax.optimization_barrier((base, rest_other))
+    d_mine, d_pair = call(
+        functools.partial(pair_kernel, rows),
+        [(half, cols, width), (rows, cols, width)],
+        (place, pair, base, d_right[0], from_near, from_middle, from_far, open_right, slope_right, mine, other),
+    )
+    d_other = other_half(d_mine)
+    _, gate_late = lax.optimization_barrier((d_mine, gate))
+    (update,) = call(
+        functools.partial(update_kernel, rows),
+        [(rows, cols, width)],
+        (place, *outs, rest_other, gate_late),
+        scratch=[(rows, cols, width)],
+    )
+    d_other, update = lax.optimization_barrier((d_other, update))
+    d_pair = lax.dynamic_update_slice_in_dim(d_pair, d_other, (1 - side) * half, 0)
+    return (update, d_pair)
 
 
 def passed_along(block, axis, distance):
@@ -20,7 +455,7 @@
     return (centered * scale, scale)
 
 
-def on_device(pair, pair_mask, w_proj, w_gate, w_out, cotangent):
+def on_ring(pair, pair_mask, w_proj, w_gate, w_out, cotangent):
     highest = lax.Precision.HIGHEST
     normed, pair_scale = normalize(pair)
     proj = jnp.einsum("rqz,pzc->pcrq", normed, w_proj, precision=highest)
@@ -96,8 +531,10 @@
 
 
 def solution(mesh):
+    sizes = mesh.shape
+    tiled = sizes["row"] == 8 and sizes["ch"] == 2 and sizes["sub"] == 1
     return jax.shard_map(
-        on_device,
+        on_tiles if tiled else on_ring,
         mesh=mesh,
         in_specs=(
             P(("grp", "row"), "sub", None),

time: 268 us -> 127 us (0.47)
  waiting for transfers between devices: 142 us -> 36.5 us
  Pallas kernels: 0 us -> 44.6 us
  matrix products: 44.3 us -> 0 us
  local copies, waits for them, and re-layouts: 48.3 us -> 11.7 us
  starting transfers between devices: 1.19 us -> 32.2 us
  between operations: 14 us -> 0.97 us
  blocking collectives: 9.22 us -> 0 us
  other arithmetic: 8.23 us -> 0.26 us
    psum x2 -> x0, waiting for transfers between devices: 63.8 us -> none  [the longest x1 35.8 us: on_device(): d_normed = lax.psum(d_normed_part, 'ch')]
    pallas_call x0 -> x13, Pallas kernels: none -> 44.6 us  [call(): pl.pallas_call(kernel, out_shape=[jax.ShapeDtypeStruct(shape, F32) for sh...]
    dot_general x16 -> x0, matrix products: 44.3 us -> none  [the longest x1 9.16 us: on_device(): jnp.einsum('cij,cik->jck', d_mixed_full, left, precision=highest)]
    reduce_scatter x1 -> x0, waiting for transfers between devices: 41.8 us -> none  [on_device(): lax.psum_scatter(jnp.einsum('cij,cik->jck', d_mixed_full, left, precision...]
    dynamic_update_slice x23 -> x1, local copies, waits for them, and re-layouts: 34.4 us -> 1.08 us  [on_tiles(): lax.dynamic_update_slice_in_dim(d_pair, d_other, (1 - side) * half, 0)]
    ppermute x7 -> x20, starting transfers between devices: 0.85 us -> 32.2 us  [the longest x10 20.7 us: along(): lax.ppermute(block, 'row', [(2 * a + core, 2 * b + core) for a, b in pair...]
    psum x1 -> x0, blocking collectives: 9.22 us -> none  [on_device(): lax.psum((projected, first, second, col_total), 'ch')]
    unnamed x26 -> x42, local copies, waits for them, and re-layouts: 4.87 us -> 10.6 us
  transfers between devices with their start and end apart: 10 -> 20, of which waited for: 10 -> 8; matrix products, arithmetic and copies ran while one was open for 18% -> 0% of each run, Pallas kernels for 0% -> 28%
where the time goes in v2:
time: 127 us; the launch traced here: 126 us
  Pallas kernels  44.6 us (35%)
  waiting for transfers between devices  36.5 us (29%)
  starting transfers between devices  32.2 us (25%)
  local copies, waits for them, and re-layouts  11.7 us (9%)
    pallas_call x13, Pallas kernels, call(): pl.pallas_call(kernel, out_shape=[jax.ShapeDtypeStruct(shape, F32) for sh...  44.6 us
    ppermute x7, waiting for transfers between devices, other_half(): return lax.ppermute(block, 'ch', [(0, 1), (1, 0)])  28.5 us
    ppermute x10, starting transfers between devices, along(): lax.ppermute(block, 'row', [(2 * a + core, 2 * b + core) for a, b in pair...  20.7 us
    ppermute x7, starting transfers between devices, other_half(): return lax.ppermute(block, 'ch', [(0, 1), (1, 0)])  10.9 us
    unnamed x42, local copies, waits for them, and re-layouts  10.6 us
    ppermute x10, waiting for transfers between devices, along(): lax.ppermute(block, 'row', [(2 * a + core, 2 * b + core) for a, b in pair...  7.93 us
  transfers between devices with their start and end apart: 20, of which 8 were waited for; matrix products, arithmetic and copies ran while one was open for 0% of the time, Pallas kernels for 28%

profile of v2, /device:TPU:0, one launch (start us, length us, event | category | flops | bytes accessed | tf_op | source)
XLA Modules:
  0.0 126.3 jit_solution(18383541836458930891)
XLA Ops:
  0.6 0.1 pad_add_fusion.place
  0.7 1.2 copy-done.3
  2.0 1.2 copy-done.5
  3.2 0.7 copy-done.17
  3.9 0.6 shard_map.78
  4.5 0.5 collective-permute-start.1
  5.1 2.7 %collective-permute-start = (f32[256,128]{1,0:T(8,128)S(1)}, f32[256,128]{1,0:T(8,128)S(1)}, u32[]{:S(2)}, u32[]{:S(2)}) collective-permute-start(f32[256,128]{1,0:T(8,128)S(1)} %bitcast.14), channel_id=1, source_target_pairs={{0,1},{1,0},{2,3},{3,2},{4,5},{5,4},{6,7},{7,6},{8,9},{9,8},{10,11... | collective-permute-start | bytes 393224 | tf_op jit(solution)/shard_map/ppermute | solution.py:328
  7.7 4.0 %collective-permute-done = f32[256,128]{1,0:T(8,128)S(1)} collective-permute-done((f32[256,128]{1,0:T(8,128)S(1)}, f32[256,128]{1,0:T(8,128)S(1)}, u32[]{:S(2)}, u32[]{:S(2)}) %collective-permute-start) | collective-permute-done | bytes 131104 | tf_op jit(solution)/shard_map/ppermute | solution.py:328
  11.7 1.8 %shard_map.77 = (f32[8,128,128]{2,1,0:T(8,128)S(1)}, f32[8,128,128]{2,1,0:T(8,128)S(1)}, f32[8,128,128]{2,1,0:T(8,128)S(1)}) custom-call(s32[3]{0:T(128)S(1)} %pad_add_fusion.place, f32[16,128,128]{2,1,0:T(8,128)S(1)} %copy-done.3, s32[16,128]{1,0:T(8,128)S(1)} %copy-done.17, f32[4,64,128]{2,1,0:T(8,128)S(1)} %bitcast.15, f32[4,64,128]{2,1,0:T(8,128)S(1)} %bitcast.19), custom_call_target="tpu_custom_call" | custom-call | flops 1000 | bytes 1000 | tf_op jit(solution)/shard_map/pallas_call | solution.py:40
  13.6 0.8 copy-done.8
  14.3 1.8 %collective-permute-start.3 = (f32[8,128,128]{2,1,0:T(8,128)S(1)}, f32[8,128,128]{2,1,0:T(8,128)S(1)}, u32[]{:S(2)}, u32[]{:S(2)}) collective-permute-start(f32[8,128,128]{2,1,0:T(8,128)S(1)} %get-tuple-element.59.refs_0_), channel_id=1, source_target_pairs={{0,4},{2,6},{4,0},{6,2},{8,12},{10,14},{12,8},{14,10},{1,5},{3,7},... | collective-permute-start | bytes 1572872 | tf_op jit(solution)/shard_map/ppermute | solution.py:320
  16.2 0.7 collective-permute-start.4
  16.9 1.6 %collective-permute-start.2 = (f32[64,128]{1,0:T(8,128)S(1)}, f32[64,128]{1,0:T(8,128)S(1)}, u32[]{:S(2)}, u32[]{:S(2)}) collective-permute-start(f32[64,128]{1,0:T(8,128)S(1)} %copy-done.16), channel_id=1, source_target_pairs={{0,1},{1,0},{2,3},{3,2},{4,5},{5,4},{6,7},{7,6},{8,9},{9,8},{10,11... | collective-permute-start | bytes 98312 | tf_op jit(solution)/shard_map/ppermute | solution.py:328
  18.4 2.4 %collective-permute-done.2.other_out = f32[64,128]{1,0:T(8,128)S(1)} collective-permute-done((f32[64,128]{1,0:T(8,128)S(1)}, f32[64,128]{1,0:T(8,128)S(1)}, u32[]{:S(2)}, u32[]{:S(2)}) %collective-permute-start.2) | collective-permute-done | bytes 32800 | tf_op jit(solution)/shard_map/ppermute | solution.py:328
  20.8 0.0 collective-permute-done.1.there
  20.9 1.1 copy-done.18
  22.0 8.0 %shard_map.79 = (f32[16,128,128]{2,1,0:T(8,128)S(1)}, f32[16,128,128]{2,1,0:T(8,128)}, f32[8,128,128]{2,1,0:T(8,128)S(1)}, f32[8,128,128]{2,1,0:T(8,128)S(1)}, f...) custom-call(s32[3]{0:T(128)S(1)} %pad_add_fusion.place, ...), custom_call_target="tpu_custom_call" | custom-call | flops 1000 | bytes 1000 | tf_op jit(solution)/shard_map/pallas_call | solution.py:40
  30.0 0.8 copy-done.9
  30.8 0.7 collective-permute-start.5
  31.5 1.3 %collective-permute-start.6 = (f32[8,128,128]{2,1,0:T(8,128)S(1)}, f32[8,128,128]{2,1,0:T(8,128)S(1)}, u32[]{:S(2)}, u32[]{:S(2)}) collective-permute-start(f32[8,128,128]{2,1,0:T(8,128)S(1)} %collective-permute-done.4.refs_0_), channel_id=1, source_target_pairs={{4,0},{6,2},{8,12},{10,14},{5,1},{7,3},{9,13},{11,15},{20,16},{22,... | collective-permute-start | bytes 1572872 | tf_op jit(solution)/shard_map/ppermute | solution.py:320
  32.8 0.0 copy-start
  32.8 1.2 copy-done
  34.0 3.8 %shard_map.80 = (f32[16,8,128]{2,1,0:T(8,128)S(1)}, f32[16,8,128]{2,1,0:T(8,128)S(1)}, f32[256,128]{1,0:T(8,128)S(1)}, f32[8,128,128]{2,1,0:T(8,128)S(1)}) custom-call(s32[3]{0:T(128)S(1)} %pad_add_fusion.place, f32[8,128,128]{2,1,0:T(8,128)S(1)} %get-tuple-element.59.refs_0_, f32[16,128,128]{2,1,0:T(8,128)S(1)} %get-tuple-element.60.refs_1_.refs_2_, ...), custom_call_target="tpu_custom_call" | custom-call | flops 1000 | bytes 1000 | tf_op jit(solution)/shard_map/pallas_call | solution.py:40
  37.8 3.8 %shard_map.81 = (f32[16,8,128]{2,1,0:T(8,128)S(1)}, f32[16,8,128]{2,1,0:T(8,128)S(1)}, f32[256,128]{1,0:T(8,128)S(1)}, f32[8,128,128]{2,1,0:T(8,128)S(1)}) custom-call(s32[3]{0:T(128)S(1)} %pad_add_fusion.place, f32[8,128,128]{2,1,0:T(8,128)S(1)} %collective-permute-done.3.refs_0_.refs_1_, f32[16,128,128]{2,1,0:T(8,128)S(1)} %get-tuple-element.60.refs_1_.refs_2_, ...), custom_call_target="tpu_custom_call" | custom-call | flops 1000 | bytes 1000 | tf_op jit(solution)/shard_map/pallas_call | solution.py:40
  41.6 0.1 collective-permute-start.7
  41.6 2.9 %shard_map.82 = (f32[16,128,128]{2,1,0:T(8,128)S(1)}, f32[16,128,128]{2,1,0:T(8,128)S(1)}) custom-call(s32[3]{0:T(128)S(1)} %pad_add_fusion.place, f32[8,128,128]{2,1,0:T(8,128)S(1)} %get-tuple-element.59.refs_0_, f32[8,128,128]{2,1,0:T(8,128)S(1)} %collective-permute-done.3.refs_0_.refs_1_, f32[256,128]{1,0:T(8,128)S(1)} %get-tuple-element.72.refs_2_, ...), custom_call_target="tpu_custom_call" | custom-call | flops 1000 | bytes 1000 | tf_op jit(solution)/shard_map/pallas_call | solution.py:40
  44.6 1.0 copy-done.7
  45.5 0.0 collective-permute-done.7.refs_4_
  45.5 0.0 collective-permute-done.5.refs_0_
  45.5 3.0 %collective-permute-done.6.refs_1_ = f32[8,128,128]{2,1,0:T(8,128)S(1)} collective-permute-done((f32[8,128,128]{2,1,0:T(8,128)S(1)}, f32[8,128,128]{2,1,0:T(8,128)S(1)}, u32[]{:S(2)}, u32[]{:S(2)}) %collective-permute-start.6) | collective-permute-done | bytes 524320 | tf_op jit(solution)/shard_map/ppermute | solution.py:320
  48.6 1.3 %collective-permute-start.8 = (f32[8,128,128]{2,1,0:T(8,128)S(1)}, f32[8,128,128]{2,1,0:T(8,128)S(1)}, u32[]{:S(2)}, u32[]{:S(2)}) collective-permute-start(f32[8,128,128]{2,1,0:T(8,128)S(1)} %collective-permute-done.5.refs_0_), channel_id=1, source_target_pairs={{4,0},{6,2},{8,12},{10,14},{5,1},{7,3},{9,13},{11,15},{20,16},{22,... | collective-permute-start | bytes 1572872 | tf_op jit(solution)/shard_map/ppermute | solution.py:320
  49.9 4.6 %shard_map.83 = (f32[16,8,128]{2,1,0:T(8,128)S(1)}, f32[16,8,128]{2,1,0:T(8,128)S(1)}, f32[256,128]{1,0:T(8,128)S(1)}, f32[8,128,128]{2,1,0:T(8,128)S(1)}, f32[8,128,128]{2,1,0:T(8,128)S(1)}) custom-call(s32[3]{0:T(128)S(1)} %pad_add_fusion.place, f32[8,128,128]{2,1,0:T(8,128)S(1)} %collective-permute-done.5.refs_0_, ...), custom_call_target="tpu_custom_call" | custom-call | flops 1000 | bytes 1000 | tf_op jit(solution)/shard_map/pallas_call | solution.py:40
  54.4 4.6 %collective-permute-start.9 = (f32[8,128,128]{2,1,0:T(8,128)S(1)}, f32[8,128,128]{2,1,0:T(8,128)S(1)}, u32[]{:S(2)}, u32[]{:S(2)}) collective-permute-start(f32[8,128,128]{2,1,0:T(8,128)S(1)} %get-tuple-element.82), channel_id=1, source_target_pairs={{0,4},{2,6},{12,8},{14,10},{1,5},{3,7},{13,9},{15,11},{16,20},{18,... | collective-permute-start | bytes 1572872 | tf_op jit(solution)/shard_map/ppermute | solution.py:320
  59.0 0.7 collective-permute-start.10
  59.8 1.6 %collective-permute-start.11 = (f32[2,2,16,8,128]{4,3,2,1,0:T(8,128)S(1)}, f32[2,2,16,8,128]{4,3,2,1,0:T(8,128)S(1)}, u32[]{:S(2)}, u32[]{:S(2)}) collective-permute-start(f32[2,2,16,8,128]{4,3,2,1,0:T(8,128)S(1)} %pad_maximum_fusion), channel_id=1, source_target_pairs={{0,1},{1,0},{2,3},{3,2},{4,5},{5,4},{6,7},{7,6},{8,9},{9,8},{10,11... | collective-permute-start | bytes 786440 | tf_op jit(solution)/shard_map/ppermute | solution.py:328
  61.4 3.7 %collective-permute-done.8.refs_1_ = f32[8,128,128]{2,1,0:T(8,128)S(1)} collective-permute-done((f32[8,128,128]{2,1,0:T(8,128)S(1)}, f32[8,128,128]{2,1,0:T(8,128)S(1)}, u32[]{:S(2)}, u32[]{:S(2)}) %collective-permute-start.8) | collective-permute-done | bytes 524320 | tf_op jit(solution)/shard_map/ppermute | solution.py:320
  65.0 4.6 %shard_map.84 = (f32[16,8,128]{2,1,0:T(8,128)S(1)}, f32[16,8,128]{2,1,0:T(8,128)S(1)}, f32[256,128]{1,0:T(8,128)S(1)}, f32[8,128,128]{2,1,0:T(8,128)S(1)}, f32[8,128,128]{2,1,0:T(8,128)S(1)}) custom-call(s32[3]{0:T(128)S(1)} %pad_add_fusion.place, f32[8,128,128]{2,1,0:T(8,128)S(1)} %collective-permute-done.4.refs_0_, ...), custom_call_target="tpu_custom_call" | custom-call | flops 1000 | bytes 1000 | tf_op jit(solution)/shard_map/pallas_call | solution.py:40
  69.6 0.0 collective-permute-done.11.refs_5_
  69.6 1.2 collective-permute-done.9
  70.8 0.0 collective-permute-done.10
  70.8 4.9 %shard_map.85 = (f32[16,128,128]{2,1,0:T(8,128)S(1)}, f32[18,128,128]{2,1,0:T(8,128)}) custom-call(s32[3]{0:T(128)S(1)} %pad_add_fusion.place, f32[8,128,128]{2,1,0:T(8,128)S(1)} %get-tuple-element.85.refs_0_, f32[8,128,128]{2,1,0:T(8,128)S(1)} %get-tuple-element.86.refs_1_, f32[256,128]{1,0:T(8,128)S(1)} %get-tuple-element.87.refs_2_, ...), custom_call_target="tpu_custom_call" | custom-call | flops 1000 | bytes 1000 | tf_op jit(solution)/shard_map/pallas_call | solution.py:40
  75.7 0.0 collective-permute-start.12
  75.7 0.1 add.15
  75.8 4.1 %collective-permute-start.16 = (f32[8,128,128]{2,1,0:T(8,128)S(1)}, f32[8,128,128]{2,1,0:T(8,128)S(1)}, u32[]{:S(2)}, u32[]{:S(2)}) collective-permute-start(f32[8,128,128]{2,1,0:T(8,128)S(1)} %add.15), channel_id=1, source_target_pairs={{0,4},{2,6},{4,0},{6,2},{8,12},{10,14},{12,8},{14,10},{1,5},{3,7},... | collective-permute-start | bytes 1572872 | tf_op jit(solution)/shard_map/ppermute | solution.py:320
  79.9 0.1 add.16
  80.0 0.8 collective-permute-start.17
  80.8 4.7 %collective-permute-start.18 = (f32[8,128,128]{2,1,0:T(8,128)S(1)}, f32[8,128,128]{2,1,0:T(8,128)S(1)}, u32[]{:S(2)}, u32[]{:S(2)}) collective-permute-start(f32[8,128,128]{2,1,0:T(8,128)S(1)} %get-tuple-element.106), channel_id=1, source_target_pairs={{0,12},{2,14},{12,0},{14,2},{1,13},{3,15},{13,1},{15,3},{16,28},{1... | collective-permute-start | bytes 1572872 | tf_op jit(solution)/shard_map/ppermute | solution.py:320
  85.5 0.7 shard_map.86
  86.2 1.6 %collective-permute-start.13 = (f32[5,128,128]{2,1,0:T(8,128)S(1)}, f32[5,128,128]{2,1,0:T(8,128)S(1)}, u32[]{:S(2)}, u32[]{:S(2)}) collective-permute-start(f32[5,128,128]{2,1,0:T(8,128)S(1)} %get-tuple-element.95), channel_id=1, source_target_pairs={{0,1},{1,0},{2,3},{3,2},{4,5},{5,4},{6,7},{7,6},{8,9},{9,8},{10,11... | collective-permute-start | bytes 983048 | tf_op jit(solution)/shard_map/ppermute | solution.py:328
  87.8 0.5 collective-permute-start.14
  88.3 8.6 %collective-permute-done.13.refs_7_ = f32[5,128,128]{2,1,0:T(8,128)S(1)} collective-permute-done((f32[5,128,128]{2,1,0:T(8,128)S(1)}, f32[5,128,128]{2,1,0:T(8,128)S(1)}, u32[]{:S(2)}, u32[]{:S(2)}) %collective-permute-start.13) | collective-permute-done | bytes 327712 | tf_op jit(solution)/shard_map/ppermute | solution.py:328
  96.9 1.5 %collective-permute-start.15 = (f32[2,128,128]{2,1,0:T(8,128)S(1)}, f32[2,128,128]{2,1,0:T(8,128)S(1)}, u32[]{:S(2)}, u32[]{:S(2)}) collective-permute-start(f32[2,128,128]{2,1,0:T(8,128)S(1)} %get-tuple-element.101), channel_id=1, source_target_pairs={{0,1},{1,0},{2,3},{3,2},{4,5},{5,4},{6,7},{7,6},{8,9},{9,8},{10,11... | collective-permute-start | bytes 393224 | tf_op jit(solution)/shard_map/ppermute | solution.py:328
  98.4 5.5 %collective-permute-done.14.refs_8_ = f32[5,128,128]{2,1,0:T(8,128)S(1)} collective-permute-done((f32[5,128,128]{2,1,0:T(8,128)S(1)}, f32[5,128,128]{2,1,0:T(8,128)S(1)}, u32[]{:S(2)}, u32[]{:S(2)}) %collective-permute-start.14) | collective-permute-done | bytes 327712 | tf_op jit(solution)/shard_map/ppermute | solution.py:328
  103.9 3.5 %shard_map.87.base = f32[8,128,128]{2,1,0:T(8,128)S(1)} custom-call(s32[3]{0:T(128)S(1)} %pad_add_fusion.place, f32[16,8,128]{2,1,0:T(8,128)S(1)} %get-tuple-element.66.refs_0_, f32[16,8,128]{2,1,0:T(8,128)S(1)} %get-tuple-element.68.refs_1_, f32[16,8,128]{2,1,0:T(8,128)S(1)} %get-tuple-element.77.out_here.refs_2_, ...), custom_call_target="tpu_custom_call" | custom-call | flops 1000 | bytes 1000 | tf_op jit(solution)/shard_map/pallas_call | solution.py:40
  107.4 0.6 copy-done.14
  108.1 0.0 copy-start.4
  108.1 3.9 %shard_map.88 = (f32[8,128,128]{2,1,0:T(8,128)}, f32[16,128,128]{2,1,0:T(8,128)}) custom-call(s32[3]{0:T(128)S(1)} %pad_add_fusion.place, f32[16,128,128]{2,1,0:T(8,128)} %pair.7, f32[8,128,128]{2,1,0:T(8,128)S(1)} %shard_map.87.base, f32[8,128,128]{2,1,0:T(8,128)S(1)} %get-tuple-element.103.d_right, ...), custom_call_target="tpu_custom_call" | custom-call | flops 1000 | bytes 1000 | tf_op jit(solution)/shard_map/pallas_call | solution.py:40
  112.0 1.5 %collective-permute-start.19 = (f32[8,128,128]{2,1,0:T(8,128)}, f32[8,128,128]{2,1,0:T(8,128)}, u32[]{:S(2)}, u32[]{:S(2)}) collective-permute-start(f32[8,128,128]{2,1,0:T(8,128)} %get-tuple-element.110), channel_id=1, source_target_pairs={{0,1},{1,0},{2,3},{3,2},{4,5},{5,4},{6,7},{7,6},{8,9},{9,8},{10,11... | collective-permute-start | bytes 1572872 | tf_op jit(solution)/shard_map/ppermute | solution.py:328
  113.5 0.9 copy-done.15
  114.4 1.7 %shard_map.89 = f32[16,128,128]{2,1,0:T(8,128)} custom-call(s32[3]{0:T(128)S(1)} %pad_add_fusion.place, f32[16,8,128]{2,1,0:T(8,128)S(1)} %get-tuple-element.66.refs_0_, f32[16,8,128]{2,1,0:T(8,128)S(1)} %get-tuple-element.68.refs_1_, f32[16,8,128]{2,1,0:T(8,128)S(1)} %get-tuple-element.77.out_here.refs_2_, ...), custom_call_target="tpu_custom_call" | custom-call | flops 1000 | bytes 1000 | tf_op jit(solution)/shard_map/pallas_call | solution.py:40
  116.2 8.0 %collective-permute-done.19 = f32[8,128,128]{2,1,0:T(8,128)} collective-permute-done((f32[8,128,128]{2,1,0:T(8,128)}, f32[8,128,128]{2,1,0:T(8,128)}, u32[]{:S(2)}, u32[]{:S(2)}) %collective-permute-start.19) | collective-permute-done | bytes 524320 | tf_op jit(solution)/shard_map/ppermute | solution.py:328
  124.2 1.1 constant_dynamic-update-slice_fusion
  125.3 0.0 copy-start.20
  125.3 1.0 copy-done.20
  (38 shorter events, 0.1 us)
Async XLA Ops:
  0.7 1.2 copy-start.3
  2.0 1.2 copy-start.5
  3.2 0.7 copy-start.17
  3.9 1.2 copy-start.6
  3.9 13.0 %copy-start.16 = (f32[64,128]{1,0:T(8,128)S(1)}, f32[64,128]{1,0:T(8,128)}, u32[]{:S(2)}) copy-start(f32[64,128]{1,0:T(8,128)} %mine_out.1) | copy-start | bytes 98308
  3.9 18.1 %copy-start.13 = (f32[128,128]{1,0:T(8,128)S(1)}, f32[128,128]{1,0:T(8,128)}, u32[]{:S(2)}) copy-start(f32[128,128]{1,0:T(8,128)} %refs_11_.1) | copy-start | bytes 196612
  4.5 16.3 %collective-permute-start.1 = (f32[21,128,128]{2,1,0:T(8,128)S(1)}, f32[21,128,128]{2,1,0:T(8,128)S(1)}, u32[]{:S(2)}, u32[]{:S(2)}) collective-permute-start(f32[21,128,128]{2,1,0:T(8,128)S(1)} %shard_map.78), channel_id=1, source_target_pairs={{0,2},{2,0},{4,6},{6,4},{8,10},{10,8},{12,14},{14,12},{1,3},{3,1},... | collective-permute-start | bytes 4128776 | tf_op jit(solution)/shard_map/ppermute | solution.py:324
  5.1 6.7 %collective-permute-start = (f32[256,128]{1,0:T(8,128)S(1)}, f32[256,128]{1,0:T(8,128)S(1)}, u32[]{:S(2)}, u32[]{:S(2)}) collective-permute-start(f32[256,128]{1,0:T(8,128)S(1)} %bitcast.14), channel_id=1, source_target_pairs={{0,1},{1,0},{2,3},{3,2},{4,5},{5,4},{6,7},{7,6},{8,9},{9,8},{10,11... | collective-permute-start | bytes 393224 | tf_op jit(solution)/shard_map/ppermute | solution.py:328
  13.5 0.8 copy-start.8
  14.3 16.4 %collective-permute-start.3 = (f32[8,128,128]{2,1,0:T(8,128)S(1)}, f32[8,128,128]{2,1,0:T(8,128)S(1)}, u32[]{:S(2)}, u32[]{:S(2)}) collective-permute-start(f32[8,128,128]{2,1,0:T(8,128)S(1)} %get-tuple-element.59.refs_0_), channel_id=1, source_target_pairs={{0,4},{2,6},{4,0},{6,2},{8,12},{10,14},{12,8},{14,10},{1,5},{3,7},... | collective-permute-start | bytes 1572872 | tf_op jit(solution)/shard_map/ppermute | solution.py:320
  16.2 14.6 %collective-permute-start.4 = (f32[8,128,128]{2,1,0:T(8,128)S(1)}, f32[8,128,128]{2,1,0:T(8,128)S(1)}, u32[]{:S(2)}, u32[]{:S(2)}) collective-permute-start(f32[8,128,128]{2,1,0:T(8,128)S(1)} %get-tuple-element.59.refs_0_), channel_id=1, source_target_pairs={{4,8},{6,10},{8,4},{10,6},{5,9},{7,11},{9,5},{11,7},{20,24},{22,26... | collective-permute-start | bytes 1572872 | tf_op jit(solution)/shard_map/ppermute | solution.py:320
  16.9 4.0 %collective-permute-start.2 = (f32[64,128]{1,0:T(8,128)S(1)}, f32[64,128]{1,0:T(8,128)S(1)}, u32[]{:S(2)}, u32[]{:S(2)}) collective-permute-start(f32[64,128]{1,0:T(8,128)S(1)} %copy-done.16), channel_id=1, source_target_pairs={{0,1},{1,0},{2,3},{3,2},{4,5},{5,4},{6,7},{7,6},{8,9},{9,8},{10,11... | collective-permute-start | bytes 98312 | tf_op jit(solution)/shard_map/ppermute | solution.py:328
  20.8 1.1 copy-start.18
  30.0 0.8 copy-start.9
  30.8 7.0 %copy-start.11 = (f32[8,128,128]{2,1,0:T(8,128)}, f32[8,128,128]{2,1,0:T(8,128)S(1)}, u32[]{:S(2)}) copy-start(f32[8,128,128]{2,1,0:T(8,128)S(1)} %get-tuple-element.100.refs_14_) | copy-start | bytes 1572868
  30.8 14.7 %collective-permute-start.5 = (f32[8,128,128]{2,1,0:T(8,128)S(1)}, f32[8,128,128]{2,1,0:T(8,128)S(1)}, u32[]{:S(2)}, u32[]{:S(2)}) collective-permute-start(f32[8,128,128]{2,1,0:T(8,128)S(1)} %collective-permute-done.3.refs_0_.refs_1_), channel_id=1, source_target_pairs={{4,8},{6,10},{8,4},{10,6},{5,9},{7,11},{9,5},{11,7},{20,24},{22,26... | collective-permute-start | bytes 1572872 | tf_op jit(solution)/shard_map/ppermute | solution.py:320
  31.5 17.1 %collective-permute-start.6 = (f32[8,128,128]{2,1,0:T(8,128)S(1)}, f32[8,128,128]{2,1,0:T(8,128)S(1)}, u32[]{:S(2)}, u32[]{:S(2)}) collective-permute-start(f32[8,128,128]{2,1,0:T(8,128)S(1)} %collective-permute-done.4.refs_0_), channel_id=1, source_target_pairs={{4,0},{6,2},{8,12},{10,14},{5,1},{7,3},{9,13},{11,15},{20,16},{22,... | collective-permute-start | bytes 1572872 | tf_op jit(solution)/shard_map/ppermute | solution.py:320
  32.8 1.2 copy-start
  41.6 4.0 %collective-permute-start.7 = (f32[2,16,8,128]{3,2,1,0:T(8,128)S(1)}, f32[2,16,8,128]{3,2,1,0:T(8,128)S(1)}, u32[]{:S(2)}, u32[]{:S(2)}) collective-permute-start(f32[2,16,8,128]{3,2,1,0:T(8,128)S(1)} %pad_maximum_fusion.1), channel_id=1, source_target_pairs={{0,2},{2,0},{4,6},{6,4},{8,10},{10,8},{12,14},{14,12},{1,3},{3,1},... | collective-permute-start | bytes 393224 | tf_op jit(solution)/shard_map/ppermute | solution.py:324
  44.6 1.0 copy-start.7
  48.6 16.5 %collective-permute-start.8 = (f32[8,128,128]{2,1,0:T(8,128)S(1)}, f32[8,128,128]{2,1,0:T(8,128)S(1)}, u32[]{:S(2)}, u32[]{:S(2)}) collective-permute-start(f32[8,128,128]{2,1,0:T(8,128)S(1)} %collective-permute-done.5.refs_0_), channel_id=1, source_target_pairs={{4,0},{6,2},{8,12},{10,14},{5,1},{7,3},{9,13},{11,15},{20,16},{22,... | collective-permute-start | bytes 1572872 | tf_op jit(solution)/shard_map/ppermute | solution.py:320
  54.4 16.4 %collective-permute-start.9 = (f32[8,128,128]{2,1,0:T(8,128)S(1)}, f32[8,128,128]{2,1,0:T(8,128)S(1)}, u32[]{:S(2)}, u32[]{:S(2)}) collective-permute-start(f32[8,128,128]{2,1,0:T(8,128)S(1)} %get-tuple-element.82), channel_id=1, source_target_pairs={{0,4},{2,6},{12,8},{14,10},{1,5},{3,7},{13,9},{15,11},{16,20},{18,... | collective-permute-start | bytes 1572872 | tf_op jit(solution)/shard_map/ppermute | solution.py:320
  59.0 11.8 %collective-permute-start.10 = (f32[8,128,128]{2,1,0:T(8,128)S(1)}, f32[8,128,128]{2,1,0:T(8,128)S(1)}, u32[]{:S(2)}, u32[]{:S(2)}) collective-permute-start(f32[8,128,128]{2,1,0:T(8,128)S(1)} %get-tuple-element.82), channel_id=1, source_target_pairs={{4,8},{6,10},{8,4},{10,6},{5,9},{7,11},{9,5},{11,7},{20,24},{22,26... | collective-permute-start | bytes 1572872 | tf_op jit(solution)/shard_map/ppermute | solution.py:320
  59.8 9.8 %collective-permute-start.11 = (f32[2,2,16,8,128]{4,3,2,1,0:T(8,128)S(1)}, f32[2,2,16,8,128]{4,3,2,1,0:T(8,128)S(1)}, u32[]{:S(2)}, u32[]{:S(2)}) collective-permute-start(f32[2,2,16,8,128]{4,3,2,1,0:T(8,128)S(1)} %pad_maximum_fusion), channel_id=1, source_target_pairs={{0,1},{1,0},{2,3},{3,2},{4,5},{5,4},{6,7},{7,6},{8,9},{9,8},{10,11... | collective-permute-start | bytes 786440 | tf_op jit(solution)/shard_map/ppermute | solution.py:328
  75.7 9.8 %collective-permute-start.12 = (f32[18,128,128]{2,1,0:T(8,128)}, f32[18,128,128]{2,1,0:T(8,128)S(1)}, u32[]{:S(2)}, u32[]{:S(2)}) collective-permute-start(f32[18,128,128]{2,1,0:T(8,128)} %get-tuple-element.93), channel_id=1, source_target_pairs={{0,2},{2,0},{4,6},{6,4},{8,10},{10,8},{12,14},{14,12},{1,3},{3,1},... | collective-permute-start | bytes 3538952 | tf_op jit(solution)/shard_map/ppermute | solution.py:324
  75.8 32.3 %collective-permute-start.16 = (f32[8,128,128]{2,1,0:T(8,128)S(1)}, f32[8,128,128]{2,1,0:T(8,128)S(1)}, u32[]{:S(2)}, u32[]{:S(2)}) collective-permute-start(f32[8,128,128]{2,1,0:T(8,128)S(1)} %add.15), channel_id=1, source_target_pairs={{0,4},{2,6},{4,0},{6,2},{8,12},{10,14},{12,8},{14,10},{1,5},{3,7},... | collective-permute-start | bytes 1572872 | tf_op jit(solution)/shard_map/ppermute | solution.py:320
  79.9 24.0 %copy-start.10 = (f32[8,128,128]{2,1,0:T(8,128)S(1)}, f32[8,128,128]{2,1,0:T(8,128)}, u32[]{:S(2)}) copy-start(f32[8,128,128]{2,1,0:T(8,128)} %copy-done.9) | copy-start | bytes 1572868
  80.0 23.9 %copy-start.12 = (f32[8,128,128]{2,1,0:T(8,128)S(1)}, f32[8,128,128]{2,1,0:T(8,128)}, u32[]{:S(2)}) copy-start(f32[8,128,128]{2,1,0:T(8,128)} %copy-done.11) | copy-start | bytes 1572868
  80.0 28.1 %collective-permute-start.17 = (f32[8,128,128]{2,1,0:T(8,128)S(1)}, f32[8,128,128]{2,1,0:T(8,128)S(1)}, u32[]{:S(2)}, u32[]{:S(2)}) collective-permute-start(f32[8,128,128]{2,1,0:T(8,128)S(1)} %add.16), channel_id=1, source_target_pairs={{4,8},{6,10},{8,4},{10,6},{5,9},{7,11},{9,5},{11,7},{20,24},{22,26... | collective-permute-start | bytes 1572872 | tf_op jit(solution)/shard_map/ppermute | solution.py:320
  80.8 27.3 %collective-permute-start.18 = (f32[8,128,128]{2,1,0:T(8,128)S(1)}, f32[8,128,128]{2,1,0:T(8,128)S(1)}, u32[]{:S(2)}, u32[]{:S(2)}) collective-permute-start(f32[8,128,128]{2,1,0:T(8,128)S(1)} %get-tuple-element.106), channel_id=1, source_target_pairs={{0,12},{2,14},{12,0},{14,2},{1,13},{3,15},{13,1},{15,3},{16,28},{1... | collective-permute-start | bytes 1572872 | tf_op jit(solution)/shard_map/ppermute | solution.py:320
  85.5 18.4 %copy-start.1 = (f32[18,128,128]{2,1,0:T(8,128)}, f32[18,128,128]{2,1,0:T(8,128)S(1)}, u32[]{:S(2)}) copy-start(f32[18,128,128]{2,1,0:T(8,128)S(1)} %collective-permute-done.12.received.refs_6_) | copy-start | bytes 3538948
  86.2 10.6 %collective-permute-start.13 = (f32[5,128,128]{2,1,0:T(8,128)S(1)}, f32[5,128,128]{2,1,0:T(8,128)S(1)}, u32[]{:S(2)}, u32[]{:S(2)}) collective-permute-start(f32[5,128,128]{2,1,0:T(8,128)S(1)} %get-tuple-element.95), channel_id=1, source_target_pairs={{0,1},{1,0},{2,3},{3,2},{4,5},{5,4},{6,7},{7,6},{8,9},{9,8},{10,11... | collective-permute-start | bytes 983048 | tf_op jit(solution)/shard_map/ppermute | solution.py:328
  87.8 16.1 %collective-permute-start.14 = (f32[5,128,128]{2,1,0:T(8,128)S(1)}, f32[5,128,128]{2,1,0:T(8,128)S(1)}, u32[]{:S(2)}, u32[]{:S(2)}) collective-permute-start(f32[5,128,128]{2,1,0:T(8,128)S(1)} %get-tuple-element.96), channel_id=1, source_target_pairs={{0,1},{1,0},{2,3},{3,2},{4,5},{5,4},{6,7},{7,6},{8,9},{9,8},{10,11... | collective-permute-start | bytes 983048 | tf_op jit(solution)/shard_map/ppermute | solution.py:328
  96.9 10.5 %collective-permute-start.15 = (f32[2,128,128]{2,1,0:T(8,128)S(1)}, f32[2,128,128]{2,1,0:T(8,128)S(1)}, u32[]{:S(2)}, u32[]{:S(2)}) collective-permute-start(f32[2,128,128]{2,1,0:T(8,128)S(1)} %get-tuple-element.101), channel_id=1, source_target_pairs={{0,1},{1,0},{2,3},{3,2},{4,5},{5,4},{6,7},{7,6},{8,9},{9,8},{10,11... | collective-permute-start | bytes 393224 | tf_op jit(solution)/shard_map/ppermute | solution.py:328
  107.4 0.7 copy-start.14
  108.1 5.4 %copy-start.2 = (f32[18,128,128]{2,1,0:T(8,128)S(1)}, f32[18,128,128]{2,1,0:T(8,128)}, u32[]{:S(2)}) copy-start(f32[18,128,128]{2,1,0:T(8,128)} %copy-done.1) | copy-start | bytes 3538948
  108.1 5.4 %copy-start.4 = (f32[16,128,128]{2,1,0:T(8,128)S(1)}, f32[16,128,128]{2,1,0:T(8,128)}, u32[]{:S(2)}) copy-start(f32[16,128,128]{2,1,0:T(8,128)} %get-tuple-element.112.refs_9_.refs_10_) | copy-start | bytes 3145732
  112.0 12.2 %collective-permute-start.19 = (f32[8,128,128]{2,1,0:T(8,128)}, f32[8,128,128]{2,1,0:T(8,128)}, u32[]{:S(2)}, u32[]{:S(2)}) collective-permute-start(f32[8,128,128]{2,1,0:T(8,128)} %get-tuple-element.110), channel_id=1, source_target_pairs={{0,1},{1,0},{2,3},{3,2},{4,5},{5,4},{6,7},{7,6},{8,9},{9,8},{10,11... | collective-permute-start | bytes 1572872 | tf_op jit(solution)/shard_map/ppermute | solution.py:328
  113.5 0.9 copy-start.15
  114.4 9.8 %copy-start.19 = (f32[16,128,128]{2,1,0:T(8,128)S(1)}, f32[16,128,128]{2,1,0:T(8,128)}, u32[]{:S(2)}) copy-start(f32[16,128,128]{2,1,0:T(8,128)} %get-tuple-element.114) | copy-start | bytes 3145732
  125.3 1.0 copy-start.20

commit v3 on v2

--- a/solution.py
+++ b/solution.py
@@ -43,7 +43,7 @@
         in_specs=[smem] + [vmem] * (len(args) - 1),
         out_specs=[vmem] * len(outs),
         scratch_shapes=[pltpu.VMEM(shape, F32) for shape in scratch],
-        compiler_params=pltpu.CompilerParams(vmem_limit_bytes=50 * 1024 * 1024),
+        compiler_params=pltpu.CompilerParams(vmem_limit_bytes=24 * 1024 * 1024),
         cost_estimate=pl.CostEstimate(flops=flops, bytes_accessed=flops, transcendentals=0),
     )(*args)
 
@@ -58,16 +58,6 @@
 def first_col(place, chip, core, rows):
     half = rows // 2
     return pl.multiple_of(chip * 2 * rows + core * rows + place[2] * half, half)
-
-
-def rows_kernel(place, pair, mask, cotangent, packed):
-    rows, cols, width = pair.shape
-    half = rows // 2
-    packed[:rows] = pair[...]
-    for chip in range(cols // (2 * rows)):
-        block = cotangent[:, pl.ds(first_col(place, chip, 1 - place[1], rows), half), :]
-        packed[rows + chip] = flat(block)
-    packed[packed.shape[0] - 1, :rows] = mask[...].astype(F32)
 
 
 def both_halves(place, mine, other):
@@ -90,20 +80,37 @@
     return sig * proj[:, :chans], sig
 
 
-def right_kernel(rows, place, pair, mask, mine, other, right, open_part, slope):
+def first_kernel(place, pair, mask, cotangent, w_proj, normed, scale, keep, mine, first, second, third):
+    rows, cols, width = pair.shape
+    half = rows // 2
+    chips = cols // (2 * rows)
+    mine[...] = w_proj[...]
+    keep[...] = mask[...].astype(F32)
+    for t in range(0, half, CHUNK):
+        at = slice(t, t + CHUNK)
+        value, factor = norm(pair[pl.ds(source_row(place, t, rows), CHUNK)])
+        normed[at] = value
+        scale[at] = jnp.broadcast_to(factor, value.shape)
+    first[...] = pair[:half]
+    second[...] = pair[half:]
+    for chip in range(chips):
+        third[chip] = flat(cotangent[:, pl.ds(first_col(place, chip, 1 - place[1], rows), half), :])
+    third[chips, :rows] = keep[...]
+
+
+def right_kernel(rows, place, normed, keep, mine, other, right, open_part, slope):
     half, cols, chans = right.shape
     w = gated_weights(place, mine, other, 2)
     for t in range(0, half, CHUNK):
-        row = source_row(place, t, rows)
-        normed, _ = norm(flat(pair[pl.ds(row, CHUNK)]))
-        value, sig = gated(normed, mask[pl.ds(row, CHUNK), :].astype(F32), w)
+        at = slice(t, t + CHUNK)
+        value, sig = gated(flat(normed[at]), keep[pl.ds(source_row(place, t, rows), CHUNK), :], w)
         shape = (CHUNK, cols, chans)
-        right[t : t + CHUNK] = value.reshape(shape)
-        open_part[t : t + CHUNK] = sig.reshape(shape)
-        slope[t : t + CHUNK] = (value * (1.0 - sig)).reshape(shape)
-
-
-def prepare_kernel(rows, place, pair, mask, cotangent, there, mine, other, w_gate, mine_out, other_out, *refs):
+        right[at] = value.reshape(shape)
+        open_part[at] = sig.reshape(shape)
+        slope[at] = (value * (1.0 - sig)).reshape(shape)
+
+
+def prepare_kernel(rows, place, pair, keep, cotangent, first, second, third, mine, other, w_gate, mine_out, other_out, *refs):
     left_here, left_there, open_part, slope, gate, d_here, d_there, w_out, normed_rows = refs
     half, cols, chans = open_part.shape
     chips = cols // (2 * rows)
@@ -114,7 +121,7 @@
         row = source_row(place, t, rows)
         at = slice(t, t + CHUNK)
         normed, _ = norm(flat(pair[pl.ds(row, CHUNK)]))
-        value, sig = gated(normed, mask[pl.ds(row, CHUNK), :].astype(F32), w)
+        value, sig = gated(normed, keep[pl.ds(row, CHUNK), :], w)
         left_here[at] = value.reshape(shape)
         if t < half:
             open_part[at] = sig.reshape(shape)
@@ -123,8 +130,9 @@
         for chip in range(chips):
             near = pl.ds(first_col(place, chip, place[1], rows), half)
             d_here[chip, at] = gate[at, near, :] * cotangent[pl.ds(row, CHUNK), near, :]
-        normed, _ = norm(flat(there[pl.ds(row, CHUNK)]))
-        value, _ = gated(normed, there[there.shape[0] - 1, pl.ds(row, CHUNK), :], w)
+        their_row = row % half
+        normed, _ = norm(flat(jnp.where(row < half, first[pl.ds(their_row, CHUNK)], second[pl.ds(their_row, CHUNK)])))
+        value, _ = gated(normed, third[chips, pl.ds(row, CHUNK), :], w)
         left_there[at] = value.reshape(shape)
         normed_rows[...] = normed.reshape(CHUNK, cols, -1)
         picked = [
@@ -132,7 +140,7 @@
         ]
         opened = jax.nn.sigmoid(dot(flat(jnp.stack(picked)), w_gate[...])).reshape(chips, CHUNK, half, -1)
         for chip in range(chips):
-            d_out = there[rows + chip, pl.ds(row * half, CHUNK * half), :].reshape(CHUNK, half, -1)
+            d_out = third[chip, pl.ds(row * half, CHUNK * half), :].reshape(CHUNK, half, -1)
             d_there[chip, at] = opened[chip] * d_out
 
 
@@ -230,20 +238,21 @@
         outs[1][rows + plane - 2] = flat(base[plane][...])
 
 
-def share_kernel(place, kept, received, out_here, out_next, d_left, packed, packed_next, rest):
+def share_kernel(place, kept, *refs):
+    received, outs, (d_left, *packed, rest) = refs[0], refs[1:3], refs[3:]
     half = d_left.shape[0]
+    part = half // 2
     block = half * half
     d_left[...] = kept[:half] + received[:half]
-    part = half // 2
-    packed[:part] = kept[half : half + part] + received[half : half + part]
-    packed_next[:part] = kept[half + part :] + received[half + part : 2 * half]
-    for step, out in enumerate((out_here, out_next)):
+    for at in range(2):
+        here = slice(half + at * part, half + (at + 1) * part)
+        packed[at][:part] = kept[here] + received[here]
+    for step, out in enumerate(outs):
         at = slice(step * block, (step + 1) * block)
-        plane = 2 * half + step
-        packed[part, at] = flat(out[half:])
-        packed_next[part, at] = received[plane, block:]
+        packed[0][part, at] = flat(out[half:])
+        packed[1][part, at] = received[2 * half + step, block:]
         rest[0, at] = flat(out[:half])
-        rest[1, at] = received[plane, :block]
+        rest[1, at] = received[2 * half + step, :block]
 
 
 def gather_out(place, rows, t, out, here, early_other, early_far, received, far):
@@ -295,13 +304,12 @@
         at = slice(t, t + CHUNK)
         opened = gate[at]
         d_gate = cotangent[pl.ds(source_row(place, t, rows), CHUNK)] * (opened * out[at]) * (1.0 - opened)
-        from_other = (far if t < part else far_next)[t % part : t % part + CHUNK]
-        grad = flat(d_left[at] + from_other)
+        grad = flat(d_left[at] + (far, far_next)[t // part][t % part : t % part + CHUNK])
         both = jnp.concatenate([grad * flat(open_part[at]), grad * flat(slope[at])], axis=1)
         base[at] = (dot_t(flat(d_gate), w_gate[...]) + dot(both, w)).reshape(CHUNK, cols, -1)
 
 
-def pair_kernel(rows, place, pair, base, d_right, d_right_near, d_right_middle, d_right_far, open_part, slope, mine, other, d_mine, d_pair):
+def pair_kernel(rows, place, normed, scale, base, d_right, d_right_near, d_right_middle, d_right_far, open_part, slope, mine, other, d_mine, d_pair):
     half, cols, chans = base.shape
     w = gated_weights(place, mine, other, 2)
     for t in range(0, half, CHUNK):
@@ -309,11 +317,31 @@
         grad = flat(d_right[at] + d_right_near[at] + (d_right_middle[at] + d_right_far[at]))
         both = jnp.concatenate([grad * flat(open_part[at]), grad * flat(slope[at])], axis=1)
         d_normed = flat(base[at]) + dot(both, w)
-        normed, scale = norm(flat(pair[pl.ds(source_row(place, t, rows), CHUNK)]))
+        value = flat(normed[at])
         mean_grad = jnp.mean(d_normed, axis=-1, keepdims=True)
-        mean_cross = jnp.mean(d_normed * normed, axis=-1, keepdims=True)
-        d_mine[at] = ((d_normed - mean_grad - normed * mean_cross) * scale).reshape(CHUNK, cols, -1)
+        mean_cross = jnp.mean(d_normed * value, axis=-1, keepdims=True)
+        d_mine[at] = ((d_normed - mean_grad - value * mean_cross) * flat(scale[at])).reshape(CHUNK, cols, -1)
         d_pair[pl.ds(source_row(place, t, rows), CHUNK)] = d_mine[at]
+
+
+def join_kernel(place, other, whole, joined, sem):
+    half = other.shape[0]
+    copy = pltpu.make_async_copy(other, joined.at[pl.ds((1 - lax.axis_index("ch")) * half, half)], sem)
+    copy.start()
+    copy.wait()
+
+
+def join(place, other, whole):
+    anywhere = pl.BlockSpec(memory_space=pl.ANY)
+    return pl.pallas_call(
+        join_kernel,
+        out_shape=jax.ShapeDtypeStruct(whole.shape, F32),
+        in_specs=[pl.BlockSpec(memory_space=pltpu.SMEM), pl.BlockSpec(memory_space=pltpu.VMEM), anywhere],
+        out_specs=anywhere,
+        input_output_aliases={2: 0},
+        compiler_params=pltpu.CompilerParams(vmem_limit_bytes=2 * 1024 * 1024),
+        scratch_shapes=[pltpu.SemaphoreType.DMA],
+    )(place, other, whole)
 
 
 def along(block, pairs):
@@ -343,15 +371,18 @@
     row, side = lax.axis_index("row"), lax.axis_index("ch")
     place = jnp.stack([row // 2, row % 2, side]).astype(jnp.int32)
 
-    mine = jnp.swapaxes(w_proj, 1, 2)
-    other = other_half(flat(mine)).reshape(mine.shape)
+    w_mine = jnp.swapaxes(w_proj, 1, 2)
+    other = other_half(flat(w_mine)).reshape(w_mine.shape)
+    kept = (half, cols, chans)
+    normed, scale, keep, mine, *sent = call(
+        first_kernel,
+        [(half, cols, width)] * 2 + [(rows, cols), w_mine.shape] + [(half, cols, width)] * 2 + [(chips + 1, cols, width)],
+        (place, pair, pair_mask, cotangent, w_mine),
+    )
+    theirs = [other_core(block) for block in sent]
     other_out = other_half(w_out)
-    (sent,) = call(rows_kernel, [(rows + chips + 1, cols, width)], (place, pair, pair_mask, cotangent), flops=10**9)
-    there = other_core(sent)
-
-    kept = (half, cols, chans)
     right, open_right, slope_right = call(
-        functools.partial(right_kernel, rows), [kept] * 3, (place, pair, pair_mask, mine, other)
+        functools.partial(right_kernel, rows), [kept] * 3, (place, normed, keep, mine, other)
     )
     near = along(right, NEXT)
     middle = along(right, MIDDLE)
@@ -363,7 +394,7 @@
     left, left_there, open_left, slope_left, gate, d_here, d_there, w_all_out = call(
         functools.partial(prepare_kernel, rows),
         [(rows, cols, chans)] * 2 + [kept] * 2 + [(rows, cols, width), quarter, quarter, (chans, width)],
-        (place, pair, pair_mask, cotangent, there, mine, other, w_gate, w_out, other_out),
+        (place, pair, keep, cotangent, *theirs, mine, other, w_gate, w_out, other_out),
         scratch=[(CHUNK, cols, width)],
     )
 
@@ -388,7 +419,7 @@
         [(rows, cols, chans)] * 2,
         (place, *rights[:2], *d_x[:2]),
     )
-    cross, outer, early_other, d_left_here = lax.optimization_barrier((cross, outer, early_other, d_left_here))
+    cross, early_other, d_left_here = lax.optimization_barrier((cross, early_other, d_left_here))
     far = along(cross, OUTWARD)
     early_far = other_half(jnp.stack([jnp.stack(out_here[:2]), early_other]))
     tile(2, cross, outer)
@@ -396,26 +427,28 @@
     swapped = along(d_right[2], MIDDLE)
     far, d_x[2] = lax.optimization_barrier((far, d_x[2]))
     tile(3, middle, far)
-    from_far = along(d_right[3], ENDS)
-    inward, swapped, early_far, d_x[3] = lax.optimization_barrier((inward, swapped, early_far, d_x[3]))
     d_left_kept, d_left_sent = call(
         functools.partial(left_kernel, 2, 4),
         [(rows, cols, chans), (rows + 2, cols, chans)],
         (place, *rights[2:], *d_x[2:], d_left_here, d_left_there, out_there[2], out_there[3]),
     )
+    to_near, to_middle, early_far, d_left_sent = lax.optimization_barrier(
+        (d_right[1] + swapped, d_right[3] + inward, early_far, d_left_sent)
+    )
     received = other_core(d_left_sent)
-    from_near = along(d_right[1] + swapped, NEXT)
-    from_middle = along(d_right[3] + inward, MIDDLE)
+    from_near = along(to_near, NEXT)
+    from_middle = along(to_middle, MIDDLE)
+    from_far = along(d_right[3], ENDS)
     packed_shape = (half // 2 + 1, cols, chans)
-    d_left, shared, shared_next, rest = call(
+    d_left, *shared, rest = call(
         share_kernel,
         [kept, packed_shape, packed_shape, (2, cols, chans)],
         (place, d_left_kept, received, out_here[2], out_here[3]),
     )
-    shared_other = other_half(shared)
-    shared_other_next = other_half(shared_next)
+    shared = [other_half(part) for part in shared]
+    *shared, rest, from_far = lax.optimization_barrier((*shared, rest, from_far))
     rest_other = other_half(rest)
-    outs = (*out_here, early_other, early_far, received, shared_other, shared_other_next)
+    outs = (*out_here, early_other, early_far, received, *shared)
     (base,) = call(
         functools.partial(base_kernel, rows),
         [(half, cols, width)],
@@ -426,7 +459,7 @@
     d_mine, d_pair = call(
         functools.partial(pair_kernel, rows),
         [(half, cols, width), (rows, cols, width)],
-        (place, pair, base, d_right[0], from_near, from_middle, from_far, open_right, slope_right, mine, other),
+        (place, normed, scale, base, d_right[0], from_near, from_middle, from_far, open_right, slope_right, mine, other),
     )
     d_other = other_half(d_mine)
     _, gate_late = lax.optimization_barrier((d_mine, gate))
@@ -437,7 +470,7 @@
         scratch=[(rows, cols, width)],
     )
     d_other, update = lax.optimization_barrier((d_other, update))
-    d_pair = lax.dynamic_update_slice_in_dim(d_pair, d_other, (1 - side) * half, 0)
+    d_pair = join(place, d_other, d_pair)
     return (update, d_pair)
 
 

time: 127 us -> 114 us (0.90)
  waiting for transfers between devices: 36.5 us -> 45 us
  local copies, waits for them, and re-layouts: 11.7 us -> 4.06 us
  starting transfers between devices: 32.2 us -> 25.1 us
  Pallas kernels: 44.6 us -> 38.3 us
    ppermute x10, waiting for transfers between devices: 7.93 us -> 21.5 us  [along(): lax.ppermute(block, 'row', [(2 * a + core, 2 * b + core) for a, b in pair...]
    pallas_call x13, Pallas kernels: 44.6 us -> 36.9 us  [call(): pl.pallas_call(kernel, out_shape=[jax.ShapeDtypeStruct(shape, F32) for sh...]
    ppermute x7, waiting for transfers between devices: 28.5 us -> 21.8 us  [other_half(): return lax.ppermute(block, 'ch', [(0, 1), (1, 0)])]
    unnamed x42 -> x16, local copies, waits for them, and re-layouts: 10.6 us -> 4.06 us
    ppermute x10, starting transfers between devices: 20.7 us -> 17 us  [along(): lax.ppermute(block, 'row', [(2 * a + core, 2 * b + core) for a, b in pair...]
    ppermute x7, starting transfers between devices: 10.9 us -> 7.36 us  [other_half(): return lax.ppermute(block, 'ch', [(0, 1), (1, 0)])]
    ppermute x3 -> x5, waiting for transfers between devices: 0.01 us -> 1.64 us  [other_core(): lax.ppermute(block, 'row', [(i, i ^ 1) for i in range(lax.axis_size('row'...]
    pallas_call x0 -> x1, Pallas kernels: none -> 1.35 us  [join(): pl.pallas_call(join_kernel, out_shape=jax.ShapeDtypeStruct(whole.shape, F...]
  transfers between devices with their start and end apart: 20 -> 22, of which waited for: 8 -> 10; matrix products, arithmetic and copies ran while one was open for 0% -> 0% of each run, Pallas kernels for 28% -> 30%
where the time goes in v3:
time: 114 us
  waiting for transfers between devices  45 us (39%)
  Pallas kernels  38.3 us (34%)
  starting transfers between devices  25.1 us (22%)
  local copies, waits for them, and re-layouts  4.06 us (4%)
    pallas_call x13, Pallas kernels, call(): pl.pallas_call(kernel, out_shape=[jax.ShapeDtypeStruct(shape, F32) for sh...  36.9 us
    ppermute x7, waiting for transfers between devices, other_half(): return lax.ppermute(block, 'ch', [(0, 1), (1, 0)])  21.8 us
    ppermute x10, waiting for transfers between devices, along(): lax.ppermute(block, 'row', [(2 * a + core, 2 * b + core) for a, b in pair...  21.5 us
    ppermute x10, starting transfers between devices, along(): lax.ppermute(block, 'row', [(2 * a + core, 2 * b + core) for a, b in pair...  17 us
    ppermute x7, starting transfers between devices, other_half(): return lax.ppermute(block, 'ch', [(0, 1), (1, 0)])  7.36 us
    unnamed x16, local copies, waits for them, and re-layouts  4.06 us
  transfers between devices with their start and end apart: 22, of which 10 were waited for; matrix products, arithmetic and copies ran while one was open for 0% of the time, Pallas kernels for 30%

profile of v3, /device:TPU:0, one launch (start us, length us, event | category | flops | bytes accessed | tf_op | source)
XLA Modules:
  0.0 113.7 jit_solution(11442202852792630987)
XLA Ops:
  0.6 3.0 %collective-permute-start = (f32[256,128]{1,0:T(8,128)}, f32[256,128]{1,0:T(8,128)S(1)}, u32[]{:S(2)}, u32[]{:S(2)}) collective-permute-start(f32[256,128]{1,0:T(8,128)} %bitcast.21), channel_id=1, source_target_pairs={{0,1},{1,0},{2,3},{3,2},{4,5},{5,4},{6,7},{7,6},{8,9},{9,8},{10,11... | collective-permute-start | bytes 393224 | tf_op jit(solution)/shard_map/ppermute | solution.py:356
  3.6 0.1 pad_add_fusion.place
  3.7 1.2 %copy-done = f32[16,128,128]{2,1,0:T(8,128)S(1)} copy-done((f32[16,128,128]{2,1,0:T(8,128)S(1)}, f32[16,128,128]{2,1,0:T(8,128)}, u32[]{:S(2)}) %copy-start) | copy-done | bytes 1048600
  4.9 1.2 %copy-done.2 = f32[16,128,128]{2,1,0:T(8,128)S(1)} copy-done((f32[16,128,128]{2,1,0:T(8,128)S(1)}, f32[16,128,128]{2,1,0:T(8,128)}, u32[]{:S(2)}) %copy-start.2) | copy-done | bytes 1048600
  6.2 0.9 copy-done.5
  7.1 0.7 copy-done.7
  7.8 1.0 shard_map.77
  8.8 0.1 collective-permute-start.1
  8.8 0.5 collective-permute-start.2
  9.3 0.0 collective-permute-done
  9.3 1.6 %shard_map.78 = (f32[8,128,128]{2,1,0:T(8,128)S(1)}, f32[8,128,128]{2,1,0:T(8,128)S(1)}, f32[8,128,128]{2,1,0:T(8,128)S(1)}) custom-call(s32[3]{0:T(128)S(1)} %pad_add_fusion.place, f32[8,128,128]{2,1,0:T(8,128)S(1)} %get-tuple-element.69.normed, f32[16,128]{1,0:T(8,128)S(1)} %get-tuple-element.71.keep, f32[4,64,128]{2,1,0:T(8,128)S(1)} %get-tuple-element.72.mine.refs_15_, ...), custom_call_target="tpu_custom_call" | custom-call | flops 1000 | bytes 1000 | tf_op jit(solution)/shard_map/pallas_call | solution.py:40
  11.0 1.6 %collective-permute-start.5 = (f32[8,128,128]{2,1,0:T(8,128)S(1)}, f32[8,128,128]{2,1,0:T(8,128)S(1)}, u32[]{:S(2)}, u32[]{:S(2)}) collective-permute-start(f32[8,128,128]{2,1,0:T(8,128)S(1)} %get-tuple-element.73.refs_0_), channel_id=1, source_target_pairs={{0,4},{2,6},{4,0},{6,2},{8,12},{10,14},{12,8},{14,10},{1,5},{3,7},... | collective-permute-start | bytes 1572872 | tf_op jit(solution)/shard_map/ppermute | solution.py:348
  12.6 0.7 collective-permute-start.6
  13.3 0.6 collective-permute-start.4
  13.9 3.4 %collective-permute-done.4.other_out = f32[64,128]{1,0:T(8,128)S(1)} collective-permute-done((f32[64,128]{1,0:T(8,128)S(1)}, f32[64,128]{1,0:T(8,128)S(1)}, u32[]{:S(2)}, u32[]{:S(2)}) %collective-permute-start.4) | collective-permute-done | bytes 32800 | tf_op jit(solution)/shard_map/ppermute | solution.py:356
  17.3 0.0 collective-permute-start.3
  17.3 1.6 %collective-permute-done.3.third = f32[5,128,128]{2,1,0:T(8,128)S(1)} collective-permute-done((f32[5,128,128]{2,1,0:T(8,128)S(1)}, f32[5,128,128]{2,1,0:T(8,128)S(1)}, u32[]{:S(2)}, u32[]{:S(2)}) %collective-permute-start.3) | collective-permute-done | bytes 327712 | tf_op jit(solution)/shard_map/ppermute | solution.py:352
  18.9 0.0 collective-permute-done.1.first
  18.9 0.0 collective-permute-done.2.second
  18.9 5.5 %shard_map.79 = (f32[16,128,128]{2,1,0:T(8,128)S(1)}, f32[16,128,128]{2,1,0:T(8,128)S(1)}, f32[8,128,128]{2,1,0:T(8,128)S(1)}, f32[8,128,128]{2,1,0:T(8,128)S(1)...) custom-call(s32[3]{0:T(128)S(1)} %pad_add_fusion.place, ...), custom_call_target="tpu_custom_call" | custom-call | flops 1000 | bytes 1000 | tf_op jit(solution)/shard_map/pallas_call | solution.py:40
  24.4 0.5 collective-permute-done.5.refs_0_.refs_1_
  24.9 0.0 collective-permute-done.6.refs_0_
  24.9 0.7 collective-permute-start.7
  25.6 1.3 %collective-permute-start.9 = (f32[8,128,128]{2,1,0:T(8,128)S(1)}, f32[8,128,128]{2,1,0:T(8,128)S(1)}, u32[]{:S(2)}, u32[]{:S(2)}) collective-permute-start(f32[8,128,128]{2,1,0:T(8,128)S(1)} %collective-permute-done.6.refs_0_), channel_id=1, source_target_pairs={{4,0},{6,2},{8,12},{10,14},{5,1},{7,3},{9,13},{11,15},{20,16},{22,... | collective-permute-start | bytes 1572872 | tf_op jit(solution)/shard_map/ppermute | solution.py:348
  26.9 3.9 %shard_map.80 = (f32[16,8,128]{2,1,0:T(8,128)S(1)}, f32[16,8,128]{2,1,0:T(8,128)S(1)}, f32[256,128]{1,0:T(8,128)S(1)}, f32[8,128,128]{2,1,0:T(8,128)S(1)}) custom-call(s32[3]{0:T(128)S(1)} %pad_add_fusion.place, f32[8,128,128]{2,1,0:T(8,128)S(1)} %get-tuple-element.73.refs_0_, f32[16,128,128]{2,1,0:T(8,128)S(1)} %get-tuple-element.77.refs_1_.refs_2_, ...), custom_call_target="tpu_custom_call" | custom-call | flops 1000 | bytes 1000 | tf_op jit(solution)/shard_map/pallas_call | solution.py:40
  30.8 3.9 %shard_map.81 = (f32[16,8,128]{2,1,0:T(8,128)S(1)}, f32[16,8,128]{2,1,0:T(8,128)S(1)}, f32[256,128]{1,0:T(8,128)S(1)}, f32[8,128,128]{2,1,0:T(8,128)S(1)}) custom-call(s32[3]{0:T(128)S(1)} %pad_add_fusion.place, f32[8,128,128]{2,1,0:T(8,128)S(1)} %collective-permute-done.5.refs_0_.refs_1_, f32[16,128,128]{2,1,0:T(8,128)S(1)} %get-tuple-element.77.refs_1_.refs_2_, ...), custom_call_target="tpu_custom_call" | custom-call | flops 1000 | bytes 1000 | tf_op jit(solution)/shard_map/pallas_call | solution.py:40
  34.7 0.1 collective-permute-start.8
  34.8 2.9 %shard_map.82 = (f32[16,128,128]{2,1,0:T(8,128)S(1)}, f32[16,128,128]{2,1,0:T(8,128)S(1)}) custom-call(s32[3]{0:T(128)S(1)} %pad_add_fusion.place, f32[8,128,128]{2,1,0:T(8,128)S(1)} %get-tuple-element.73.refs_0_, f32[8,128,128]{2,1,0:T(8,128)S(1)} %collective-permute-done.5.refs_0_.refs_1_, f32[256,128]{1,0:T(8,128)S(1)} %get-tuple-element.88.refs_2_, ...), custom_call_target="tpu_custom_call" | custom-call | flops 1000 | bytes 1000 | tf_op jit(solution)/shard_map/pallas_call | solution.py:40
  37.7 0.0 collective-permute-done.8.refs_4_
  37.7 0.0 collective-permute-done.7.refs_0_
  37.7 1.3 %collective-permute-start.10 = (f32[8,128,128]{2,1,0:T(8,128)S(1)}, f32[8,128,128]{2,1,0:T(8,128)S(1)}, u32[]{:S(2)}, u32[]{:S(2)}) collective-permute-start(f32[8,128,128]{2,1,0:T(8,128)S(1)} %collective-permute-done.7.refs_0_), channel_id=1, source_target_pairs={{4,0},{6,2},{8,12},{10,14},{5,1},{7,3},{9,13},{11,15},{20,16},{22,... | collective-permute-start | bytes 1572872 | tf_op jit(solution)/shard_map/ppermute | solution.py:348
  39.0 6.2 %collective-permute-done.9.refs_1_ = f32[8,128,128]{2,1,0:T(8,128)S(1)} collective-permute-done((f32[8,128,128]{2,1,0:T(8,128)S(1)}, f32[8,128,128]{2,1,0:T(8,128)S(1)}, u32[]{:S(2)}, u32[]{:S(2)}) %collective-permute-start.9) | collective-permute-done | bytes 524320 | tf_op jit(solution)/shard_map/ppermute | solution.py:348
  45.2 3.9 %shard_map.83 = (f32[16,8,128]{2,1,0:T(8,128)S(1)}, f32[16,8,128]{2,1,0:T(8,128)S(1)}, f32[256,128]{1,0:T(8,128)S(1)}, f32[8,128,128]{2,1,0:T(8,128)S(1)}, f32[8,128,128]{2,1,0:T(8,128)S(1)}) custom-call(s32[3]{0:T(128)S(1)} %pad_add_fusion.place, f32[8,128,128]{2,1,0:T(8,128)S(1)} %collective-permute-done.7.refs_0_, ...), custom_call_target="tpu_custom_call" | custom-call | flops 1000 | bytes 1000 | tf_op jit(solution)/shard_map/pallas_call | solution.py:40
  49.1 0.7 collective-permute-start.11
  49.8 5.2 %collective-permute-start.12 = (f32[8,128,128]{2,1,0:T(8,128)S(1)}, f32[8,128,128]{2,1,0:T(8,128)S(1)}, u32[]{:S(2)}, u32[]{:S(2)}) collective-permute-start(f32[8,128,128]{2,1,0:T(8,128)S(1)} %get-tuple-element.99), channel_id=1, source_target_pairs={{0,4},{2,6},{12,8},{14,10},{1,5},{3,7},{13,9},{15,11},{16,20},{18,... | collective-permute-start | bytes 1572872 | tf_op jit(solution)/shard_map/ppermute | solution.py:348
  55.1 0.6 collective-permute-start.13
  55.7 3.5 %collective-permute-done.10.refs_1_ = f32[8,128,128]{2,1,0:T(8,128)S(1)} collective-permute-done((f32[8,128,128]{2,1,0:T(8,128)S(1)}, f32[8,128,128]{2,1,0:T(8,128)S(1)}, u32[]{:S(2)}, u32[]{:S(2)}) %collective-permute-start.10) | collective-permute-done | bytes 524320 | tf_op jit(solution)/shard_map/ppermute | solution.py:348
  59.1 3.9 %shard_map.84 = (f32[16,8,128]{2,1,0:T(8,128)S(1)}, f32[16,8,128]{2,1,0:T(8,128)S(1)}, f32[256,128]{1,0:T(8,128)S(1)}, f32[8,128,128]{2,1,0:T(8,128)S(1)}, f32[8,128,128]{2,1,0:T(8,128)S(1)}) custom-call(s32[3]{0:T(128)S(1)} %pad_add_fusion.place, f32[8,128,128]{2,1,0:T(8,128)S(1)} %collective-permute-done.6.refs_0_, ...), custom_call_target="tpu_custom_call" | custom-call | flops 1000 | bytes 1000 | tf_op jit(solution)/shard_map/pallas_call | solution.py:40
  63.1 3.0 %shard_map.85 = (f32[16,128,128]{2,1,0:T(8,128)S(1)}, f32[18,128,128]{2,1,0:T(8,128)S(1)}) custom-call(s32[3]{0:T(128)S(1)} %pad_add_fusion.place, f32[8,128,128]{2,1,0:T(8,128)S(1)} %get-tuple-element.101.refs_0_, f32[8,128,128]{2,1,0:T(8,128)S(1)} %get-tuple-element.102.refs_1_, f32[256,128]{1,0:T(8,128)S(1)} %get-tuple-element.103.refs_2_, ...), custom_call_target="tpu_custom_call" | custom-call | flops 1000 | bytes 1000 | tf_op jit(solution)/shard_map/pallas_call | solution.py:40
  66.1 0.0 collective-permute-done.11
  66.1 0.1 add.12
  66.2 0.0 collective-permute-done.12
  66.2 0.1 add.13
  66.3 0.0 collective-permute-done.13.refs_5_
  66.3 0.1 collective-permute-start.14
  66.4 4.5 %collective-permute-start.17 = (f32[8,128,128]{2,1,0:T(8,128)S(1)}, f32[8,128,128]{2,1,0:T(8,128)S(1)}, u32[]{:S(2)}, u32[]{:S(2)}) collective-permute-start(f32[8,128,128]{2,1,0:T(8,128)S(1)} %get-tuple-element.100), channel_id=1, source_target_pairs={{0,12},{2,14},{12,0},{14,2},{1,13},{3,15},{13,1},{15,3},{16,28},{1... | collective-permute-start | bytes 1572872 | tf_op jit(solution)/shard_map/ppermute | solution.py:348
  70.9 0.1 collective-permute-start.19
  71.0 0.9 collective-permute-start.20
  71.9 0.0 collective-permute-done.14.refs_0_.refs_6_
  71.9 0.7 shard_map.86
  72.6 0.6 collective-permute-start.15
  73.2 1.5 %collective-permute-start.16 = (f32[5,128,128]{2,1,0:T(8,128)S(1)}, f32[5,128,128]{2,1,0:T(8,128)S(1)}, u32[]{:S(2)}, u32[]{:S(2)}) collective-permute-start(f32[5,128,128]{2,1,0:T(8,128)S(1)} %get-tuple-element.114), channel_id=1, source_target_pairs={{0,1},{1,0},{2,3},{3,2},{4,5},{5,4},{6,7},{7,6},{8,9},{9,8},{10,11... | collective-permute-start | bytes 983048 | tf_op jit(solution)/shard_map/ppermute | solution.py:356
  74.7 10.2 %collective-permute-done.17.d_right_far = f32[8,128,128]{2,1,0:T(8,128)S(1)} collective-permute-done((f32[8,128,128]{2,1,0:T(8,128)S(1)}, f32[8,128,128]{2,1,0:T(8,128)S(1)}, u32[]{:S(2)}, u32[]{:S(2)}) %collective-permute-start.17) | collective-permute-done | bytes 524320 | tf_op jit(solution)/shard_map/ppermute | solution.py:348
  84.9 4.6 %collective-permute-done.16.refs_8_ = f32[5,128,128]{2,1,0:T(8,128)S(1)} collective-permute-done((f32[5,128,128]{2,1,0:T(8,128)S(1)}, f32[5,128,128]{2,1,0:T(8,128)S(1)}, u32[]{:S(2)}, u32[]{:S(2)}) %collective-permute-start.16) | collective-permute-done | bytes 327712 | tf_op jit(solution)/shard_map/ppermute | solution.py:356
  89.5 0.5 collective-permute-start.18
  90.0 2.2 %shard_map.87.base = f32[8,128,128]{2,1,0:T(8,128)S(1)} custom-call(s32[3]{0:T(128)S(1)} %pad_add_fusion.place, f32[16,8,128]{2,1,0:T(8,128)S(1)} %get-tuple-element.83.refs_0_, f32[16,8,128]{2,1,0:T(8,128)S(1)} %get-tuple-element.85.refs_1_, f32[16,8,128]{2,1,0:T(8,128)S(1)} %get-tuple-element.93.refs_1_.refs_2_, ...), custom_call_target="tpu_custom_call" | custom-call | flops 1000 | bytes 1000 | tf_op jit(solution)/shard_map/pallas_call | solution.py:40
  92.2 2.3 %collective-permute-done.18.refs_9_ = f32[2,128,128]{2,1,0:T(8,128)S(1)} collective-permute-done((f32[2,128,128]{2,1,0:T(8,128)S(1)}, f32[2,128,128]{2,1,0:T(8,128)S(1)}, u32[]{:S(2)}, u32[]{:S(2)}) %collective-permute-start.18) | collective-permute-done | bytes 131104 | tf_op jit(solution)/shard_map/ppermute | solution.py:356
  94.4 1.2 %collective-permute-done.19.d_right_near = f32[8,128,128]{2,1,0:T(8,128)S(1)} collective-permute-done((f32[8,128,128]{2,1,0:T(8,128)S(1)}, f32[8,128,128]{2,1,0:T(8,128)S(1)}, u32[]{:S(2)}, u32[]{:S(2)}) %collective-permute-start.19) | collective-permute-done | bytes 524320 | tf_op jit(solution)/shard_map/ppermute | solution.py:348
  95.6 0.0 collective-permute-done.20.d_right_middle
  95.6 2.7 %shard_map.88 = (f32[8,128,128]{2,1,0:T(8,128)S(1)}, f32[16,128,128]{2,1,0:T(8,128)}) custom-call(s32[3]{0:T(128)S(1)} %pad_add_fusion.place, f32[8,128,128]{2,1,0:T(8,128)S(1)} %get-tuple-element.69.normed, f32[8,128,128]{2,1,0:T(8,128)S(1)} %get-tuple-element.70.scale, f32[8,128,128]{2,1,0:T(8,128)S(1)} %shard_map.87.base, ...), custom_call_target="tpu_custom_call" | custom-call | flops 1000 | bytes 1000 | tf_op jit(solution)/shard_map/pallas_call | solution.py:40
  98.4 0.5 collective-permute-start.21
  98.9 1.8 %shard_map.89 = f32[16,128,128]{2,1,0:T(8,128)} custom-call(s32[3]{0:T(128)S(1)} %pad_add_fusion.place, f32[16,8,128]{2,1,0:T(8,128)S(1)} %get-tuple-element.83.refs_0_, f32[16,8,128]{2,1,0:T(8,128)S(1)} %get-tuple-element.85.refs_1_, f32[16,8,128]{2,1,0:T(8,128)S(1)} %get-tuple-element.93.refs_1_.refs_2_, ...), custom_call_target="tpu_custom_call" | custom-call | flops 1000 | bytes 1000 | tf_op jit(solution)/shard_map/pallas_call | solution.py:40
  100.7 11.6 %collective-permute-done.21.other = f32[8,128,128]{2,1,0:T(8,128)S(1)} collective-permute-done((f32[8,128,128]{2,1,0:T(8,128)S(1)}, f32[8,128,128]{2,1,0:T(8,128)S(1)}, u32[]{:S(2)}, u32[]{:S(2)}) %collective-permute-start.21) | collective-permute-done | bytes 524320 | tf_op jit(solution)/shard_map/ppermute | solution.py:356
  112.2 1.3 %shard_map.90 = f32[16,128,128]{2,1,0:T(8,128)} custom-call(s32[3]{0:T(128)S(1)} %pad_add_fusion.place, f32[8,128,128]{2,1,0:T(8,128)S(1)} %collective-permute-done.21.other, f32[16,128,128]{2,1,0:T(8,128)} %get-tuple-element.135.whole), custom_call_target="tpu_custom_call", output_to_operand_aliasing={{}: (2, {})} | custom-call | tf_op jit(solution)/shard_map/pallas_call | solution.py:336
  (16 shorter events, 0.1 us)
Async XLA Ops:
  0.6 8.7 %collective-permute-start = (f32[256,128]{1,0:T(8,128)}, f32[256,128]{1,0:T(8,128)S(1)}, u32[]{:S(2)}, u32[]{:S(2)}) collective-permute-start(f32[256,128]{1,0:T(8,128)} %bitcast.21), channel_id=1, source_target_pairs={{0,1},{1,0},{2,3},{3,2},{4,5},{5,4},{6,7},{7,6},{8,9},{9,8},{10,11... | collective-permute-start | bytes 393224 | tf_op jit(solution)/shard_map/ppermute | solution.py:356
  3.7 1.2 %copy-start = (f32[16,128,128]{2,1,0:T(8,128)S(1)}, f32[16,128,128]{2,1,0:T(8,128)}, u32[]{:S(2)}) copy-start(f32[16,128,128]{2,1,0:T(8,128)} %refs_10_.1) | copy-start | bytes 3145732
  4.9 1.2 %copy-start.2 = (f32[16,128,128]{2,1,0:T(8,128)S(1)}, f32[16,128,128]{2,1,0:T(8,128)}, u32[]{:S(2)}) copy-start(f32[16,128,128]{2,1,0:T(8,128)} %pair.3) | copy-start | bytes 3145732
  6.2 0.9 copy-start.5
  7.1 0.7 copy-start.7
  7.8 5.5 %copy-start.6 = (f32[64,128]{1,0:T(8,128)S(1)}, f32[64,128]{1,0:T(8,128)}, u32[]{:S(2)}) copy-start(f32[64,128]{1,0:T(8,128)} %mine_out.1) | copy-start | bytes 98308
  7.8 11.2 %copy-start.1 = (f32[16,128,128]{2,1,0:T(8,128)S(1)}, f32[16,128,128]{2,1,0:T(8,128)}, u32[]{:S(2)}) copy-start(f32[16,128,128]{2,1,0:T(8,128)} %refs_10_.1) | copy-start | bytes 3145732
  7.8 11.2 %copy-start.3 = (f32[16,128,128]{2,1,0:T(8,128)S(1)}, f32[16,128,128]{2,1,0:T(8,128)}, u32[]{:S(2)}) copy-start(f32[16,128,128]{2,1,0:T(8,128)} %pair.3) | copy-start | bytes 3145732
  7.8 11.2 %copy-start.4 = (f32[128,128]{1,0:T(8,128)S(1)}, f32[128,128]{1,0:T(8,128)}, u32[]{:S(2)}) copy-start(f32[128,128]{1,0:T(8,128)} %refs_11_.1) | copy-start | bytes 196612
  8.8 10.1 %collective-permute-start.1 = (f32[8,128,128]{2,1,0:T(8,128)S(1)}, f32[8,128,128]{2,1,0:T(8,128)S(1)}, u32[]{:S(2)}, u32[]{:S(2)}) collective-permute-start(f32[8,128,128]{2,1,0:T(8,128)S(1)} %get-tuple-element.74), channel_id=1, source_target_pairs={{0,2},{2,0},{4,6},{6,4},{8,10},{10,8},{12,14},{14,12},{1,3},{3,1},... | collective-permute-start | bytes 1572872 | tf_op jit(solution)/shard_map/ppermute | solution.py:352
  8.8 10.1 %collective-permute-start.2 = (f32[8,128,128]{2,1,0:T(8,128)S(1)}, f32[8,128,128]{2,1,0:T(8,128)S(1)}, u32[]{:S(2)}, u32[]{:S(2)}) collective-permute-start(f32[8,128,128]{2,1,0:T(8,128)S(1)} %get-tuple-element.75), channel_id=1, source_target_pairs={{0,2},{2,0},{4,6},{6,4},{8,10},{10,8},{12,14},{14,12},{1,3},{3,1},... | collective-permute-start | bytes 1572872 | tf_op jit(solution)/shard_map/ppermute | solution.py:352
  11.0 14.0 %collective-permute-start.5 = (f32[8,128,128]{2,1,0:T(8,128)S(1)}, f32[8,128,128]{2,1,0:T(8,128)S(1)}, u32[]{:S(2)}, u32[]{:S(2)}) collective-permute-start(f32[8,128,128]{2,1,0:T(8,128)S(1)} %get-tuple-element.73.refs_0_), channel_id=1, source_target_pairs={{0,4},{2,6},{4,0},{6,2},{8,12},{10,14},{12,8},{14,10},{1,5},{3,7},... | collective-permute-start | bytes 1572872 | tf_op jit(solution)/shard_map/ppermute | solution.py:348
  12.6 12.3 %collective-permute-start.6 = (f32[8,128,128]{2,1,0:T(8,128)S(1)}, f32[8,128,128]{2,1,0:T(8,128)S(1)}, u32[]{:S(2)}, u32[]{:S(2)}) collective-permute-start(f32[8,128,128]{2,1,0:T(8,128)S(1)} %get-tuple-element.73.refs_0_), channel_id=1, source_target_pairs={{4,8},{6,10},{8,4},{10,6},{5,9},{7,11},{9,5},{11,7},{20,24},{22,26... | collective-permute-start | bytes 1572872 | tf_op jit(solution)/shard_map/ppermute | solution.py:348
  13.3 4.0 %collective-permute-start.4 = (f32[64,128]{1,0:T(8,128)S(1)}, f32[64,128]{1,0:T(8,128)S(1)}, u32[]{:S(2)}, u32[]{:S(2)}) collective-permute-start(f32[64,128]{1,0:T(8,128)S(1)} %copy-done.6), channel_id=1, source_target_pairs={{0,1},{1,0},{2,3},{3,2},{4,5},{5,4},{6,7},{7,6},{8,9},{9,8},{10,11... | collective-permute-start | bytes 98312 | tf_op jit(solution)/shard_map/ppermute | solution.py:356
  17.3 1.6 %collective-permute-start.3 = (f32[5,128,128]{2,1,0:T(8,128)S(1)}, f32[5,128,128]{2,1,0:T(8,128)S(1)}, u32[]{:S(2)}, u32[]{:S(2)}) collective-permute-start(f32[5,128,128]{2,1,0:T(8,128)S(1)} %get-tuple-element.76), channel_id=1, source_target_pairs={{0,2},{2,0},{4,6},{6,4},{8,10},{10,8},{12,14},{14,12},{1,3},{3,1},... | collective-permute-start | bytes 983048 | tf_op jit(solution)/shard_map/ppermute | solution.py:352
  24.9 12.8 %collective-permute-start.7 = (f32[8,128,128]{2,1,0:T(8,128)S(1)}, f32[8,128,128]{2,1,0:T(8,128)S(1)}, u32[]{:S(2)}, u32[]{:S(2)}) collective-permute-start(f32[8,128,128]{2,1,0:T(8,128)S(1)} %collective-permute-done.5.refs_0_.refs_1_), channel_id=1, source_target_pairs={{4,8},{6,10},{8,4},{10,6},{5,9},{7,11},{9,5},{11,7},{20,24},{22,26... | collective-permute-start | bytes 1572872 | tf_op jit(solution)/shard_map/ppermute | solution.py:348
  25.6 19.5 %collective-permute-start.9 = (f32[8,128,128]{2,1,0:T(8,128)S(1)}, f32[8,128,128]{2,1,0:T(8,128)S(1)}, u32[]{:S(2)}, u32[]{:S(2)}) collective-permute-start(f32[8,128,128]{2,1,0:T(8,128)S(1)} %collective-permute-done.6.refs_0_), channel_id=1, source_target_pairs={{4,0},{6,2},{8,12},{10,14},{5,1},{7,3},{9,13},{11,15},{20,16},{22,... | collective-permute-start | bytes 1572872 | tf_op jit(solution)/shard_map/ppermute | solution.py:348
  34.7 3.0 %collective-permute-start.8 = (f32[2,16,8,128]{3,2,1,0:T(8,128)S(1)}, f32[2,16,8,128]{3,2,1,0:T(8,128)S(1)}, u32[]{:S(2)}, u32[]{:S(2)}) collective-permute-start(f32[2,16,8,128]{3,2,1,0:T(8,128)S(1)} %pad_maximum_fusion.1), channel_id=1, source_target_pairs={{0,2},{2,0},{4,6},{6,4},{8,10},{10,8},{12,14},{14,12},{1,3},{3,1},... | collective-permute-start | bytes 393224 | tf_op jit(solution)/shard_map/ppermute | solution.py:352
  37.7 21.4 %collective-permute-start.10 = (f32[8,128,128]{2,1,0:T(8,128)S(1)}, f32[8,128,128]{2,1,0:T(8,128)S(1)}, u32[]{:S(2)}, u32[]{:S(2)}) collective-permute-start(f32[8,128,128]{2,1,0:T(8,128)S(1)} %collective-permute-done.7.refs_0_), channel_id=1, source_target_pairs={{4,0},{6,2},{8,12},{10,14},{5,1},{7,3},{9,13},{11,15},{20,16},{22,... | collective-permute-start | bytes 1572872 | tf_op jit(solution)/shard_map/ppermute | solution.py:348
  49.1 17.0 %collective-permute-start.11 = (f32[8,128,128]{2,1,0:T(8,128)S(1)}, f32[8,128,128]{2,1,0:T(8,128)S(1)}, u32[]{:S(2)}, u32[]{:S(2)}) collective-permute-start(f32[8,128,128]{2,1,0:T(8,128)S(1)} %get-tuple-element.99), channel_id=1, source_target_pairs={{4,8},{6,10},{8,4},{10,6},{5,9},{7,11},{9,5},{11,7},{20,24},{22,26... | collective-permute-start | bytes 1572872 | tf_op jit(solution)/shard_map/ppermute | solution.py:348
  49.8 16.4 %collective-permute-start.12 = (f32[8,128,128]{2,1,0:T(8,128)S(1)}, f32[8,128,128]{2,1,0:T(8,128)S(1)}, u32[]{:S(2)}, u32[]{:S(2)}) collective-permute-start(f32[8,128,128]{2,1,0:T(8,128)S(1)} %get-tuple-element.99), channel_id=1, source_target_pairs={{0,4},{2,6},{12,8},{14,10},{1,5},{3,7},{13,9},{15,11},{16,20},{18,... | collective-permute-start | bytes 1572872 | tf_op jit(solution)/shard_map/ppermute | solution.py:348
  55.1 11.2 %collective-permute-start.13 = (f32[2,2,16,8,128]{4,3,2,1,0:T(8,128)S(1)}, f32[2,2,16,8,128]{4,3,2,1,0:T(8,128)S(1)}, u32[]{:S(2)}, u32[]{:S(2)}) collective-permute-start(f32[2,2,16,8,128]{4,3,2,1,0:T(8,128)S(1)} %pad_maximum_fusion), channel_id=1, source_target_pairs={{0,1},{1,0},{2,3},{3,2},{4,5},{5,4},{6,7},{7,6},{8,9},{9,8},{10,11... | collective-permute-start | bytes 786440 | tf_op jit(solution)/shard_map/ppermute | solution.py:356
  66.3 5.6 %collective-permute-start.14 = (f32[18,128,128]{2,1,0:T(8,128)S(1)}, f32[18,128,128]{2,1,0:T(8,128)S(1)}, u32[]{:S(2)}, u32[]{:S(2)}) collective-permute-start(f32[18,128,128]{2,1,0:T(8,128)S(1)} %get-tuple-element.111), channel_id=1, source_target_pairs={{0,2},{2,0},{4,6},{6,4},{8,10},{10,8},{12,14},{14,12},{1,3},{3,1},... | collective-permute-start | bytes 3538952 | tf_op jit(solution)/shard_map/ppermute | solution.py:352
  66.4 18.5 %collective-permute-start.17 = (f32[8,128,128]{2,1,0:T(8,128)S(1)}, f32[8,128,128]{2,1,0:T(8,128)S(1)}, u32[]{:S(2)}, u32[]{:S(2)}) collective-permute-start(f32[8,128,128]{2,1,0:T(8,128)S(1)} %get-tuple-element.100), channel_id=1, source_target_pairs={{0,12},{2,14},{12,0},{14,2},{1,13},{3,15},{13,1},{15,3},{16,28},{1... | collective-permute-start | bytes 1572872 | tf_op jit(solution)/shard_map/ppermute | solution.py:348
  70.9 24.7 %collective-permute-start.19 = (f32[8,128,128]{2,1,0:T(8,128)S(1)}, f32[8,128,128]{2,1,0:T(8,128)S(1)}, u32[]{:S(2)}, u32[]{:S(2)}) collective-permute-start(f32[8,128,128]{2,1,0:T(8,128)S(1)} %add.12), channel_id=1, source_target_pairs={{0,4},{2,6},{4,0},{6,2},{8,12},{10,14},{12,8},{14,10},{1,5},{3,7},... | collective-permute-start | bytes 1572872 | tf_op jit(solution)/shard_map/ppermute | solution.py:348
  71.0 24.6 %collective-permute-start.20 = (f32[8,128,128]{2,1,0:T(8,128)S(1)}, f32[8,128,128]{2,1,0:T(8,128)S(1)}, u32[]{:S(2)}, u32[]{:S(2)}) collective-permute-start(f32[8,128,128]{2,1,0:T(8,128)S(1)} %add.13), channel_id=1, source_target_pairs={{4,8},{6,10},{8,4},{10,6},{5,9},{7,11},{9,5},{11,7},{20,24},{22,26... | collective-permute-start | bytes 1572872 | tf_op jit(solution)/shard_map/ppermute | solution.py:348
  72.6 12.3 %collective-permute-start.15 = (f32[5,128,128]{2,1,0:T(8,128)S(1)}, f32[5,128,128]{2,1,0:T(8,128)S(1)}, u32[]{:S(2)}, u32[]{:S(2)}) collective-permute-start(f32[5,128,128]{2,1,0:T(8,128)S(1)} %get-tuple-element.113), channel_id=1, source_target_pairs={{0,1},{1,0},{2,3},{3,2},{4,5},{5,4},{6,7},{7,6},{8,9},{9,8},{10,11... | collective-permute-start | bytes 983048 | tf_op jit(solution)/shard_map/ppermute | solution.py:356
  73.2 16.3 %collective-permute-start.16 = (f32[5,128,128]{2,1,0:T(8,128)S(1)}, f32[5,128,128]{2,1,0:T(8,128)S(1)}, u32[]{:S(2)}, u32[]{:S(2)}) collective-permute-start(f32[5,128,128]{2,1,0:T(8,128)S(1)} %get-tuple-element.114), channel_id=1, source_target_pairs={{0,1},{1,0},{2,3},{3,2},{4,5},{5,4},{6,7},{7,6},{8,9},{9,8},{10,11... | collective-permute-start | bytes 983048 | tf_op jit(solution)/shard_map/ppermute | solution.py:356
  89.5 5.0 %collective-permute-start.18 = (f32[2,128,128]{2,1,0:T(8,128)S(1)}, f32[2,128,128]{2,1,0:T(8,128)S(1)}, u32[]{:S(2)}, u32[]{:S(2)}) collective-permute-start(f32[2,128,128]{2,1,0:T(8,128)S(1)} %get-tuple-element.122), channel_id=1, source_target_pairs={{0,1},{1,0},{2,3},{3,2},{4,5},{5,4},{6,7},{7,6},{8,9},{9,8},{10,11... | collective-permute-start | bytes 393224 | tf_op jit(solution)/shard_map/ppermute | solution.py:356
  98.4 13.9 %collective-permute-start.21 = (f32[8,128,128]{2,1,0:T(8,128)S(1)}, f32[8,128,128]{2,1,0:T(8,128)S(1)}, u32[]{:S(2)}, u32[]{:S(2)}) collective-permute-start(f32[8,128,128]{2,1,0:T(8,128)S(1)} %get-tuple-element.130), channel_id=1, source_target_pairs={{0,1},{1,0},{2,3},{3,2},{4,5},{5,4},{6,7},{7,6},{8,9},{9,8},{10,11... | collective-permute-start | bytes 1572872 | tf_op jit(solution)/shard_map/ppermute | solution.py:356

commit v4 on v3

--- a/solution.py
+++ b/solution.py
@@ -14,12 +14,23 @@
 GROUP = 8
 
 
+def halves(values):
+    high = values.astype(jnp.bfloat16)
+    return high, (values - high.astype(F32)).astype(jnp.bfloat16)
+
+
+def contract(a, b, dims):
+    (a_high, a_low), (b_high, b_low) = halves(a), halves(b)
+    one = lambda x, y: lax.dot_general(x, y, (dims, ((), ())), preferred_element_type=F32)
+    return one(a_high, b_high) + (one(a_high, b_low) + one(a_low, b_high))
+
+
 def dot(a, b):
-    return lax.dot_general(a, b, (((1,), (0,)), ((), ())), precision=HIGHEST, preferred_element_type=F32)
+    return contract(a, b, ((1,), (0,)))
 
 
 def dot_t(a, b):
-    return lax.dot_general(a, b, (((1,), (1,)), ((), ())), precision=HIGHEST, preferred_element_type=F32)
+    return contract(a, b, ((1,), (1,)))
 
 
 def norm(values):
@@ -34,17 +45,20 @@
     return values.reshape(-1, values.shape[-1])
 
 
-def call(kernel, outs, args, scratch=(), flops=1000):
-    smem = pl.BlockSpec(memory_space=pltpu.SMEM)
+def call(kernel, outs, args, scratch=(), distant=0, sems=0):
     vmem = pl.BlockSpec(memory_space=pltpu.VMEM)
+    spaces = [pl.BlockSpec(memory_space=pltpu.SMEM)] + [pl.BlockSpec(memory_space=pltpu.HBM)] * distant
+    args = list(args)
+    args[1 : 1 + distant] = [pltpu.with_memory_space_constraint(a, pltpu.HBM) for a in args[1 : 1 + distant]]
     return pl.pallas_call(
         kernel,
         out_shape=[jax.ShapeDtypeStruct(shape, F32) for shape in outs],
-        in_specs=[smem] + [vmem] * (len(args) - 1),
+        in_specs=spaces + [vmem] * (len(args) - len(spaces)),
         out_specs=[vmem] * len(outs),
-        scratch_shapes=[pltpu.VMEM(shape, F32) for shape in scratch],
+        scratch_shapes=[pltpu.VMEM(*shape) if isinstance(shape[0], tuple) else pltpu.VMEM(shape, F32) for shape in scratch]
+        + ([pltpu.SemaphoreType.DMA((sems,))] if sems else []),
         compiler_params=pltpu.CompilerParams(vmem_limit_bytes=24 * 1024 * 1024),
-        cost_estimate=pl.CostEstimate(flops=flops, bytes_accessed=flops, transcendentals=0),
+        cost_estimate=pl.CostEstimate(flops=1000, bytes_accessed=1000, transcendentals=0),
     )(*args)
 
 
@@ -80,22 +94,34 @@
     return sig * proj[:, :chans], sig
 
 
-def first_kernel(place, pair, mask, cotangent, w_proj, normed, scale, keep, mine, first, second, third):
-    rows, cols, width = pair.shape
-    half = rows // 2
-    chips = cols // (2 * rows)
-    mine[...] = w_proj[...]
-    keep[...] = mask[...].astype(F32)
+def first_kernel(place, pair, mask, w_proj, normed, scale, keep, mine, first, second, flags, sems):
+    half = first.shape[0]
+    moves = ((pair.at[:half], first), (pair.at[half:], second), (mask, flags), (w_proj, mine))
+    copies = [pltpu.make_async_copy(source, target, sems.at[at]) for at, (source, target) in enumerate(moves)]
+    for copy in copies:
+        copy.start()
+    for copy in copies:
+        copy.wait()
+    keep[...] = flags[...].astype(F32)
     for t in range(0, half, CHUNK):
         at = slice(t, t + CHUNK)
-        value, factor = norm(pair[pl.ds(source_row(place, t, rows), CHUNK)])
+        value, factor = norm(jnp.where(place[2] == 0, first[at], second[at]))
         normed[at] = value
         scale[at] = jnp.broadcast_to(factor, value.shape)
-    first[...] = pair[:half]
-    second[...] = pair[half:]
+
+
+def third_kernel(place, cotangent, keep, packed, sems):
+    rows = cotangent.shape[0]
+    half, chips = rows // 2, packed.shape[0] - 1
+    copies = []
     for chip in range(chips):
-        third[chip] = flat(cotangent[:, pl.ds(first_col(place, chip, 1 - place[1], rows), half), :])
-    third[chips, :rows] = keep[...]
+        source = cotangent.at[:, pl.ds(first_col(place, chip, 1 - place[1], rows), half), :]
+        copies.append(pltpu.make_async_copy(source, packed.at[chip], sems.at[chip]))
+    for copy in copies:
+        copy.start()
+    packed[chips, :, 0, :] = keep[...]
+    for copy in copies:
+        copy.wait()
 
 
 def right_kernel(rows, place, normed, keep, mine, other, right, open_part, slope):
@@ -132,7 +158,7 @@
             d_here[chip, at] = gate[at, near, :] * cotangent[pl.ds(row, CHUNK), near, :]
         their_row = row % half
         normed, _ = norm(flat(jnp.where(row < half, first[pl.ds(their_row, CHUNK)], second[pl.ds(their_row, CHUNK)])))
-        value, _ = gated(normed, third[chips, pl.ds(row, CHUNK), :], w)
+        value, _ = gated(normed, third[chips, pl.ds(row, CHUNK), 0, :], w)
         left_there[at] = value.reshape(shape)
         normed_rows[...] = normed.reshape(CHUNK, cols, -1)
         picked = [
@@ -140,8 +166,7 @@
         ]
         opened = jax.nn.sigmoid(dot(flat(jnp.stack(picked)), w_gate[...])).reshape(chips, CHUNK, half, -1)
         for chip in range(chips):
-            d_out = third[chip, pl.ds(row * half, CHUNK * half), :].reshape(CHUNK, half, -1)
-            d_there[chip, at] = opened[chip] * d_out
+            d_there[chip, at] = opened[chip] * third[chip, pl.ds(row, CHUNK)]
 
 
 def tile_body(step, place, right, left_here, left_there, d_here, d_there, w_out, out_here, out_there, d_x, d_right, partial, x):
@@ -209,50 +234,53 @@
         tile_body(step, place, rights[0], *rest)
 
 
-def left_kernel(tiles, bases, place, *refs):
-    rights, d_xs = refs[:tiles], refs[tiles : 2 * tiles]
-    base = refs[2 * tiles : 2 * tiles + bases]
-    outs = refs[2 * tiles + bases :]
-    half, cols, chans = rights[0].shape
-    rows = outs[0].shape[0]
-    for which, out in enumerate(outs):
-
-        def body(pair_at, _):
-            i = pair_at * 2
-            if bases:
-                totals = [base[which][i], base[which][i + 1]]
-            else:
-                totals = [jnp.zeros((cols, chans), F32)] * 2
-            for right, d_x in zip(rights, d_xs):
-                for j in range(half):
-                    value = right[j]
-                    for u in range(2):
-                        at = (which * rows + i + u) * half + j
-                        totals[u] = totals[u] + value * d_x[pl.ds(at, 1), :]
-            out[i] = totals[0]
-            out[i + 1] = totals[1]
-            return 0
-
-        lax.fori_loop(0, rows // 2, body, 0)
-    for plane in range(2, bases):
-        outs[1][rows + plane - 2] = flat(base[plane][...])
-
-
-def share_kernel(place, kept, *refs):
-    received, outs, (d_left, *packed, rest) = refs[0], refs[1:3], refs[3:]
+def left_rows(tiles, base, out, first, count, start):
+    half, cols, chans = tiles[0][0].shape
+
+    def body(pair_at, _):
+        i = pair_at * 2
+        totals = [jnp.zeros((cols, chans), F32)] * 2 if base is None else [base[start + i], base[start + i + 1]]
+        for right, d_x in tiles:
+            for j in range(half):
+                value = right[j]
+                for u in range(2):
+                    totals[u] = totals[u] + value * d_x[pl.ds((first + i + u) * half + j, 1), :]
+        out[start + i] = totals[0]
+        out[start + i + 1] = totals[1]
+        return 0
+
+    lax.fori_loop(0, count // 2, body, 0)
+
+
+def left_kernel(tiles, based, place, *refs):
+    pairs = tuple(zip(refs[:tiles], refs[tiles : 2 * tiles]))
+    bases = refs[2 * tiles : 2 * tiles + 2] if based else (None, None)
+    rows = refs[-1].shape[0]
+    for which, out in enumerate(refs[-2:]):
+        left_rows(pairs, bases[which], out, which * rows, rows, 0)
+
+
+def last_left_kernel(place, right, d_x, here, there, out_next, out_last, kept, sent):
+    tiles = ((right, d_x),)
+    rows = here.shape[0]
+    left_rows(tiles, here, kept, 0, rows, 0)
+    left_rows(tiles, there, sent, rows, rows, 0)
+    sent[rows] = flat(out_next[...])
+    sent[rows + 1] = flat(out_last[...])
+
+
+def share_kernel(place, kept, received, out_next, out_last, d_left, packed, rest):
     half = d_left.shape[0]
-    part = half // 2
     block = half * half
     d_left[...] = kept[:half] + received[:half]
-    for at in range(2):
-        here = slice(half + at * part, half + (at + 1) * part)
-        packed[at][:part] = kept[here] + received[here]
-    for step, out in enumerate(outs):
+    packed[...] = kept[half:] + received[half : 2 * half]
+    for step, out in enumerate((out_next, out_last)):
         at = slice(step * block, (step + 1) * block)
-        packed[0][part, at] = flat(out[half:])
-        packed[1][part, at] = received[2 * half + step, block:]
-        rest[0, at] = flat(out[:half])
-        rest[1, at] = received[2 * half + step, :block]
+        plane = 2 * half + step
+        rest[0, at] = flat(out[half:])
+        rest[1, at] = received[plane, block:]
+        rest[2, at] = flat(out[:half])
+        rest[3, at] = received[plane, :block]
 
 
 def gather_out(place, rows, t, out, here, early_other, early_far, received, far):
@@ -284,27 +312,25 @@
 
 
 def update_kernel(rows, place, *refs):
-    here, early_other, early_far, received, far, far_next, rest, gate, update, out = refs[:4], *refs[4:]
+    here, early_other, early_far, received, rest, gate, update, out = refs[:4], *refs[4:]
     half = rows // 2
-    part = half // 2
-    gather_out(place, rows, 0, out, here, early_other, early_far, received, ((far, part), (far_next, part)))
-    gather_out(place, rows, half, out, here, early_other, early_far, received, ((rest, 0), (rest, 1)))
+    gather_out(place, rows, 0, out, here, early_other, early_far, received, ((rest, 0), (rest, 1)))
+    gather_out(place, rows, half, out, here, early_other, early_far, received, ((rest, 2), (rest, 3)))
     for t in range(0, rows, CHUNK):
         update[pl.ds(source_row(place, t, rows), CHUNK)] = gate[t : t + CHUNK] * out[t : t + CHUNK]
 
 
 def base_kernel(rows, place, *refs):
-    here, early_other, early_far, received, far, far_next = refs[:4], *refs[4:9]
-    gate, cotangent, w_gate, d_left, open_part, slope, mine, other, base, out = refs[9:]
+    here, early_other, early_far, received, rest = refs[:4], *refs[4:8]
+    gate, cotangent, w_gate, d_left, far, open_part, slope, mine, other, base, out = refs[8:]
     half, cols, chans = base.shape
-    part = half // 2
-    gather_out(place, rows, 0, out, here, early_other, early_far, received, ((far, part), (far_next, part)))
+    gather_out(place, rows, 0, out, here, early_other, early_far, received, ((rest, 0), (rest, 1)))
     w = gated_weights(place, mine, other, 0)
     for t in range(0, half, CHUNK):
         at = slice(t, t + CHUNK)
         opened = gate[at]
         d_gate = cotangent[pl.ds(source_row(place, t, rows), CHUNK)] * (opened * out[at]) * (1.0 - opened)
-        grad = flat(d_left[at] + (far, far_next)[t // part][t % part : t % part + CHUNK])
+        grad = flat(d_left[at] + far[at])
         both = jnp.concatenate([grad * flat(open_part[at]), grad * flat(slope[at])], axis=1)
         base[at] = (dot_t(flat(d_gate), w_gate[...]) + dot(both, w)).reshape(CHUNK, cols, -1)
 
@@ -374,18 +400,27 @@
     w_mine = jnp.swapaxes(w_proj, 1, 2)
     other = other_half(flat(w_mine)).reshape(w_mine.shape)
     kept = (half, cols, chans)
+    other_out = other_half(w_out)
     normed, scale, keep, mine, *sent = call(
         first_kernel,
-        [(half, cols, width)] * 2 + [(rows, cols), w_mine.shape] + [(half, cols, width)] * 2 + [(chips + 1, cols, width)],
-        (place, pair, pair_mask, cotangent, w_mine),
+        [(half, cols, width)] * 2 + [(rows, cols), w_mine.shape] + [(half, cols, width)] * 2,
+        (place, pair, pair_mask, w_mine),
+        scratch=[((rows, cols), jnp.int32)],
+        distant=3,
+        sems=4,
     )
     theirs = [other_core(block) for block in sent]
-    other_out = other_half(w_out)
+    other, other_out = lax.optimization_barrier((other, other_out))
     right, open_right, slope_right = call(
         functools.partial(right_kernel, rows), [kept] * 3, (place, normed, keep, mine, other)
     )
     near = along(right, NEXT)
     middle = along(right, MIDDLE)
+    _, cotangent_late = lax.optimization_barrier((right, cotangent))
+    (third,) = call(
+        third_kernel, [(chips + 1, rows, half, width)], (place, cotangent_late, keep), distant=1, sems=chips
+    )
+    theirs.append(other_core(third))
     quarter = (chips, rows, half, width)
     tile_outs = [(rows, half, width)] * 2 + [(2 * rows * half, chans), kept]
     tile_scratch = [(4, half * GROUP, chans), (2 * rows * half, chans)]
@@ -408,14 +443,14 @@
         out_here[step], out_there[step], d_x[step], d_right[step] = got[:4]
         rights[step] = got[4] if len(blocks) == 2 else blocks[0]
 
-    near, middle, d_here = lax.optimization_barrier((near, middle, d_here))
+    near, d_here = lax.optimization_barrier((near, d_here))
     cross = along(near, MIDDLE)
     outer = along(middle, OUTWARD)
     tile(0, right)
     tile(1, near)
     early_other = other_core(jnp.stack(out_there[:2]))
     d_left_here, d_left_there = call(
-        functools.partial(left_kernel, 2, 0),
+        functools.partial(left_kernel, 2, False),
         [(rows, cols, chans)] * 2,
         (place, *rights[:2], *d_x[:2]),
     )
@@ -425,37 +460,41 @@
     tile(2, cross, outer)
     inward = along(d_right[2], INWARD)
     swapped = along(d_right[2], MIDDLE)
-    far, d_x[2] = lax.optimization_barrier((far, d_x[2]))
+    d_left_here, d_left_there = call(
+        functools.partial(left_kernel, 1, True),
+        [(rows, cols, chans)] * 2,
+        (place, rights[2], d_x[2], d_left_here, d_left_there),
+    )
+    far, d_left_here = lax.optimization_barrier((far, d_left_here))
     tile(3, middle, far)
+    from_far = along(d_right[3], ENDS)
     d_left_kept, d_left_sent = call(
-        functools.partial(left_kernel, 2, 4),
+        last_left_kernel,
         [(rows, cols, chans), (rows + 2, cols, chans)],
-        (place, *rights[2:], *d_x[2:], d_left_here, d_left_there, out_there[2], out_there[3]),
-    )
-    to_near, to_middle, early_far, d_left_sent = lax.optimization_barrier(
-        (d_right[1] + swapped, d_right[3] + inward, early_far, d_left_sent)
+        (place, rights[3], d_x[3], d_left_here, d_left_there, out_there[2], out_there[3]),
+    )
+    to_middle, to_near, early_far, d_left_sent = lax.optimization_barrier(
+        (d_right[3] + inward, d_right[1] + swapped, early_far, d_left_sent)
     )
     received = other_core(d_left_sent)
+    d_left, packed, rest = call(
+        share_kernel,
+        [kept, kept, (4, cols, chans)],
+        (place, d_left_kept, received, out_here[2], out_here[3]),
+    )
+    d_left_other = other_half(packed)
+    to_near, to_middle, _ = lax.optimization_barrier((to_near, to_middle, packed))
     from_near = along(to_near, NEXT)
     from_middle = along(to_middle, MIDDLE)
-    from_far = along(d_right[3], ENDS)
-    packed_shape = (half // 2 + 1, cols, chans)
-    d_left, *shared, rest = call(
-        share_kernel,
-        [kept, packed_shape, packed_shape, (2, cols, chans)],
-        (place, d_left_kept, received, out_here[2], out_here[3]),
-    )
-    shared = [other_half(part) for part in shared]
-    *shared, rest, from_far = lax.optimization_barrier((*shared, rest, from_far))
+    rest, from_far = lax.optimization_barrier((rest, from_far))
     rest_other = other_half(rest)
-    outs = (*out_here, early_other, early_far, received, *shared)
+    outs = (*out_here, early_other, early_far, received, rest_other)
     (base,) = call(
         functools.partial(base_kernel, rows),
         [(half, cols, width)],
-        (place, *outs, gate, cotangent, w_gate, d_left, open_left, slope_left, mine, other),
+        (place, *outs, gate, cotangent, w_gate, d_left, d_left_other, open_left, slope_left, mine, other),
         scratch=[(half, cols, width)],
     )
-    base, rest_other = lax.optimization_barrier((base, rest_other))
     d_mine, d_pair = call(
         functools.partial(pair_kernel, rows),
         [(half, cols, width), (rows, cols, width)],
@@ -466,7 +505,7 @@
     (update,) = call(
         functools.partial(update_kernel, rows),
         [(rows, cols, width)],
-        (place, *outs, rest_other, gate_late),
+        (place, *outs, gate_late),
         scratch=[(rows, cols, width)],
     )
     d_other, update = lax.optimization_barrier((d_other, update))

time: 114 us -> 106 us (0.930)
  waiting for transfers between devices: 45 us -> 39.6 us
  local copies, waits for them, and re-layouts: 4.06 us -> 0.02 us
  starting transfers between devices: 25.1 us -> 26.9 us
    unnamed x16 -> x8, local copies, waits for them, and re-layouts: 4.06 us -> 0.02 us
    ppermute x7 -> x6, waiting for transfers between devices: 21.8 us -> 18 us  [other_half(): return lax.ppermute(block, 'ch', [(0, 1), (1, 0)])]
    ppermute x7 -> x6, starting transfers between devices: 7.36 us -> 9.27 us  [other_half(): return lax.ppermute(block, 'ch', [(0, 1), (1, 0)])]
    ppermute x10, waiting for transfers between devices: 21.5 us -> 20 us  [along(): lax.ppermute(block, 'row', [(2 * a + core, 2 * b + core) for a, b in pair...]
    pallas_call x13 -> x15, Pallas kernels: 36.9 us -> 36.9 us  [call(): pl.pallas_call(kernel, out_shape=[jax.ShapeDtypeStruct(shape, F32) for sh...]
  transfers between devices with their start and end apart: 22 -> 21, of which waited for: 10 -> 9; matrix products, arithmetic and copies ran while one was open for 0% -> 0% of each run, Pallas kernels for 30% -> 33%
where the time goes in v4:
time: 106 us
  waiting for transfers between devices  39.6 us (37%)
  Pallas kernels  38.2 us (36%)
  starting transfers between devices  26.9 us (25%)
    pallas_call x15, Pallas kernels, call(): pl.pallas_call(kernel, out_shape=[jax.ShapeDtypeStruct(shape, F32) for sh...  36.9 us
    ppermute x10, waiting for transfers between devices, along(): lax.ppermute(block, 'row', [(2 * a + core, 2 * b + core) for a, b in pair...  20 us
    ppermute x6, waiting for transfers between devices, other_half(): return lax.ppermute(block, 'ch', [(0, 1), (1, 0)])  18 us
    ppermute x10, starting transfers between devices, along(): lax.ppermute(block, 'row', [(2 * a + core, 2 * b + core) for a, b in pair...  16.8 us
    ppermute x6, starting transfers between devices, other_half(): return lax.ppermute(block, 'ch', [(0, 1), (1, 0)])  9.27 us
  transfers between devices with their start and end apart: 21, of which 9 were waited for; matrix products, arithmetic and copies ran while one was open for 0% of the time, Pallas kernels for 33%

profile of v4, /device:TPU:0, one launch (start us, length us, event | category | flops | bytes accessed | tf_op | source)
XLA Modules:
  0.0 105.9 jit_solution(4298113287374695025)
XLA Ops:
  0.6 3.0 %collective-permute-start = (f32[256,128]{1,0:T(8,128)}, f32[256,128]{1,0:T(8,128)S(1)}, u32[]{:S(2)}, u32[]{:S(2)}) collective-permute-start(f32[256,128]{1,0:T(8,128)} %bitcast.23), channel_id=1, source_target_pairs={{0,1},{1,0},{2,3},{3,2},{4,5},{5,4},{6,7},{7,6},{8,9},{9,8},{10,11... | collective-permute-start | bytes 393224 | tf_op jit(solution)/shard_map/ppermute | solution.py:382
  3.6 0.1 collective-permute-start.1
  3.7 0.1 pad_add_fusion.place
  3.8 2.2 %shard_map.77 = (f32[8,128,128]{2,1,0:T(8,128)S(1)}, f32[8,128,128]{2,1,0:T(8,128)S(1)}, f32[16,128]{1,0:T(8,128)S(1)}, f32[4,64,128]{2,1,0:T(8,128)S(1)}, f32[8...) custom-call(s32[3]{0:T(128)S(1)} %pad_add_fusion.place, f32[16,128,128]{2,1,0:T(8,128)} %pair.3, s32[16,128]{1,0:T(8,128)} %mask.1, ...), custom_call_target="tpu_custom_call" | custom-call | flops 1000 | bytes 1000 | tf_op jit(solution)/shard_map/pallas_call | solution.py:53
  6.0 0.0 copy-start
  6.0 0.0 copy-start.1
  6.0 0.0 copy-start.2
  6.0 0.1 collective-permute-start.2
  6.1 0.5 collective-permute-start.3
  6.6 1.4 %collective-permute-done.1.other_out = f32[64,128]{1,0:T(8,128)S(1)} collective-permute-done((f32[64,128]{1,0:T(8,128)}, f32[64,128]{1,0:T(8,128)S(1)}, u32[]{:S(2)}, u32[]{:S(2)}) %collective-permute-start.1) | collective-permute-done | bytes 32800 | tf_op jit(solution)/shard_map/ppermute | solution.py:382
  8.0 0.0 collective-permute-done
  8.0 1.2 %shard_map.78 = (f32[8,128,128]{2,1,0:T(8,128)S(1)}, f32[8,128,128]{2,1,0:T(8,128)S(1)}, f32[8,128,128]{2,1,0:T(8,128)S(1)}) custom-call(s32[3]{0:T(128)S(1)} %pad_add_fusion.place, f32[8,128,128]{2,1,0:T(8,128)S(1)} %get-tuple-element.69.normed, f32[16,128]{1,0:T(8,128)S(1)} %get-tuple-element.71.keep, f32[4,64,128]{2,1,0:T(8,128)S(1)} %get-tuple-element.72.mine.refs_15_, ...), custom_call_target="tpu_custom_call" | custom-call | flops 1000 | bytes 1000 | tf_op jit(solution)/shard_map/pallas_call | solution.py:53
  9.3 1.9 %collective-permute-start.5 = (f32[8,128,128]{2,1,0:T(8,128)S(1)}, f32[8,128,128]{2,1,0:T(8,128)S(1)}, u32[]{:S(2)}, u32[]{:S(2)}) collective-permute-start(f32[8,128,128]{2,1,0:T(8,128)S(1)} %get-tuple-element.74.refs_0_), channel_id=1, source_target_pairs={{0,4},{2,6},{4,0},{6,2},{8,12},{10,14},{12,8},{14,10},{1,5},{3,7},... | collective-permute-start | bytes 1572872 | tf_op jit(solution)/shard_map/ppermute | solution.py:374
  11.1 0.7 collective-permute-start.8
  11.8 1.5 %shard_map.79 = f32[5,16,8,128]{3,2,1,0:T(8,128)S(1)} custom-call(s32[3]{0:T(128)S(1)} %pad_add_fusion.place, f32[16,128,128]{2,1,0:T(8,128)} %refs_9_.1, f32[16,128]{1,0:T(8,128)S(1)} %get-tuple-element.71.keep), custom_call_target="tpu_custom_call" | custom-call | flops 1000 | bytes 1000 | tf_op jit(solution)/shard_map/pallas_call | solution.py:53
  13.4 0.1 collective-permute-start.4
  13.4 1.6 %collective-permute-done.4.third = f32[5,16,8,128]{3,2,1,0:T(8,128)S(1)} collective-permute-done((f32[5,16,8,128]{3,2,1,0:T(8,128)S(1)}, f32[5,16,8,128]{3,2,1,0:T(8,128)S(1)}, u32[]{:S(2)}, u32[]{:S(2)}) %collective-permute-start.4) | collective-permute-done | bytes 327712 | tf_op jit(solution)/shard_map/ppermute | solution.py:378
  15.0 0.0 collective-permute-done.2.first
  15.1 0.0 collective-permute-done.3.second
  15.1 3.8 %shard_map.80 = (f32[16,128,128]{2,1,0:T(8,128)S(1)}, f32[16,128,128]{2,1,0:T(8,128)S(1)}, f32[8,128,128]{2,1,0:T(8,128)S(1)}, f32[8,128,128]{2,1,0:T(8,128)S(1)...) custom-call(s32[3]{0:T(128)S(1)} %pad_add_fusion.place, ...), custom_call_target="tpu_custom_call" | custom-call | flops 1000 | bytes 1000 | tf_op jit(solution)/shard_map/pallas_call | solution.py:53
  18.9 3.5 %collective-permute-done.5.refs_0_.refs_1_ = f32[8,128,128]{2,1,0:T(8,128)S(1)} collective-permute-done((f32[8,128,128]{2,1,0:T(8,128)S(1)}, f32[8,128,128]{2,1,0:T(8,128)S(1)}, u32[]{:S(2)}, u32[]{:S(2)}) %collective-permute-start.5) | collective-permute-done | bytes 524320 | tf_op jit(solution)/shard_map/ppermute | solution.py:374
  22.4 0.7 collective-permute-start.6
  23.1 0.0 collective-permute-done.8.refs_0_
  23.1 1.3 %collective-permute-start.9 = (f32[8,128,128]{2,1,0:T(8,128)S(1)}, f32[8,128,128]{2,1,0:T(8,128)S(1)}, u32[]{:S(2)}, u32[]{:S(2)}) collective-permute-start(f32[8,128,128]{2,1,0:T(8,128)S(1)} %collective-permute-done.8.refs_0_), channel_id=1, source_target_pairs={{4,0},{6,2},{8,12},{10,14},{5,1},{7,3},{9,13},{11,15},{20,16},{22,... | collective-permute-start | bytes 1572872 | tf_op jit(solution)/shard_map/ppermute | solution.py:374
  24.4 3.8 %shard_map.81 = (f32[16,8,128]{2,1,0:T(8,128)S(1)}, f32[16,8,128]{2,1,0:T(8,128)S(1)}, f32[256,128]{1,0:T(8,128)S(1)}, f32[8,128,128]{2,1,0:T(8,128)S(1)}) custom-call(s32[3]{0:T(128)S(1)} %pad_add_fusion.place, f32[8,128,128]{2,1,0:T(8,128)S(1)} %get-tuple-element.74.refs_0_, f32[16,128,128]{2,1,0:T(8,128)S(1)} %get-tuple-element.79.refs_1_.refs_2_, ...), custom_call_target="tpu_custom_call" | custom-call | flops 1000 | bytes 1000 | tf_op jit(solution)/shard_map/pallas_call | solution.py:53
  28.2 3.8 %shard_map.82 = (f32[16,8,128]{2,1,0:T(8,128)S(1)}, f32[16,8,128]{2,1,0:T(8,128)S(1)}, f32[256,128]{1,0:T(8,128)S(1)}, f32[8,128,128]{2,1,0:T(8,128)S(1)}) custom-call(s32[3]{0:T(128)S(1)} %pad_add_fusion.place, f32[8,128,128]{2,1,0:T(8,128)S(1)} %collective-permute-done.5.refs_0_.refs_1_, f32[16,128,128]{2,1,0:T(8,128)S(1)} %get-tuple-element.79.refs_1_.refs_2_, ...), custom_call_target="tpu_custom_call" | custom-call | flops 1000 | bytes 1000 | tf_op jit(solution)/shard_map/pallas_call | solution.py:53
  32.0 0.1 collective-permute-start.7
  32.1 2.9 %shard_map.83 = (f32[16,128,128]{2,1,0:T(8,128)S(1)}, f32[16,128,128]{2,1,0:T(8,128)S(1)}) custom-call(s32[3]{0:T(128)S(1)} %pad_add_fusion.place, f32[8,128,128]{2,1,0:T(8,128)S(1)} %get-tuple-element.74.refs_0_, f32[8,128,128]{2,1,0:T(8,128)S(1)} %collective-permute-done.5.refs_0_.refs_1_, f32[256,128]{1,0:T(8,128)S(1)} %get-tuple-element.90.refs_2_, ...), custom_call_target="tpu_custom_call" | custom-call | flops 1000 | bytes 1000 | tf_op jit(solution)/shard_map/pallas_call | solution.py:53
  35.0 0.0 collective-permute-done.7.refs_4_
  35.0 0.0 collective-permute-done.6.refs_0_
  35.0 1.3 %collective-permute-start.10 = (f32[8,128,128]{2,1,0:T(8,128)S(1)}, f32[8,128,128]{2,1,0:T(8,128)S(1)}, u32[]{:S(2)}, u32[]{:S(2)}) collective-permute-start(f32[8,128,128]{2,1,0:T(8,128)S(1)} %collective-permute-done.6.refs_0_), channel_id=1, source_target_pairs={{4,0},{6,2},{8,12},{10,14},{5,1},{7,3},{9,13},{11,15},{20,16},{22,... | collective-permute-start | bytes 1572872 | tf_op jit(solution)/shard_map/ppermute | solution.py:374
  36.3 2.4 %collective-permute-done.9.refs_1_ = f32[8,128,128]{2,1,0:T(8,128)S(1)} collective-permute-done((f32[8,128,128]{2,1,0:T(8,128)S(1)}, f32[8,128,128]{2,1,0:T(8,128)S(1)}, u32[]{:S(2)}, u32[]{:S(2)}) %collective-permute-start.9) | collective-permute-done | bytes 524320 | tf_op jit(solution)/shard_map/ppermute | solution.py:374
  38.7 3.8 %shard_map.84 = (f32[16,8,128]{2,1,0:T(8,128)S(1)}, f32[16,8,128]{2,1,0:T(8,128)S(1)}, f32[256,128]{1,0:T(8,128)S(1)}, f32[8,128,128]{2,1,0:T(8,128)S(1)}, f32[8,128,128]{2,1,0:T(8,128)S(1)}) custom-call(s32[3]{0:T(128)S(1)} %pad_add_fusion.place, f32[8,128,128]{2,1,0:T(8,128)S(1)} %collective-permute-done.6.refs_0_, ...), custom_call_target="tpu_custom_call" | custom-call | flops 1000 | bytes 1000 | tf_op jit(solution)/shard_map/pallas_call | solution.py:53
  42.6 3.9 %collective-permute-start.11 = (f32[8,128,128]{2,1,0:T(8,128)S(1)}, f32[8,128,128]{2,1,0:T(8,128)S(1)}, u32[]{:S(2)}, u32[]{:S(2)}) collective-permute-start(f32[8,128,128]{2,1,0:T(8,128)S(1)} %get-tuple-element.104), channel_id=1, source_target_pairs={{0,4},{2,6},{12,8},{14,10},{1,5},{3,7},{13,9},{15,11},{16,20},{18,... | collective-permute-start | bytes 1572872 | tf_op jit(solution)/shard_map/ppermute | solution.py:374
  46.4 0.7 collective-permute-start.12
  47.2 1.6 %collective-permute-start.13 = (f32[2,2,16,8,128]{4,3,2,1,0:T(8,128)S(1)}, f32[2,2,16,8,128]{4,3,2,1,0:T(8,128)S(1)}, u32[]{:S(2)}, u32[]{:S(2)}) collective-permute-start(f32[2,2,16,8,128]{4,3,2,1,0:T(8,128)S(1)} %pad_maximum_fusion), channel_id=1, source_target_pairs={{0,1},{1,0},{2,3},{3,2},{4,5},{5,4},{6,7},{7,6},{8,9},{9,8},{10,11... | collective-permute-start | bytes 786440 | tf_op jit(solution)/shard_map/ppermute | solution.py:382
  48.8 1.9 %shard_map.85 = (f32[16,128,128]{2,1,0:T(8,128)S(1)}, f32[16,128,128]{2,1,0:T(8,128)S(1)}) custom-call(s32[3]{0:T(128)S(1)} %pad_add_fusion.place, f32[8,128,128]{2,1,0:T(8,128)S(1)} %get-tuple-element.95.refs_0_, f32[256,128]{1,0:T(8,128)S(1)} %get-tuple-element.96.refs_1_, f32[16,128,128]{2,1,0:T(8,128)S(1)} %get-tuple-element.97.refs_2_, ...), custom_call_target="tpu_custom_call" | custom-call | flops 1000 | bytes 1000 | tf_op jit(solution)/shard_map/pallas_call | solution.py:53
  50.7 2.5 %collective-permute-done.10.refs_1_ = f32[8,128,128]{2,1,0:T(8,128)S(1)} collective-permute-done((f32[8,128,128]{2,1,0:T(8,128)S(1)}, f32[8,128,128]{2,1,0:T(8,128)S(1)}, u32[]{:S(2)}, u32[]{:S(2)}) %collective-permute-start.10) | collective-permute-done | bytes 524320 | tf_op jit(solution)/shard_map/ppermute | solution.py:374
  53.2 3.8 %shard_map.86 = (f32[16,8,128]{2,1,0:T(8,128)S(1)}, f32[16,8,128]{2,1,0:T(8,128)S(1)}, f32[256,128]{1,0:T(8,128)S(1)}, f32[8,128,128]{2,1,0:T(8,128)S(1)}, f32[8,128,128]{2,1,0:T(8,128)S(1)}) custom-call(s32[3]{0:T(128)S(1)} %pad_add_fusion.place, f32[8,128,128]{2,1,0:T(8,128)S(1)} %collective-permute-done.8.refs_0_, ...), custom_call_target="tpu_custom_call" | custom-call | flops 1000 | bytes 1000 | tf_op jit(solution)/shard_map/pallas_call | solution.py:53
  57.0 1.9 %shard_map.87 = (f32[16,128,128]{2,1,0:T(8,128)S(1)}, f32[18,128,128]{2,1,0:T(8,128)S(1)}) custom-call(s32[3]{0:T(128)S(1)} %pad_add_fusion.place, f32[8,128,128]{2,1,0:T(8,128)S(1)} %get-tuple-element.106.right, f32[256,128]{1,0:T(8,128)S(1)} %get-tuple-element.107.d_x, f32[16,128,128]{2,1,0:T(8,128)S(1)} %get-tuple-element.108.here, ...), custom_call_target="tpu_custom_call" | custom-call | flops 1000 | bytes 1000 | tf_op jit(solution)/shard_map/pallas_call | solution.py:53
  59.0 0.0 collective-permute-done.11
  59.0 0.1 add.12
  59.1 0.0 collective-permute-done.12
  59.1 0.1 add.13
  59.1 0.0 collective-permute-done.13.refs_5_
  59.1 0.1 collective-permute-start.14
  59.2 4.5 %collective-permute-start.15 = (f32[8,128,128]{2,1,0:T(8,128)S(1)}, f32[8,128,128]{2,1,0:T(8,128)S(1)}, u32[]{:S(2)}, u32[]{:S(2)}) collective-permute-start(f32[8,128,128]{2,1,0:T(8,128)S(1)} %get-tuple-element.103), channel_id=1, source_target_pairs={{0,12},{2,14},{12,0},{14,2},{1,13},{3,15},{13,1},{15,3},{16,28},{1... | collective-permute-start | bytes 1572872 | tf_op jit(solution)/shard_map/ppermute | solution.py:374
  63.7 0.0 collective-permute-done.14.received.refs_6_
  63.7 0.7 shard_map.88
  64.4 1.6 %collective-permute-start.17 = (f32[8,128,128]{2,1,0:T(8,128)S(1)}, f32[8,128,128]{2,1,0:T(8,128)S(1)}, u32[]{:S(2)}, u32[]{:S(2)}) collective-permute-start(f32[8,128,128]{2,1,0:T(8,128)S(1)} %get-tuple-element.120), channel_id=1, source_target_pairs={{0,1},{1,0},{2,3},{3,2},{4,5},{5,4},{6,7},{7,6},{8,9},{9,8},{10,11... | collective-permute-start | bytes 1572872 | tf_op jit(solution)/shard_map/ppermute | solution.py:382
  66.0 1.3 %collective-permute-start.18 = (f32[8,128,128]{2,1,0:T(8,128)S(1)}, f32[8,128,128]{2,1,0:T(8,128)S(1)}, u32[]{:S(2)}, u32[]{:S(2)}) collective-permute-start(f32[8,128,128]{2,1,0:T(8,128)S(1)} %add.13), channel_id=1, source_target_pairs={{0,4},{2,6},{4,0},{6,2},{8,12},{10,14},{12,8},{14,10},{1,5},{3,7},... | collective-permute-start | bytes 1572872 | tf_op jit(solution)/shard_map/ppermute | solution.py:374
  67.3 0.7 collective-permute-start.19
  67.9 9.8 %collective-permute-done.15.d_right_far = f32[8,128,128]{2,1,0:T(8,128)S(1)} collective-permute-done((f32[8,128,128]{2,1,0:T(8,128)S(1)}, f32[8,128,128]{2,1,0:T(8,128)S(1)}, u32[]{:S(2)}, u32[]{:S(2)}) %collective-permute-start.15) | collective-permute-done | bytes 524320 | tf_op jit(solution)/shard_map/ppermute | solution.py:374
  77.7 1.5 %collective-permute-start.16 = (f32[4,128,128]{2,1,0:T(8,128)S(1)}, f32[4,128,128]{2,1,0:T(8,128)S(1)}, u32[]{:S(2)}, u32[]{:S(2)}) collective-permute-start(f32[4,128,128]{2,1,0:T(8,128)S(1)} %get-tuple-element.117), channel_id=1, source_target_pairs={{0,1},{1,0},{2,3},{3,2},{4,5},{5,4},{6,7},{7,6},{8,9},{9,8},{10,11... | collective-permute-start | bytes 786440 | tf_op jit(solution)/shard_map/ppermute | solution.py:382
  79.2 6.0 %collective-permute-done.16.refs_7_ = f32[4,128,128]{2,1,0:T(8,128)S(1)} collective-permute-done((f32[4,128,128]{2,1,0:T(8,128)S(1)}, f32[4,128,128]{2,1,0:T(8,128)S(1)}, u32[]{:S(2)}, u32[]{:S(2)}) %collective-permute-start.16) | collective-permute-done | bytes 262176 | tf_op jit(solution)/shard_map/ppermute | solution.py:382
  85.2 0.0 collective-permute-done.17.refs_12_
  85.2 1.4 %shard_map.89.base = f32[8,128,128]{2,1,0:T(8,128)S(1)} custom-call(s32[3]{0:T(128)S(1)} %pad_add_fusion.place, f32[16,8,128]{2,1,0:T(8,128)S(1)} %get-tuple-element.85.refs_0_, f32[16,8,128]{2,1,0:T(8,128)S(1)} %get-tuple-element.87.refs_1_, f32[16,8,128]{2,1,0:T(8,128)S(1)} %get-tuple-element.94.out_next.refs_2_, ...), custom_call_target="tpu_custom_call" | custom-call | flops 1000 | bytes 1000 | tf_op jit(solution)/shard_map/pallas_call | solution.py:53
  86.7 1.8 %collective-permute-done.18.d_right_near = f32[8,128,128]{2,1,0:T(8,128)S(1)} collective-permute-done((f32[8,128,128]{2,1,0:T(8,128)S(1)}, f32[8,128,128]{2,1,0:T(8,128)S(1)}, u32[]{:S(2)}, u32[]{:S(2)}) %collective-permute-start.18) | collective-permute-done | bytes 524320 | tf_op jit(solution)/shard_map/ppermute | solution.py:374
  88.5 0.0 collective-permute-done.19.d_right_middle
  88.5 2.3 %shard_map.90 = (f32[8,128,128]{2,1,0:T(8,128)S(1)}, f32[16,128,128]{2,1,0:T(8,128)}) custom-call(s32[3]{0:T(128)S(1)} %pad_add_fusion.place, f32[8,128,128]{2,1,0:T(8,128)S(1)} %get-tuple-element.69.normed, f32[8,128,128]{2,1,0:T(8,128)S(1)} %get-tuple-element.70.scale, f32[8,128,128]{2,1,0:T(8,128)S(1)} %shard_map.89.base, ...), custom_call_target="tpu_custom_call" | custom-call | flops 1000 | bytes 1000 | tf_op jit(solution)/shard_map/pallas_call | solution.py:53
  90.7 1.5 %collective-permute-start.20 = (f32[8,128,128]{2,1,0:T(8,128)S(1)}, f32[8,128,128]{2,1,0:T(8,128)S(1)}, u32[]{:S(2)}, u32[]{:S(2)}) collective-permute-start(f32[8,128,128]{2,1,0:T(8,128)S(1)} %get-tuple-element.131), channel_id=1, source_target_pairs={{0,1},{1,0},{2,3},{3,2},{4,5},{5,4},{6,7},{7,6},{8,9},{9,8},{10,11... | collective-permute-start | bytes 1572872 | tf_op jit(solution)/shard_map/ppermute | solution.py:382
  92.2 1.8 %shard_map.91 = f32[16,128,128]{2,1,0:T(8,128)} custom-call(s32[3]{0:T(128)S(1)} %pad_add_fusion.place, f32[16,8,128]{2,1,0:T(8,128)S(1)} %get-tuple-element.85.refs_0_, f32[16,8,128]{2,1,0:T(8,128)S(1)} %get-tuple-element.87.refs_1_, f32[16,8,128]{2,1,0:T(8,128)S(1)} %get-tuple-element.94.out_next.refs_2_, ...), custom_call_target="tpu_custom_call" | custom-call | flops 1000 | bytes 1000 | tf_op jit(solution)/shard_map/pallas_call | solution.py:53
  94.0 10.6 %collective-permute-done.20.other = f32[8,128,128]{2,1,0:T(8,128)S(1)} collective-permute-done((f32[8,128,128]{2,1,0:T(8,128)S(1)}, f32[8,128,128]{2,1,0:T(8,128)S(1)}, u32[]{:S(2)}, u32[]{:S(2)}) %collective-permute-start.20) | collective-permute-done | bytes 524320 | tf_op jit(solution)/shard_map/ppermute | solution.py:382
  104.6 1.3 %shard_map.92 = f32[16,128,128]{2,1,0:T(8,128)} custom-call(s32[3]{0:T(128)S(1)} %pad_add_fusion.place, f32[8,128,128]{2,1,0:T(8,128)S(1)} %collective-permute-done.20.other, f32[16,128,128]{2,1,0:T(8,128)} %get-tuple-element.135.whole), custom_call_target="tpu_custom_call", output_to_operand_aliasing={{}: (2, {})} | custom-call | tf_op jit(solution)/shard_map/pallas_call | solution.py:362
  (8 shorter events, 0.1 us)
Async XLA Ops:
  0.6 7.4 %collective-permute-start = (f32[256,128]{1,0:T(8,128)}, f32[256,128]{1,0:T(8,128)S(1)}, u32[]{:S(2)}, u32[]{:S(2)}) collective-permute-start(f32[256,128]{1,0:T(8,128)} %bitcast.23), channel_id=1, source_target_pairs={{0,1},{1,0},{2,3},{3,2},{4,5},{5,4},{6,7},{7,6},{8,9},{9,8},{10,11... | collective-permute-start | bytes 393224 | tf_op jit(solution)/shard_map/ppermute | solution.py:382
  3.6 4.4 %collective-permute-start.1 = (f32[64,128]{1,0:T(8,128)}, f32[64,128]{1,0:T(8,128)S(1)}, u32[]{:S(2)}, u32[]{:S(2)}) collective-permute-start(f32[64,128]{1,0:T(8,128)} %mine_out.1), channel_id=1, source_target_pairs={{0,1},{1,0},{2,3},{3,2},{4,5},{5,4},{6,7},{7,6},{8,9},{9,8},{10,11... | collective-permute-start | bytes 98312 | tf_op jit(solution)/shard_map/ppermute | solution.py:382
  3.8 11.3 %copy-start.3 = (f32[64,128]{1,0:T(8,128)S(1)}, f32[64,128]{1,0:T(8,128)}, u32[]{:S(2)}) copy-start(f32[64,128]{1,0:T(8,128)} %mine_out.1) | copy-start | bytes 98308
  6.0 9.1 %copy-start = (f32[16,128,128]{2,1,0:T(8,128)S(1)}, f32[16,128,128]{2,1,0:T(8,128)}, u32[]{:S(2)}) copy-start(f32[16,128,128]{2,1,0:T(8,128)} %refs_9_.1) | copy-start | bytes 3145732
  6.0 9.1 %copy-start.1 = (f32[16,128,128]{2,1,0:T(8,128)S(1)}, f32[16,128,128]{2,1,0:T(8,128)}, u32[]{:S(2)}) copy-start(f32[16,128,128]{2,1,0:T(8,128)} %pair.3) | copy-start | bytes 3145732
  6.0 9.1 %copy-start.2 = (f32[128,128]{1,0:T(8,128)S(1)}, f32[128,128]{1,0:T(8,128)}, u32[]{:S(2)}) copy-start(f32[128,128]{1,0:T(8,128)} %refs_10_.1) | copy-start | bytes 196612
  6.0 9.0 %collective-permute-start.2 = (f32[8,128,128]{2,1,0:T(8,128)S(1)}, f32[8,128,128]{2,1,0:T(8,128)S(1)}, u32[]{:S(2)}, u32[]{:S(2)}) collective-permute-start(f32[8,128,128]{2,1,0:T(8,128)S(1)} %get-tuple-element.75), channel_id=1, source_target_pairs={{0,2},{2,0},{4,6},{6,4},{8,10},{10,8},{12,14},{14,12},{1,3},{3,1},... | collective-permute-start | bytes 1572872 | tf_op jit(solution)/shard_map/ppermute | solution.py:378
  6.1 8.9 %collective-permute-start.3 = (f32[8,128,128]{2,1,0:T(8,128)S(1)}, f32[8,128,128]{2,1,0:T(8,128)S(1)}, u32[]{:S(2)}, u32[]{:S(2)}) collective-permute-start(f32[8,128,128]{2,1,0:T(8,128)S(1)} %get-tuple-element.76), channel_id=1, source_target_pairs={{0,2},{2,0},{4,6},{6,4},{8,10},{10,8},{12,14},{14,12},{1,3},{3,1},... | collective-permute-start | bytes 1572872 | tf_op jit(solution)/shard_map/ppermute | solution.py:378
  9.3 13.2 %collective-permute-start.5 = (f32[8,128,128]{2,1,0:T(8,128)S(1)}, f32[8,128,128]{2,1,0:T(8,128)S(1)}, u32[]{:S(2)}, u32[]{:S(2)}) collective-permute-start(f32[8,128,128]{2,1,0:T(8,128)S(1)} %get-tuple-element.74.refs_0_), channel_id=1, source_target_pairs={{0,4},{2,6},{4,0},{6,2},{8,12},{10,14},{12,8},{14,10},{1,5},{3,7},... | collective-permute-start | bytes 1572872 | tf_op jit(solution)/shard_map/ppermute | solution.py:374
  11.1 12.0 %collective-permute-start.8 = (f32[8,128,128]{2,1,0:T(8,128)S(1)}, f32[8,128,128]{2,1,0:T(8,128)S(1)}, u32[]{:S(2)}, u32[]{:S(2)}) collective-permute-start(f32[8,128,128]{2,1,0:T(8,128)S(1)} %get-tuple-element.74.refs_0_), channel_id=1, source_target_pairs={{4,8},{6,10},{8,4},{10,6},{5,9},{7,11},{9,5},{11,7},{20,24},{22,26... | collective-permute-start | bytes 1572872 | tf_op jit(solution)/shard_map/ppermute | solution.py:374
  13.4 1.7 %collective-permute-start.4 = (f32[5,16,8,128]{3,2,1,0:T(8,128)S(1)}, f32[5,16,8,128]{3,2,1,0:T(8,128)S(1)}, u32[]{:S(2)}, u32[]{:S(2)}) collective-permute-start(f32[5,16,8,128]{3,2,1,0:T(8,128)S(1)} %shard_map.79), channel_id=1, source_target_pairs={{0,2},{2,0},{4,6},{6,4},{8,10},{10,8},{12,14},{14,12},{1,3},{3,1},... | collective-permute-start | bytes 983048 | tf_op jit(solution)/shard_map/ppermute | solution.py:378
  22.4 12.6 %collective-permute-start.6 = (f32[8,128,128]{2,1,0:T(8,128)S(1)}, f32[8,128,128]{2,1,0:T(8,128)S(1)}, u32[]{:S(2)}, u32[]{:S(2)}) collective-permute-start(f32[8,128,128]{2,1,0:T(8,128)S(1)} %collective-permute-done.5.refs_0_.refs_1_), channel_id=1, source_target_pairs={{4,8},{6,10},{8,4},{10,6},{5,9},{7,11},{9,5},{11,7},{20,24},{22,26... | collective-permute-start | bytes 1572872 | tf_op jit(solution)/shard_map/ppermute | solution.py:374
  23.1 15.6 %collective-permute-start.9 = (f32[8,128,128]{2,1,0:T(8,128)S(1)}, f32[8,128,128]{2,1,0:T(8,128)S(1)}, u32[]{:S(2)}, u32[]{:S(2)}) collective-permute-start(f32[8,128,128]{2,1,0:T(8,128)S(1)} %collective-permute-done.8.refs_0_), channel_id=1, source_target_pairs={{4,0},{6,2},{8,12},{10,14},{5,1},{7,3},{9,13},{11,15},{20,16},{22,... | collective-permute-start | bytes 1572872 | tf_op jit(solution)/shard_map/ppermute | solution.py:374
  32.0 3.0 %collective-permute-start.7 = (f32[2,16,8,128]{3,2,1,0:T(8,128)S(1)}, f32[2,16,8,128]{3,2,1,0:T(8,128)S(1)}, u32[]{:S(2)}, u32[]{:S(2)}) collective-permute-start(f32[2,16,8,128]{3,2,1,0:T(8,128)S(1)} %pad_maximum_fusion.1), channel_id=1, source_target_pairs={{0,2},{2,0},{4,6},{6,4},{8,10},{10,8},{12,14},{14,12},{1,3},{3,1},... | collective-permute-start | bytes 393224 | tf_op jit(solution)/shard_map/ppermute | solution.py:378
  35.0 18.2 %collective-permute-start.10 = (f32[8,128,128]{2,1,0:T(8,128)S(1)}, f32[8,128,128]{2,1,0:T(8,128)S(1)}, u32[]{:S(2)}, u32[]{:S(2)}) collective-permute-start(f32[8,128,128]{2,1,0:T(8,128)S(1)} %collective-permute-done.6.refs_0_), channel_id=1, source_target_pairs={{4,0},{6,2},{8,12},{10,14},{5,1},{7,3},{9,13},{11,15},{20,16},{22,... | collective-permute-start | bytes 1572872 | tf_op jit(solution)/shard_map/ppermute | solution.py:374
  42.6 16.4 %collective-permute-start.11 = (f32[8,128,128]{2,1,0:T(8,128)S(1)}, f32[8,128,128]{2,1,0:T(8,128)S(1)}, u32[]{:S(2)}, u32[]{:S(2)}) collective-permute-start(f32[8,128,128]{2,1,0:T(8,128)S(1)} %get-tuple-element.104), channel_id=1, source_target_pairs={{0,4},{2,6},{12,8},{14,10},{1,5},{3,7},{13,9},{15,11},{16,20},{18,... | collective-permute-start | bytes 1572872 | tf_op jit(solution)/shard_map/ppermute | solution.py:374
  46.4 12.6 %collective-permute-start.12 = (f32[8,128,128]{2,1,0:T(8,128)S(1)}, f32[8,128,128]{2,1,0:T(8,128)S(1)}, u32[]{:S(2)}, u32[]{:S(2)}) collective-permute-start(f32[8,128,128]{2,1,0:T(8,128)S(1)} %get-tuple-element.104), channel_id=1, source_target_pairs={{4,8},{6,10},{8,4},{10,6},{5,9},{7,11},{9,5},{11,7},{20,24},{22,26... | collective-permute-start | bytes 1572872 | tf_op jit(solution)/shard_map/ppermute | solution.py:374
  47.2 11.9 %collective-permute-start.13 = (f32[2,2,16,8,128]{4,3,2,1,0:T(8,128)S(1)}, f32[2,2,16,8,128]{4,3,2,1,0:T(8,128)S(1)}, u32[]{:S(2)}, u32[]{:S(2)}) collective-permute-start(f32[2,2,16,8,128]{4,3,2,1,0:T(8,128)S(1)} %pad_maximum_fusion), channel_id=1, source_target_pairs={{0,1},{1,0},{2,3},{3,2},{4,5},{5,4},{6,7},{7,6},{8,9},{9,8},{10,11... | collective-permute-start | bytes 786440 | tf_op jit(solution)/shard_map/ppermute | solution.py:382
  59.1 4.5 %collective-permute-start.14 = (f32[18,128,128]{2,1,0:T(8,128)S(1)}, f32[18,128,128]{2,1,0:T(8,128)S(1)}, u32[]{:S(2)}, u32[]{:S(2)}) collective-permute-start(f32[18,128,128]{2,1,0:T(8,128)S(1)} %get-tuple-element.114), channel_id=1, source_target_pairs={{0,2},{2,0},{4,6},{6,4},{8,10},{10,8},{12,14},{14,12},{1,3},{3,1},... | collective-permute-start | bytes 3538952 | tf_op jit(solution)/shard_map/ppermute | solution.py:378
  59.2 18.5 %collective-permute-start.15 = (f32[8,128,128]{2,1,0:T(8,128)S(1)}, f32[8,128,128]{2,1,0:T(8,128)S(1)}, u32[]{:S(2)}, u32[]{:S(2)}) collective-permute-start(f32[8,128,128]{2,1,0:T(8,128)S(1)} %get-tuple-element.103), channel_id=1, source_target_pairs={{0,12},{2,14},{12,0},{14,2},{1,13},{3,15},{13,1},{15,3},{16,28},{1... | collective-permute-start | bytes 1572872 | tf_op jit(solution)/shard_map/ppermute | solution.py:374
  64.4 20.9 %collective-permute-start.17 = (f32[8,128,128]{2,1,0:T(8,128)S(1)}, f32[8,128,128]{2,1,0:T(8,128)S(1)}, u32[]{:S(2)}, u32[]{:S(2)}) collective-permute-start(f32[8,128,128]{2,1,0:T(8,128)S(1)} %get-tuple-element.120), channel_id=1, source_target_pairs={{0,1},{1,0},{2,3},{3,2},{4,5},{5,4},{6,7},{7,6},{8,9},{9,8},{10,11... | collective-permute-start | bytes 1572872 | tf_op jit(solution)/shard_map/ppermute | solution.py:382
  66.0 22.5 %collective-permute-start.18 = (f32[8,128,128]{2,1,0:T(8,128)S(1)}, f32[8,128,128]{2,1,0:T(8,128)S(1)}, u32[]{:S(2)}, u32[]{:S(2)}) collective-permute-start(f32[8,128,128]{2,1,0:T(8,128)S(1)} %add.13), channel_id=1, source_target_pairs={{0,4},{2,6},{4,0},{6,2},{8,12},{10,14},{12,8},{14,10},{1,5},{3,7},... | collective-permute-start | bytes 1572872 | tf_op jit(solution)/shard_map/ppermute | solution.py:374
  67.3 21.2 %collective-permute-start.19 = (f32[8,128,128]{2,1,0:T(8,128)S(1)}, f32[8,128,128]{2,1,0:T(8,128)S(1)}, u32[]{:S(2)}, u32[]{:S(2)}) collective-permute-start(f32[8,128,128]{2,1,0:T(8,128)S(1)} %add.12), channel_id=1, source_target_pairs={{4,8},{6,10},{8,4},{10,6},{5,9},{7,11},{9,5},{11,7},{20,24},{22,26... | collective-permute-start | bytes 1572872 | tf_op jit(solution)/shard_map/ppermute | solution.py:374
  77.7 7.5 %collective-permute-start.16 = (f32[4,128,128]{2,1,0:T(8,128)S(1)}, f32[4,128,128]{2,1,0:T(8,128)S(1)}, u32[]{:S(2)}, u32[]{:S(2)}) collective-permute-start(f32[4,128,128]{2,1,0:T(8,128)S(1)} %get-tuple-element.117), channel_id=1, source_target_pairs={{0,1},{1,0},{2,3},{3,2},{4,5},{5,4},{6,7},{7,6},{8,9},{9,8},{10,11... | collective-permute-start | bytes 786440 | tf_op jit(solution)/shard_map/ppermute | solution.py:382
  90.7 13.8 %collective-permute-start.20 = (f32[8,128,128]{2,1,0:T(8,128)S(1)}, f32[8,128,128]{2,1,0:T(8,128)S(1)}, u32[]{:S(2)}, u32[]{:S(2)}) collective-permute-start(f32[8,128,128]{2,1,0:T(8,128)S(1)} %get-tuple-element.131), channel_id=1, source_target_pairs={{0,1},{1,0},{2,3},{3,2},{4,5},{5,4},{6,7},{7,6},{8,9},{9,8},{10,11... | collective-permute-start | bytes 1572872 | tf_op jit(solution)/shard_map/ppermute | solution.py:382

commit v5 on v4

--- a/solution.py
+++ b/solution.py
@@ -260,13 +260,15 @@
         left_rows(pairs, bases[which], out, which * rows, rows, 0)
 
 
-def last_left_kernel(place, right, d_x, here, there, out_next, out_last, kept, sent):
-    tiles = ((right, d_x),)
-    rows = here.shape[0]
-    left_rows(tiles, here, kept, 0, rows, 0)
-    left_rows(tiles, there, sent, rows, rows, 0)
+def last_sent_kernel(place, right, d_x, there, out_next, out_last, sent):
+    rows = there.shape[0]
+    left_rows(((right, d_x),), there, sent, rows, rows, 0)
     sent[rows] = flat(out_next[...])
     sent[rows + 1] = flat(out_last[...])
+
+
+def last_kept_kernel(place, right, d_x, here, kept):
+    left_rows(((right, d_x),), here, kept, 0, here.shape[0], 0)
 
 
 def share_kernel(place, kept, received, out_next, out_last, d_left, packed, rest):
@@ -335,39 +337,46 @@
         base[at] = (dot_t(flat(d_gate), w_gate[...]) + dot(both, w)).reshape(CHUNK, cols, -1)
 
 
-def pair_kernel(rows, place, normed, scale, base, d_right, d_right_near, d_right_middle, d_right_far, open_part, slope, mine, other, d_mine, d_pair):
-    half, cols, chans = base.shape
+def pair_kernel(first, place, normed, scale, base, d_right, d_right_near, d_right_middle, d_right_far, open_part, slope, mine, other, d_mine):
+    count, cols, chans = d_mine.shape
     w = gated_weights(place, mine, other, 2)
-    for t in range(0, half, CHUNK):
-        at = slice(t, t + CHUNK)
-        grad = flat(d_right[at] + d_right_near[at] + (d_right_middle[at] + d_right_far[at]))
-        both = jnp.concatenate([grad * flat(open_part[at]), grad * flat(slope[at])], axis=1)
-        d_normed = flat(base[at]) + dot(both, w)
-        value = flat(normed[at])
-        mean_grad = jnp.mean(d_normed, axis=-1, keepdims=True)
-        mean_cross = jnp.mean(d_normed * value, axis=-1, keepdims=True)
-        d_mine[at] = ((d_normed - mean_grad - value * mean_cross) * flat(scale[at])).reshape(CHUNK, cols, -1)
-        d_pair[pl.ds(source_row(place, t, rows), CHUNK)] = d_mine[at]
-
-
-def join_kernel(place, other, whole, joined, sem):
-    half = other.shape[0]
-    copy = pltpu.make_async_copy(other, joined.at[pl.ds((1 - lax.axis_index("ch")) * half, half)], sem)
-    copy.start()
-    copy.wait()
-
-
-def join(place, other, whole):
+    at = slice(first, first + count)
+    grad = flat(d_right[at] + d_right_near[at] + (d_right_middle[at] + d_right_far[at]))
+    both = jnp.concatenate([grad * flat(open_part[at]), grad * flat(slope[at])], axis=1)
+    d_normed = flat(base[at]) + dot(both, w)
+    value = flat(normed[at])
+    mean_grad = jnp.mean(d_normed, axis=-1, keepdims=True)
+    mean_cross = jnp.mean(d_normed * value, axis=-1, keepdims=True)
+    d_mine[...] = ((d_normed - mean_grad - value * mean_cross) * flat(scale[at])).reshape(count, cols, -1)
+
+
+def join_kernel(firsts, sides, *refs):
+    blocks, whole, sems = refs[: len(firsts)], refs[-2], refs[-1]
+    side = lax.axis_index("ch")
+    half = whole.shape[0] // 2
+    copies = []
+    for at, (block, first, mine) in enumerate(zip(blocks, firsts, sides)):
+        start = (side if mine else 1 - side) * half + first
+        copies.append(pltpu.make_async_copy(block, whole.at[pl.ds(start, block.shape[0])], sems.at[at]))
+    for copy in copies:
+        copy.start()
+    for copy in copies:
+        copy.wait()
+
+
+def join(blocks, firsts, sides, shape, whole=None):
     anywhere = pl.BlockSpec(memory_space=pl.ANY)
+    vmem = pl.BlockSpec(memory_space=pltpu.VMEM)
+    given = [] if whole is None else [whole]
     return pl.pallas_call(
-        join_kernel,
-        out_shape=jax.ShapeDtypeStruct(whole.shape, F32),
-        in_specs=[pl.BlockSpec(memory_space=pltpu.SMEM), pl.BlockSpec(memory_space=pltpu.VMEM), anywhere],
+        functools.partial(join_kernel, firsts, sides),
+        out_shape=jax.ShapeDtypeStruct(shape, F32),
+        in_specs=[vmem] * len(blocks) + [anywhere] * len(given),
         out_specs=anywhere,
-        input_output_aliases={2: 0},
+        input_output_aliases={len(blocks): 0} if given else {},
+        scratch_shapes=[pltpu.SemaphoreType.DMA((len(blocks),))],
         compiler_params=pltpu.CompilerParams(vmem_limit_bytes=2 * 1024 * 1024),
-        scratch_shapes=[pltpu.SemaphoreType.DMA],
-    )(place, other, whole)
+    )(*blocks, *given)
 
 
 def along(block, pairs):
@@ -468,15 +477,17 @@
     far, d_left_here = lax.optimization_barrier((far, d_left_here))
     tile(3, middle, far)
     from_far = along(d_right[3], ENDS)
-    d_left_kept, d_left_sent = call(
-        last_left_kernel,
-        [(rows, cols, chans), (rows + 2, cols, chans)],
-        (place, rights[3], d_x[3], d_left_here, d_left_there, out_there[2], out_there[3]),
+    (d_left_sent,) = call(
+        last_sent_kernel,
+        [(rows + 2, cols, chans)],
+        (place, rights[3], d_x[3], d_left_there, out_there[2], out_there[3]),
     )
     to_middle, to_near, early_far, d_left_sent = lax.optimization_barrier(
         (d_right[3] + inward, d_right[1] + swapped, early_far, d_left_sent)
     )
     received = other_core(d_left_sent)
+    _, d_left_here = lax.optimization_barrier((d_left_sent, d_left_here))
+    (d_left_kept,) = call(last_kept_kernel, [(rows, cols, chans)], (place, rights[3], d_x[3], d_left_here))
     d_left, packed, rest = call(
         share_kernel,
         [kept, kept, (4, cols, chans)],
@@ -495,21 +506,29 @@
         (place, *outs, gate, cotangent, w_gate, d_left, d_left_other, open_left, slope_left, mine, other),
         scratch=[(half, cols, width)],
     )
-    d_mine, d_pair = call(
-        functools.partial(pair_kernel, rows),
-        [(half, cols, width), (rows, cols, width)],
-        (place, normed, scale, base, d_right[0], from_near, from_middle, from_far, open_right, slope_right, mine, other),
-    )
-    d_other = other_half(d_mine)
-    _, gate_late = lax.optimization_barrier((d_mine, gate))
+    cut = (5 * half) // 8
+    mine_parts, other_parts = [], []
+    for first, last in ((0, cut), (cut, half)):
+        (part,) = call(
+            functools.partial(pair_kernel, first),
+            [(last - first, cols, width)],
+            (place, normed, scale, base, d_right[0], from_near, from_middle, from_far, open_right, slope_right, mine, other),
+        )
+        mine_parts.append(part)
+        other_parts.append(other_half(part))
+    _, gate_late = lax.optimization_barrier((mine_parts[1], gate))
     (update,) = call(
         functools.partial(update_kernel, rows),
         [(rows, cols, width)],
         (place, *outs, gate_late),
         scratch=[(rows, cols, width)],
     )
-    d_other, update = lax.optimization_barrier((d_other, update))
-    d_pair = join(place, d_other, d_pair)
+    firsts = (0, cut)
+    d_pair = join(mine_parts, firsts, (True, True), pair.shape)
+    other_parts[0], update, d_pair = lax.optimization_barrier((other_parts[0], update, d_pair))
+    d_pair = join(other_parts[:1], firsts[:1], (False,), pair.shape, d_pair)
+    other_parts[1], d_pair = lax.optimization_barrier((other_parts[1], d_pair))
+    d_pair = join(other_parts[1:], firsts[1:], (False,), pair.shape, d_pair)
     return (update, d_pair)
 
 

time: 106 us -> 104 us (0.981)
  waiting for transfers between devices: 39.6 us -> 35.8 us
  Pallas kernels: 38.2 us -> 39.4 us
    ppermute x6 -> x7, waiting for transfers between devices: 18 us -> 15 us  [other_half(): return lax.ppermute(block, 'ch', [(0, 1), (1, 0)])]
    pallas_call x1 -> x3, Pallas kernels: 1.35 us -> 2.22 us  [join(): pl.pallas_call(functools.partial(join_kernel, firsts, sides), out_shape=j...]
    ppermute x6 -> x7, starting transfers between devices: 9.27 us -> 9.88 us  [other_half(): return lax.ppermute(block, 'ch', [(0, 1), (1, 0)])]
    pallas_call x15 -> x17, Pallas kernels: 36.9 us -> 37.2 us  [call(): pl.pallas_call(kernel, out_shape=[jax.ShapeDtypeStruct(shape, F32) for sh...]
  transfers between devices with their start and end apart: 21 -> 22, of which waited for: 9 -> 10; matrix products, arithmetic and copies ran while one was open for 0% -> 0% of each run, Pallas kernels for 33% -> 36%
where the time goes in v5:
time: 104 us
  Pallas kernels  39.4 us (38%)
  waiting for transfers between devices  35.8 us (34%)
  starting transfers between devices  27 us (26%)
    pallas_call x17, Pallas kernels, call(): pl.pallas_call(kernel, out_shape=[jax.ShapeDtypeStruct(shape, F32) for sh...  37.2 us
    ppermute x10, waiting for transfers between devices, along(): lax.ppermute(block, 'row', [(2 * a + core, 2 * b + core) for a, b in pair...  19.2 us
    ppermute x10, starting transfers between devices, along(): lax.ppermute(block, 'row', [(2 * a + core, 2 * b + core) for a, b in pair...  16.3 us
    ppermute x7, waiting for transfers between devices, other_half(): return lax.ppermute(block, 'ch', [(0, 1), (1, 0)])  15 us
    ppermute x7, starting transfers between devices, other_half(): return lax.ppermute(block, 'ch', [(0, 1), (1, 0)])  9.88 us
    pallas_call x3, Pallas kernels, join(): pl.pallas_call(functools.partial(join_kernel, firsts, sides), out_shape=j...  2.22 us
  transfers between devices with their start and end apart: 22, of which 10 were waited for; matrix products, arithmetic and copies ran while one was open for 0% of the time, Pallas kernels for 36%

profile of v5, /device:TPU:0, one launch (start us, length us, event | category | flops | bytes accessed | tf_op | source)
XLA Modules:
  0.0 103.5 jit_solution(4289810977323776907)
XLA Ops:
  0.6 3.0 %collective-permute-start = (f32[256,128]{1,0:T(8,128)}, f32[256,128]{1,0:T(8,128)S(1)}, u32[]{:S(2)}, u32[]{:S(2)}) collective-permute-start(f32[256,128]{1,0:T(8,128)} %bitcast.24), channel_id=1, source_target_pairs={{0,1},{1,0},{2,3},{3,2},{4,5},{5,4},{6,7},{7,6},{8,9},{9,8},{10,11... | collective-permute-start | bytes 393224 | tf_op jit(solution)/shard_map/ppermute | solution.py:391
  3.6 0.1 collective-permute-start.1
  3.7 0.1 pad_add_fusion.place
  3.8 2.2 %shard_map.77 = (f32[8,128,128]{2,1,0:T(8,128)S(1)}, f32[8,128,128]{2,1,0:T(8,128)S(1)}, f32[16,128]{1,0:T(8,128)S(1)}, f32[4,64,128]{2,1,0:T(8,128)S(1)}, f32[8...) custom-call(s32[3]{0:T(128)S(1)} %pad_add_fusion.place, f32[16,128,128]{2,1,0:T(8,128)} %pair.3, s32[16,128]{1,0:T(8,128)} %mask.1, ...), custom_call_target="tpu_custom_call" | custom-call | flops 1000 | bytes 1000 | tf_op jit(solution)/shard_map/pallas_call | solution.py:53
  6.0 0.0 copy-start
  6.0 0.0 copy-start.1
  6.0 0.0 copy-start.2
  6.0 0.1 collective-permute-start.2
  6.1 0.5 collective-permute-start.3
  6.6 1.4 %collective-permute-done.1.other_out = f32[64,128]{1,0:T(8,128)S(1)} collective-permute-done((f32[64,128]{1,0:T(8,128)}, f32[64,128]{1,0:T(8,128)S(1)}, u32[]{:S(2)}, u32[]{:S(2)}) %collective-permute-start.1) | collective-permute-done | bytes 32800 | tf_op jit(solution)/shard_map/ppermute | solution.py:391
  8.0 1.2 %shard_map.78 = (f32[8,128,128]{2,1,0:T(8,128)S(1)}, f32[8,128,128]{2,1,0:T(8,128)S(1)}, f32[8,128,128]{2,1,0:T(8,128)S(1)}) custom-call(s32[3]{0:T(128)S(1)} %pad_add_fusion.place, f32[8,128,128]{2,1,0:T(8,128)S(1)} %get-tuple-element.69.normed, f32[16,128]{1,0:T(8,128)S(1)} %get-tuple-element.71.keep, f32[4,64,128]{2,1,0:T(8,128)S(1)} %get-tuple-element.72.mine.refs_15_, ...), custom_call_target="tpu_custom_call" | custom-call | flops 1000 | bytes 1000 | tf_op jit(solution)/shard_map/pallas_call | solution.py:53
  9.3 1.9 %collective-permute-start.5 = (f32[8,128,128]{2,1,0:T(8,128)S(1)}, f32[8,128,128]{2,1,0:T(8,128)S(1)}, u32[]{:S(2)}, u32[]{:S(2)}) collective-permute-start(f32[8,128,128]{2,1,0:T(8,128)S(1)} %get-tuple-element.74.refs_0_), channel_id=1, source_target_pairs={{0,4},{2,6},{4,0},{6,2},{8,12},{10,14},{12,8},{14,10},{1,5},{3,7},... | collective-permute-start | bytes 1572872 | tf_op jit(solution)/shard_map/ppermute | solution.py:383
  11.1 0.7 collective-permute-start.8
  11.8 1.5 %shard_map.79 = f32[5,16,8,128]{3,2,1,0:T(8,128)S(1)} custom-call(s32[3]{0:T(128)S(1)} %pad_add_fusion.place, f32[16,128,128]{2,1,0:T(8,128)} %refs_9_.1, f32[16,128]{1,0:T(8,128)S(1)} %get-tuple-element.71.keep), custom_call_target="tpu_custom_call" | custom-call | flops 1000 | bytes 1000 | tf_op jit(solution)/shard_map/pallas_call | solution.py:53
  13.3 0.1 collective-permute-start.4
  13.4 1.6 %collective-permute-done.4.third = f32[5,16,8,128]{3,2,1,0:T(8,128)S(1)} collective-permute-done((f32[5,16,8,128]{3,2,1,0:T(8,128)S(1)}, f32[5,16,8,128]{3,2,1,0:T(8,128)S(1)}, u32[]{:S(2)}, u32[]{:S(2)}) %collective-permute-start.4) | collective-permute-done | bytes 327712 | tf_op jit(solution)/shard_map/ppermute | solution.py:387
  15.0 0.0 collective-permute-done.2.first
  15.0 0.0 collective-permute-done.3.second
  15.1 3.8 %shard_map.80 = (f32[16,128,128]{2,1,0:T(8,128)S(1)}, f32[16,128,128]{2,1,0:T(8,128)S(1)}, f32[8,128,128]{2,1,0:T(8,128)S(1)}, f32[8,128,128]{2,1,0:T(8,128)S(1)...) custom-call(s32[3]{0:T(128)S(1)} %pad_add_fusion.place, ...), custom_call_target="tpu_custom_call" | custom-call | flops 1000 | bytes 1000 | tf_op jit(solution)/shard_map/pallas_call | solution.py:53
  18.9 3.5 %collective-permute-done.5.refs_0_.refs_1_ = f32[8,128,128]{2,1,0:T(8,128)S(1)} collective-permute-done((f32[8,128,128]{2,1,0:T(8,128)S(1)}, f32[8,128,128]{2,1,0:T(8,128)S(1)}, u32[]{:S(2)}, u32[]{:S(2)}) %collective-permute-start.5) | collective-permute-done | bytes 524320 | tf_op jit(solution)/shard_map/ppermute | solution.py:383
  22.4 0.7 collective-permute-start.6
  23.1 0.0 collective-permute-done.8.refs_0_
  23.1 1.3 %collective-permute-start.9 = (f32[8,128,128]{2,1,0:T(8,128)S(1)}, f32[8,128,128]{2,1,0:T(8,128)S(1)}, u32[]{:S(2)}, u32[]{:S(2)}) collective-permute-start(f32[8,128,128]{2,1,0:T(8,128)S(1)} %collective-permute-done.8.refs_0_), channel_id=1, source_target_pairs={{4,0},{6,2},{8,12},{10,14},{5,1},{7,3},{9,13},{11,15},{20,16},{22,... | collective-permute-start | bytes 1572872 | tf_op jit(solution)/shard_map/ppermute | solution.py:383
  24.4 3.8 %shard_map.81 = (f32[16,8,128]{2,1,0:T(8,128)S(1)}, f32[16,8,128]{2,1,0:T(8,128)S(1)}, f32[256,128]{1,0:T(8,128)S(1)}, f32[8,128,128]{2,1,0:T(8,128)S(1)}) custom-call(s32[3]{0:T(128)S(1)} %pad_add_fusion.place, f32[8,128,128]{2,1,0:T(8,128)S(1)} %get-tuple-element.74.refs_0_, f32[16,128,128]{2,1,0:T(8,128)S(1)} %get-tuple-element.79.refs_1_.refs_2_, ...), custom_call_target="tpu_custom_call" | custom-call | flops 1000 | bytes 1000 | tf_op jit(solution)/shard_map/pallas_call | solution.py:53
  28.2 3.8 %shard_map.82 = (f32[16,8,128]{2,1,0:T(8,128)S(1)}, f32[16,8,128]{2,1,0:T(8,128)S(1)}, f32[256,128]{1,0:T(8,128)S(1)}, f32[8,128,128]{2,1,0:T(8,128)S(1)}) custom-call(s32[3]{0:T(128)S(1)} %pad_add_fusion.place, f32[8,128,128]{2,1,0:T(8,128)S(1)} %collective-permute-done.5.refs_0_.refs_1_, f32[16,128,128]{2,1,0:T(8,128)S(1)} %get-tuple-element.79.refs_1_.refs_2_, ...), custom_call_target="tpu_custom_call" | custom-call | flops 1000 | bytes 1000 | tf_op jit(solution)/shard_map/pallas_call | solution.py:53
  32.0 0.1 collective-permute-start.7
  32.1 2.9 %shard_map.83 = (f32[16,128,128]{2,1,0:T(8,128)S(1)}, f32[16,128,128]{2,1,0:T(8,128)S(1)}) custom-call(s32[3]{0:T(128)S(1)} %pad_add_fusion.place, f32[8,128,128]{2,1,0:T(8,128)S(1)} %get-tuple-element.74.refs_0_, f32[8,128,128]{2,1,0:T(8,128)S(1)} %collective-permute-done.5.refs_0_.refs_1_, f32[256,128]{1,0:T(8,128)S(1)} %get-tuple-element.90.refs_2_, ...), custom_call_target="tpu_custom_call" | custom-call | flops 1000 | bytes 1000 | tf_op jit(solution)/shard_map/pallas_call | solution.py:53
  35.0 0.0 collective-permute-done.7.refs_4_
  35.0 0.0 collective-permute-done.6.refs_0_
  35.0 1.3 %collective-permute-start.10 = (f32[8,128,128]{2,1,0:T(8,128)S(1)}, f32[8,128,128]{2,1,0:T(8,128)S(1)}, u32[]{:S(2)}, u32[]{:S(2)}) collective-permute-start(f32[8,128,128]{2,1,0:T(8,128)S(1)} %collective-permute-done.6.refs_0_), channel_id=1, source_target_pairs={{4,0},{6,2},{8,12},{10,14},{5,1},{7,3},{9,13},{11,15},{20,16},{22,... | collective-permute-start | bytes 1572872 | tf_op jit(solution)/shard_map/ppermute | solution.py:383
  36.3 2.4 %collective-permute-done.9.refs_1_ = f32[8,128,128]{2,1,0:T(8,128)S(1)} collective-permute-done((f32[8,128,128]{2,1,0:T(8,128)S(1)}, f32[8,128,128]{2,1,0:T(8,128)S(1)}, u32[]{:S(2)}, u32[]{:S(2)}) %collective-permute-start.9) | collective-permute-done | bytes 524320 | tf_op jit(solution)/shard_map/ppermute | solution.py:383
  38.7 3.8 %shard_map.84 = (f32[16,8,128]{2,1,0:T(8,128)S(1)}, f32[16,8,128]{2,1,0:T(8,128)S(1)}, f32[256,128]{1,0:T(8,128)S(1)}, f32[8,128,128]{2,1,0:T(8,128)S(1)}, f32[8,128,128]{2,1,0:T(8,128)S(1)}) custom-call(s32[3]{0:T(128)S(1)} %pad_add_fusion.place, f32[8,128,128]{2,1,0:T(8,128)S(1)} %collective-permute-done.6.refs_0_, ...), custom_call_target="tpu_custom_call" | custom-call | flops 1000 | bytes 1000 | tf_op jit(solution)/shard_map/pallas_call | solution.py:53
  42.6 3.9 %collective-permute-start.11 = (f32[8,128,128]{2,1,0:T(8,128)S(1)}, f32[8,128,128]{2,1,0:T(8,128)S(1)}, u32[]{:S(2)}, u32[]{:S(2)}) collective-permute-start(f32[8,128,128]{2,1,0:T(8,128)S(1)} %get-tuple-element.104), channel_id=1, source_target_pairs={{0,4},{2,6},{12,8},{14,10},{1,5},{3,7},{13,9},{15,11},{16,20},{18,... | collective-permute-start | bytes 1572872 | tf_op jit(solution)/shard_map/ppermute | solution.py:383
  46.5 0.7 collective-permute-start.12
  47.2 1.6 %collective-permute-start.13 = (f32[2,2,16,8,128]{4,3,2,1,0:T(8,128)S(1)}, f32[2,2,16,8,128]{4,3,2,1,0:T(8,128)S(1)}, u32[]{:S(2)}, u32[]{:S(2)}) collective-permute-start(f32[2,2,16,8,128]{4,3,2,1,0:T(8,128)S(1)} %pad_maximum_fusion), channel_id=1, source_target_pairs={{0,1},{1,0},{2,3},{3,2},{4,5},{5,4},{6,7},{7,6},{8,9},{9,8},{10,11... | collective-permute-start | bytes 786440 | tf_op jit(solution)/shard_map/ppermute | solution.py:391
  48.8 1.9 %shard_map.85 = (f32[16,128,128]{2,1,0:T(8,128)S(1)}, f32[16,128,128]{2,1,0:T(8,128)S(1)}) custom-call(s32[3]{0:T(128)S(1)} %pad_add_fusion.place, f32[8,128,128]{2,1,0:T(8,128)S(1)} %get-tuple-element.95.refs_0_, f32[256,128]{1,0:T(8,128)S(1)} %get-tuple-element.96.refs_1_, f32[16,128,128]{2,1,0:T(8,128)S(1)} %get-tuple-element.97.refs_2_, ...), custom_call_target="tpu_custom_call" | custom-call | flops 1000 | bytes 1000 | tf_op jit(solution)/shard_map/pallas_call | solution.py:53
  50.7 2.5 %collective-permute-done.10.refs_1_ = f32[8,128,128]{2,1,0:T(8,128)S(1)} collective-permute-done((f32[8,128,128]{2,1,0:T(8,128)S(1)}, f32[8,128,128]{2,1,0:T(8,128)S(1)}, u32[]{:S(2)}, u32[]{:S(2)}) %collective-permute-start.10) | collective-permute-done | bytes 524320 | tf_op jit(solution)/shard_map/ppermute | solution.py:383
  53.2 3.8 %shard_map.86 = (f32[16,8,128]{2,1,0:T(8,128)S(1)}, f32[16,8,128]{2,1,0:T(8,128)S(1)}, f32[256,128]{1,0:T(8,128)S(1)}, f32[8,128,128]{2,1,0:T(8,128)S(1)}, f32[8,128,128]{2,1,0:T(8,128)S(1)}) custom-call(s32[3]{0:T(128)S(1)} %pad_add_fusion.place, f32[8,128,128]{2,1,0:T(8,128)S(1)} %collective-permute-done.8.refs_0_, ...), custom_call_target="tpu_custom_call" | custom-call | flops 1000 | bytes 1000 | tf_op jit(solution)/shard_map/pallas_call | solution.py:53
  57.0 1.2 %shard_map.87 = f32[18,128,128]{2,1,0:T(8,128)S(1)} custom-call(s32[3]{0:T(128)S(1)} %pad_add_fusion.place, f32[8,128,128]{2,1,0:T(8,128)S(1)} %get-tuple-element.106.right, f32[256,128]{1,0:T(8,128)S(1)} %get-tuple-element.107.d_x, f32[16,128,128]{2,1,0:T(8,128)S(1)} %get-tuple-element.108.there, f32[16,8,128]{2,1,0:T(8,128)S(1)} %get-tuple-element.109.out_next, ...), custom_call_target="tpu_custom_call" | custom-call | flops 1000 | bytes 1000 | tf_op jit(solution)/shard_map/pallas_call | solution.py:53
  58.3 0.0 collective-permute-done.11
  58.3 0.1 add.12
  58.4 0.1 add.13
  58.5 0.1 collective-permute-start.14
  58.6 4.5 %collective-permute-start.15 = (f32[8,128,128]{2,1,0:T(8,128)S(1)}, f32[8,128,128]{2,1,0:T(8,128)S(1)}, u32[]{:S(2)}, u32[]{:S(2)}) collective-permute-start(f32[8,128,128]{2,1,0:T(8,128)S(1)} %get-tuple-element.103), channel_id=1, source_target_pairs={{0,12},{2,14},{12,0},{14,2},{1,13},{3,15},{13,1},{15,3},{16,28},{1... | collective-permute-start | bytes 1572872 | tf_op jit(solution)/shard_map/ppermute | solution.py:383
  63.0 1.2 %shard_map.88.kept = f32[16,128,128]{2,1,0:T(8,128)S(1)} custom-call(s32[3]{0:T(128)S(1)} %pad_add_fusion.place, f32[8,128,128]{2,1,0:T(8,128)S(1)} %get-tuple-element.106.right, f32[256,128]{1,0:T(8,128)S(1)} %get-tuple-element.107.d_x, f32[16,128,128]{2,1,0:T(8,128)S(1)} %get-tuple-element.114.here), custom_call_target="tpu_custom_call" | custom-call | flops 1000 | bytes 1000 | tf_op jit(solution)/shard_map/pallas_call | solution.py:53
  64.3 0.7 shard_map.89
  64.9 1.6 %collective-permute-start.17 = (f32[8,128,128]{2,1,0:T(8,128)S(1)}, f32[8,128,128]{2,1,0:T(8,128)S(1)}, u32[]{:S(2)}, u32[]{:S(2)}) collective-permute-start(f32[8,128,128]{2,1,0:T(8,128)S(1)} %get-tuple-element.119), channel_id=1, source_target_pairs={{0,1},{1,0},{2,3},{3,2},{4,5},{5,4},{6,7},{7,6},{8,9},{9,8},{10,11... | collective-permute-start | bytes 1572872 | tf_op jit(solution)/shard_map/ppermute | solution.py:391
  66.5 0.8 collective-permute-start.18
  67.3 0.7 collective-permute-start.19
  68.0 9.1 %collective-permute-done.15.d_right_far = f32[8,128,128]{2,1,0:T(8,128)S(1)} collective-permute-done((f32[8,128,128]{2,1,0:T(8,128)S(1)}, f32[8,128,128]{2,1,0:T(8,128)S(1)}, u32[]{:S(2)}, u32[]{:S(2)}) %collective-permute-start.15) | collective-permute-done | bytes 524320 | tf_op jit(solution)/shard_map/ppermute | solution.py:383
  77.0 1.5 %collective-permute-start.16 = (f32[4,128,128]{2,1,0:T(8,128)S(1)}, f32[4,128,128]{2,1,0:T(8,128)S(1)}, u32[]{:S(2)}, u32[]{:S(2)}) collective-permute-start(f32[4,128,128]{2,1,0:T(8,128)S(1)} %get-tuple-element.116), channel_id=1, source_target_pairs={{0,1},{1,0},{2,3},{3,2},{4,5},{5,4},{6,7},{7,6},{8,9},{9,8},{10,11... | collective-permute-start | bytes 786440 | tf_op jit(solution)/shard_map/ppermute | solution.py:391
  78.6 6.1 %collective-permute-done.16.refs_7_ = f32[4,128,128]{2,1,0:T(8,128)S(1)} collective-permute-done((f32[4,128,128]{2,1,0:T(8,128)S(1)}, f32[4,128,128]{2,1,0:T(8,128)S(1)}, u32[]{:S(2)}, u32[]{:S(2)}) %collective-permute-start.16) | collective-permute-done | bytes 262176 | tf_op jit(solution)/shard_map/ppermute | solution.py:391
  84.7 1.4 %shard_map.90.base = f32[8,128,128]{2,1,0:T(8,128)S(1)} custom-call(s32[3]{0:T(128)S(1)} %pad_add_fusion.place, f32[16,8,128]{2,1,0:T(8,128)S(1)} %get-tuple-element.85.refs_0_, f32[16,8,128]{2,1,0:T(8,128)S(1)} %get-tuple-element.87.refs_1_, f32[16,8,128]{2,1,0:T(8,128)S(1)} %get-tuple-element.94.out_next.refs_2_, ...), custom_call_target="tpu_custom_call" | custom-call | flops 1000 | bytes 1000 | tf_op jit(solution)/shard_map/pallas_call | solution.py:53
  86.1 1.7 %collective-permute-done.18.d_right_near = f32[8,128,128]{2,1,0:T(8,128)S(1)} collective-permute-done((f32[8,128,128]{2,1,0:T(8,128)S(1)}, f32[8,128,128]{2,1,0:T(8,128)S(1)}, u32[]{:S(2)}, u32[]{:S(2)}) %collective-permute-start.18) | collective-permute-done | bytes 524320 | tf_op jit(solution)/shard_map/ppermute | solution.py:383
  87.8 1.1 %shard_map.91.refs_0_ = f32[5,128,128]{2,1,0:T(8,128)S(1)} custom-call(s32[3]{0:T(128)S(1)} %pad_add_fusion.place, f32[8,128,128]{2,1,0:T(8,128)S(1)} %get-tuple-element.69.normed, f32[8,128,128]{2,1,0:T(8,128)S(1)} %get-tuple-element.70.scale, f32[8,128,128]{2,1,0:T(8,128)S(1)} %shard_map.90.base, f32[8,128,128]{2,1,0:T(8,128)S(1)} %get-tuple-element.122.d_right, ...), custom_call_target="tpu_custom_call" | custom-call | flops 1000 | bytes 1000 | tf_op jit(solution)/shard_map/pallas_call | solution.py:53
  88.9 1.6 %collective-permute-start.20 = (f32[5,128,128]{2,1,0:T(8,128)S(1)}, f32[5,128,128]{2,1,0:T(8,128)S(1)}, u32[]{:S(2)}, u32[]{:S(2)}) collective-permute-start(f32[5,128,128]{2,1,0:T(8,128)S(1)} %shard_map.91.refs_0_), channel_id=1, source_target_pairs={{0,1},{1,0},{2,3},{3,2},{4,5},{5,4},{6,7},{7,6},{8,9},{9,8},{10,11... | collective-permute-start | bytes 983048 | tf_op jit(solution)/shard_map/ppermute | solution.py:391
  90.5 1.0 shard_map.92.refs_1_
  91.5 0.6 collective-permute-start.21
  92.1 1.8 %shard_map.93 = f32[16,128,128]{2,1,0:T(8,128)} custom-call(s32[3]{0:T(128)S(1)} %pad_add_fusion.place, f32[16,8,128]{2,1,0:T(8,128)S(1)} %get-tuple-element.85.refs_0_, f32[16,8,128]{2,1,0:T(8,128)S(1)} %get-tuple-element.87.refs_1_, f32[16,8,128]{2,1,0:T(8,128)S(1)} %get-tuple-element.94.out_next.refs_2_, ...), custom_call_target="tpu_custom_call" | custom-call | flops 1000 | bytes 1000 | tf_op jit(solution)/shard_map/pallas_call | solution.py:53
  93.8 0.8 shard_map.94.refs_1_
  94.7 4.9 %collective-permute-done.20.refs_0_ = f32[5,128,128]{2,1,0:T(8,128)S(1)} collective-permute-done((f32[5,128,128]{2,1,0:T(8,128)S(1)}, f32[5,128,128]{2,1,0:T(8,128)S(1)}, u32[]{:S(2)}, u32[]{:S(2)}) %collective-permute-start.20) | collective-permute-done | bytes 327712 | tf_op jit(solution)/shard_map/ppermute | solution.py:391
  99.6 0.7 shard_map.95.refs_1_
  100.3 2.5 %collective-permute-done.21.refs_0_ = f32[3,128,128]{2,1,0:T(8,128)S(1)} collective-permute-done((f32[3,128,128]{2,1,0:T(8,128)S(1)}, f32[3,128,128]{2,1,0:T(8,128)S(1)}, u32[]{:S(2)}, u32[]{:S(2)}) %collective-permute-start.21) | collective-permute-done | bytes 196640 | tf_op jit(solution)/shard_map/ppermute | solution.py:391
  102.8 0.7 shard_map.96
  (14 shorter events, 0.1 us)
Async XLA Ops:
  0.6 7.4 %collective-permute-start = (f32[256,128]{1,0:T(8,128)}, f32[256,128]{1,0:T(8,128)S(1)}, u32[]{:S(2)}, u32[]{:S(2)}) collective-permute-start(f32[256,128]{1,0:T(8,128)} %bitcast.24), channel_id=1, source_target_pairs={{0,1},{1,0},{2,3},{3,2},{4,5},{5,4},{6,7},{7,6},{8,9},{9,8},{10,11... | collective-permute-start | bytes 393224 | tf_op jit(solution)/shard_map/ppermute | solution.py:391
  3.6 4.4 %collective-permute-start.1 = (f32[64,128]{1,0:T(8,128)}, f32[64,128]{1,0:T(8,128)S(1)}, u32[]{:S(2)}, u32[]{:S(2)}) collective-permute-start(f32[64,128]{1,0:T(8,128)} %mine_out.1), channel_id=1, source_target_pairs={{0,1},{1,0},{2,3},{3,2},{4,5},{5,4},{6,7},{7,6},{8,9},{9,8},{10,11... | collective-permute-start | bytes 98312 | tf_op jit(solution)/shard_map/ppermute | solution.py:391
  3.8 11.3 %copy-start.3 = (f32[64,128]{1,0:T(8,128)S(1)}, f32[64,128]{1,0:T(8,128)}, u32[]{:S(2)}) copy-start(f32[64,128]{1,0:T(8,128)} %mine_out.1) | copy-start | bytes 98308
  6.0 9.1 %copy-start = (f32[16,128,128]{2,1,0:T(8,128)S(1)}, f32[16,128,128]{2,1,0:T(8,128)}, u32[]{:S(2)}) copy-start(f32[16,128,128]{2,1,0:T(8,128)} %refs_9_.1) | copy-start | bytes 3145732
  6.0 9.1 %copy-start.1 = (f32[16,128,128]{2,1,0:T(8,128)S(1)}, f32[16,128,128]{2,1,0:T(8,128)}, u32[]{:S(2)}) copy-start(f32[16,128,128]{2,1,0:T(8,128)} %pair.3) | copy-start | bytes 3145732
  6.0 9.1 %copy-start.2 = (f32[128,128]{1,0:T(8,128)S(1)}, f32[128,128]{1,0:T(8,128)}, u32[]{:S(2)}) copy-start(f32[128,128]{1,0:T(8,128)} %refs_10_.1) | copy-start | bytes 196612
  6.0 9.0 %collective-permute-start.2 = (f32[8,128,128]{2,1,0:T(8,128)S(1)}, f32[8,128,128]{2,1,0:T(8,128)S(1)}, u32[]{:S(2)}, u32[]{:S(2)}) collective-permute-start(f32[8,128,128]{2,1,0:T(8,128)S(1)} %get-tuple-element.75), channel_id=1, source_target_pairs={{0,2},{2,0},{4,6},{6,4},{8,10},{10,8},{12,14},{14,12},{1,3},{3,1},... | collective-permute-start | bytes 1572872 | tf_op jit(solution)/shard_map/ppermute | solution.py:387
  6.1 8.9 %collective-permute-start.3 = (f32[8,128,128]{2,1,0:T(8,128)S(1)}, f32[8,128,128]{2,1,0:T(8,128)S(1)}, u32[]{:S(2)}, u32[]{:S(2)}) collective-permute-start(f32[8,128,128]{2,1,0:T(8,128)S(1)} %get-tuple-element.76), channel_id=1, source_target_pairs={{0,2},{2,0},{4,6},{6,4},{8,10},{10,8},{12,14},{14,12},{1,3},{3,1},... | collective-permute-start | bytes 1572872 | tf_op jit(solution)/shard_map/ppermute | solution.py:387
  9.3 13.2 %collective-permute-start.5 = (f32[8,128,128]{2,1,0:T(8,128)S(1)}, f32[8,128,128]{2,1,0:T(8,128)S(1)}, u32[]{:S(2)}, u32[]{:S(2)}) collective-permute-start(f32[8,128,128]{2,1,0:T(8,128)S(1)} %get-tuple-element.74.refs_0_), channel_id=1, source_target_pairs={{0,4},{2,6},{4,0},{6,2},{8,12},{10,14},{12,8},{14,10},{1,5},{3,7},... | collective-permute-start | bytes 1572872 | tf_op jit(solution)/shard_map/ppermute | solution.py:383
  11.1 12.0 %collective-permute-start.8 = (f32[8,128,128]{2,1,0:T(8,128)S(1)}, f32[8,128,128]{2,1,0:T(8,128)S(1)}, u32[]{:S(2)}, u32[]{:S(2)}) collective-permute-start(f32[8,128,128]{2,1,0:T(8,128)S(1)} %get-tuple-element.74.refs_0_), channel_id=1, source_target_pairs={{4,8},{6,10},{8,4},{10,6},{5,9},{7,11},{9,5},{11,7},{20,24},{22,26... | collective-permute-start | bytes 1572872 | tf_op jit(solution)/shard_map/ppermute | solution.py:383
  13.3 1.7 %collective-permute-start.4 = (f32[5,16,8,128]{3,2,1,0:T(8,128)S(1)}, f32[5,16,8,128]{3,2,1,0:T(8,128)S(1)}, u32[]{:S(2)}, u32[]{:S(2)}) collective-permute-start(f32[5,16,8,128]{3,2,1,0:T(8,128)S(1)} %shard_map.79), channel_id=1, source_target_pairs={{0,2},{2,0},{4,6},{6,4},{8,10},{10,8},{12,14},{14,12},{1,3},{3,1},... | collective-permute-start | bytes 983048 | tf_op jit(solution)/shard_map/ppermute | solution.py:387
  22.4 12.6 %collective-permute-start.6 = (f32[8,128,128]{2,1,0:T(8,128)S(1)}, f32[8,128,128]{2,1,0:T(8,128)S(1)}, u32[]{:S(2)}, u32[]{:S(2)}) collective-permute-start(f32[8,128,128]{2,1,0:T(8,128)S(1)} %collective-permute-done.5.refs_0_.refs_1_), channel_id=1, source_target_pairs={{4,8},{6,10},{8,4},{10,6},{5,9},{7,11},{9,5},{11,7},{20,24},{22,26... | collective-permute-start | bytes 1572872 | tf_op jit(solution)/shard_map/ppermute | solution.py:383
  23.1 15.6 %collective-permute-start.9 = (f32[8,128,128]{2,1,0:T(8,128)S(1)}, f32[8,128,128]{2,1,0:T(8,128)S(1)}, u32[]{:S(2)}, u32[]{:S(2)}) collective-permute-start(f32[8,128,128]{2,1,0:T(8,128)S(1)} %collective-permute-done.8.refs_0_), channel_id=1, source_target_pairs={{4,0},{6,2},{8,12},{10,14},{5,1},{7,3},{9,13},{11,15},{20,16},{22,... | collective-permute-start | bytes 1572872 | tf_op jit(solution)/shard_map/ppermute | solution.py:383
  32.0 3.0 %collective-permute-start.7 = (f32[2,16,8,128]{3,2,1,0:T(8,128)S(1)}, f32[2,16,8,128]{3,2,1,0:T(8,128)S(1)}, u32[]{:S(2)}, u32[]{:S(2)}) collective-permute-start(f32[2,16,8,128]{3,2,1,0:T(8,128)S(1)} %pad_maximum_fusion.1), channel_id=1, source_target_pairs={{0,2},{2,0},{4,6},{6,4},{8,10},{10,8},{12,14},{14,12},{1,3},{3,1},... | collective-permute-start | bytes 393224 | tf_op jit(solution)/shard_map/ppermute | solution.py:387
  35.0 18.2 %collective-permute-start.10 = (f32[8,128,128]{2,1,0:T(8,128)S(1)}, f32[8,128,128]{2,1,0:T(8,128)S(1)}, u32[]{:S(2)}, u32[]{:S(2)}) collective-permute-start(f32[8,128,128]{2,1,0:T(8,128)S(1)} %collective-permute-done.6.refs_0_), channel_id=1, source_target_pairs={{4,0},{6,2},{8,12},{10,14},{5,1},{7,3},{9,13},{11,15},{20,16},{22,... | collective-permute-start | bytes 1572872 | tf_op jit(solution)/shard_map/ppermute | solution.py:383
  42.6 15.7 %collective-permute-start.11 = (f32[8,128,128]{2,1,0:T(8,128)S(1)}, f32[8,128,128]{2,1,0:T(8,128)S(1)}, u32[]{:S(2)}, u32[]{:S(2)}) collective-permute-start(f32[8,128,128]{2,1,0:T(8,128)S(1)} %get-tuple-element.104), channel_id=1, source_target_pairs={{0,4},{2,6},{12,8},{14,10},{1,5},{3,7},{13,9},{15,11},{16,20},{18,... | collective-permute-start | bytes 1572872 | tf_op jit(solution)/shard_map/ppermute | solution.py:383
  46.5 11.9 %collective-permute-start.12 = (f32[8,128,128]{2,1,0:T(8,128)S(1)}, f32[8,128,128]{2,1,0:T(8,128)S(1)}, u32[]{:S(2)}, u32[]{:S(2)}) collective-permute-start(f32[8,128,128]{2,1,0:T(8,128)S(1)} %get-tuple-element.104), channel_id=1, source_target_pairs={{4,8},{6,10},{8,4},{10,6},{5,9},{7,11},{9,5},{11,7},{20,24},{22,26... | collective-permute-start | bytes 1572872 | tf_op jit(solution)/shard_map/ppermute | solution.py:383
  47.2 11.3 %collective-permute-start.13 = (f32[2,2,16,8,128]{4,3,2,1,0:T(8,128)S(1)}, f32[2,2,16,8,128]{4,3,2,1,0:T(8,128)S(1)}, u32[]{:S(2)}, u32[]{:S(2)}) collective-permute-start(f32[2,2,16,8,128]{4,3,2,1,0:T(8,128)S(1)} %pad_maximum_fusion), channel_id=1, source_target_pairs={{0,1},{1,0},{2,3},{3,2},{4,5},{5,4},{6,7},{7,6},{8,9},{9,8},{10,11... | collective-permute-start | bytes 786440 | tf_op jit(solution)/shard_map/ppermute | solution.py:391
  58.5 5.8 %collective-permute-start.14 = (f32[18,128,128]{2,1,0:T(8,128)S(1)}, f32[18,128,128]{2,1,0:T(8,128)S(1)}, u32[]{:S(2)}, u32[]{:S(2)}) collective-permute-start(f32[18,128,128]{2,1,0:T(8,128)S(1)} %shard_map.87), channel_id=1, source_target_pairs={{0,2},{2,0},{4,6},{6,4},{8,10},{10,8},{12,14},{14,12},{1,3},{3,1},... | collective-permute-start | bytes 3538952 | tf_op jit(solution)/shard_map/ppermute | solution.py:387
  58.6 18.5 %collective-permute-start.15 = (f32[8,128,128]{2,1,0:T(8,128)S(1)}, f32[8,128,128]{2,1,0:T(8,128)S(1)}, u32[]{:S(2)}, u32[]{:S(2)}) collective-permute-start(f32[8,128,128]{2,1,0:T(8,128)S(1)} %get-tuple-element.103), channel_id=1, source_target_pairs={{0,12},{2,14},{12,0},{14,2},{1,13},{3,15},{13,1},{15,3},{16,28},{1... | collective-permute-start | bytes 1572872 | tf_op jit(solution)/shard_map/ppermute | solution.py:383
  64.9 19.7 %collective-permute-start.17 = (f32[8,128,128]{2,1,0:T(8,128)S(1)}, f32[8,128,128]{2,1,0:T(8,128)S(1)}, u32[]{:S(2)}, u32[]{:S(2)}) collective-permute-start(f32[8,128,128]{2,1,0:T(8,128)S(1)} %get-tuple-element.119), channel_id=1, source_target_pairs={{0,1},{1,0},{2,3},{3,2},{4,5},{5,4},{6,7},{7,6},{8,9},{9,8},{10,11... | collective-permute-start | bytes 1572872 | tf_op jit(solution)/shard_map/ppermute | solution.py:391
  66.5 21.3 %collective-permute-start.18 = (f32[8,128,128]{2,1,0:T(8,128)S(1)}, f32[8,128,128]{2,1,0:T(8,128)S(1)}, u32[]{:S(2)}, u32[]{:S(2)}) collective-permute-start(f32[8,128,128]{2,1,0:T(8,128)S(1)} %add.13), channel_id=1, source_target_pairs={{0,4},{2,6},{4,0},{6,2},{8,12},{10,14},{12,8},{14,10},{1,5},{3,7},... | collective-permute-start | bytes 1572872 | tf_op jit(solution)/shard_map/ppermute | solution.py:383
  67.3 20.5 %collective-permute-start.19 = (f32[8,128,128]{2,1,0:T(8,128)S(1)}, f32[8,128,128]{2,1,0:T(8,128)S(1)}, u32[]{:S(2)}, u32[]{:S(2)}) collective-permute-start(f32[8,128,128]{2,1,0:T(8,128)S(1)} %add.12), channel_id=1, source_target_pairs={{4,8},{6,10},{8,4},{10,6},{5,9},{7,11},{9,5},{11,7},{20,24},{22,26... | collective-permute-start | bytes 1572872 | tf_op jit(solution)/shard_map/ppermute | solution.py:383
  77.0 7.6 %collective-permute-start.16 = (f32[4,128,128]{2,1,0:T(8,128)S(1)}, f32[4,128,128]{2,1,0:T(8,128)S(1)}, u32[]{:S(2)}, u32[]{:S(2)}) collective-permute-start(f32[4,128,128]{2,1,0:T(8,128)S(1)} %get-tuple-element.116), channel_id=1, source_target_pairs={{0,1},{1,0},{2,3},{3,2},{4,5},{5,4},{6,7},{7,6},{8,9},{9,8},{10,11... | collective-permute-start | bytes 786440 | tf_op jit(solution)/shard_map/ppermute | solution.py:391
  88.9 10.6 %collective-permute-start.20 = (f32[5,128,128]{2,1,0:T(8,128)S(1)}, f32[5,128,128]{2,1,0:T(8,128)S(1)}, u32[]{:S(2)}, u32[]{:S(2)}) collective-permute-start(f32[5,128,128]{2,1,0:T(8,128)S(1)} %shard_map.91.refs_0_), channel_id=1, source_target_pairs={{0,1},{1,0},{2,3},{3,2},{4,5},{5,4},{6,7},{7,6},{8,9},{9,8},{10,11... | collective-permute-start | bytes 983048 | tf_op jit(solution)/shard_map/ppermute | solution.py:391
  91.5 11.4 %collective-permute-start.21 = (f32[3,128,128]{2,1,0:T(8,128)S(1)}, f32[3,128,128]{2,1,0:T(8,128)S(1)}, u32[]{:S(2)}, u32[]{:S(2)}) collective-permute-start(f32[3,128,128]{2,1,0:T(8,128)S(1)} %shard_map.92.refs_1_), channel_id=1, source_target_pairs={{0,1},{1,0},{2,3},{3,2},{4,5},{5,4},{6,7},{7,6},{8,9},{9,8},{10,11... | collective-permute-start | bytes 589832 | tf_op jit(solution)/shard_map/ppermute | solution.py:391

commit v6 on v5

--- a/solution.py
+++ b/solution.py
@@ -271,26 +271,27 @@
     left_rows(((right, d_x),), here, kept, 0, here.shape[0], 0)
 
 
-def share_kernel(place, kept, received, out_next, out_last, d_left, packed, rest):
+def share_kernel(place, kept, received, out_next, out_last, d_left, packed, packed_next):
     half = d_left.shape[0]
-    block = half * half
+    part, block = half // 2, half * half
     d_left[...] = kept[:half] + received[:half]
-    packed[...] = kept[half:] + received[half : 2 * half]
+    packed[:part] = kept[half : half + part] + received[half : half + part]
+    packed_next[:part] = kept[half + part :] + received[half + part : 2 * half]
     for step, out in enumerate((out_next, out_last)):
         at = slice(step * block, (step + 1) * block)
         plane = 2 * half + step
-        rest[0, at] = flat(out[half:])
-        rest[1, at] = received[plane, block:]
-        rest[2, at] = flat(out[:half])
-        rest[3, at] = received[plane, :block]
-
-
-def gather_out(place, rows, t, out, here, early_other, early_far, received, far):
+        packed[part, at] = flat(out[half:])
+        packed[part + 1, at] = received[plane, block:]
+        packed_next[part, at] = flat(out[:half])
+        packed_next[part + 1, at] = received[plane, :block]
+
+
+def gather_out(place, rows, t, count, start, out, here, early_other, early_far, received, far):
     half = rows // 2
-    block = half * half
+    part, block = half // 2, half * half
     for far_half in (0, 1):
         source = (t + far_half * half) % rows
-        at, wide = slice(source, source + half), slice(source * half, source * half + block)
+        at, wide = slice(source, source + count), slice(source * half, (source + count) * half)
         for far_core in (0, 1):
             core = place[1] + far_core * (1 - 2 * place[1])
             side = place[2] + far_half * (1 - 2 * place[2])
@@ -301,49 +302,48 @@
                     if step < 2:
                         value = early_far[far_core, step, at]
                     else:
-                        ref, plane = far[far_core]
-                        value = ref[plane, (step - 2) * block : (step - 1) * block].reshape(half, half, -1)
+                        begin = (step - 2) * block + (t % half) * half
+                        value = far[part + far_core, begin : begin + count * half].reshape(count, half, -1)
                 elif far_core:
                     if step < 2:
                         value = early_other[step, at]
                     else:
-                        value = received[rows + step - 2, wide].reshape(half, half, -1)
+                        value = received[rows + step - 2, wide].reshape(count, half, -1)
                 else:
                     value = here[step][at]
-                out[t : t + half, pl.ds(first, half), :] = value
+                out[start : start + count, pl.ds(first, half), :] = value
 
 
 def update_kernel(rows, place, *refs):
-    here, early_other, early_far, received, rest, gate, update, out = refs[:4], *refs[4:]
+    here, early_other, early_far, received, far, far_next, gate, update, out = refs[:4], *refs[4:]
     half = rows // 2
-    gather_out(place, rows, 0, out, here, early_other, early_far, received, ((rest, 0), (rest, 1)))
-    gather_out(place, rows, half, out, here, early_other, early_far, received, ((rest, 2), (rest, 3)))
+    gather_out(place, rows, 0, half, 0, out, here, early_other, early_far, received, far)
+    gather_out(place, rows, half, half, half, out, here, early_other, early_far, received, far_next)
     for t in range(0, rows, CHUNK):
         update[pl.ds(source_row(place, t, rows), CHUNK)] = gate[t : t + CHUNK] * out[t : t + CHUNK]
 
 
-def base_kernel(rows, place, *refs):
-    here, early_other, early_far, received, rest = refs[:4], *refs[4:8]
-    gate, cotangent, w_gate, d_left, far, open_part, slope, mine, other, base, out = refs[8:]
-    half, cols, chans = base.shape
-    gather_out(place, rows, 0, out, here, early_other, early_far, received, ((rest, 0), (rest, 1)))
+def base_kernel(rows, t, place, *refs):
+    here, early_other, early_far, received, far, far_rows = refs[:4], *refs[4:9]
+    gate, cotangent, w_gate, d_left, open_part, slope, mine, other, base, out = refs[9:]
+    count, cols, chans = base.shape
+    gather_out(place, rows, t, count, 0, out, here, early_other, early_far, received, far)
     w = gated_weights(place, mine, other, 0)
-    for t in range(0, half, CHUNK):
-        at = slice(t, t + CHUNK)
-        opened = gate[at]
-        d_gate = cotangent[pl.ds(source_row(place, t, rows), CHUNK)] * (opened * out[at]) * (1.0 - opened)
-        grad = flat(d_left[at] + far[at])
-        both = jnp.concatenate([grad * flat(open_part[at]), grad * flat(slope[at])], axis=1)
-        base[at] = (dot_t(flat(d_gate), w_gate[...]) + dot(both, w)).reshape(CHUNK, cols, -1)
-
-
-def pair_kernel(first, place, normed, scale, base, d_right, d_right_near, d_right_middle, d_right_far, open_part, slope, mine, other, d_mine):
+    at = slice(t, t + count)
+    opened = gate[at]
+    d_gate = cotangent[pl.ds(source_row(place, t, rows), count)] * (opened * out[...]) * (1.0 - opened)
+    grad = flat(d_left[at] + far_rows[:count])
+    both = jnp.concatenate([grad * flat(open_part[at]), grad * flat(slope[at])], axis=1)
+    base[...] = (dot_t(flat(d_gate), w_gate[...]) + dot(both, w)).reshape(count, cols, -1)
+
+
+def pair_kernel(first, place, normed, scale, base, d_right, d_right_near, d_right_across, open_part, slope, mine, other, d_mine):
     count, cols, chans = d_mine.shape
     w = gated_weights(place, mine, other, 2)
     at = slice(first, first + count)
-    grad = flat(d_right[at] + d_right_near[at] + (d_right_middle[at] + d_right_far[at]))
+    grad = flat(d_right[at] + d_right_near[...] + d_right_across[...])
     both = jnp.concatenate([grad * flat(open_part[at]), grad * flat(slope[at])], axis=1)
-    d_normed = flat(base[at]) + dot(both, w)
+    d_normed = flat(base[...]) + dot(both, w)
     value = flat(normed[at])
     mean_grad = jnp.mean(d_normed, axis=-1, keepdims=True)
     mean_cross = jnp.mean(d_normed * value, axis=-1, keepdims=True)
@@ -395,7 +395,7 @@
 MIDDLE = [(1, 2), (2, 1)]
 OUTWARD = [(1, 0), (2, 3)]
 INWARD = [(0, 1), (3, 2)]
-ENDS = [(0, 3), (3, 0)]
+ACROSS = [(0, 3), (3, 0), (1, 2), (2, 1)]
 
 
 def on_tiles(pair, pair_mask, w_proj, w_gate, w_out, cotangent):
@@ -476,54 +476,55 @@
     )
     far, d_left_here = lax.optimization_barrier((far, d_left_here))
     tile(3, middle, far)
-    from_far = along(d_right[3], ENDS)
     (d_left_sent,) = call(
         last_sent_kernel,
         [(rows + 2, cols, chans)],
         (place, rights[3], d_x[3], d_left_there, out_there[2], out_there[3]),
     )
-    to_middle, to_near, early_far, d_left_sent = lax.optimization_barrier(
+    part = half // 2
+    to_across, to_near, early_far, d_left_sent = lax.optimization_barrier(
         (d_right[3] + inward, d_right[1] + swapped, early_far, d_left_sent)
     )
+    from_across, from_near = [along(to_across[:part], ACROSS)], [along(to_near[:part], NEXT)]
     received = other_core(d_left_sent)
     _, d_left_here = lax.optimization_barrier((d_left_sent, d_left_here))
     (d_left_kept,) = call(last_kept_kernel, [(rows, cols, chans)], (place, rights[3], d_x[3], d_left_here))
-    d_left, packed, rest = call(
+    packed_shape = (part + 2, cols, chans)
+    d_left, *packed = call(
         share_kernel,
-        [kept, kept, (4, cols, chans)],
+        [kept, packed_shape, packed_shape],
         (place, d_left_kept, received, out_here[2], out_here[3]),
     )
-    d_left_other = other_half(packed)
-    to_near, to_middle, _ = lax.optimization_barrier((to_near, to_middle, packed))
-    from_near = along(to_near, NEXT)
-    from_middle = along(to_middle, MIDDLE)
-    rest, from_far = lax.optimization_barrier((rest, from_far))
-    rest_other = other_half(rest)
-    outs = (*out_here, early_other, early_far, received, rest_other)
-    (base,) = call(
-        functools.partial(base_kernel, rows),
-        [(half, cols, width)],
-        (place, *outs, gate, cotangent, w_gate, d_left, d_left_other, open_left, slope_left, mine, other),
-        scratch=[(half, cols, width)],
-    )
-    cut = (5 * half) // 8
+    far_parts = [other_half(block) for block in packed]
+    from_across.append(along(to_across[part:], ACROSS))
+    from_across[0], last_near = lax.optimization_barrier((from_across[0], to_near[part:]))
+    from_near.append(along(last_near, NEXT))
+    outs = (*out_here, early_other, early_far, received)
     mine_parts, other_parts = [], []
-    for first, last in ((0, cut), (cut, half)):
-        (part,) = call(
+    for at, first in enumerate((0, part)):
+        (base,) = call(
+            functools.partial(base_kernel, rows, first),
+            [(part, cols, width)],
+            (place, *outs, far_parts[0], far_parts[at], gate, cotangent, w_gate, d_left, open_left, slope_left, mine, other),
+            scratch=[(part, cols, width)],
+        )
+        if at:
+            base, mine_parts[0] = lax.optimization_barrier((base, mine_parts[0]))
+        (rows_done,) = call(
             functools.partial(pair_kernel, first),
-            [(last - first, cols, width)],
-            (place, normed, scale, base, d_right[0], from_near, from_middle, from_far, open_right, slope_right, mine, other),
+            [(part, cols, width)],
+            (place, normed, scale, base, d_right[0], from_near[at], from_across[at], open_right, slope_right, mine, other),
         )
-        mine_parts.append(part)
-        other_parts.append(other_half(part))
+        mine_parts.append(rows_done)
+        other_parts.append(other_half(rows_done))
     _, gate_late = lax.optimization_barrier((mine_parts[1], gate))
     (update,) = call(
         functools.partial(update_kernel, rows),
         [(rows, cols, width)],
-        (place, *outs, gate_late),
+        (place, *outs, *far_parts, gate_late),
         scratch=[(rows, cols, width)],
     )
-    firsts = (0, cut)
+    firsts = (0, part)
     d_pair = join(mine_parts, firsts, (True, True), pair.shape)
     other_parts[0], update, d_pair = lax.optimization_barrier((other_parts[0], update, d_pair))
     d_pair = join(other_parts[:1], firsts[:1], (False,), pair.shape, d_pair)

time: 104 us -> 96.9 us (0.932)
  waiting for transfers between devices: 35.8 us -> 21.2 us
  starting transfers between devices: 27 us -> 33.8 us
    ppermute x10 -> x11, waiting for transfers between devices: 19.2 us -> 10.5 us  [along(): lax.ppermute(block, 'row', [(2 * a + core, 2 * b + core) for a, b in pair...]
    ppermute x10 -> x11, starting transfers between devices: 16.3 us -> 23.1 us  [along(): lax.ppermute(block, 'row', [(2 * a + core, 2 * b + core) for a, b in pair...]
    ppermute x7, waiting for transfers between devices: 15 us -> 9.12 us  [other_half(): return lax.ppermute(block, 'ch', [(0, 1), (1, 0)])]
    pallas_call x17 -> x18, Pallas kernels: 37.2 us -> 37.9 us  [call(): pl.pallas_call(kernel, out_shape=[jax.ShapeDtypeStruct(shape, F32) for sh...]
  transfers between devices with their start and end apart: 22 -> 23, of which waited for: 10 -> 8; matrix products, arithmetic and copies ran while one was open for 0% -> 0% of each run, Pallas kernels for 36% -> 41%
where the time goes in v6:
time: 96.9 us; the launch traced here: 96.6 us
  Pallas kernels  40.2 us (41%)
  starting transfers between devices  33.8 us (35%)
  waiting for transfers between devices  21.2 us (22%)
  between operations  1.01 us (1%)
    pallas_call x18, Pallas kernels, call(): pl.pallas_call(kernel, out_shape=[jax.ShapeDtypeStruct(shape, F32) for sh...  37.9 us
    ppermute x11, starting transfers between devices, along(): lax.ppermute(block, 'row', [(2 * a + core, 2 * b + core) for a, b in pair...  23.1 us
    ppermute x11, waiting for transfers between devices, along(): lax.ppermute(block, 'row', [(2 * a + core, 2 * b + core) for a, b in pair...  10.5 us
    ppermute x7, starting transfers between devices, other_half(): return lax.ppermute(block, 'ch', [(0, 1), (1, 0)])  9.88 us
    ppermute x7, waiting for transfers between devices, other_half(): return lax.ppermute(block, 'ch', [(0, 1), (1, 0)])  9.12 us
    pallas_call x3, Pallas kernels, join(): pl.pallas_call(functools.partial(join_kernel, firsts, sides), out_shape=j...  2.24 us
  transfers between devices with their start and end apart: 23, of which 8 were waited for; matrix products, arithmetic and copies ran while one was open for 0% of the time, Pallas kernels for 41%

profile of v6, /device:TPU:0, one launch (start us, length us, event | category | flops | bytes accessed | tf_op | source)
XLA Modules:
  0.0 96.6 jit_solution(15591251962224967465)
XLA Ops:
  0.6 3.0 %collective-permute-start = (f32[256,128]{1,0:T(8,128)}, f32[256,128]{1,0:T(8,128)S(1)}, u32[]{:S(2)}, u32[]{:S(2)}) collective-permute-start(f32[256,128]{1,0:T(8,128)} %bitcast.25), channel_id=1, source_target_pairs={{0,1},{1,0},{2,3},{3,2},{4,5},{5,4},{6,7},{7,6},{8,9},{9,8},{10,11... | collective-permute-start | bytes 393224 | tf_op jit(solution)/shard_map/ppermute | solution.py:391
  3.6 0.1 collective-permute-start.1
  3.7 0.1 pad_add_fusion.place
  3.8 2.2 %shard_map.77 = (f32[8,128,128]{2,1,0:T(8,128)S(1)}, f32[8,128,128]{2,1,0:T(8,128)S(1)}, f32[16,128]{1,0:T(8,128)S(1)}, f32[4,64,128]{2,1,0:T(8,128)S(1)}, f32[8...) custom-call(s32[3]{0:T(128)S(1)} %pad_add_fusion.place, f32[16,128,128]{2,1,0:T(8,128)} %pair.3, s32[16,128]{1,0:T(8,128)} %mask.1, ...), custom_call_target="tpu_custom_call" | custom-call | flops 1000 | bytes 1000 | tf_op jit(solution)/shard_map/pallas_call | solution.py:53
  6.0 0.0 copy-start
  6.0 0.0 copy-start.1
  6.0 0.0 copy-start.2
  6.0 0.1 collective-permute-start.2
  6.1 0.5 collective-permute-start.3
  6.6 1.4 %collective-permute-done.1.other_out = f32[64,128]{1,0:T(8,128)S(1)} collective-permute-done((f32[64,128]{1,0:T(8,128)}, f32[64,128]{1,0:T(8,128)S(1)}, u32[]{:S(2)}, u32[]{:S(2)}) %collective-permute-start.1) | collective-permute-done | bytes 32800 | tf_op jit(solution)/shard_map/ppermute | solution.py:391
  8.0 0.0 collective-permute-done
  8.0 1.2 %shard_map.78 = (f32[8,128,128]{2,1,0:T(8,128)S(1)}, f32[8,128,128]{2,1,0:T(8,128)S(1)}, f32[8,128,128]{2,1,0:T(8,128)S(1)}) custom-call(s32[3]{0:T(128)S(1)} %pad_add_fusion.place, f32[8,128,128]{2,1,0:T(8,128)S(1)} %get-tuple-element.69.normed, f32[16,128]{1,0:T(8,128)S(1)} %get-tuple-element.71.keep, f32[4,64,128]{2,1,0:T(8,128)S(1)} %get-tuple-element.72.mine.refs_15_, ...), custom_call_target="tpu_custom_call" | custom-call | flops 1000 | bytes 1000 | tf_op jit(solution)/shard_map/pallas_call | solution.py:53
  9.3 1.9 %collective-permute-start.5 = (f32[8,128,128]{2,1,0:T(8,128)S(1)}, f32[8,128,128]{2,1,0:T(8,128)S(1)}, u32[]{:S(2)}, u32[]{:S(2)}) collective-permute-start(f32[8,128,128]{2,1,0:T(8,128)S(1)} %get-tuple-element.74.refs_0_), channel_id=1, source_target_pairs={{0,4},{2,6},{4,0},{6,2},{8,12},{10,14},{12,8},{14,10},{1,5},{3,7},... | collective-permute-start | bytes 1572872 | tf_op jit(solution)/shard_map/ppermute | solution.py:383
  11.1 0.7 collective-permute-start.8
  11.8 1.5 %shard_map.79 = f32[5,16,8,128]{3,2,1,0:T(8,128)S(1)} custom-call(s32[3]{0:T(128)S(1)} %pad_add_fusion.place, f32[16,128,128]{2,1,0:T(8,128)} %refs_10_.3, f32[16,128]{1,0:T(8,128)S(1)} %get-tuple-element.71.keep), custom_call_target="tpu_custom_call" | custom-call | flops 1000 | bytes 1000 | tf_op jit(solution)/shard_map/pallas_call | solution.py:53
  13.3 0.1 collective-permute-start.4
  13.4 1.6 %collective-permute-done.4.third = f32[5,16,8,128]{3,2,1,0:T(8,128)S(1)} collective-permute-done((f32[5,16,8,128]{3,2,1,0:T(8,128)S(1)}, f32[5,16,8,128]{3,2,1,0:T(8,128)S(1)}, u32[]{:S(2)}, u32[]{:S(2)}) %collective-permute-start.4) | collective-permute-done | bytes 327712 | tf_op jit(solution)/shard_map/ppermute | solution.py:387
  15.1 3.8 %shard_map.80 = (f32[16,128,128]{2,1,0:T(8,128)S(1)}, f32[16,128,128]{2,1,0:T(8,128)S(1)}, f32[8,128,128]{2,1,0:T(8,128)S(1)}, f32[8,128,128]{2,1,0:T(8,128)S(1)...) custom-call(s32[3]{0:T(128)S(1)} %pad_add_fusion.place, ...), custom_call_target="tpu_custom_call" | custom-call | flops 1000 | bytes 1000 | tf_op jit(solution)/shard_map/pallas_call | solution.py:53
  18.9 3.5 %collective-permute-done.5.refs_0_.refs_1_ = f32[8,128,128]{2,1,0:T(8,128)S(1)} collective-permute-done((f32[8,128,128]{2,1,0:T(8,128)S(1)}, f32[8,128,128]{2,1,0:T(8,128)S(1)}, u32[]{:S(2)}, u32[]{:S(2)}) %collective-permute-start.5) | collective-permute-done | bytes 524320 | tf_op jit(solution)/shard_map/ppermute | solution.py:383
  22.4 0.7 collective-permute-start.6
  23.1 1.3 %collective-permute-start.9 = (f32[8,128,128]{2,1,0:T(8,128)S(1)}, f32[8,128,128]{2,1,0:T(8,128)S(1)}, u32[]{:S(2)}, u32[]{:S(2)}) collective-permute-start(f32[8,128,128]{2,1,0:T(8,128)S(1)} %collective-permute-done.8.refs_0_), channel_id=1, source_target_pairs={{4,0},{6,2},{8,12},{10,14},{5,1},{7,3},{9,13},{11,15},{20,16},{22,... | collective-permute-start | bytes 1572872 | tf_op jit(solution)/shard_map/ppermute | solution.py:383
  24.4 3.8 %shard_map.81 = (f32[16,8,128]{2,1,0:T(8,128)S(1)}, f32[16,8,128]{2,1,0:T(8,128)S(1)}, f32[256,128]{1,0:T(8,128)S(1)}, f32[8,128,128]{2,1,0:T(8,128)S(1)}) custom-call(s32[3]{0:T(128)S(1)} %pad_add_fusion.place, f32[8,128,128]{2,1,0:T(8,128)S(1)} %get-tuple-element.74.refs_0_, f32[16,128,128]{2,1,0:T(8,128)S(1)} %get-tuple-element.79.refs_1_.refs_2_, ...), custom_call_target="tpu_custom_call" | custom-call | flops 1000 | bytes 1000 | tf_op jit(solution)/shard_map/pallas_call | solution.py:53
  28.2 3.8 %shard_map.82 = (f32[16,8,128]{2,1,0:T(8,128)S(1)}, f32[16,8,128]{2,1,0:T(8,128)S(1)}, f32[256,128]{1,0:T(8,128)S(1)}, f32[8,128,128]{2,1,0:T(8,128)S(1)}) custom-call(s32[3]{0:T(128)S(1)} %pad_add_fusion.place, f32[8,128,128]{2,1,0:T(8,128)S(1)} %collective-permute-done.5.refs_0_.refs_1_, f32[16,128,128]{2,1,0:T(8,128)S(1)} %get-tuple-element.79.refs_1_.refs_2_, ...), custom_call_target="tpu_custom_call" | custom-call | flops 1000 | bytes 1000 | tf_op jit(solution)/shard_map/pallas_call | solution.py:53
  32.0 0.1 collective-permute-start.7
  32.1 2.9 %shard_map.83 = (f32[16,128,128]{2,1,0:T(8,128)S(1)}, f32[16,128,128]{2,1,0:T(8,128)S(1)}) custom-call(s32[3]{0:T(128)S(1)} %pad_add_fusion.place, f32[8,128,128]{2,1,0:T(8,128)S(1)} %get-tuple-element.74.refs_0_, f32[8,128,128]{2,1,0:T(8,128)S(1)} %collective-permute-done.5.refs_0_.refs_1_, f32[256,128]{1,0:T(8,128)S(1)} %get-tuple-element.90.refs_2_, ...), custom_call_target="tpu_custom_call" | custom-call | flops 1000 | bytes 1000 | tf_op jit(solution)/shard_map/pallas_call | solution.py:53
  35.0 0.0 collective-permute-done.7.refs_4_
  35.0 1.3 %collective-permute-start.10 = (f32[8,128,128]{2,1,0:T(8,128)S(1)}, f32[8,128,128]{2,1,0:T(8,128)S(1)}, u32[]{:S(2)}, u32[]{:S(2)}) collective-permute-start(f32[8,128,128]{2,1,0:T(8,128)S(1)} %collective-permute-done.6.refs_0_), channel_id=1, source_target_pairs={{4,0},{6,2},{8,12},{10,14},{5,1},{7,3},{9,13},{11,15},{20,16},{22,... | collective-permute-start | bytes 1572872 | tf_op jit(solution)/shard_map/ppermute | solution.py:383
  36.3 2.4 %collective-permute-done.9.refs_1_ = f32[8,128,128]{2,1,0:T(8,128)S(1)} collective-permute-done((f32[8,128,128]{2,1,0:T(8,128)S(1)}, f32[8,128,128]{2,1,0:T(8,128)S(1)}, u32[]{:S(2)}, u32[]{:S(2)}) %collective-permute-start.9) | collective-permute-done | bytes 524320 | tf_op jit(solution)/shard_map/ppermute | solution.py:383
  38.7 3.8 %shard_map.84 = (f32[16,8,128]{2,1,0:T(8,128)S(1)}, f32[16,8,128]{2,1,0:T(8,128)S(1)}, f32[256,128]{1,0:T(8,128)S(1)}, f32[8,128,128]{2,1,0:T(8,128)S(1)}, f32[8,128,128]{2,1,0:T(8,128)S(1)}) custom-call(s32[3]{0:T(128)S(1)} %pad_add_fusion.place, f32[8,128,128]{2,1,0:T(8,128)S(1)} %collective-permute-done.6.refs_0_, ...), custom_call_target="tpu_custom_call" | custom-call | flops 1000 | bytes 1000 | tf_op jit(solution)/shard_map/pallas_call | solution.py:53
  42.6 3.9 %collective-permute-start.11 = (f32[8,128,128]{2,1,0:T(8,128)S(1)}, f32[8,128,128]{2,1,0:T(8,128)S(1)}, u32[]{:S(2)}, u32[]{:S(2)}) collective-permute-start(f32[8,128,128]{2,1,0:T(8,128)S(1)} %get-tuple-element.104), channel_id=1, source_target_pairs={{0,4},{2,6},{12,8},{14,10},{1,5},{3,7},{13,9},{15,11},{16,20},{18,... | collective-permute-start | bytes 1572872 | tf_op jit(solution)/shard_map/ppermute | solution.py:383
  46.5 0.7 collective-permute-start.12
  47.2 1.6 %collective-permute-start.13 = (f32[2,2,16,8,128]{4,3,2,1,0:T(8,128)S(1)}, f32[2,2,16,8,128]{4,3,2,1,0:T(8,128)S(1)}, u32[]{:S(2)}, u32[]{:S(2)}) collective-permute-start(f32[2,2,16,8,128]{4,3,2,1,0:T(8,128)S(1)} %pad_maximum_fusion), channel_id=1, source_target_pairs={{0,1},{1,0},{2,3},{3,2},{4,5},{5,4},{6,7},{7,6},{8,9},{9,8},{10,11... | collective-permute-start | bytes 786440 | tf_op jit(solution)/shard_map/ppermute | solution.py:391
  48.8 1.9 %shard_map.85 = (f32[16,128,128]{2,1,0:T(8,128)S(1)}, f32[16,128,128]{2,1,0:T(8,128)S(1)}) custom-call(s32[3]{0:T(128)S(1)} %pad_add_fusion.place, f32[8,128,128]{2,1,0:T(8,128)S(1)} %get-tuple-element.95.refs_0_, f32[256,128]{1,0:T(8,128)S(1)} %get-tuple-element.96.refs_1_, f32[16,128,128]{2,1,0:T(8,128)S(1)} %get-tuple-element.97.refs_2_, ...), custom_call_target="tpu_custom_call" | custom-call | flops 1000 | bytes 1000 | tf_op jit(solution)/shard_map/pallas_call | solution.py:53
  50.7 2.5 %collective-permute-done.10.refs_1_ = f32[8,128,128]{2,1,0:T(8,128)S(1)} collective-permute-done((f32[8,128,128]{2,1,0:T(8,128)S(1)}, f32[8,128,128]{2,1,0:T(8,128)S(1)}, u32[]{:S(2)}, u32[]{:S(2)}) %collective-permute-start.10) | collective-permute-done | bytes 524320 | tf_op jit(solution)/shard_map/ppermute | solution.py:383
  53.2 3.8 %shard_map.86 = (f32[16,8,128]{2,1,0:T(8,128)S(1)}, f32[16,8,128]{2,1,0:T(8,128)S(1)}, f32[256,128]{1,0:T(8,128)S(1)}, f32[8,128,128]{2,1,0:T(8,128)S(1)}, f32[8,128,128]{2,1,0:T(8,128)S(1)}) custom-call(s32[3]{0:T(128)S(1)} %pad_add_fusion.place, f32[8,128,128]{2,1,0:T(8,128)S(1)} %collective-permute-done.8.refs_0_, ...), custom_call_target="tpu_custom_call" | custom-call | flops 1000 | bytes 1000 | tf_op jit(solution)/shard_map/pallas_call | solution.py:53
  57.0 1.2 %shard_map.87 = f32[18,128,128]{2,1,0:T(8,128)S(1)} custom-call(s32[3]{0:T(128)S(1)} %pad_add_fusion.place, f32[8,128,128]{2,1,0:T(8,128)S(1)} %get-tuple-element.106.right, f32[256,128]{1,0:T(8,128)S(1)} %get-tuple-element.107.d_x, f32[16,128,128]{2,1,0:T(8,128)S(1)} %get-tuple-element.108.there, f32[16,8,128]{2,1,0:T(8,128)S(1)} %get-tuple-element.109.out_next, ...), custom_call_target="tpu_custom_call" | custom-call | flops 1000 | bytes 1000 | tf_op jit(solution)/shard_map/pallas_call | solution.py:53
  58.3 0.0 collective-permute-done.11
  58.3 0.1 add.12
  58.4 0.0 collective-permute-done.12
  58.4 0.1 add.13
  58.5 0.0 collective-permute-done.13.refs_5_
  58.5 0.1 collective-permute-start.14
  58.6 2.6 %collective-permute-start.17 = (f32[4,128,128]{2,1,0:T(8,128)S(1)}, f32[4,128,128]{2,1,0:T(8,128)S(1)}, u32[]{:S(2)}, u32[]{:S(2)}) collective-permute-start(f32[4,128,128]{2,1,0:T(8,128)S(1)} %get-tuple-element.137), channel_id=1, source_target_pairs={{0,12},{2,14},{12,0},{14,2},{4,8},{6,10},{8,4},{10,6},{1,13},{3,15... | collective-permute-start | bytes 786440 | tf_op jit(solution)/shard_map/ppermute | solution.py:383
  61.2 1.2 %shard_map.88.kept = f32[16,128,128]{2,1,0:T(8,128)S(1)} custom-call(s32[3]{0:T(128)S(1)} %pad_add_fusion.place, f32[8,128,128]{2,1,0:T(8,128)S(1)} %get-tuple-element.106.right, f32[256,128]{1,0:T(8,128)S(1)} %get-tuple-element.107.d_x, f32[16,128,128]{2,1,0:T(8,128)S(1)} %get-tuple-element.114.here), custom_call_target="tpu_custom_call" | custom-call | flops 1000 | bytes 1000 | tf_op jit(solution)/shard_map/pallas_call | solution.py:53
  62.5 0.7 shard_map.89
  63.2 1.6 %collective-permute-start.15 = (f32[6,128,128]{2,1,0:T(8,128)S(1)}, f32[6,128,128]{2,1,0:T(8,128)S(1)}, u32[]{:S(2)}, u32[]{:S(2)}) collective-permute-start(f32[6,128,128]{2,1,0:T(8,128)S(1)} %get-tuple-element.115), channel_id=1, source_target_pairs={{0,1},{1,0},{2,3},{3,2},{4,5},{5,4},{6,7},{7,6},{8,9},{9,8},{10,11... | collective-permute-start | bytes 1179656 | tf_op jit(solution)/shard_map/ppermute | solution.py:391
  64.8 0.5 collective-permute-start.19
  65.3 2.8 %collective-permute-start.16 = (f32[4,128,128]{2,1,0:T(8,128)S(1)}, f32[4,128,128]{2,1,0:T(8,128)S(1)}, u32[]{:S(2)}, u32[]{:S(2)}) collective-permute-start(f32[4,128,128]{2,1,0:T(8,128)S(1)} %get-tuple-element.139), channel_id=1, source_target_pairs={{0,4},{2,6},{4,0},{6,2},{8,12},{10,14},{12,8},{14,10},{1,5},{3,7},... | collective-permute-start | bytes 786440 | tf_op jit(solution)/shard_map/ppermute | solution.py:383
  68.1 2.4 %collective-permute-start.21 = (f32[4,128,128]{2,1,0:T(8,128)S(1)}, f32[4,128,128]{2,1,0:T(8,128)S(1)}, u32[]{:S(2)}, u32[]{:S(2)}) collective-permute-start(f32[4,128,128]{2,1,0:T(8,128)S(1)} %get-tuple-element.136), channel_id=1, source_target_pairs={{0,12},{2,14},{12,0},{14,2},{4,8},{6,10},{8,4},{10,6},{1,13},{3,15... | collective-permute-start | bytes 786440 | tf_op jit(solution)/shard_map/ppermute | solution.py:383
  70.5 0.0 collective-permute-done.17.d_right_across
  70.5 4.9 %collective-permute-start.20 = (f32[4,128,128]{2,1,0:T(8,128)S(1)}, f32[4,128,128]{2,1,0:T(8,128)S(1)}, u32[]{:S(2)}, u32[]{:S(2)}) collective-permute-start(f32[4,128,128]{2,1,0:T(8,128)S(1)} %get-tuple-element.128), channel_id=1, source_target_pairs={{0,4},{2,6},{4,0},{6,2},{8,12},{10,14},{12,8},{14,10},{1,5},{3,7},... | collective-permute-start | bytes 786440 | tf_op jit(solution)/shard_map/ppermute | solution.py:383
  75.4 1.1 %shard_map.90.base = f32[4,128,128]{2,1,0:T(8,128)S(1)} custom-call(s32[3]{0:T(128)S(1)} %pad_add_fusion.place, f32[16,8,128]{2,1,0:T(8,128)S(1)} %get-tuple-element.85.refs_0_, f32[16,8,128]{2,1,0:T(8,128)S(1)} %get-tuple-element.87.refs_1_, f32[16,8,128]{2,1,0:T(8,128)S(1)} %get-tuple-element.94.out_next.refs_2_, ...), custom_call_target="tpu_custom_call" | custom-call | flops 1000 | bytes 1000 | tf_op jit(solution)/shard_map/pallas_call | solution.py:53
  76.5 1.0 %shard_map.91.refs_0_ = f32[4,128,128]{2,1,0:T(8,128)S(1)} custom-call(s32[3]{0:T(128)S(1)} %pad_add_fusion.place, f32[8,128,128]{2,1,0:T(8,128)S(1)} %get-tuple-element.69.normed, f32[8,128,128]{2,1,0:T(8,128)S(1)} %get-tuple-element.70.scale, f32[4,128,128]{2,1,0:T(8,128)S(1)} %shard_map.90.base, f32[8,128,128]{2,1,0:T(8,128)S(1)} %get-tuple-element.120.d_right, ...), custom_call_target="tpu_custom_call" | custom-call | flops 1000 | bytes 1000 | tf_op jit(solution)/shard_map/pallas_call | solution.py:53
  77.5 1.6 %collective-permute-start.18 = (f32[4,128,128]{2,1,0:T(8,128)S(1)}, f32[4,128,128]{2,1,0:T(8,128)S(1)}, u32[]{:S(2)}, u32[]{:S(2)}) collective-permute-start(f32[4,128,128]{2,1,0:T(8,128)S(1)} %shard_map.91.refs_0_), channel_id=1, source_target_pairs={{0,1},{1,0},{2,3},{3,2},{4,5},{5,4},{6,7},{7,6},{8,9},{9,8},{10,11... | collective-permute-start | bytes 786440 | tf_op jit(solution)/shard_map/ppermute | solution.py:391
  79.1 4.5 %collective-permute-done.19.refs_8_ = f32[6,128,128]{2,1,0:T(8,128)S(1)} collective-permute-done((f32[6,128,128]{2,1,0:T(8,128)S(1)}, f32[6,128,128]{2,1,0:T(8,128)S(1)}, u32[]{:S(2)}, u32[]{:S(2)}) %collective-permute-start.19) | collective-permute-done | bytes 393248 | tf_op jit(solution)/shard_map/ppermute | solution.py:391
  83.6 1.1 %shard_map.92.base = f32[4,128,128]{2,1,0:T(8,128)S(1)} custom-call(s32[3]{0:T(128)S(1)} %pad_add_fusion.place, f32[16,8,128]{2,1,0:T(8,128)S(1)} %get-tuple-element.85.refs_0_, f32[16,8,128]{2,1,0:T(8,128)S(1)} %get-tuple-element.87.refs_1_, f32[16,8,128]{2,1,0:T(8,128)S(1)} %get-tuple-element.94.out_next.refs_2_, ...), custom_call_target="tpu_custom_call" | custom-call | flops 1000 | bytes 1000 | tf_op jit(solution)/shard_map/pallas_call | solution.py:53
  84.7 2.0 %collective-permute-done.20.d_right_near = f32[4,128,128]{2,1,0:T(8,128)S(1)} collective-permute-done((f32[4,128,128]{2,1,0:T(8,128)S(1)}, f32[4,128,128]{2,1,0:T(8,128)S(1)}, u32[]{:S(2)}, u32[]{:S(2)}) %collective-permute-start.20) | collective-permute-done | bytes 262176 | tf_op jit(solution)/shard_map/ppermute | solution.py:383
  86.8 1.0 %shard_map.93.refs_1_ = f32[4,128,128]{2,1,0:T(8,128)S(1)} custom-call(s32[3]{0:T(128)S(1)} %pad_add_fusion.place, f32[8,128,128]{2,1,0:T(8,128)S(1)} %get-tuple-element.69.normed, f32[8,128,128]{2,1,0:T(8,128)S(1)} %get-tuple-element.70.scale, f32[4,128,128]{2,1,0:T(8,128)S(1)} %shard_map.92.base, f32[8,128,128]{2,1,0:T(8,128)S(1)} %get-tuple-element.120.d_right, ...), custom_call_target="tpu_custom_call" | custom-call | flops 1000 | bytes 1000 | tf_op jit(solution)/shard_map/pallas_call | solution.py:53
  87.8 1.6 %collective-permute-start.22 = (f32[4,128,128]{2,1,0:T(8,128)S(1)}, f32[4,128,128]{2,1,0:T(8,128)S(1)}, u32[]{:S(2)}, u32[]{:S(2)}) collective-permute-start(f32[4,128,128]{2,1,0:T(8,128)S(1)} %shard_map.93.refs_1_), channel_id=1, source_target_pairs={{0,1},{1,0},{2,3},{3,2},{4,5},{5,4},{6,7},{7,6},{8,9},{9,8},{10,11... | collective-permute-start | bytes 786440 | tf_op jit(solution)/shard_map/ppermute | solution.py:391
  89.4 1.8 %shard_map.94 = f32[16,128,128]{2,1,0:T(8,128)} custom-call(s32[3]{0:T(128)S(1)} %pad_add_fusion.place, f32[16,8,128]{2,1,0:T(8,128)S(1)} %get-tuple-element.85.refs_0_, f32[16,8,128]{2,1,0:T(8,128)S(1)} %get-tuple-element.87.refs_1_, f32[16,8,128]{2,1,0:T(8,128)S(1)} %get-tuple-element.94.out_next.refs_2_, ...), custom_call_target="tpu_custom_call" | custom-call | flops 1000 | bytes 1000 | tf_op jit(solution)/shard_map/pallas_call | solution.py:53
  91.2 0.8 shard_map.95.refs_1_
  92.0 0.7 shard_map.96.refs_1_
  92.7 3.1 %collective-permute-done.22.refs_0_ = f32[4,128,128]{2,1,0:T(8,128)S(1)} collective-permute-done((f32[4,128,128]{2,1,0:T(8,128)S(1)}, f32[4,128,128]{2,1,0:T(8,128)S(1)}, u32[]{:S(2)}, u32[]{:S(2)}) %collective-permute-start.22) | collective-permute-done | bytes 262176 | tf_op jit(solution)/shard_map/ppermute | solution.py:391
  95.9 0.7 shard_map.97
  (19 shorter events, 0.1 us)
Async XLA Ops:
  0.6 7.4 %collective-permute-start = (f32[256,128]{1,0:T(8,128)}, f32[256,128]{1,0:T(8,128)S(1)}, u32[]{:S(2)}, u32[]{:S(2)}) collective-permute-start(f32[256,128]{1,0:T(8,128)} %bitcast.25), channel_id=1, source_target_pairs={{0,1},{1,0},{2,3},{3,2},{4,5},{5,4},{6,7},{7,6},{8,9},{9,8},{10,11... | collective-permute-start | bytes 393224 | tf_op jit(solution)/shard_map/ppermute | solution.py:391
  3.6 4.4 %collective-permute-start.1 = (f32[64,128]{1,0:T(8,128)}, f32[64,128]{1,0:T(8,128)S(1)}, u32[]{:S(2)}, u32[]{:S(2)}) collective-permute-start(f32[64,128]{1,0:T(8,128)} %mine_out.1), channel_id=1, source_target_pairs={{0,1},{1,0},{2,3},{3,2},{4,5},{5,4},{6,7},{7,6},{8,9},{9,8},{10,11... | collective-permute-start | bytes 98312 | tf_op jit(solution)/shard_map/ppermute | solution.py:391
  3.8 11.3 %copy-start.3 = (f32[64,128]{1,0:T(8,128)S(1)}, f32[64,128]{1,0:T(8,128)}, u32[]{:S(2)}) copy-start(f32[64,128]{1,0:T(8,128)} %mine_out.1) | copy-start | bytes 98308
  6.0 9.1 %copy-start = (f32[16,128,128]{2,1,0:T(8,128)S(1)}, f32[16,128,128]{2,1,0:T(8,128)}, u32[]{:S(2)}) copy-start(f32[16,128,128]{2,1,0:T(8,128)} %refs_10_.3) | copy-start | bytes 3145732
  6.0 9.1 %copy-start.1 = (f32[16,128,128]{2,1,0:T(8,128)S(1)}, f32[16,128,128]{2,1,0:T(8,128)}, u32[]{:S(2)}) copy-start(f32[16,128,128]{2,1,0:T(8,128)} %pair.3) | copy-start | bytes 3145732
  6.0 9.0 %copy-start.2 = (f32[128,128]{1,0:T(8,128)S(1)}, f32[128,128]{1,0:T(8,128)}, u32[]{:S(2)}) copy-start(f32[128,128]{1,0:T(8,128)} %refs_11_.3) | copy-start | bytes 196612
  6.0 9.0 %collective-permute-start.2 = (f32[8,128,128]{2,1,0:T(8,128)S(1)}, f32[8,128,128]{2,1,0:T(8,128)S(1)}, u32[]{:S(2)}, u32[]{:S(2)}) collective-permute-start(f32[8,128,128]{2,1,0:T(8,128)S(1)} %get-tuple-element.75), channel_id=1, source_target_pairs={{0,2},{2,0},{4,6},{6,4},{8,10},{10,8},{12,14},{14,12},{1,3},{3,1},... | collective-permute-start | bytes 1572872 | tf_op jit(solution)/shard_map/ppermute | solution.py:387
  6.1 8.9 %collective-permute-start.3 = (f32[8,128,128]{2,1,0:T(8,128)S(1)}, f32[8,128,128]{2,1,0:T(8,128)S(1)}, u32[]{:S(2)}, u32[]{:S(2)}) collective-permute-start(f32[8,128,128]{2,1,0:T(8,128)S(1)} %get-tuple-element.76), channel_id=1, source_target_pairs={{0,2},{2,0},{4,6},{6,4},{8,10},{10,8},{12,14},{14,12},{1,3},{3,1},... | collective-permute-start | bytes 1572872 | tf_op jit(solution)/shard_map/ppermute | solution.py:387
  9.3 13.2 %collective-permute-start.5 = (f32[8,128,128]{2,1,0:T(8,128)S(1)}, f32[8,128,128]{2,1,0:T(8,128)S(1)}, u32[]{:S(2)}, u32[]{:S(2)}) collective-permute-start(f32[8,128,128]{2,1,0:T(8,128)S(1)} %get-tuple-element.74.refs_0_), channel_id=1, source_target_pairs={{0,4},{2,6},{4,0},{6,2},{8,12},{10,14},{12,8},{14,10},{1,5},{3,7},... | collective-permute-start | bytes 1572872 | tf_op jit(solution)/shard_map/ppermute | solution.py:383
  11.1 12.0 %collective-permute-start.8 = (f32[8,128,128]{2,1,0:T(8,128)S(1)}, f32[8,128,128]{2,1,0:T(8,128)S(1)}, u32[]{:S(2)}, u32[]{:S(2)}) collective-permute-start(f32[8,128,128]{2,1,0:T(8,128)S(1)} %get-tuple-element.74.refs_0_), channel_id=1, source_target_pairs={{4,8},{6,10},{8,4},{10,6},{5,9},{7,11},{9,5},{11,7},{20,24},{22,26... | collective-permute-start | bytes 1572872 | tf_op jit(solution)/shard_map/ppermute | solution.py:383
  13.3 1.7 %collective-permute-start.4 = (f32[5,16,8,128]{3,2,1,0:T(8,128)S(1)}, f32[5,16,8,128]{3,2,1,0:T(8,128)S(1)}, u32[]{:S(2)}, u32[]{:S(2)}) collective-permute-start(f32[5,16,8,128]{3,2,1,0:T(8,128)S(1)} %shard_map.79), channel_id=1, source_target_pairs={{0,2},{2,0},{4,6},{6,4},{8,10},{10,8},{12,14},{14,12},{1,3},{3,1},... | collective-permute-start | bytes 983048 | tf_op jit(solution)/shard_map/ppermute | solution.py:387
  22.4 12.6 %collective-permute-start.6 = (f32[8,128,128]{2,1,0:T(8,128)S(1)}, f32[8,128,128]{2,1,0:T(8,128)S(1)}, u32[]{:S(2)}, u32[]{:S(2)}) collective-permute-start(f32[8,128,128]{2,1,0:T(8,128)S(1)} %collective-permute-done.5.refs_0_.refs_1_), channel_id=1, source_target_pairs={{4,8},{6,10},{8,4},{10,6},{5,9},{7,11},{9,5},{11,7},{20,24},{22,26... | collective-permute-start | bytes 1572872 | tf_op jit(solution)/shard_map/ppermute | solution.py:383
  23.1 15.6 %collective-permute-start.9 = (f32[8,128,128]{2,1,0:T(8,128)S(1)}, f32[8,128,128]{2,1,0:T(8,128)S(1)}, u32[]{:S(2)}, u32[]{:S(2)}) collective-permute-start(f32[8,128,128]{2,1,0:T(8,128)S(1)} %collective-permute-done.8.refs_0_), channel_id=1, source_target_pairs={{4,0},{6,2},{8,12},{10,14},{5,1},{7,3},{9,13},{11,15},{20,16},{22,... | collective-permute-start | bytes 1572872 | tf_op jit(solution)/shard_map/ppermute | solution.py:383
  32.0 3.0 %collective-permute-start.7 = (f32[2,16,8,128]{3,2,1,0:T(8,128)S(1)}, f32[2,16,8,128]{3,2,1,0:T(8,128)S(1)}, u32[]{:S(2)}, u32[]{:S(2)}) collective-permute-start(f32[2,16,8,128]{3,2,1,0:T(8,128)S(1)} %pad_maximum_fusion.1), channel_id=1, source_target_pairs={{0,2},{2,0},{4,6},{6,4},{8,10},{10,8},{12,14},{14,12},{1,3},{3,1},... | collective-permute-start | bytes 393224 | tf_op jit(solution)/shard_map/ppermute | solution.py:387
  35.0 18.2 %collective-permute-start.10 = (f32[8,128,128]{2,1,0:T(8,128)S(1)}, f32[8,128,128]{2,1,0:T(8,128)S(1)}, u32[]{:S(2)}, u32[]{:S(2)}) collective-permute-start(f32[8,128,128]{2,1,0:T(8,128)S(1)} %collective-permute-done.6.refs_0_), channel_id=1, source_target_pairs={{4,0},{6,2},{8,12},{10,14},{5,1},{7,3},{9,13},{11,15},{20,16},{22,... | collective-permute-start | bytes 1572872 | tf_op jit(solution)/shard_map/ppermute | solution.py:383
  42.6 15.7 %collective-permute-start.11 = (f32[8,128,128]{2,1,0:T(8,128)S(1)}, f32[8,128,128]{2,1,0:T(8,128)S(1)}, u32[]{:S(2)}, u32[]{:S(2)}) collective-permute-start(f32[8,128,128]{2,1,0:T(8,128)S(1)} %get-tuple-element.104), channel_id=1, source_target_pairs={{0,4},{2,6},{12,8},{14,10},{1,5},{3,7},{13,9},{15,11},{16,20},{18,... | collective-permute-start | bytes 1572872 | tf_op jit(solution)/shard_map/ppermute | solution.py:383
  46.5 11.9 %collective-permute-start.12 = (f32[8,128,128]{2,1,0:T(8,128)S(1)}, f32[8,128,128]{2,1,0:T(8,128)S(1)}, u32[]{:S(2)}, u32[]{:S(2)}) collective-permute-start(f32[8,128,128]{2,1,0:T(8,128)S(1)} %get-tuple-element.104), channel_id=1, source_target_pairs={{4,8},{6,10},{8,4},{10,6},{5,9},{7,11},{9,5},{11,7},{20,24},{22,26... | collective-permute-start | bytes 1572872 | tf_op jit(solution)/shard_map/ppermute | solution.py:383
  47.2 11.3 %collective-permute-start.13 = (f32[2,2,16,8,128]{4,3,2,1,0:T(8,128)S(1)}, f32[2,2,16,8,128]{4,3,2,1,0:T(8,128)S(1)}, u32[]{:S(2)}, u32[]{:S(2)}) collective-permute-start(f32[2,2,16,8,128]{4,3,2,1,0:T(8,128)S(1)} %pad_maximum_fusion), channel_id=1, source_target_pairs={{0,1},{1,0},{2,3},{3,2},{4,5},{5,4},{6,7},{7,6},{8,9},{9,8},{10,11... | collective-permute-start | bytes 786440 | tf_op jit(solution)/shard_map/ppermute | solution.py:391
  58.5 4.0 %collective-permute-start.14 = (f32[18,128,128]{2,1,0:T(8,128)S(1)}, f32[18,128,128]{2,1,0:T(8,128)S(1)}, u32[]{:S(2)}, u32[]{:S(2)}) collective-permute-start(f32[18,128,128]{2,1,0:T(8,128)S(1)} %shard_map.87), channel_id=1, source_target_pairs={{0,2},{2,0},{4,6},{6,4},{8,10},{10,8},{12,14},{14,12},{1,3},{3,1},... | collective-permute-start | bytes 3538952 | tf_op jit(solution)/shard_map/ppermute | solution.py:387
  58.6 11.9 %collective-permute-start.17 = (f32[4,128,128]{2,1,0:T(8,128)S(1)}, f32[4,128,128]{2,1,0:T(8,128)S(1)}, u32[]{:S(2)}, u32[]{:S(2)}) collective-permute-start(f32[4,128,128]{2,1,0:T(8,128)S(1)} %get-tuple-element.137), channel_id=1, source_target_pairs={{0,12},{2,14},{12,0},{14,2},{4,8},{6,10},{8,4},{10,6},{1,13},{3,15... | collective-permute-start | bytes 786440 | tf_op jit(solution)/shard_map/ppermute | solution.py:383
  63.2 12.2 %collective-permute-start.15 = (f32[6,128,128]{2,1,0:T(8,128)S(1)}, f32[6,128,128]{2,1,0:T(8,128)S(1)}, u32[]{:S(2)}, u32[]{:S(2)}) collective-permute-start(f32[6,128,128]{2,1,0:T(8,128)S(1)} %get-tuple-element.115), channel_id=1, source_target_pairs={{0,1},{1,0},{2,3},{3,2},{4,5},{5,4},{6,7},{7,6},{8,9},{9,8},{10,11... | collective-permute-start | bytes 1179656 | tf_op jit(solution)/shard_map/ppermute | solution.py:391
  64.8 18.8 %collective-permute-start.19 = (f32[6,128,128]{2,1,0:T(8,128)S(1)}, f32[6,128,128]{2,1,0:T(8,128)S(1)}, u32[]{:S(2)}, u32[]{:S(2)}) collective-permute-start(f32[6,128,128]{2,1,0:T(8,128)S(1)} %get-tuple-element.126), channel_id=1, source_target_pairs={{0,1},{1,0},{2,3},{3,2},{4,5},{5,4},{6,7},{7,6},{8,9},{9,8},{10,11... | collective-permute-start | bytes 1179656 | tf_op jit(solution)/shard_map/ppermute | solution.py:391
  65.3 11.2 %collective-permute-start.16 = (f32[4,128,128]{2,1,0:T(8,128)S(1)}, f32[4,128,128]{2,1,0:T(8,128)S(1)}, u32[]{:S(2)}, u32[]{:S(2)}) collective-permute-start(f32[4,128,128]{2,1,0:T(8,128)S(1)} %get-tuple-element.139), channel_id=1, source_target_pairs={{0,4},{2,6},{4,0},{6,2},{8,12},{10,14},{12,8},{14,10},{1,5},{3,7},... | collective-permute-start | bytes 786440 | tf_op jit(solution)/shard_map/ppermute | solution.py:383
  68.1 16.6 %collective-permute-start.21 = (f32[4,128,128]{2,1,0:T(8,128)S(1)}, f32[4,128,128]{2,1,0:T(8,128)S(1)}, u32[]{:S(2)}, u32[]{:S(2)}) collective-permute-start(f32[4,128,128]{2,1,0:T(8,128)S(1)} %get-tuple-element.136), channel_id=1, source_target_pairs={{0,12},{2,14},{12,0},{14,2},{4,8},{6,10},{8,4},{10,6},{1,13},{3,15... | collective-permute-start | bytes 786440 | tf_op jit(solution)/shard_map/ppermute | solution.py:383
  70.5 16.3 %collective-permute-start.20 = (f32[4,128,128]{2,1,0:T(8,128)S(1)}, f32[4,128,128]{2,1,0:T(8,128)S(1)}, u32[]{:S(2)}, u32[]{:S(2)}) collective-permute-start(f32[4,128,128]{2,1,0:T(8,128)S(1)} %get-tuple-element.128), channel_id=1, source_target_pairs={{0,4},{2,6},{4,0},{6,2},{8,12},{10,14},{12,8},{14,10},{1,5},{3,7},... | collective-permute-start | bytes 786440 | tf_op jit(solution)/shard_map/ppermute | solution.py:383
  77.5 14.5 %collective-permute-start.18 = (f32[4,128,128]{2,1,0:T(8,128)S(1)}, f32[4,128,128]{2,1,0:T(8,128)S(1)}, u32[]{:S(2)}, u32[]{:S(2)}) collective-permute-start(f32[4,128,128]{2,1,0:T(8,128)S(1)} %shard_map.91.refs_0_), channel_id=1, source_target_pairs={{0,1},{1,0},{2,3},{3,2},{4,5},{5,4},{6,7},{7,6},{8,9},{9,8},{10,11... | collective-permute-start | bytes 786440 | tf_op jit(solution)/shard_map/ppermute | solution.py:391
  87.8 8.1 %collective-permute-start.22 = (f32[4,128,128]{2,1,0:T(8,128)S(1)}, f32[4,128,128]{2,1,0:T(8,128)S(1)}, u32[]{:S(2)}, u32[]{:S(2)}) collective-permute-start(f32[4,128,128]{2,1,0:T(8,128)S(1)} %shard_map.93.refs_1_), channel_id=1, source_target_pairs={{0,1},{1,0},{2,3},{3,2},{4,5},{5,4},{6,7},{7,6},{8,9},{9,8},{10,11... | collective-permute-start | bytes 786440 | tf_op jit(solution)/shard_map/ppermute | solution.py:391

commit v7 on v6

--- a/solution.py
+++ b/solution.py
@@ -11,6 +11,7 @@
 HIGHEST = lax.Precision.HIGHEST
 F32 = jnp.float32
 CHUNK = 4
+CUTS = (0, 4, 8)
 GROUP = 8
 
 
@@ -252,43 +253,47 @@
     lax.fori_loop(0, count // 2, body, 0)
 
 
-def left_kernel(tiles, based, place, *refs):
+def left_kernel(tiles, place, *refs):
     pairs = tuple(zip(refs[:tiles], refs[tiles : 2 * tiles]))
-    bases = refs[2 * tiles : 2 * tiles + 2] if based else (None, None)
     rows = refs[-1].shape[0]
     for which, out in enumerate(refs[-2:]):
-        left_rows(pairs, bases[which], out, which * rows, rows, 0)
-
-
-def last_sent_kernel(place, right, d_x, there, out_next, out_last, sent):
+        left_rows(pairs, None, out, which * rows, rows, 0)
+
+
+def last_tile_kernel(step, place, one, two, left_here, left_there, d_here, d_there, w_out, there, out_next, *refs):
+    out_here, out_there, d_x, d_right, right, sent, partial, x = refs
     rows = there.shape[0]
+    right[...] = one[...] + two[...]
+    tile_body(step, place, right, left_here, left_there, d_here, d_there, w_out, out_here, out_there, d_x, d_right, partial, x)
     left_rows(((right, d_x),), there, sent, rows, rows, 0)
     sent[rows] = flat(out_next[...])
-    sent[rows + 1] = flat(out_last[...])
+    sent[rows + 1] = flat(out_there[...])
 
 
 def last_kept_kernel(place, right, d_x, here, kept):
     left_rows(((right, d_x),), here, kept, 0, here.shape[0], 0)
 
 
-def share_kernel(place, kept, received, out_next, out_last, d_left, packed, packed_next):
+def share_kernel(cuts, place, kept, received, out_next, out_last, d_left, *packed):
     half = d_left.shape[0]
-    part, block = half // 2, half * half
+    block = half * half
     d_left[...] = kept[:half] + received[:half]
-    packed[:part] = kept[half : half + part] + received[half : half + part]
-    packed_next[:part] = kept[half + part :] + received[half + part : 2 * half]
+    for first, last, part in zip(cuts, cuts[1:], packed):
+        at = slice(half + first, half + last)
+        part[: last - first] = kept[at] + received[at]
+    early, late = packed[0], packed[-1]
     for step, out in enumerate((out_next, out_last)):
         at = slice(step * block, (step + 1) * block)
         plane = 2 * half + step
-        packed[part, at] = flat(out[half:])
-        packed[part + 1, at] = received[plane, block:]
-        packed_next[part, at] = flat(out[:half])
-        packed_next[part + 1, at] = received[plane, :block]
+        early[early.shape[0] - 2, at] = flat(out[half:])
+        early[early.shape[0] - 1, at] = received[plane, block:]
+        late[late.shape[0] - 2, at] = flat(out[:half])
+        late[late.shape[0] - 1, at] = received[plane, :block]
 
 
 def gather_out(place, rows, t, count, start, out, here, early_other, early_far, received, far):
     half = rows // 2
-    part, block = half // 2, half * half
+    block = half * half
     for far_half in (0, 1):
         source = (t + far_half * half) % rows
         at, wide = slice(source, source + count), slice(source * half, (source + count) * half)
@@ -303,7 +308,7 @@
                         value = early_far[far_core, step, at]
                     else:
                         begin = (step - 2) * block + (t % half) * half
-                        value = far[part + far_core, begin : begin + count * half].reshape(count, half, -1)
+                        value = far[far.shape[0] - 2 + far_core, begin : begin + count * half].reshape(count, half, -1)
                 elif far_core:
                     if step < 2:
                         value = early_other[step, at]
@@ -419,10 +424,10 @@
         sems=4,
     )
     theirs = [other_core(block) for block in sent]
-    other, other_out = lax.optimization_barrier((other, other_out))
     right, open_right, slope_right = call(
         functools.partial(right_kernel, rows), [kept] * 3, (place, normed, keep, mine, other)
     )
+    right, other_out = lax.optimization_barrier((right, other_out))
     near = along(right, NEXT)
     middle = along(right, MIDDLE)
     _, cotangent_late = lax.optimization_barrier((right, cotangent))
@@ -458,78 +463,77 @@
     tile(0, right)
     tile(1, near)
     early_other = other_core(jnp.stack(out_there[:2]))
-    d_left_here, d_left_there = call(
-        functools.partial(left_kernel, 2, False),
-        [(rows, cols, chans)] * 2,
-        (place, *rights[:2], *d_x[:2]),
-    )
-    cross, early_other, d_left_here = lax.optimization_barrier((cross, early_other, d_left_here))
+    cross, early_other, d_x[1] = lax.optimization_barrier((cross, early_other, d_x[1]))
     far = along(cross, OUTWARD)
     early_far = other_half(jnp.stack([jnp.stack(out_here[:2]), early_other]))
     tile(2, cross, outer)
     inward = along(d_right[2], INWARD)
     swapped = along(d_right[2], MIDDLE)
     d_left_here, d_left_there = call(
-        functools.partial(left_kernel, 1, True),
+        functools.partial(left_kernel, 3),
         [(rows, cols, chans)] * 2,
-        (place, rights[2], d_x[2], d_left_here, d_left_there),
+        (place, *rights[:3], *d_x[:3]),
     )
     far, d_left_here = lax.optimization_barrier((far, d_left_here))
-    tile(3, middle, far)
-    (d_left_sent,) = call(
-        last_sent_kernel,
-        [(rows + 2, cols, chans)],
-        (place, rights[3], d_x[3], d_left_there, out_there[2], out_there[3]),
-    )
-    part = half // 2
+    out_here[3], out_there[3], d_x[3], d_right[3], rights[3], d_left_sent = call(
+        functools.partial(last_tile_kernel, 3),
+        tile_outs + [kept, (rows + 2, cols, chans)],
+        (place, middle, far, left, left_there, d_here, d_there, w_all_out, d_left_there, out_there[2]),
+        scratch=tile_scratch,
+    )
+    cuts = [half * eighths // 8 for eighths in CUTS]
+    spans = list(zip(cuts, cuts[1:]))
+    swapped, to_across = lax.optimization_barrier((swapped, d_right[3] + inward))
     to_across, to_near, early_far, d_left_sent = lax.optimization_barrier(
-        (d_right[3] + inward, d_right[1] + swapped, early_far, d_left_sent)
-    )
-    from_across, from_near = [along(to_across[:part], ACROSS)], [along(to_near[:part], NEXT)]
+        (to_across, d_right[1] + swapped, early_far, d_left_sent)
+    )
+    from_across, from_near = [along(to_across[: cuts[1]], ACROSS)], [along(to_near[: cuts[1]], NEXT)]
     received = other_core(d_left_sent)
     _, d_left_here = lax.optimization_barrier((d_left_sent, d_left_here))
     (d_left_kept,) = call(last_kept_kernel, [(rows, cols, chans)], (place, rights[3], d_x[3], d_left_here))
-    packed_shape = (part + 2, cols, chans)
+    sizes = [last - first for first, last in spans]
+    sizes[0] += 2
+    sizes[-1] += 2
     d_left, *packed = call(
-        share_kernel,
-        [kept, packed_shape, packed_shape],
+        functools.partial(share_kernel, cuts),
+        [kept] + [(size, cols, chans) for size in sizes],
         (place, d_left_kept, received, out_here[2], out_here[3]),
     )
     far_parts = [other_half(block) for block in packed]
-    from_across.append(along(to_across[part:], ACROSS))
-    from_across[0], last_near = lax.optimization_barrier((from_across[0], to_near[part:]))
-    from_near.append(along(last_near, NEXT))
+    for first, last in spans[1:]:
+        from_across.append(along(to_across[first:last], ACROSS))
+        from_across[-2], last_near = lax.optimization_barrier((from_across[-2], to_near[first:last]))
+        from_near.append(along(last_near, NEXT))
     outs = (*out_here, early_other, early_far, received)
     mine_parts, other_parts = [], []
-    for at, first in enumerate((0, part)):
+    for at, (first, last) in enumerate(spans):
         (base,) = call(
             functools.partial(base_kernel, rows, first),
-            [(part, cols, width)],
+            [(last - first, cols, width)],
             (place, *outs, far_parts[0], far_parts[at], gate, cotangent, w_gate, d_left, open_left, slope_left, mine, other),
-            scratch=[(part, cols, width)],
+            scratch=[(last - first, cols, width)],
         )
         if at:
-            base, mine_parts[0] = lax.optimization_barrier((base, mine_parts[0]))
+            base, mine_parts[-1] = lax.optimization_barrier((base, mine_parts[-1]))
         (rows_done,) = call(
             functools.partial(pair_kernel, first),
-            [(part, cols, width)],
+            [(last - first, cols, width)],
             (place, normed, scale, base, d_right[0], from_near[at], from_across[at], open_right, slope_right, mine, other),
         )
         mine_parts.append(rows_done)
         other_parts.append(other_half(rows_done))
-    _, gate_late = lax.optimization_barrier((mine_parts[1], gate))
+    _, gate_late = lax.optimization_barrier((mine_parts[-1], gate))
     (update,) = call(
         functools.partial(update_kernel, rows),
         [(rows, cols, width)],
-        (place, *outs, *far_parts, gate_late),
+        (place, *outs, far_parts[0], far_parts[-1], gate_late),
         scratch=[(rows, cols, width)],
     )
-    firsts = (0, part)
-    d_pair = join(mine_parts, firsts, (True, True), pair.shape)
-    other_parts[0], update, d_pair = lax.optimization_barrier((other_parts[0], update, d_pair))
-    d_pair = join(other_parts[:1], firsts[:1], (False,), pair.shape, d_pair)
-    other_parts[1], d_pair = lax.optimization_barrier((other_parts[1], d_pair))
-    d_pair = join(other_parts[1:], firsts[1:], (False,), pair.shape, d_pair)
+    d_pair = join(mine_parts, cuts[:-1], (True,) * len(spans), pair.shape)
+    d_pair, update = lax.optimization_barrier((d_pair, update))
+    for first, part in zip(cuts, other_parts):
+        d_pair, part = lax.optimization_barrier((d_pair, part))
+        d_pair = join([part], (first,), (False,), pair.shape, d_pair)
     return (update, d_pair)
 
 

time: 96.9 us -> 96.2 us (level)
  starting transfers between devices: 33.8 us -> 31.7 us
  waiting for transfers between devices: 21.2 us -> 22.8 us
    ppermute x5, waiting for transfers between devices: 1.63 us -> 2.96 us  [other_core(): lax.ppermute(block, 'row', [(i, i ^ 1) for i in range(lax.axis_size('row'...]
    ppermute x11, starting transfers between devices: 23.1 us -> 21.8 us  [along(): lax.ppermute(block, 'row', [(2 * a + core, 2 * b + core) for a, b in pair...]
    pallas_call x18 -> x16, Pallas kernels: 37.9 us -> 37.9 us  [call(): pl.pallas_call(kernel, out_shape=[jax.ShapeDtypeStruct(shape, F32) for sh...]
  transfers between devices with their start and end apart: 23 -> 23, of which waited for: 8 -> 9; matrix products, arithmetic and copies ran while one was open for 0% -> 0% of each run, Pallas kernels for 41% -> 41%
where the time goes in v7:
time: 96.2 us; the launch traced here: 95.9 us
  Pallas kernels  40.1 us (42%)
  starting transfers between devices  31.7 us (33%)
  waiting for transfers between devices  22.8 us (24%)
  between operations  1 us (1%)
    pallas_call x16, Pallas kernels, call(): pl.pallas_call(kernel, out_shape=[jax.ShapeDtypeStruct(shape, F32) for sh...  37.9 us
    ppermute x11, starting transfers between devices, along(): lax.ppermute(block, 'row', [(2 * a + core, 2 * b + core) for a, b in pair...  21.8 us
    ppermute x11, waiting for transfers between devices, along(): lax.ppermute(block, 'row', [(2 * a + core, 2 * b + core) for a, b in pair...  11.1 us
    ppermute x7, starting transfers between devices, other_half(): return lax.ppermute(block, 'ch', [(0, 1), (1, 0)])  9.11 us
    ppermute x7, waiting for transfers between devices, other_half(): return lax.ppermute(block, 'ch', [(0, 1), (1, 0)])  8.71 us
    ppermute x5, waiting for transfers between devices, other_core(): lax.ppermute(block, 'row', [(i, i ^ 1) for i in range(lax.axis_size('row'...  2.96 us
    pallas_call x3, Pallas kernels, join(): pl.pallas_call(functools.partial(join_kernel, firsts, sides), out_shape=j...  2.24 us
  transfers between devices with their start and end apart: 23, of which 9 were waited for; matrix products, arithmetic and copies ran while one was open for 0% of the time, Pallas kernels for 41%

profile of v7, /device:TPU:0, one launch (start us, length us, event | category | flops | bytes accessed | tf_op | source)
XLA Modules:
  0.0 95.9 jit_solution(17113537325175426650)
XLA Ops:
  0.6 3.0 %collective-permute-start = (f32[256,128]{1,0:T(8,128)}, f32[256,128]{1,0:T(8,128)S(1)}, u32[]{:S(2)}, u32[]{:S(2)}) collective-permute-start(f32[256,128]{1,0:T(8,128)} %bitcast.25), channel_id=1, source_target_pairs={{0,1},{1,0},{2,3},{3,2},{4,5},{5,4},{6,7},{7,6},{8,9},{9,8},{10,11... | collective-permute-start | bytes 393224 | tf_op jit(solution)/shard_map/ppermute | solution.py:396
  3.6 0.1 collective-permute-start.1
  3.7 0.1 pad_add_fusion.place
  3.8 2.2 %shard_map.77 = (f32[8,128,128]{2,1,0:T(8,128)S(1)}, f32[8,128,128]{2,1,0:T(8,128)S(1)}, f32[16,128]{1,0:T(8,128)S(1)}, f32[4,64,128]{2,1,0:T(8,128)S(1)}, f32[8...) custom-call(s32[3]{0:T(128)S(1)} %pad_add_fusion.place, f32[16,128,128]{2,1,0:T(8,128)} %pair.3, s32[16,128]{1,0:T(8,128)} %mask.1, ...), custom_call_target="tpu_custom_call" | custom-call | flops 1000 | bytes 1000 | tf_op jit(solution)/shard_map/pallas_call | solution.py:54
  6.0 0.0 copy-start
  6.0 0.0 copy-start.1
  6.0 0.0 copy-start.2
  6.0 0.1 collective-permute-start.2
  6.1 0.5 collective-permute-start.3
  6.6 1.1 %collective-permute-done = f32[256,128]{1,0:T(8,128)S(1)} collective-permute-done((f32[256,128]{1,0:T(8,128)}, f32[256,128]{1,0:T(8,128)S(1)}, u32[]{:S(2)}, u32[]{:S(2)}) %collective-permute-start) | collective-permute-done | bytes 131104 | tf_op jit(solution)/shard_map/ppermute | solution.py:396
  7.7 1.2 %shard_map.78 = (f32[8,128,128]{2,1,0:T(8,128)S(1)}, f32[8,128,128]{2,1,0:T(8,128)S(1)}, f32[8,128,128]{2,1,0:T(8,128)S(1)}) custom-call(s32[3]{0:T(128)S(1)} %pad_add_fusion.place, f32[8,128,128]{2,1,0:T(8,128)S(1)} %get-tuple-element.70.normed, f32[16,128]{1,0:T(8,128)S(1)} %get-tuple-element.71.keep, f32[4,64,128]{2,1,0:T(8,128)S(1)} %get-tuple-element.72.mine.refs_15_, ...), custom_call_target="tpu_custom_call" | custom-call | flops 1000 | bytes 1000 | tf_op jit(solution)/shard_map/pallas_call | solution.py:54
  8.9 0.0 collective-permute-done.1.other_out
  8.9 1.9 %collective-permute-start.5 = (f32[8,128,128]{2,1,0:T(8,128)S(1)}, f32[8,128,128]{2,1,0:T(8,128)S(1)}, u32[]{:S(2)}, u32[]{:S(2)}) collective-permute-start(f32[8,128,128]{2,1,0:T(8,128)S(1)} %get-tuple-element.74.refs_0_), channel_id=1, source_target_pairs={{0,4},{2,6},{4,0},{6,2},{8,12},{10,14},{12,8},{14,10},{1,5},{3,7},... | collective-permute-start | bytes 1572872 | tf_op jit(solution)/shard_map/ppermute | solution.py:388
  10.8 0.7 collective-permute-start.8
  11.5 1.5 %shard_map.79 = f32[5,16,8,128]{3,2,1,0:T(8,128)S(1)} custom-call(s32[3]{0:T(128)S(1)} %pad_add_fusion.place, f32[16,128,128]{2,1,0:T(8,128)} %refs_10_.3, f32[16,128]{1,0:T(8,128)S(1)} %get-tuple-element.71.keep), custom_call_target="tpu_custom_call" | custom-call | flops 1000 | bytes 1000 | tf_op jit(solution)/shard_map/pallas_call | solution.py:54
  13.0 0.1 collective-permute-start.4
  13.1 1.6 %collective-permute-done.4.third = f32[5,16,8,128]{3,2,1,0:T(8,128)S(1)} collective-permute-done((f32[5,16,8,128]{3,2,1,0:T(8,128)S(1)}, f32[5,16,8,128]{3,2,1,0:T(8,128)S(1)}, u32[]{:S(2)}, u32[]{:S(2)}) %collective-permute-start.4) | collective-permute-done | bytes 327712 | tf_op jit(solution)/shard_map/ppermute | solution.py:392
  14.7 0.0 collective-permute-done.2.first
  14.8 3.8 %shard_map.80 = (f32[16,128,128]{2,1,0:T(8,128)S(1)}, f32[16,128,128]{2,1,0:T(8,128)S(1)}, f32[8,128,128]{2,1,0:T(8,128)S(1)}, f32[8,128,128]{2,1,0:T(8,128)S(1)...) custom-call(s32[3]{0:T(128)S(1)} %pad_add_fusion.place, ...), custom_call_target="tpu_custom_call" | custom-call | flops 1000 | bytes 1000 | tf_op jit(solution)/shard_map/pallas_call | solution.py:54
  18.6 3.5 %collective-permute-done.5.refs_0_.refs_1_ = f32[8,128,128]{2,1,0:T(8,128)S(1)} collective-permute-done((f32[8,128,128]{2,1,0:T(8,128)S(1)}, f32[8,128,128]{2,1,0:T(8,128)S(1)}, u32[]{:S(2)}, u32[]{:S(2)}) %collective-permute-start.5) | collective-permute-done | bytes 524320 | tf_op jit(solution)/shard_map/ppermute | solution.py:388
  22.1 0.7 collective-permute-start.6
  22.8 0.0 collective-permute-done.8.one
  22.8 1.3 %collective-permute-start.9 = (f32[8,128,128]{2,1,0:T(8,128)S(1)}, f32[8,128,128]{2,1,0:T(8,128)S(1)}, u32[]{:S(2)}, u32[]{:S(2)}) collective-permute-start(f32[8,128,128]{2,1,0:T(8,128)S(1)} %collective-permute-done.8.one), channel_id=1, source_target_pairs={{4,0},{6,2},{8,12},{10,14},{5,1},{7,3},{9,13},{11,15},{20,16},{22,... | collective-permute-start | bytes 1572872 | tf_op jit(solution)/shard_map/ppermute | solution.py:388
  24.1 3.8 %shard_map.81 = (f32[16,8,128]{2,1,0:T(8,128)S(1)}, f32[16,8,128]{2,1,0:T(8,128)S(1)}, f32[256,128]{1,0:T(8,128)S(1)}, f32[8,128,128]{2,1,0:T(8,128)S(1)}) custom-call(s32[3]{0:T(128)S(1)} %pad_add_fusion.place, f32[8,128,128]{2,1,0:T(8,128)S(1)} %get-tuple-element.74.refs_0_, f32[16,128,128]{2,1,0:T(8,128)S(1)} %get-tuple-element.79.refs_1_.refs_2_.left_here, ...), custom_call_target="tpu_custom_call" | custom-call | flops 1000 | bytes 1000 | tf_op jit(solution)/shard_map/pallas_call | solution.py:54
  27.9 3.7 %shard_map.82 = (f32[16,8,128]{2,1,0:T(8,128)S(1)}, f32[16,8,128]{2,1,0:T(8,128)S(1)}, f32[256,128]{1,0:T(8,128)S(1)}, f32[8,128,128]{2,1,0:T(8,128)S(1)}) custom-call(s32[3]{0:T(128)S(1)} %pad_add_fusion.place, f32[8,128,128]{2,1,0:T(8,128)S(1)} %collective-permute-done.5.refs_0_.refs_1_, f32[16,128,128]{2,1,0:T(8,128)S(1)} %get-tuple-element.79.refs_1_.refs_2_.left_here, ...), custom_call_target="tpu_custom_call" | custom-call | flops 1000 | bytes 1000 | tf_op jit(solution)/shard_map/pallas_call | solution.py:54
  31.6 0.1 collective-permute-start.7
  31.7 1.3 %collective-permute-done.7.refs_4_ = f32[2,16,8,128]{3,2,1,0:T(8,128)S(1)} collective-permute-done((f32[2,16,8,128]{3,2,1,0:T(8,128)S(1)}, f32[2,16,8,128]{3,2,1,0:T(8,128)S(1)}, u32[]{:S(2)}, u32[]{:S(2)}) %collective-permute-start.7) | collective-permute-done | bytes 131104 | tf_op jit(solution)/shard_map/ppermute | solution.py:392
  33.1 0.0 collective-permute-done.6.refs_0_
  33.1 1.3 %collective-permute-start.10 = (f32[8,128,128]{2,1,0:T(8,128)S(1)}, f32[8,128,128]{2,1,0:T(8,128)S(1)}, u32[]{:S(2)}, u32[]{:S(2)}) collective-permute-start(f32[8,128,128]{2,1,0:T(8,128)S(1)} %collective-permute-done.6.refs_0_), channel_id=1, source_target_pairs={{4,0},{6,2},{8,12},{10,14},{5,1},{7,3},{9,13},{11,15},{20,16},{22,... | collective-permute-start | bytes 1572872 | tf_op jit(solution)/shard_map/ppermute | solution.py:388
  34.3 4.4 %collective-permute-done.9.refs_1_ = f32[8,128,128]{2,1,0:T(8,128)S(1)} collective-permute-done((f32[8,128,128]{2,1,0:T(8,128)S(1)}, f32[8,128,128]{2,1,0:T(8,128)S(1)}, u32[]{:S(2)}, u32[]{:S(2)}) %collective-permute-start.9) | collective-permute-done | bytes 524320 | tf_op jit(solution)/shard_map/ppermute | solution.py:388
  38.7 3.8 %shard_map.83 = (f32[16,8,128]{2,1,0:T(8,128)S(1)}, f32[16,8,128]{2,1,0:T(8,128)S(1)}, f32[256,128]{1,0:T(8,128)S(1)}, f32[8,128,128]{2,1,0:T(8,128)S(1)}, f32[8,128,128]{2,1,0:T(8,128)S(1)}) custom-call(s32[3]{0:T(128)S(1)} %pad_add_fusion.place, f32[8,128,128]{2,1,0:T(8,128)S(1)} %collective-permute-done.6.refs_0_, ...), custom_call_target="tpu_custom_call" | custom-call | flops 1000 | bytes 1000 | tf_op jit(solution)/shard_map/pallas_call | solution.py:54
  42.6 3.4 %collective-permute-start.12 = (f32[8,128,128]{2,1,0:T(8,128)S(1)}, f32[8,128,128]{2,1,0:T(8,128)S(1)}, u32[]{:S(2)}, u32[]{:S(2)}) collective-permute-start(f32[8,128,128]{2,1,0:T(8,128)S(1)} %get-tuple-element.103), channel_id=1, source_target_pairs={{0,4},{2,6},{12,8},{14,10},{1,5},{3,7},{13,9},{15,11},{16,20},{18,... | collective-permute-start | bytes 1572872 | tf_op jit(solution)/shard_map/ppermute | solution.py:388
  45.9 0.7 collective-permute-start.11
  46.7 1.6 %collective-permute-start.13 = (f32[2,2,16,8,128]{4,3,2,1,0:T(8,128)S(1)}, f32[2,2,16,8,128]{4,3,2,1,0:T(8,128)S(1)}, u32[]{:S(2)}, u32[]{:S(2)}) collective-permute-start(f32[2,2,16,8,128]{4,3,2,1,0:T(8,128)S(1)} %pad_maximum_fusion), channel_id=1, source_target_pairs={{0,1},{1,0},{2,3},{3,2},{4,5},{5,4},{6,7},{7,6},{8,9},{9,8},{10,11... | collective-permute-start | bytes 786440 | tf_op jit(solution)/shard_map/ppermute | solution.py:396
  48.2 4.8 %shard_map.84 = (f32[16,128,128]{2,1,0:T(8,128)S(1)}, f32[16,128,128]{2,1,0:T(8,128)S(1)}) custom-call(s32[3]{0:T(128)S(1)} %pad_add_fusion.place, f32[8,128,128]{2,1,0:T(8,128)S(1)} %get-tuple-element.74.refs_0_, f32[8,128,128]{2,1,0:T(8,128)S(1)} %collective-permute-done.5.refs_0_.refs_1_, f32[8,128,128]{2,1,0:T(8,128)S(1)} %get-tuple-element.93.refs_2_, ...), custom_call_target="tpu_custom_call" | custom-call | flops 1000 | bytes 1000 | tf_op jit(solution)/shard_map/pallas_call | solution.py:54
  53.0 0.0 collective-permute-done.10.two
  53.0 5.1 %shard_map.85 = (f32[16,8,128]{2,1,0:T(8,128)S(1)}, f32[16,8,128]{2,1,0:T(8,128)}, f32[256,128]{1,0:T(8,128)S(1)}, f32[8,128,128]{2,1,0:T(8,128)S(1)}, f32[8,128...) custom-call(s32[3]{0:T(128)S(1)} %pad_add_fusion.place, f32[8,128,128]{2,1,0:T(8,128)S(1)} %collective-permute-done.8.one, ...), custom_call_target="tpu_custom_call" | custom-call | flops 1000 | bytes 1000 | tf_op jit(solution)/shard_map/pallas_call | solution.py:54
  58.1 0.1 add.12
  58.2 0.1 add.13
  58.3 0.1 collective-permute-start.14
  58.4 2.0 %collective-permute-start.18 = (f32[4,128,128]{2,1,0:T(8,128)S(1)}, f32[4,128,128]{2,1,0:T(8,128)S(1)}, u32[]{:S(2)}, u32[]{:S(2)}) collective-permute-start(f32[4,128,128]{2,1,0:T(8,128)S(1)} %get-tuple-element.139), channel_id=1, source_target_pairs={{0,12},{2,14},{12,0},{14,2},{4,8},{6,10},{8,4},{10,6},{1,13},{3,15... | collective-permute-start | bytes 786440 | tf_op jit(solution)/shard_map/ppermute | solution.py:388
  60.4 1.2 %shard_map.86.kept = f32[16,128,128]{2,1,0:T(8,128)S(1)} custom-call(s32[3]{0:T(128)S(1)} %pad_add_fusion.place, f32[8,128,128]{2,1,0:T(8,128)S(1)} %get-tuple-element.111.right, f32[256,128]{1,0:T(8,128)S(1)} %get-tuple-element.112.d_x, f32[16,128,128]{2,1,0:T(8,128)S(1)} %get-tuple-element.114.here), custom_call_target="tpu_custom_call" | custom-call | flops 1000 | bytes 1000 | tf_op jit(solution)/shard_map/pallas_call | solution.py:54
  61.7 0.7 shard_map.87
  62.3 0.6 collective-permute-start.15
  62.9 1.5 %collective-permute-start.16 = (f32[6,128,128]{2,1,0:T(8,128)S(1)}, f32[6,128,128]{2,1,0:T(8,128)S(1)}, u32[]{:S(2)}, u32[]{:S(2)}) collective-permute-start(f32[6,128,128]{2,1,0:T(8,128)S(1)} %get-tuple-element.116), channel_id=1, source_target_pairs={{0,1},{1,0},{2,3},{3,2},{4,5},{5,4},{6,7},{7,6},{8,9},{9,8},{10,11... | collective-permute-start | bytes 1179656 | tf_op jit(solution)/shard_map/ppermute | solution.py:396
  64.5 1.4 %collective-permute-start.17 = (f32[4,128,128]{2,1,0:T(8,128)S(1)}, f32[4,128,128]{2,1,0:T(8,128)S(1)}, u32[]{:S(2)}, u32[]{:S(2)}) collective-permute-start(f32[4,128,128]{2,1,0:T(8,128)S(1)} %get-tuple-element.141), channel_id=1, source_target_pairs={{0,4},{2,6},{4,0},{6,2},{8,12},{10,14},{12,8},{14,10},{1,5},{3,7},... | collective-permute-start | bytes 786440 | tf_op jit(solution)/shard_map/ppermute | solution.py:388
  65.9 2.4 %collective-permute-start.20 = (f32[4,128,128]{2,1,0:T(8,128)S(1)}, f32[4,128,128]{2,1,0:T(8,128)S(1)}, u32[]{:S(2)}, u32[]{:S(2)}) collective-permute-start(f32[4,128,128]{2,1,0:T(8,128)S(1)} %get-tuple-element.138), channel_id=1, source_target_pairs={{0,12},{2,14},{12,0},{14,2},{4,8},{6,10},{8,4},{10,6},{1,13},{3,15... | collective-permute-start | bytes 786440 | tf_op jit(solution)/shard_map/ppermute | solution.py:388
  68.3 1.1 %collective-permute-done.18.d_right_across = f32[4,128,128]{2,1,0:T(8,128)S(1)} collective-permute-done((f32[4,128,128]{2,1,0:T(8,128)S(1)}, f32[4,128,128]{2,1,0:T(8,128)S(1)}, u32[]{:S(2)}, u32[]{:S(2)}) %collective-permute-start.18) | collective-permute-done | bytes 262176 | tf_op jit(solution)/shard_map/ppermute | solution.py:388
  69.4 6.1 %collective-permute-start.19 = (f32[4,128,128]{2,1,0:T(8,128)S(1)}, f32[4,128,128]{2,1,0:T(8,128)S(1)}, u32[]{:S(2)}, u32[]{:S(2)}) collective-permute-start(f32[4,128,128]{2,1,0:T(8,128)S(1)} %get-tuple-element.130), channel_id=1, source_target_pairs={{0,4},{2,6},{4,0},{6,2},{8,12},{10,14},{12,8},{14,10},{1,5},{3,7},... | collective-permute-start | bytes 786440 | tf_op jit(solution)/shard_map/ppermute | solution.py:388
  75.5 0.0 collective-permute-done.15.refs_7_.refs_8_
  75.5 1.1 %shard_map.89.base = f32[4,128,128]{2,1,0:T(8,128)S(1)} custom-call(s32[3]{0:T(128)S(1)} %pad_add_fusion.place, f32[16,8,128]{2,1,0:T(8,128)S(1)} %get-tuple-element.85.refs_0_, f32[16,8,128]{2,1,0:T(8,128)S(1)} %get-tuple-element.87.refs_1_, f32[16,8,128]{2,1,0:T(8,128)S(1)} %get-tuple-element.92.out_next.refs_2_, ...), custom_call_target="tpu_custom_call" | custom-call | flops 1000 | bytes 1000 | tf_op jit(solution)/shard_map/pallas_call | solution.py:54
  76.6 1.0 %shard_map.90.refs_0_ = f32[4,128,128]{2,1,0:T(8,128)S(1)} custom-call(s32[3]{0:T(128)S(1)} %pad_add_fusion.place, f32[8,128,128]{2,1,0:T(8,128)S(1)} %get-tuple-element.70.normed, f32[8,128,128]{2,1,0:T(8,128)S(1)} %get-tuple-element.121.scale, f32[4,128,128]{2,1,0:T(8,128)S(1)} %shard_map.89.base, f32[8,128,128]{2,1,0:T(8,128)S(1)} %get-tuple-element.122.d_right, ...), custom_call_target="tpu_custom_call" | custom-call | flops 1000 | bytes 1000 | tf_op jit(solution)/shard_map/pallas_call | solution.py:54
  77.7 1.4 %collective-permute-start.21 = (f32[4,128,128]{2,1,0:T(8,128)S(1)}, f32[4,128,128]{2,1,0:T(8,128)S(1)}, u32[]{:S(2)}, u32[]{:S(2)}) collective-permute-start(f32[4,128,128]{2,1,0:T(8,128)S(1)} %shard_map.90.refs_0_), channel_id=1, source_target_pairs={{0,1},{1,0},{2,3},{3,2},{4,5},{5,4},{6,7},{7,6},{8,9},{9,8},{10,11... | collective-permute-start | bytes 786440 | tf_op jit(solution)/shard_map/ppermute | solution.py:396
  79.0 3.7 %collective-permute-done.16.refs_8_ = f32[6,128,128]{2,1,0:T(8,128)S(1)} collective-permute-done((f32[6,128,128]{2,1,0:T(8,128)S(1)}, f32[6,128,128]{2,1,0:T(8,128)S(1)}, u32[]{:S(2)}, u32[]{:S(2)}) %collective-permute-start.16) | collective-permute-done | bytes 393248 | tf_op jit(solution)/shard_map/ppermute | solution.py:396
  82.8 1.1 %shard_map.88.base = f32[4,128,128]{2,1,0:T(8,128)S(1)} custom-call(s32[3]{0:T(128)S(1)} %pad_add_fusion.place, f32[16,8,128]{2,1,0:T(8,128)S(1)} %get-tuple-element.85.refs_0_, f32[16,8,128]{2,1,0:T(8,128)S(1)} %get-tuple-element.87.refs_1_, f32[16,8,128]{2,1,0:T(8,128)S(1)} %get-tuple-element.92.out_next.refs_2_, ...), custom_call_target="tpu_custom_call" | custom-call | flops 1000 | bytes 1000 | tf_op jit(solution)/shard_map/pallas_call | solution.py:54
  83.9 0.0 collective-permute-done.20.d_right_across
  83.9 2.1 %collective-permute-done.19.d_right_near = f32[4,128,128]{2,1,0:T(8,128)S(1)} collective-permute-done((f32[4,128,128]{2,1,0:T(8,128)S(1)}, f32[4,128,128]{2,1,0:T(8,128)S(1)}, u32[]{:S(2)}, u32[]{:S(2)}) %collective-permute-start.19) | collective-permute-done | bytes 262176 | tf_op jit(solution)/shard_map/ppermute | solution.py:388
  85.9 1.0 %shard_map.91.refs_1_ = f32[4,128,128]{2,1,0:T(8,128)S(1)} custom-call(s32[3]{0:T(128)S(1)} %pad_add_fusion.place, f32[8,128,128]{2,1,0:T(8,128)S(1)} %get-tuple-element.70.normed, f32[8,128,128]{2,1,0:T(8,128)S(1)} %get-tuple-element.121.scale, f32[4,128,128]{2,1,0:T(8,128)S(1)} %shard_map.88.base, f32[8,128,128]{2,1,0:T(8,128)S(1)} %get-tuple-element.122.d_right, ...), custom_call_target="tpu_custom_call" | custom-call | flops 1000 | bytes 1000 | tf_op jit(solution)/shard_map/pallas_call | solution.py:54
  87.0 1.0 %collective-permute-start.22 = (f32[4,128,128]{2,1,0:T(8,128)S(1)}, f32[4,128,128]{2,1,0:T(8,128)S(1)}, u32[]{:S(2)}, u32[]{:S(2)}) collective-permute-start(f32[4,128,128]{2,1,0:T(8,128)S(1)} %shard_map.91.refs_1_), channel_id=1, source_target_pairs={{0,1},{1,0},{2,3},{3,2},{4,5},{5,4},{6,7},{7,6},{8,9},{9,8},{10,11... | collective-permute-start | bytes 786440 | tf_op jit(solution)/shard_map/ppermute | solution.py:396
  88.0 1.8 %shard_map.93 = f32[16,128,128]{2,1,0:T(8,128)} custom-call(s32[3]{0:T(128)S(1)} %pad_add_fusion.place, f32[16,8,128]{2,1,0:T(8,128)S(1)} %get-tuple-element.85.refs_0_, f32[16,8,128]{2,1,0:T(8,128)S(1)} %get-tuple-element.87.refs_1_, f32[16,8,128]{2,1,0:T(8,128)S(1)} %get-tuple-element.92.out_next.refs_2_, ...), custom_call_target="tpu_custom_call" | custom-call | flops 1000 | bytes 1000 | tf_op jit(solution)/shard_map/pallas_call | solution.py:54
  89.8 0.8 shard_map.92.refs_1_
  90.6 0.7 shard_map.94.refs_1_
  91.3 3.9 %collective-permute-done.22.refs_0_ = f32[4,128,128]{2,1,0:T(8,128)S(1)} collective-permute-done((f32[4,128,128]{2,1,0:T(8,128)S(1)}, f32[4,128,128]{2,1,0:T(8,128)S(1)}, u32[]{:S(2)}, u32[]{:S(2)}) %collective-permute-start.22) | collective-permute-done | bytes 262176 | tf_op jit(solution)/shard_map/ppermute | solution.py:396
  95.2 0.7 shard_map.95
  (17 shorter events, 0.1 us)
Async XLA Ops:
  0.6 7.1 %collective-permute-start = (f32[256,128]{1,0:T(8,128)}, f32[256,128]{1,0:T(8,128)S(1)}, u32[]{:S(2)}, u32[]{:S(2)}) collective-permute-start(f32[256,128]{1,0:T(8,128)} %bitcast.25), channel_id=1, source_target_pairs={{0,1},{1,0},{2,3},{3,2},{4,5},{5,4},{6,7},{7,6},{8,9},{9,8},{10,11... | collective-permute-start | bytes 393224 | tf_op jit(solution)/shard_map/ppermute | solution.py:396
  3.6 5.3 %collective-permute-start.1 = (f32[64,128]{1,0:T(8,128)}, f32[64,128]{1,0:T(8,128)S(1)}, u32[]{:S(2)}, u32[]{:S(2)}) collective-permute-start(f32[64,128]{1,0:T(8,128)} %mine_out.1), channel_id=1, source_target_pairs={{0,1},{1,0},{2,3},{3,2},{4,5},{5,4},{6,7},{7,6},{8,9},{9,8},{10,11... | collective-permute-start | bytes 98312 | tf_op jit(solution)/shard_map/ppermute | solution.py:396
  3.8 10.9 %copy-start.3 = (f32[64,128]{1,0:T(8,128)S(1)}, f32[64,128]{1,0:T(8,128)}, u32[]{:S(2)}) copy-start(f32[64,128]{1,0:T(8,128)} %mine_out.1) | copy-start | bytes 98308
  6.0 8.7 %copy-start = (f32[16,128,128]{2,1,0:T(8,128)S(1)}, f32[16,128,128]{2,1,0:T(8,128)}, u32[]{:S(2)}) copy-start(f32[16,128,128]{2,1,0:T(8,128)} %refs_10_.3) | copy-start | bytes 3145732
  6.0 8.7 %copy-start.1 = (f32[16,128,128]{2,1,0:T(8,128)S(1)}, f32[16,128,128]{2,1,0:T(8,128)}, u32[]{:S(2)}) copy-start(f32[16,128,128]{2,1,0:T(8,128)} %pair.3) | copy-start | bytes 3145732
  6.0 8.7 %copy-start.2 = (f32[128,128]{1,0:T(8,128)S(1)}, f32[128,128]{1,0:T(8,128)}, u32[]{:S(2)}) copy-start(f32[128,128]{1,0:T(8,128)} %refs_11_.3) | copy-start | bytes 196612
  6.0 8.7 %collective-permute-start.2 = (f32[8,128,128]{2,1,0:T(8,128)S(1)}, f32[8,128,128]{2,1,0:T(8,128)S(1)}, u32[]{:S(2)}, u32[]{:S(2)}) collective-permute-start(f32[8,128,128]{2,1,0:T(8,128)S(1)} %get-tuple-element.75), channel_id=1, source_target_pairs={{0,2},{2,0},{4,6},{6,4},{8,10},{10,8},{12,14},{14,12},{1,3},{3,1},... | collective-permute-start | bytes 1572872 | tf_op jit(solution)/shard_map/ppermute | solution.py:392
  6.1 8.6 %collective-permute-start.3 = (f32[8,128,128]{2,1,0:T(8,128)S(1)}, f32[8,128,128]{2,1,0:T(8,128)S(1)}, u32[]{:S(2)}, u32[]{:S(2)}) collective-permute-start(f32[8,128,128]{2,1,0:T(8,128)S(1)} %get-tuple-element.76), channel_id=1, source_target_pairs={{0,2},{2,0},{4,6},{6,4},{8,10},{10,8},{12,14},{14,12},{1,3},{3,1},... | collective-permute-start | bytes 1572872 | tf_op jit(solution)/shard_map/ppermute | solution.py:392
  8.9 13.2 %collective-permute-start.5 = (f32[8,128,128]{2,1,0:T(8,128)S(1)}, f32[8,128,128]{2,1,0:T(8,128)S(1)}, u32[]{:S(2)}, u32[]{:S(2)}) collective-permute-start(f32[8,128,128]{2,1,0:T(8,128)S(1)} %get-tuple-element.74.refs_0_), channel_id=1, source_target_pairs={{0,4},{2,6},{4,0},{6,2},{8,12},{10,14},{12,8},{14,10},{1,5},{3,7},... | collective-permute-start | bytes 1572872 | tf_op jit(solution)/shard_map/ppermute | solution.py:388
  10.8 12.0 %collective-permute-start.8 = (f32[8,128,128]{2,1,0:T(8,128)S(1)}, f32[8,128,128]{2,1,0:T(8,128)S(1)}, u32[]{:S(2)}, u32[]{:S(2)}) collective-permute-start(f32[8,128,128]{2,1,0:T(8,128)S(1)} %get-tuple-element.74.refs_0_), channel_id=1, source_target_pairs={{4,8},{6,10},{8,4},{10,6},{5,9},{7,11},{9,5},{11,7},{20,24},{22,26... | collective-permute-start | bytes 1572872 | tf_op jit(solution)/shard_map/ppermute | solution.py:388
  13.0 1.7 %collective-permute-start.4 = (f32[5,16,8,128]{3,2,1,0:T(8,128)S(1)}, f32[5,16,8,128]{3,2,1,0:T(8,128)S(1)}, u32[]{:S(2)}, u32[]{:S(2)}) collective-permute-start(f32[5,16,8,128]{3,2,1,0:T(8,128)S(1)} %shard_map.79), channel_id=1, source_target_pairs={{0,2},{2,0},{4,6},{6,4},{8,10},{10,8},{12,14},{14,12},{1,3},{3,1},... | collective-permute-start | bytes 983048 | tf_op jit(solution)/shard_map/ppermute | solution.py:392
  22.1 10.9 %collective-permute-start.6 = (f32[8,128,128]{2,1,0:T(8,128)S(1)}, f32[8,128,128]{2,1,0:T(8,128)S(1)}, u32[]{:S(2)}, u32[]{:S(2)}) collective-permute-start(f32[8,128,128]{2,1,0:T(8,128)S(1)} %collective-permute-done.5.refs_0_.refs_1_), channel_id=1, source_target_pairs={{4,8},{6,10},{8,4},{10,6},{5,9},{7,11},{9,5},{11,7},{20,24},{22,26... | collective-permute-start | bytes 1572872 | tf_op jit(solution)/shard_map/ppermute | solution.py:388
  22.8 15.9 %collective-permute-start.9 = (f32[8,128,128]{2,1,0:T(8,128)S(1)}, f32[8,128,128]{2,1,0:T(8,128)S(1)}, u32[]{:S(2)}, u32[]{:S(2)}) collective-permute-start(f32[8,128,128]{2,1,0:T(8,128)S(1)} %collective-permute-done.8.one), channel_id=1, source_target_pairs={{4,0},{6,2},{8,12},{10,14},{5,1},{7,3},{9,13},{11,15},{20,16},{22,... | collective-permute-start | bytes 1572872 | tf_op jit(solution)/shard_map/ppermute | solution.py:388
  31.6 1.4 %collective-permute-start.7 = (f32[2,16,8,128]{3,2,1,0:T(8,128)S(1)}, f32[2,16,8,128]{3,2,1,0:T(8,128)S(1)}, u32[]{:S(2)}, u32[]{:S(2)}) collective-permute-start(f32[2,16,8,128]{3,2,1,0:T(8,128)S(1)} %pad_maximum_fusion.1), channel_id=1, source_target_pairs={{0,2},{2,0},{4,6},{6,4},{8,10},{10,8},{12,14},{14,12},{1,3},{3,1},... | collective-permute-start | bytes 393224 | tf_op jit(solution)/shard_map/ppermute | solution.py:392
  33.1 19.9 %collective-permute-start.10 = (f32[8,128,128]{2,1,0:T(8,128)S(1)}, f32[8,128,128]{2,1,0:T(8,128)S(1)}, u32[]{:S(2)}, u32[]{:S(2)}) collective-permute-start(f32[8,128,128]{2,1,0:T(8,128)S(1)} %collective-permute-done.6.refs_0_), channel_id=1, source_target_pairs={{4,0},{6,2},{8,12},{10,14},{5,1},{7,3},{9,13},{11,15},{20,16},{22,... | collective-permute-start | bytes 1572872 | tf_op jit(solution)/shard_map/ppermute | solution.py:388
  42.6 15.6 %collective-permute-start.12 = (f32[8,128,128]{2,1,0:T(8,128)S(1)}, f32[8,128,128]{2,1,0:T(8,128)S(1)}, u32[]{:S(2)}, u32[]{:S(2)}) collective-permute-start(f32[8,128,128]{2,1,0:T(8,128)S(1)} %get-tuple-element.103), channel_id=1, source_target_pairs={{0,4},{2,6},{12,8},{14,10},{1,5},{3,7},{13,9},{15,11},{16,20},{18,... | collective-permute-start | bytes 1572872 | tf_op jit(solution)/shard_map/ppermute | solution.py:388
  45.9 12.3 %collective-permute-start.11 = (f32[8,128,128]{2,1,0:T(8,128)S(1)}, f32[8,128,128]{2,1,0:T(8,128)S(1)}, u32[]{:S(2)}, u32[]{:S(2)}) collective-permute-start(f32[8,128,128]{2,1,0:T(8,128)S(1)} %get-tuple-element.103), channel_id=1, source_target_pairs={{4,8},{6,10},{8,4},{10,6},{5,9},{7,11},{9,5},{11,7},{20,24},{22,26... | collective-permute-start | bytes 1572872 | tf_op jit(solution)/shard_map/ppermute | solution.py:388
  46.7 11.6 %collective-permute-start.13 = (f32[2,2,16,8,128]{4,3,2,1,0:T(8,128)S(1)}, f32[2,2,16,8,128]{4,3,2,1,0:T(8,128)S(1)}, u32[]{:S(2)}, u32[]{:S(2)}) collective-permute-start(f32[2,2,16,8,128]{4,3,2,1,0:T(8,128)S(1)} %pad_maximum_fusion), channel_id=1, source_target_pairs={{0,1},{1,0},{2,3},{3,2},{4,5},{5,4},{6,7},{7,6},{8,9},{9,8},{10,11... | collective-permute-start | bytes 786440 | tf_op jit(solution)/shard_map/ppermute | solution.py:396
  58.3 3.4 %collective-permute-start.14 = (f32[18,128,128]{2,1,0:T(8,128)S(1)}, f32[18,128,128]{2,1,0:T(8,128)S(1)}, u32[]{:S(2)}, u32[]{:S(2)}) collective-permute-start(f32[18,128,128]{2,1,0:T(8,128)S(1)} %get-tuple-element.110), channel_id=1, source_target_pairs={{0,2},{2,0},{4,6},{6,4},{8,10},{10,8},{12,14},{14,12},{1,3},{3,1},... | collective-permute-start | bytes 3538952 | tf_op jit(solution)/shard_map/ppermute | solution.py:392
  58.4 11.0 %collective-permute-start.18 = (f32[4,128,128]{2,1,0:T(8,128)S(1)}, f32[4,128,128]{2,1,0:T(8,128)S(1)}, u32[]{:S(2)}, u32[]{:S(2)}) collective-permute-start(f32[4,128,128]{2,1,0:T(8,128)S(1)} %get-tuple-element.139), channel_id=1, source_target_pairs={{0,12},{2,14},{12,0},{14,2},{4,8},{6,10},{8,4},{10,6},{1,13},{3,15... | collective-permute-start | bytes 786440 | tf_op jit(solution)/shard_map/ppermute | solution.py:388
  62.3 13.2 %collective-permute-start.15 = (f32[6,128,128]{2,1,0:T(8,128)S(1)}, f32[6,128,128]{2,1,0:T(8,128)S(1)}, u32[]{:S(2)}, u32[]{:S(2)}) collective-permute-start(f32[6,128,128]{2,1,0:T(8,128)S(1)} %get-tuple-element.115), channel_id=1, source_target_pairs={{0,1},{1,0},{2,3},{3,2},{4,5},{5,4},{6,7},{7,6},{8,9},{9,8},{10,11... | collective-permute-start | bytes 1179656 | tf_op jit(solution)/shard_map/ppermute | solution.py:396
  62.9 19.9 %collective-permute-start.16 = (f32[6,128,128]{2,1,0:T(8,128)S(1)}, f32[6,128,128]{2,1,0:T(8,128)S(1)}, u32[]{:S(2)}, u32[]{:S(2)}) collective-permute-start(f32[6,128,128]{2,1,0:T(8,128)S(1)} %get-tuple-element.116), channel_id=1, source_target_pairs={{0,1},{1,0},{2,3},{3,2},{4,5},{5,4},{6,7},{7,6},{8,9},{9,8},{10,11... | collective-permute-start | bytes 1179656 | tf_op jit(solution)/shard_map/ppermute | solution.py:396
  64.5 12.2 %collective-permute-start.17 = (f32[4,128,128]{2,1,0:T(8,128)S(1)}, f32[4,128,128]{2,1,0:T(8,128)S(1)}, u32[]{:S(2)}, u32[]{:S(2)}) collective-permute-start(f32[4,128,128]{2,1,0:T(8,128)S(1)} %get-tuple-element.141), channel_id=1, source_target_pairs={{0,4},{2,6},{4,0},{6,2},{8,12},{10,14},{12,8},{14,10},{1,5},{3,7},... | collective-permute-start | bytes 786440 | tf_op jit(solution)/shard_map/ppermute | solution.py:388
  65.9 18.0 %collective-permute-start.20 = (f32[4,128,128]{2,1,0:T(8,128)S(1)}, f32[4,128,128]{2,1,0:T(8,128)S(1)}, u32[]{:S(2)}, u32[]{:S(2)}) collective-permute-start(f32[4,128,128]{2,1,0:T(8,128)S(1)} %get-tuple-element.138), channel_id=1, source_target_pairs={{0,12},{2,14},{12,0},{14,2},{4,8},{6,10},{8,4},{10,6},{1,13},{3,15... | collective-permute-start | bytes 786440 | tf_op jit(solution)/shard_map/ppermute | solution.py:388
  69.4 16.5 %collective-permute-start.19 = (f32[4,128,128]{2,1,0:T(8,128)S(1)}, f32[4,128,128]{2,1,0:T(8,128)S(1)}, u32[]{:S(2)}, u32[]{:S(2)}) collective-permute-start(f32[4,128,128]{2,1,0:T(8,128)S(1)} %get-tuple-element.130), channel_id=1, source_target_pairs={{0,4},{2,6},{4,0},{6,2},{8,12},{10,14},{12,8},{14,10},{1,5},{3,7},... | collective-permute-start | bytes 786440 | tf_op jit(solution)/shard_map/ppermute | solution.py:388
  77.7 12.9 %collective-permute-start.21 = (f32[4,128,128]{2,1,0:T(8,128)S(1)}, f32[4,128,128]{2,1,0:T(8,128)S(1)}, u32[]{:S(2)}, u32[]{:S(2)}) collective-permute-start(f32[4,128,128]{2,1,0:T(8,128)S(1)} %shard_map.90.refs_0_), channel_id=1, source_target_pairs={{0,1},{1,0},{2,3},{3,2},{4,5},{5,4},{6,7},{7,6},{8,9},{9,8},{10,11... | collective-permute-start | bytes 786440 | tf_op jit(solution)/shard_map/ppermute | solution.py:396
  87.0 8.2 %collective-permute-start.22 = (f32[4,128,128]{2,1,0:T(8,128)S(1)}, f32[4,128,128]{2,1,0:T(8,128)S(1)}, u32[]{:S(2)}, u32[]{:S(2)}) collective-permute-start(f32[4,128,128]{2,1,0:T(8,128)S(1)} %shard_map.91.refs_1_), channel_id=1, source_target_pairs={{0,1},{1,0},{2,3},{3,2},{4,5},{5,4},{6,7},{7,6},{8,9},{9,8},{10,11... | collective-permute-start | bytes 786440 | tf_op jit(solution)/shard_map/ppermute | solution.py:396

commit v8 on v7

--- a/solution.py
+++ b/solution.py
@@ -253,11 +253,12 @@
     lax.fori_loop(0, count // 2, body, 0)
 
 
-def left_kernel(tiles, place, *refs):
+def left_kernel(tiles, based, place, *refs):
     pairs = tuple(zip(refs[:tiles], refs[tiles : 2 * tiles]))
+    bases = refs[2 * tiles : 2 * tiles + 2] if based else (None, None)
     rows = refs[-1].shape[0]
     for which, out in enumerate(refs[-2:]):
-        left_rows(pairs, None, out, which * rows, rows, 0)
+        left_rows(pairs, bases[which], out, which * rows, rows, 0)
 
 
 def last_tile_kernel(step, place, one, two, left_here, left_there, d_here, d_there, w_out, there, out_next, *refs):
@@ -463,16 +464,19 @@
     tile(0, right)
     tile(1, near)
     early_other = other_core(jnp.stack(out_there[:2]))
-    cross, early_other, d_x[1] = lax.optimization_barrier((cross, early_other, d_x[1]))
+    d_left_here, d_left_there = call(
+        functools.partial(left_kernel, 1, False), [(rows, cols, chans)] * 2, (place, rights[0], d_x[0])
+    )
+    cross, early_other, d_left_here = lax.optimization_barrier((cross, early_other, d_left_here))
     far = along(cross, OUTWARD)
     early_far = other_half(jnp.stack([jnp.stack(out_here[:2]), early_other]))
     tile(2, cross, outer)
     inward = along(d_right[2], INWARD)
     swapped = along(d_right[2], MIDDLE)
     d_left_here, d_left_there = call(
-        functools.partial(left_kernel, 3),
+        functools.partial(left_kernel, 2, True),
         [(rows, cols, chans)] * 2,
-        (place, *rights[:3], *d_x[:3]),
+        (place, *rights[1:3], *d_x[1:3], d_left_here, d_left_there),
     )
     far, d_left_here = lax.optimization_barrier((far, d_left_here))
     out_here[3], out_there[3], d_x[3], d_right[3], rights[3], d_left_sent = call(
@@ -501,9 +505,9 @@
     )
     far_parts = [other_half(block) for block in packed]
     for first, last in spans[1:]:
-        from_across.append(along(to_across[first:last], ACROSS))
-        from_across[-2], last_near = lax.optimization_barrier((from_across[-2], to_near[first:last]))
-        from_near.append(along(last_near, NEXT))
+        from_near.append(along(to_near[first:last], NEXT))
+        from_across[-1], last_across = lax.optimization_barrier((from_across[-1], to_across[first:last]))
+        from_across.append(along(last_across, ACROSS))
     outs = (*out_here, early_other, early_far, received)
     mine_parts, other_parts = [], []
     for at, (first, last) in enumerate(spans):

time: 96.2 us -> 95.2 us (0.990)
  starting transfers between devices: 31.7 us -> 28.2 us
  waiting for transfers between devices: 22.8 us -> 24.4 us
    ppermute x11, starting transfers between devices: 21.8 us -> 17.6 us  [along(): lax.ppermute(block, 'row', [(2 * a + core, 2 * b + core) for a, b in pair...]
    ppermute x7, waiting for transfers between devices: 8.71 us -> 11.2 us  [other_half(): return lax.ppermute(block, 'ch', [(0, 1), (1, 0)])]
    ppermute x5, waiting for transfers between devices: 2.96 us -> 1.63 us  [other_core(): lax.ppermute(block, 'row', [(i, i ^ 1) for i in range(lax.axis_size('row'...]
    pallas_call x16 -> x17, Pallas kernels: 37.9 us -> 38.7 us  [call(): pl.pallas_call(kernel, out_shape=[jax.ShapeDtypeStruct(shape, F32) for sh...]
  transfers between devices with their start and end apart: 23 -> 23, of which waited for: 9 -> 9; matrix products, arithmetic and copies ran while one was open for 0% -> 0% of each run, Pallas kernels for 41% -> 42%
where the time goes in v8:
time: 95.2 us; the launch traced here: 94.9 us
  Pallas kernels  40.9 us (43%)
  starting transfers between devices  28.2 us (30%)
  waiting for transfers between devices  24.4 us (26%)
  between operations  1.02 us (1%)
    pallas_call x17, Pallas kernels, call(): pl.pallas_call(kernel, out_shape=[jax.ShapeDtypeStruct(shape, F32) for sh...  38.7 us
    ppermute x11, starting transfers between devices, along(): lax.ppermute(block, 'row', [(2 * a + core, 2 * b + core) for a, b in pair...  17.6 us
    ppermute x11, waiting for transfers between devices, along(): lax.ppermute(block, 'row', [(2 * a + core, 2 * b + core) for a, b in pair...  11.6 us
    ppermute x7, waiting for transfers between devices, other_half(): return lax.ppermute(block, 'ch', [(0, 1), (1, 0)])  11.2 us
    ppermute x7, starting transfers between devices, other_half(): return lax.ppermute(block, 'ch', [(0, 1), (1, 0)])  9.76 us
    pallas_call x3, Pallas kernels, join(): pl.pallas_call(functools.partial(join_kernel, firsts, sides), out_shape=j...  2.24 us
  transfers between devices with their start and end apart: 23, of which 9 were waited for; matrix products, arithmetic and copies ran while one was open for 0% of the time, Pallas kernels for 42%

profile of v8, /device:TPU:0, one launch (start us, length us, event | category | flops | bytes accessed | tf_op | source)
XLA Modules:
  0.0 94.9 jit_solution(1992077177212094037)
XLA Ops:
  0.6 3.0 %collective-permute-start = (f32[256,128]{1,0:T(8,128)}, f32[256,128]{1,0:T(8,128)S(1)}, u32[]{:S(2)}, u32[]{:S(2)}) collective-permute-start(f32[256,128]{1,0:T(8,128)} %bitcast.25), channel_id=1, source_target_pairs={{0,1},{1,0},{2,3},{3,2},{4,5},{5,4},{6,7},{7,6},{8,9},{9,8},{10,11... | collective-permute-start | bytes 393224 | tf_op jit(solution)/shard_map/ppermute | solution.py:397
  3.6 0.1 collective-permute-start.1
  3.7 0.1 pad_add_fusion.place
  3.8 2.2 %shard_map.77 = (f32[8,128,128]{2,1,0:T(8,128)S(1)}, f32[8,128,128]{2,1,0:T(8,128)S(1)}, f32[16,128]{1,0:T(8,128)S(1)}, f32[4,64,128]{2,1,0:T(8,128)S(1)}, f32[8...) custom-call(s32[3]{0:T(128)S(1)} %pad_add_fusion.place, f32[16,128,128]{2,1,0:T(8,128)} %pair.3, s32[16,128]{1,0:T(8,128)} %mask.1, ...), custom_call_target="tpu_custom_call" | custom-call | flops 1000 | bytes 1000 | tf_op jit(solution)/shard_map/pallas_call | solution.py:54
  6.0 0.0 copy-start
  6.0 0.0 copy-start.1
  6.0 0.0 copy-start.2
  6.0 0.1 collective-permute-start.2
  6.1 0.5 collective-permute-start.3
  6.6 1.1 %collective-permute-done = f32[256,128]{1,0:T(8,128)S(1)} collective-permute-done((f32[256,128]{1,0:T(8,128)}, f32[256,128]{1,0:T(8,128)S(1)}, u32[]{:S(2)}, u32[]{:S(2)}) %collective-permute-start) | collective-permute-done | bytes 131104 | tf_op jit(solution)/shard_map/ppermute | solution.py:397
  7.7 1.2 %shard_map.78 = (f32[8,128,128]{2,1,0:T(8,128)S(1)}, f32[8,128,128]{2,1,0:T(8,128)S(1)}, f32[8,128,128]{2,1,0:T(8,128)S(1)}) custom-call(s32[3]{0:T(128)S(1)} %pad_add_fusion.place, f32[8,128,128]{2,1,0:T(8,128)S(1)} %get-tuple-element.72.normed, f32[16,128]{1,0:T(8,128)S(1)} %get-tuple-element.73.keep, f32[4,64,128]{2,1,0:T(8,128)S(1)} %get-tuple-element.74.mine.refs_15_, ...), custom_call_target="tpu_custom_call" | custom-call | flops 1000 | bytes 1000 | tf_op jit(solution)/shard_map/pallas_call | solution.py:54
  8.9 0.0 collective-permute-done.1.other_out
  8.9 1.9 %collective-permute-start.5 = (f32[8,128,128]{2,1,0:T(8,128)S(1)}, f32[8,128,128]{2,1,0:T(8,128)S(1)}, u32[]{:S(2)}, u32[]{:S(2)}) collective-permute-start(f32[8,128,128]{2,1,0:T(8,128)S(1)} %get-tuple-element.76.refs_0_), channel_id=1, source_target_pairs={{0,4},{2,6},{4,0},{6,2},{8,12},{10,14},{12,8},{14,10},{1,5},{3,7},... | collective-permute-start | bytes 1572872 | tf_op jit(solution)/shard_map/ppermute | solution.py:389
  10.8 0.7 collective-permute-start.8
  11.5 1.5 %shard_map.79 = f32[5,16,8,128]{3,2,1,0:T(8,128)S(1)} custom-call(s32[3]{0:T(128)S(1)} %pad_add_fusion.place, f32[16,128,128]{2,1,0:T(8,128)} %refs_10_.3, f32[16,128]{1,0:T(8,128)S(1)} %get-tuple-element.73.keep), custom_call_target="tpu_custom_call" | custom-call | flops 1000 | bytes 1000 | tf_op jit(solution)/shard_map/pallas_call | solution.py:54
  13.0 0.1 collective-permute-start.4
  13.1 1.6 %collective-permute-done.4.third = f32[5,16,8,128]{3,2,1,0:T(8,128)S(1)} collective-permute-done((f32[5,16,8,128]{3,2,1,0:T(8,128)S(1)}, f32[5,16,8,128]{3,2,1,0:T(8,128)S(1)}, u32[]{:S(2)}, u32[]{:S(2)}) %collective-permute-start.4) | collective-permute-done | bytes 327712 | tf_op jit(solution)/shard_map/ppermute | solution.py:393
  14.7 0.0 collective-permute-done.2.first
  14.7 0.0 collective-permute-done.3.second
  14.8 3.8 %shard_map.80 = (f32[16,128,128]{2,1,0:T(8,128)S(1)}, f32[16,128,128]{2,1,0:T(8,128)S(1)}, f32[8,128,128]{2,1,0:T(8,128)S(1)}, f32[8,128,128]{2,1,0:T(8,128)S(1)...) custom-call(s32[3]{0:T(128)S(1)} %pad_add_fusion.place, ...), custom_call_target="tpu_custom_call" | custom-call | flops 1000 | bytes 1000 | tf_op jit(solution)/shard_map/pallas_call | solution.py:54
  18.6 3.5 %collective-permute-done.5.refs_0_ = f32[8,128,128]{2,1,0:T(8,128)S(1)} collective-permute-done((f32[8,128,128]{2,1,0:T(8,128)S(1)}, f32[8,128,128]{2,1,0:T(8,128)S(1)}, u32[]{:S(2)}, u32[]{:S(2)}) %collective-permute-start.5) | collective-permute-done | bytes 524320 | tf_op jit(solution)/shard_map/ppermute | solution.py:389
  22.1 0.7 collective-permute-start.6
  22.8 1.3 %collective-permute-start.9 = (f32[8,128,128]{2,1,0:T(8,128)S(1)}, f32[8,128,128]{2,1,0:T(8,128)S(1)}, u32[]{:S(2)}, u32[]{:S(2)}) collective-permute-start(f32[8,128,128]{2,1,0:T(8,128)S(1)} %collective-permute-done.8.one), channel_id=1, source_target_pairs={{4,0},{6,2},{8,12},{10,14},{5,1},{7,3},{9,13},{11,15},{20,16},{22,... | collective-permute-start | bytes 1572872 | tf_op jit(solution)/shard_map/ppermute | solution.py:389
  24.1 3.8 %shard_map.81 = (f32[16,8,128]{2,1,0:T(8,128)S(1)}, f32[16,8,128]{2,1,0:T(8,128)S(1)}, f32[256,128]{1,0:T(8,128)S(1)}, f32[8,128,128]{2,1,0:T(8,128)S(1)}) custom-call(s32[3]{0:T(128)S(1)} %pad_add_fusion.place, f32[8,128,128]{2,1,0:T(8,128)S(1)} %get-tuple-element.76.refs_0_, f32[16,128,128]{2,1,0:T(8,128)S(1)} %get-tuple-element.81.refs_1_.refs_2_.left_here, ...), custom_call_target="tpu_custom_call" | custom-call | flops 1000 | bytes 1000 | tf_op jit(solution)/shard_map/pallas_call | solution.py:54
  27.9 3.7 %shard_map.82 = (f32[16,8,128]{2,1,0:T(8,128)S(1)}, f32[16,8,128]{2,1,0:T(8,128)S(1)}, f32[256,128]{1,0:T(8,128)S(1)}, f32[8,128,128]{2,1,0:T(8,128)S(1)}) custom-call(s32[3]{0:T(128)S(1)} %pad_add_fusion.place, f32[8,128,128]{2,1,0:T(8,128)S(1)} %collective-permute-done.5.refs_0_, f32[16,128,128]{2,1,0:T(8,128)S(1)} %get-tuple-element.81.refs_1_.refs_2_.left_here, ...), custom_call_target="tpu_custom_call" | custom-call | flops 1000 | bytes 1000 | tf_op jit(solution)/shard_map/pallas_call | solution.py:54
  31.6 0.1 collective-permute-start.7
  31.7 1.8 %shard_map.83 = (f32[16,128,128]{2,1,0:T(8,128)S(1)}, f32[16,128,128]{2,1,0:T(8,128)S(1)}) custom-call(s32[3]{0:T(128)S(1)} %pad_add_fusion.place, f32[8,128,128]{2,1,0:T(8,128)S(1)} %get-tuple-element.76.refs_0_, f32[256,128]{1,0:T(8,128)S(1)} %get-tuple-element.92.refs_1_), custom_call_target="tpu_custom_call" | custom-call | flops 1000 | bytes 1000 | tf_op jit(solution)/shard_map/pallas_call | solution.py:54
  33.5 0.0 collective-permute-done.7.refs_4_
  33.5 0.0 collective-permute-done.6.refs_0_
  33.5 1.3 %collective-permute-start.10 = (f32[8,128,128]{2,1,0:T(8,128)S(1)}, f32[8,128,128]{2,1,0:T(8,128)S(1)}, u32[]{:S(2)}, u32[]{:S(2)}) collective-permute-start(f32[8,128,128]{2,1,0:T(8,128)S(1)} %collective-permute-done.6.refs_0_), channel_id=1, source_target_pairs={{4,0},{6,2},{8,12},{10,14},{5,1},{7,3},{9,13},{11,15},{20,16},{22,... | collective-permute-start | bytes 1572872 | tf_op jit(solution)/shard_map/ppermute | solution.py:389
  34.8 3.9 %collective-permute-done.9.refs_1_ = f32[8,128,128]{2,1,0:T(8,128)S(1)} collective-permute-done((f32[8,128,128]{2,1,0:T(8,128)S(1)}, f32[8,128,128]{2,1,0:T(8,128)S(1)}, u32[]{:S(2)}, u32[]{:S(2)}) %collective-permute-start.9) | collective-permute-done | bytes 524320 | tf_op jit(solution)/shard_map/ppermute | solution.py:389
  38.7 3.8 %shard_map.84 = (f32[16,8,128]{2,1,0:T(8,128)S(1)}, f32[16,8,128]{2,1,0:T(8,128)S(1)}, f32[256,128]{1,0:T(8,128)S(1)}, f32[8,128,128]{2,1,0:T(8,128)S(1)}, f32[8,128,128]{2,1,0:T(8,128)S(1)}) custom-call(s32[3]{0:T(128)S(1)} %pad_add_fusion.place, f32[8,128,128]{2,1,0:T(8,128)S(1)} %collective-permute-done.6.refs_0_, ...), custom_call_target="tpu_custom_call" | custom-call | flops 1000 | bytes 1000 | tf_op jit(solution)/shard_map/pallas_call | solution.py:54
  42.5 3.4 %collective-permute-start.12 = (f32[8,128,128]{2,1,0:T(8,128)S(1)}, f32[8,128,128]{2,1,0:T(8,128)S(1)}, u32[]{:S(2)}, u32[]{:S(2)}) collective-permute-start(f32[8,128,128]{2,1,0:T(8,128)S(1)} %get-tuple-element.107), channel_id=1, source_target_pairs={{0,4},{2,6},{12,8},{14,10},{1,5},{3,7},{13,9},{15,11},{16,20},{18,... | collective-permute-start | bytes 1572872 | tf_op jit(solution)/shard_map/ppermute | solution.py:389
  45.9 0.7 collective-permute-start.11
  46.7 1.6 %collective-permute-start.13 = (f32[2,2,16,8,128]{4,3,2,1,0:T(8,128)S(1)}, f32[2,2,16,8,128]{4,3,2,1,0:T(8,128)S(1)}, u32[]{:S(2)}, u32[]{:S(2)}) collective-permute-start(f32[2,2,16,8,128]{4,3,2,1,0:T(8,128)S(1)} %pad_maximum_fusion), channel_id=1, source_target_pairs={{0,1},{1,0},{2,3},{3,2},{4,5},{5,4},{6,7},{7,6},{8,9},{9,8},{10,11... | collective-permute-start | bytes 786440 | tf_op jit(solution)/shard_map/ppermute | solution.py:397
  48.2 3.8 %shard_map.85 = (f32[16,128,128]{2,1,0:T(8,128)S(1)}, f32[16,128,128]{2,1,0:T(8,128)S(1)}) custom-call(s32[3]{0:T(128)S(1)} %pad_add_fusion.place, f32[8,128,128]{2,1,0:T(8,128)S(1)} %collective-permute-done.5.refs_0_, f32[8,128,128]{2,1,0:T(8,128)S(1)} %get-tuple-element.96.refs_1_, f32[256,128]{1,0:T(8,128)S(1)} %get-tuple-element.97.refs_2_, ...), custom_call_target="tpu_custom_call" | custom-call | flops 1000 | bytes 1000 | tf_op jit(solution)/shard_map/pallas_call | solution.py:54
  52.0 0.0 collective-permute-done.10.two
  52.0 5.1 %shard_map.86 = (f32[16,8,128]{2,1,0:T(8,128)S(1)}, f32[16,8,128]{2,1,0:T(8,128)}, f32[256,128]{1,0:T(8,128)S(1)}, f32[8,128,128]{2,1,0:T(8,128)S(1)}, f32[8,128...) custom-call(s32[3]{0:T(128)S(1)} %pad_add_fusion.place, f32[8,128,128]{2,1,0:T(8,128)S(1)} %collective-permute-done.8.one, ...), custom_call_target="tpu_custom_call" | custom-call | flops 1000 | bytes 1000 | tf_op jit(solution)/shard_map/pallas_call | solution.py:54
  57.2 0.1 add.12
  57.3 0.1 add.13
  57.3 0.1 collective-permute-start.14
  57.5 2.4 %collective-permute-start.18 = (f32[4,128,128]{2,1,0:T(8,128)S(1)}, f32[4,128,128]{2,1,0:T(8,128)S(1)}, u32[]{:S(2)}, u32[]{:S(2)}) collective-permute-start(f32[4,128,128]{2,1,0:T(8,128)S(1)} %get-tuple-element.145), channel_id=1, source_target_pairs={{0,12},{2,14},{12,0},{14,2},{4,8},{6,10},{8,4},{10,6},{1,13},{3,15... | collective-permute-start | bytes 786440 | tf_op jit(solution)/shard_map/ppermute | solution.py:389
  59.9 1.2 %shard_map.87.kept = f32[16,128,128]{2,1,0:T(8,128)S(1)} custom-call(s32[3]{0:T(128)S(1)} %pad_add_fusion.place, f32[8,128,128]{2,1,0:T(8,128)S(1)} %get-tuple-element.115.right, f32[256,128]{1,0:T(8,128)S(1)} %get-tuple-element.116.d_x, f32[16,128,128]{2,1,0:T(8,128)S(1)} %get-tuple-element.118.here), custom_call_target="tpu_custom_call" | custom-call | flops 1000 | bytes 1000 | tf_op jit(solution)/shard_map/pallas_call | solution.py:54
  61.2 0.7 shard_map.88
  61.8 1.5 %collective-permute-start.15 = (f32[6,128,128]{2,1,0:T(8,128)S(1)}, f32[6,128,128]{2,1,0:T(8,128)S(1)}, u32[]{:S(2)}, u32[]{:S(2)}) collective-permute-start(f32[6,128,128]{2,1,0:T(8,128)S(1)} %get-tuple-element.119), channel_id=1, source_target_pairs={{0,1},{1,0},{2,3},{3,2},{4,5},{5,4},{6,7},{7,6},{8,9},{9,8},{10,11... | collective-permute-start | bytes 1179656 | tf_op jit(solution)/shard_map/ppermute | solution.py:397
  63.4 0.6 collective-permute-start.16
  64.0 2.8 %collective-permute-start.17 = (f32[4,128,128]{2,1,0:T(8,128)S(1)}, f32[4,128,128]{2,1,0:T(8,128)S(1)}, u32[]{:S(2)}, u32[]{:S(2)}) collective-permute-start(f32[4,128,128]{2,1,0:T(8,128)S(1)} %get-tuple-element.143), channel_id=1, source_target_pairs={{0,4},{2,6},{4,0},{6,2},{8,12},{10,14},{12,8},{14,10},{1,5},{3,7},... | collective-permute-start | bytes 786440 | tf_op jit(solution)/shard_map/ppermute | solution.py:389
  66.8 0.1 collective-permute-start.19
  66.8 1.4 %collective-permute-done.18.d_right_across = f32[4,128,128]{2,1,0:T(8,128)S(1)} collective-permute-done((f32[4,128,128]{2,1,0:T(8,128)S(1)}, f32[4,128,128]{2,1,0:T(8,128)S(1)}, u32[]{:S(2)}, u32[]{:S(2)}) %collective-permute-start.18) | collective-permute-done | bytes 262176 | tf_op jit(solution)/shard_map/ppermute | solution.py:389
  68.2 2.4 %collective-permute-start.20 = (f32[4,128,128]{2,1,0:T(8,128)S(1)}, f32[4,128,128]{2,1,0:T(8,128)S(1)}, u32[]{:S(2)}, u32[]{:S(2)}) collective-permute-start(f32[4,128,128]{2,1,0:T(8,128)S(1)} %get-tuple-element.134), channel_id=1, source_target_pairs={{0,12},{2,14},{12,0},{14,2},{4,8},{6,10},{8,4},{10,6},{1,13},{3,15... | collective-permute-start | bytes 786440 | tf_op jit(solution)/shard_map/ppermute | solution.py:389
  70.6 3.2 %collective-permute-done.15.refs_7_.refs_8_ = f32[6,128,128]{2,1,0:T(8,128)S(1)} collective-permute-done((f32[6,128,128]{2,1,0:T(8,128)S(1)}, f32[6,128,128]{2,1,0:T(8,128)S(1)}, u32[]{:S(2)}, u32[]{:S(2)}) %collective-permute-start.15) | collective-permute-done | bytes 393248 | tf_op jit(solution)/shard_map/ppermute | solution.py:397
  73.9 1.1 %shard_map.90.base = f32[4,128,128]{2,1,0:T(8,128)S(1)} custom-call(s32[3]{0:T(128)S(1)} %pad_add_fusion.place, f32[16,8,128]{2,1,0:T(8,128)S(1)} %get-tuple-element.87.refs_0_, f32[16,8,128]{2,1,0:T(8,128)S(1)} %get-tuple-element.89.refs_1_, f32[16,8,128]{2,1,0:T(8,128)S(1)} %get-tuple-element.95.out_next.refs_2_, ...), custom_call_target="tpu_custom_call" | custom-call | flops 1000 | bytes 1000 | tf_op jit(solution)/shard_map/pallas_call | solution.py:54
  75.0 1.0 %shard_map.91.refs_0_ = f32[4,128,128]{2,1,0:T(8,128)S(1)} custom-call(s32[3]{0:T(128)S(1)} %pad_add_fusion.place, f32[8,128,128]{2,1,0:T(8,128)S(1)} %get-tuple-element.72.normed, f32[8,128,128]{2,1,0:T(8,128)S(1)} %get-tuple-element.125.scale, f32[4,128,128]{2,1,0:T(8,128)S(1)} %shard_map.90.base, f32[8,128,128]{2,1,0:T(8,128)S(1)} %get-tuple-element.126.d_right, ...), custom_call_target="tpu_custom_call" | custom-call | flops 1000 | bytes 1000 | tf_op jit(solution)/shard_map/pallas_call | solution.py:54
  76.0 1.5 %collective-permute-start.21 = (f32[4,128,128]{2,1,0:T(8,128)S(1)}, f32[4,128,128]{2,1,0:T(8,128)S(1)}, u32[]{:S(2)}, u32[]{:S(2)}) collective-permute-start(f32[4,128,128]{2,1,0:T(8,128)S(1)} %shard_map.91.refs_0_), channel_id=1, source_target_pairs={{0,1},{1,0},{2,3},{3,2},{4,5},{5,4},{6,7},{7,6},{8,9},{9,8},{10,11... | collective-permute-start | bytes 786440 | tf_op jit(solution)/shard_map/ppermute | solution.py:397
  77.5 4.8 %collective-permute-done.16.refs_8_ = f32[6,128,128]{2,1,0:T(8,128)S(1)} collective-permute-done((f32[6,128,128]{2,1,0:T(8,128)S(1)}, f32[6,128,128]{2,1,0:T(8,128)S(1)}, u32[]{:S(2)}, u32[]{:S(2)}) %collective-permute-start.16) | collective-permute-done | bytes 393248 | tf_op jit(solution)/shard_map/ppermute | solution.py:397
  82.3 1.1 %shard_map.89.base = f32[4,128,128]{2,1,0:T(8,128)S(1)} custom-call(s32[3]{0:T(128)S(1)} %pad_add_fusion.place, f32[16,8,128]{2,1,0:T(8,128)S(1)} %get-tuple-element.87.refs_0_, f32[16,8,128]{2,1,0:T(8,128)S(1)} %get-tuple-element.89.refs_1_, f32[16,8,128]{2,1,0:T(8,128)S(1)} %get-tuple-element.95.out_next.refs_2_, ...), custom_call_target="tpu_custom_call" | custom-call | flops 1000 | bytes 1000 | tf_op jit(solution)/shard_map/pallas_call | solution.py:54
  83.4 2.9 %collective-permute-done.20.d_right_across = f32[4,128,128]{2,1,0:T(8,128)S(1)} collective-permute-done((f32[4,128,128]{2,1,0:T(8,128)S(1)}, f32[4,128,128]{2,1,0:T(8,128)S(1)}, u32[]{:S(2)}, u32[]{:S(2)}) %collective-permute-start.20) | collective-permute-done | bytes 262176 | tf_op jit(solution)/shard_map/ppermute | solution.py:389
  86.2 1.0 %shard_map.92.refs_1_ = f32[4,128,128]{2,1,0:T(8,128)S(1)} custom-call(s32[3]{0:T(128)S(1)} %pad_add_fusion.place, f32[8,128,128]{2,1,0:T(8,128)S(1)} %get-tuple-element.72.normed, f32[8,128,128]{2,1,0:T(8,128)S(1)} %get-tuple-element.125.scale, f32[4,128,128]{2,1,0:T(8,128)S(1)} %shard_map.89.base, f32[8,128,128]{2,1,0:T(8,128)S(1)} %get-tuple-element.126.d_right, ...), custom_call_target="tpu_custom_call" | custom-call | flops 1000 | bytes 1000 | tf_op jit(solution)/shard_map/pallas_call | solution.py:54
  87.3 1.5 %collective-permute-start.22 = (f32[4,128,128]{2,1,0:T(8,128)S(1)}, f32[4,128,128]{2,1,0:T(8,128)S(1)}, u32[]{:S(2)}, u32[]{:S(2)}) collective-permute-start(f32[4,128,128]{2,1,0:T(8,128)S(1)} %shard_map.92.refs_1_), channel_id=1, source_target_pairs={{0,1},{1,0},{2,3},{3,2},{4,5},{5,4},{6,7},{7,6},{8,9},{9,8},{10,11... | collective-permute-start | bytes 786440 | tf_op jit(solution)/shard_map/ppermute | solution.py:397
  88.8 1.8 %shard_map.94 = f32[16,128,128]{2,1,0:T(8,128)} custom-call(s32[3]{0:T(128)S(1)} %pad_add_fusion.place, f32[16,8,128]{2,1,0:T(8,128)S(1)} %get-tuple-element.87.refs_0_, f32[16,8,128]{2,1,0:T(8,128)S(1)} %get-tuple-element.89.refs_1_, f32[16,8,128]{2,1,0:T(8,128)S(1)} %get-tuple-element.95.out_next.refs_2_, ...), custom_call_target="tpu_custom_call" | custom-call | flops 1000 | bytes 1000 | tf_op jit(solution)/shard_map/pallas_call | solution.py:54
  90.6 0.8 shard_map.93.refs_1_
  91.4 0.7 shard_map.95.refs_1_
  92.1 2.1 %collective-permute-done.22.refs_0_ = f32[4,128,128]{2,1,0:T(8,128)S(1)} collective-permute-done((f32[4,128,128]{2,1,0:T(8,128)S(1)}, f32[4,128,128]{2,1,0:T(8,128)S(1)}, u32[]{:S(2)}, u32[]{:S(2)}) %collective-permute-start.22) | collective-permute-done | bytes 262176 | tf_op jit(solution)/shard_map/ppermute | solution.py:397
  94.2 0.7 shard_map.96
  (18 shorter events, 0.1 us)
Async XLA Ops:
  0.6 7.1 %collective-permute-start = (f32[256,128]{1,0:T(8,128)}, f32[256,128]{1,0:T(8,128)S(1)}, u32[]{:S(2)}, u32[]{:S(2)}) collective-permute-start(f32[256,128]{1,0:T(8,128)} %bitcast.25), channel_id=1, source_target_pairs={{0,1},{1,0},{2,3},{3,2},{4,5},{5,4},{6,7},{7,6},{8,9},{9,8},{10,11... | collective-permute-start | bytes 393224 | tf_op jit(solution)/shard_map/ppermute | solution.py:397
  3.6 5.3 %collective-permute-start.1 = (f32[64,128]{1,0:T(8,128)}, f32[64,128]{1,0:T(8,128)S(1)}, u32[]{:S(2)}, u32[]{:S(2)}) collective-permute-start(f32[64,128]{1,0:T(8,128)} %mine_out.1), channel_id=1, source_target_pairs={{0,1},{1,0},{2,3},{3,2},{4,5},{5,4},{6,7},{7,6},{8,9},{9,8},{10,11... | collective-permute-start | bytes 98312 | tf_op jit(solution)/shard_map/ppermute | solution.py:397
  3.8 10.9 %copy-start.3 = (f32[64,128]{1,0:T(8,128)S(1)}, f32[64,128]{1,0:T(8,128)}, u32[]{:S(2)}) copy-start(f32[64,128]{1,0:T(8,128)} %mine_out.1) | copy-start | bytes 98308
  6.0 8.7 %copy-start = (f32[16,128,128]{2,1,0:T(8,128)S(1)}, f32[16,128,128]{2,1,0:T(8,128)}, u32[]{:S(2)}) copy-start(f32[16,128,128]{2,1,0:T(8,128)} %refs_10_.3) | copy-start | bytes 3145732
  6.0 8.7 %copy-start.1 = (f32[16,128,128]{2,1,0:T(8,128)S(1)}, f32[16,128,128]{2,1,0:T(8,128)}, u32[]{:S(2)}) copy-start(f32[16,128,128]{2,1,0:T(8,128)} %pair.3) | copy-start | bytes 3145732
  6.0 8.7 %copy-start.2 = (f32[128,128]{1,0:T(8,128)S(1)}, f32[128,128]{1,0:T(8,128)}, u32[]{:S(2)}) copy-start(f32[128,128]{1,0:T(8,128)} %refs_11_.3) | copy-start | bytes 196612
  6.0 8.7 %collective-permute-start.2 = (f32[8,128,128]{2,1,0:T(8,128)S(1)}, f32[8,128,128]{2,1,0:T(8,128)S(1)}, u32[]{:S(2)}, u32[]{:S(2)}) collective-permute-start(f32[8,128,128]{2,1,0:T(8,128)S(1)} %get-tuple-element.77), channel_id=1, source_target_pairs={{0,2},{2,0},{4,6},{6,4},{8,10},{10,8},{12,14},{14,12},{1,3},{3,1},... | collective-permute-start | bytes 1572872 | tf_op jit(solution)/shard_map/ppermute | solution.py:393
  6.1 8.6 %collective-permute-start.3 = (f32[8,128,128]{2,1,0:T(8,128)S(1)}, f32[8,128,128]{2,1,0:T(8,128)S(1)}, u32[]{:S(2)}, u32[]{:S(2)}) collective-permute-start(f32[8,128,128]{2,1,0:T(8,128)S(1)} %get-tuple-element.78), channel_id=1, source_target_pairs={{0,2},{2,0},{4,6},{6,4},{8,10},{10,8},{12,14},{14,12},{1,3},{3,1},... | collective-permute-start | bytes 1572872 | tf_op jit(solution)/shard_map/ppermute | solution.py:393
  8.9 13.2 %collective-permute-start.5 = (f32[8,128,128]{2,1,0:T(8,128)S(1)}, f32[8,128,128]{2,1,0:T(8,128)S(1)}, u32[]{:S(2)}, u32[]{:S(2)}) collective-permute-start(f32[8,128,128]{2,1,0:T(8,128)S(1)} %get-tuple-element.76.refs_0_), channel_id=1, source_target_pairs={{0,4},{2,6},{4,0},{6,2},{8,12},{10,14},{12,8},{14,10},{1,5},{3,7},... | collective-permute-start | bytes 1572872 | tf_op jit(solution)/shard_map/ppermute | solution.py:389
  10.8 12.0 %collective-permute-start.8 = (f32[8,128,128]{2,1,0:T(8,128)S(1)}, f32[8,128,128]{2,1,0:T(8,128)S(1)}, u32[]{:S(2)}, u32[]{:S(2)}) collective-permute-start(f32[8,128,128]{2,1,0:T(8,128)S(1)} %get-tuple-element.76.refs_0_), channel_id=1, source_target_pairs={{4,8},{6,10},{8,4},{10,6},{5,9},{7,11},{9,5},{11,7},{20,24},{22,26... | collective-permute-start | bytes 1572872 | tf_op jit(solution)/shard_map/ppermute | solution.py:389
  13.0 1.7 %collective-permute-start.4 = (f32[5,16,8,128]{3,2,1,0:T(8,128)S(1)}, f32[5,16,8,128]{3,2,1,0:T(8,128)S(1)}, u32[]{:S(2)}, u32[]{:S(2)}) collective-permute-start(f32[5,16,8,128]{3,2,1,0:T(8,128)S(1)} %shard_map.79), channel_id=1, source_target_pairs={{0,2},{2,0},{4,6},{6,4},{8,10},{10,8},{12,14},{14,12},{1,3},{3,1},... | collective-permute-start | bytes 983048 | tf_op jit(solution)/shard_map/ppermute | solution.py:393
  22.1 11.4 %collective-permute-start.6 = (f32[8,128,128]{2,1,0:T(8,128)S(1)}, f32[8,128,128]{2,1,0:T(8,128)S(1)}, u32[]{:S(2)}, u32[]{:S(2)}) collective-permute-start(f32[8,128,128]{2,1,0:T(8,128)S(1)} %collective-permute-done.5.refs_0_), channel_id=1, source_target_pairs={{4,8},{6,10},{8,4},{10,6},{5,9},{7,11},{9,5},{11,7},{20,24},{22,26... | collective-permute-start | bytes 1572872 | tf_op jit(solution)/shard_map/ppermute | solution.py:389
  22.8 15.9 %collective-permute-start.9 = (f32[8,128,128]{2,1,0:T(8,128)S(1)}, f32[8,128,128]{2,1,0:T(8,128)S(1)}, u32[]{:S(2)}, u32[]{:S(2)}) collective-permute-start(f32[8,128,128]{2,1,0:T(8,128)S(1)} %collective-permute-done.8.one), channel_id=1, source_target_pairs={{4,0},{6,2},{8,12},{10,14},{5,1},{7,3},{9,13},{11,15},{20,16},{22,... | collective-permute-start | bytes 1572872 | tf_op jit(solution)/shard_map/ppermute | solution.py:389
  31.6 1.9 %collective-permute-start.7 = (f32[2,16,8,128]{3,2,1,0:T(8,128)S(1)}, f32[2,16,8,128]{3,2,1,0:T(8,128)S(1)}, u32[]{:S(2)}, u32[]{:S(2)}) collective-permute-start(f32[2,16,8,128]{3,2,1,0:T(8,128)S(1)} %pad_maximum_fusion.1), channel_id=1, source_target_pairs={{0,2},{2,0},{4,6},{6,4},{8,10},{10,8},{12,14},{14,12},{1,3},{3,1},... | collective-permute-start | bytes 393224 | tf_op jit(solution)/shard_map/ppermute | solution.py:393
  33.5 18.5 %collective-permute-start.10 = (f32[8,128,128]{2,1,0:T(8,128)S(1)}, f32[8,128,128]{2,1,0:T(8,128)S(1)}, u32[]{:S(2)}, u32[]{:S(2)}) collective-permute-start(f32[8,128,128]{2,1,0:T(8,128)S(1)} %collective-permute-done.6.refs_0_), channel_id=1, source_target_pairs={{4,0},{6,2},{8,12},{10,14},{5,1},{7,3},{9,13},{11,15},{20,16},{22,... | collective-permute-start | bytes 1572872 | tf_op jit(solution)/shard_map/ppermute | solution.py:389
  42.5 14.7 %collective-permute-start.12 = (f32[8,128,128]{2,1,0:T(8,128)S(1)}, f32[8,128,128]{2,1,0:T(8,128)S(1)}, u32[]{:S(2)}, u32[]{:S(2)}) collective-permute-start(f32[8,128,128]{2,1,0:T(8,128)S(1)} %get-tuple-element.107), channel_id=1, source_target_pairs={{0,4},{2,6},{12,8},{14,10},{1,5},{3,7},{13,9},{15,11},{16,20},{18,... | collective-permute-start | bytes 1572872 | tf_op jit(solution)/shard_map/ppermute | solution.py:389
  45.9 11.3 %collective-permute-start.11 = (f32[8,128,128]{2,1,0:T(8,128)S(1)}, f32[8,128,128]{2,1,0:T(8,128)S(1)}, u32[]{:S(2)}, u32[]{:S(2)}) collective-permute-start(f32[8,128,128]{2,1,0:T(8,128)S(1)} %get-tuple-element.107), channel_id=1, source_target_pairs={{4,8},{6,10},{8,4},{10,6},{5,9},{7,11},{9,5},{11,7},{20,24},{22,26... | collective-permute-start | bytes 1572872 | tf_op jit(solution)/shard_map/ppermute | solution.py:389
  46.7 10.7 %collective-permute-start.13 = (f32[2,2,16,8,128]{4,3,2,1,0:T(8,128)S(1)}, f32[2,2,16,8,128]{4,3,2,1,0:T(8,128)S(1)}, u32[]{:S(2)}, u32[]{:S(2)}) collective-permute-start(f32[2,2,16,8,128]{4,3,2,1,0:T(8,128)S(1)} %pad_maximum_fusion), channel_id=1, source_target_pairs={{0,1},{1,0},{2,3},{3,2},{4,5},{5,4},{6,7},{7,6},{8,9},{9,8},{10,11... | collective-permute-start | bytes 786440 | tf_op jit(solution)/shard_map/ppermute | solution.py:397
  57.3 3.8 %collective-permute-start.14 = (f32[18,128,128]{2,1,0:T(8,128)S(1)}, f32[18,128,128]{2,1,0:T(8,128)S(1)}, u32[]{:S(2)}, u32[]{:S(2)}) collective-permute-start(f32[18,128,128]{2,1,0:T(8,128)S(1)} %get-tuple-element.114), channel_id=1, source_target_pairs={{0,2},{2,0},{4,6},{6,4},{8,10},{10,8},{12,14},{14,12},{1,3},{3,1},... | collective-permute-start | bytes 3538952 | tf_op jit(solution)/shard_map/ppermute | solution.py:393
  57.5 10.8 %collective-permute-start.18 = (f32[4,128,128]{2,1,0:T(8,128)S(1)}, f32[4,128,128]{2,1,0:T(8,128)S(1)}, u32[]{:S(2)}, u32[]{:S(2)}) collective-permute-start(f32[4,128,128]{2,1,0:T(8,128)S(1)} %get-tuple-element.145), channel_id=1, source_target_pairs={{0,12},{2,14},{12,0},{14,2},{4,8},{6,10},{8,4},{10,6},{1,13},{3,15... | collective-permute-start | bytes 786440 | tf_op jit(solution)/shard_map/ppermute | solution.py:389
  61.8 12.0 %collective-permute-start.15 = (f32[6,128,128]{2,1,0:T(8,128)S(1)}, f32[6,128,128]{2,1,0:T(8,128)S(1)}, u32[]{:S(2)}, u32[]{:S(2)}) collective-permute-start(f32[6,128,128]{2,1,0:T(8,128)S(1)} %get-tuple-element.119), channel_id=1, source_target_pairs={{0,1},{1,0},{2,3},{3,2},{4,5},{5,4},{6,7},{7,6},{8,9},{9,8},{10,11... | collective-permute-start | bytes 1179656 | tf_op jit(solution)/shard_map/ppermute | solution.py:397
  63.4 18.9 %collective-permute-start.16 = (f32[6,128,128]{2,1,0:T(8,128)S(1)}, f32[6,128,128]{2,1,0:T(8,128)S(1)}, u32[]{:S(2)}, u32[]{:S(2)}) collective-permute-start(f32[6,128,128]{2,1,0:T(8,128)S(1)} %get-tuple-element.120), channel_id=1, source_target_pairs={{0,1},{1,0},{2,3},{3,2},{4,5},{5,4},{6,7},{7,6},{8,9},{9,8},{10,11... | collective-permute-start | bytes 1179656 | tf_op jit(solution)/shard_map/ppermute | solution.py:397
  64.0 11.0 %collective-permute-start.17 = (f32[4,128,128]{2,1,0:T(8,128)S(1)}, f32[4,128,128]{2,1,0:T(8,128)S(1)}, u32[]{:S(2)}, u32[]{:S(2)}) collective-permute-start(f32[4,128,128]{2,1,0:T(8,128)S(1)} %get-tuple-element.143), channel_id=1, source_target_pairs={{0,4},{2,6},{4,0},{6,2},{8,12},{10,14},{12,8},{14,10},{1,5},{3,7},... | collective-permute-start | bytes 786440 | tf_op jit(solution)/shard_map/ppermute | solution.py:389
  66.8 16.6 %collective-permute-start.19 = (f32[4,128,128]{2,1,0:T(8,128)S(1)}, f32[4,128,128]{2,1,0:T(8,128)S(1)}, u32[]{:S(2)}, u32[]{:S(2)}) collective-permute-start(f32[4,128,128]{2,1,0:T(8,128)S(1)} %get-tuple-element.142), channel_id=1, source_target_pairs={{0,4},{2,6},{4,0},{6,2},{8,12},{10,14},{12,8},{14,10},{1,5},{3,7},... | collective-permute-start | bytes 786440 | tf_op jit(solution)/shard_map/ppermute | solution.py:389
  68.2 18.0 %collective-permute-start.20 = (f32[4,128,128]{2,1,0:T(8,128)S(1)}, f32[4,128,128]{2,1,0:T(8,128)S(1)}, u32[]{:S(2)}, u32[]{:S(2)}) collective-permute-start(f32[4,128,128]{2,1,0:T(8,128)S(1)} %get-tuple-element.134), channel_id=1, source_target_pairs={{0,12},{2,14},{12,0},{14,2},{4,8},{6,10},{8,4},{10,6},{1,13},{3,15... | collective-permute-start | bytes 786440 | tf_op jit(solution)/shard_map/ppermute | solution.py:389
  76.0 15.4 %collective-permute-start.21 = (f32[4,128,128]{2,1,0:T(8,128)S(1)}, f32[4,128,128]{2,1,0:T(8,128)S(1)}, u32[]{:S(2)}, u32[]{:S(2)}) collective-permute-start(f32[4,128,128]{2,1,0:T(8,128)S(1)} %shard_map.91.refs_0_), channel_id=1, source_target_pairs={{0,1},{1,0},{2,3},{3,2},{4,5},{5,4},{6,7},{7,6},{8,9},{9,8},{10,11... | collective-permute-start | bytes 786440 | tf_op jit(solution)/shard_map/ppermute | solution.py:397
  87.3 6.9 %collective-permute-start.22 = (f32[4,128,128]{2,1,0:T(8,128)S(1)}, f32[4,128,128]{2,1,0:T(8,128)S(1)}, u32[]{:S(2)}, u32[]{:S(2)}) collective-permute-start(f32[4,128,128]{2,1,0:T(8,128)S(1)} %shard_map.92.refs_1_), channel_id=1, source_target_pairs={{0,1},{1,0},{2,3},{3,2},{4,5},{5,4},{6,7},{7,6},{8,9},{9,8},{10,11... | collective-permute-start | bytes 786440 | tf_op jit(solution)/shard_map/ppermute | solution.py:397

commit v9 on v8

--- a/solution.py
+++ b/solution.py
@@ -8,7 +8,6 @@
 
 C = 128
 EPS = 1e-05
-HIGHEST = lax.Precision.HIGHEST
 F32 = jnp.float32
 CHUNK = 4
 CUTS = (0, 4, 8)
@@ -86,7 +85,7 @@
 
 
 def gated(normed, keep_rows, w):
-    count, cols = keep_rows.shape
+    count = keep_rows.shape[0]
     chans = w.shape[0] // 2
     spread = jnp.transpose(jnp.concatenate([keep_rows] * (8 // count), axis=0))
     keep = jnp.concatenate([spread[:, u : u + 1] for u in range(count)], axis=0)
@@ -332,7 +331,7 @@
 def base_kernel(rows, t, place, *refs):
     here, early_other, early_far, received, far, far_rows = refs[:4], *refs[4:9]
     gate, cotangent, w_gate, d_left, open_part, slope, mine, other, base, out = refs[9:]
-    count, cols, chans = base.shape
+    count, cols = base.shape[:2]
     gather_out(place, rows, t, count, 0, out, here, early_other, early_far, received, far)
     w = gated_weights(place, mine, other, 0)
     at = slice(t, t + count)
@@ -344,7 +343,7 @@
 
 
 def pair_kernel(first, place, normed, scale, base, d_right, d_right_near, d_right_across, open_part, slope, mine, other, d_mine):
-    count, cols, chans = d_mine.shape
+    count, cols = d_mine.shape[:2]
     w = gated_weights(place, mine, other, 2)
     at = slice(first, first + count)
     grad = flat(d_right[at] + d_right_near[...] + d_right_across[...])

time: 95.2 us -> 95.2 us (level)
  no operation moved by 1% of the time
where the time goes in v9:
time: 95.2 us; the launch traced here: 94.9 us
  Pallas kernels  40.9 us (43%)
  starting transfers between devices  28.2 us (30%)
  waiting for transfers between devices  24.4 us (26%)
  between operations  1.02 us (1%)
    pallas_call x17, Pallas kernels, call(): pl.pallas_call(kernel, out_shape=[jax.ShapeDtypeStruct(shape, F32) for sh...  38.7 us
    ppermute x11, starting transfers between devices, along(): lax.ppermute(block, 'row', [(2 * a + core, 2 * b + core) for a, b in pair...  17.6 us
    ppermute x11, waiting for transfers between devices, along(): lax.ppermute(block, 'row', [(2 * a + core, 2 * b + core) for a, b in pair...  11.6 us
    ppermute x7, waiting for transfers between devices, other_half(): return lax.ppermute(block, 'ch', [(0, 1), (1, 0)])  11.2 us
    ppermute x7, starting transfers between devices, other_half(): return lax.ppermute(block, 'ch', [(0, 1), (1, 0)])  9.76 us
    pallas_call x3, Pallas kernels, join(): pl.pallas_call(functools.partial(join_kernel, firsts, sides), out_shape=j...  2.24 us
  transfers between devices with their start and end apart: 23, of which 9 were waited for; matrix products, arithmetic and copies ran while one was open for 0% of the time, Pallas kernels for 42%

profile of v9, /device:TPU:0, one launch (start us, length us, event | category | flops | bytes accessed | tf_op | source)
XLA Modules:
  0.0 94.9 jit_solution(1992077177212094037)
XLA Ops:
  0.6 3.0 %collective-permute-start = (f32[256,128]{1,0:T(8,128)}, f32[256,128]{1,0:T(8,128)S(1)}, u32[]{:S(2)}, u32[]{:S(2)}) collective-permute-start(f32[256,128]{1,0:T(8,128)} %bitcast.25), channel_id=1, source_target_pairs={{0,1},{1,0},{2,3},{3,2},{4,5},{5,4},{6,7},{7,6},{8,9},{9,8},{10,11... | collective-permute-start | bytes 393224 | tf_op jit(solution)/shard_map/ppermute | solution.py:396
  3.6 0.1 collective-permute-start.1
  3.7 0.1 pad_add_fusion.place
  3.8 2.2 %shard_map.77 = (f32[8,128,128]{2,1,0:T(8,128)S(1)}, f32[8,128,128]{2,1,0:T(8,128)S(1)}, f32[16,128]{1,0:T(8,128)S(1)}, f32[4,64,128]{2,1,0:T(8,128)S(1)}, f32[8...) custom-call(s32[3]{0:T(128)S(1)} %pad_add_fusion.place, f32[16,128,128]{2,1,0:T(8,128)} %pair.3, s32[16,128]{1,0:T(8,128)} %mask.1, ...), custom_call_target="tpu_custom_call" | custom-call | flops 1000 | bytes 1000 | tf_op jit(solution)/shard_map/pallas_call | solution.py:53
  6.0 0.0 copy-start
  6.0 0.0 copy-start.1
  6.0 0.0 copy-start.2
  6.0 0.1 collective-permute-start.2
  6.1 0.5 collective-permute-start.3
  6.6 1.1 %collective-permute-done = f32[256,128]{1,0:T(8,128)S(1)} collective-permute-done((f32[256,128]{1,0:T(8,128)}, f32[256,128]{1,0:T(8,128)S(1)}, u32[]{:S(2)}, u32[]{:S(2)}) %collective-permute-start) | collective-permute-done | bytes 131104 | tf_op jit(solution)/shard_map/ppermute | solution.py:396
  7.7 1.2 %shard_map.78 = (f32[8,128,128]{2,1,0:T(8,128)S(1)}, f32[8,128,128]{2,1,0:T(8,128)S(1)}, f32[8,128,128]{2,1,0:T(8,128)S(1)}) custom-call(s32[3]{0:T(128)S(1)} %pad_add_fusion.place, f32[8,128,128]{2,1,0:T(8,128)S(1)} %get-tuple-element.72.normed, f32[16,128]{1,0:T(8,128)S(1)} %get-tuple-element.73.keep, f32[4,64,128]{2,1,0:T(8,128)S(1)} %get-tuple-element.74.mine.refs_15_, ...), custom_call_target="tpu_custom_call" | custom-call | flops 1000 | bytes 1000 | tf_op jit(solution)/shard_map/pallas_call | solution.py:53
  8.9 0.0 collective-permute-done.1.other_out
  8.9 1.9 %collective-permute-start.5 = (f32[8,128,128]{2,1,0:T(8,128)S(1)}, f32[8,128,128]{2,1,0:T(8,128)S(1)}, u32[]{:S(2)}, u32[]{:S(2)}) collective-permute-start(f32[8,128,128]{2,1,0:T(8,128)S(1)} %get-tuple-element.76.refs_0_), channel_id=1, source_target_pairs={{0,4},{2,6},{4,0},{6,2},{8,12},{10,14},{12,8},{14,10},{1,5},{3,7},... | collective-permute-start | bytes 1572872 | tf_op jit(solution)/shard_map/ppermute | solution.py:388
  10.8 0.7 collective-permute-start.8
  11.5 1.5 %shard_map.79 = f32[5,16,8,128]{3,2,1,0:T(8,128)S(1)} custom-call(s32[3]{0:T(128)S(1)} %pad_add_fusion.place, f32[16,128,128]{2,1,0:T(8,128)} %refs_10_.3, f32[16,128]{1,0:T(8,128)S(1)} %get-tuple-element.73.keep), custom_call_target="tpu_custom_call" | custom-call | flops 1000 | bytes 1000 | tf_op jit(solution)/shard_map/pallas_call | solution.py:53
  13.0 0.1 collective-permute-start.4
  13.1 1.6 %collective-permute-done.4.third = f32[5,16,8,128]{3,2,1,0:T(8,128)S(1)} collective-permute-done((f32[5,16,8,128]{3,2,1,0:T(8,128)S(1)}, f32[5,16,8,128]{3,2,1,0:T(8,128)S(1)}, u32[]{:S(2)}, u32[]{:S(2)}) %collective-permute-start.4) | collective-permute-done | bytes 327712 | tf_op jit(solution)/shard_map/ppermute | solution.py:392
  14.7 0.0 collective-permute-done.2.first
  14.7 0.0 collective-permute-done.3.second
  14.8 3.8 %shard_map.80 = (f32[16,128,128]{2,1,0:T(8,128)S(1)}, f32[16,128,128]{2,1,0:T(8,128)S(1)}, f32[8,128,128]{2,1,0:T(8,128)S(1)}, f32[8,128,128]{2,1,0:T(8,128)S(1)...) custom-call(s32[3]{0:T(128)S(1)} %pad_add_fusion.place, ...), custom_call_target="tpu_custom_call" | custom-call | flops 1000 | bytes 1000 | tf_op jit(solution)/shard_map/pallas_call | solution.py:53
  18.6 3.5 %collective-permute-done.5.refs_0_ = f32[8,128,128]{2,1,0:T(8,128)S(1)} collective-permute-done((f32[8,128,128]{2,1,0:T(8,128)S(1)}, f32[8,128,128]{2,1,0:T(8,128)S(1)}, u32[]{:S(2)}, u32[]{:S(2)}) %collective-permute-start.5) | collective-permute-done | bytes 524320 | tf_op jit(solution)/shard_map/ppermute | solution.py:388
  22.1 0.7 collective-permute-start.6
  22.8 1.3 %collective-permute-start.9 = (f32[8,128,128]{2,1,0:T(8,128)S(1)}, f32[8,128,128]{2,1,0:T(8,128)S(1)}, u32[]{:S(2)}, u32[]{:S(2)}) collective-permute-start(f32[8,128,128]{2,1,0:T(8,128)S(1)} %collective-permute-done.8.one), channel_id=1, source_target_pairs={{4,0},{6,2},{8,12},{10,14},{5,1},{7,3},{9,13},{11,15},{20,16},{22,... | collective-permute-start | bytes 1572872 | tf_op jit(solution)/shard_map/ppermute | solution.py:388
  24.1 3.8 %shard_map.81 = (f32[16,8,128]{2,1,0:T(8,128)S(1)}, f32[16,8,128]{2,1,0:T(8,128)S(1)}, f32[256,128]{1,0:T(8,128)S(1)}, f32[8,128,128]{2,1,0:T(8,128)S(1)}) custom-call(s32[3]{0:T(128)S(1)} %pad_add_fusion.place, f32[8,128,128]{2,1,0:T(8,128)S(1)} %get-tuple-element.76.refs_0_, f32[16,128,128]{2,1,0:T(8,128)S(1)} %get-tuple-element.81.refs_1_.refs_2_.left_here, ...), custom_call_target="tpu_custom_call" | custom-call | flops 1000 | bytes 1000 | tf_op jit(solution)/shard_map/pallas_call | solution.py:53
  27.9 3.7 %shard_map.82 = (f32[16,8,128]{2,1,0:T(8,128)S(1)}, f32[16,8,128]{2,1,0:T(8,128)S(1)}, f32[256,128]{1,0:T(8,128)S(1)}, f32[8,128,128]{2,1,0:T(8,128)S(1)}) custom-call(s32[3]{0:T(128)S(1)} %pad_add_fusion.place, f32[8,128,128]{2,1,0:T(8,128)S(1)} %collective-permute-done.5.refs_0_, f32[16,128,128]{2,1,0:T(8,128)S(1)} %get-tuple-element.81.refs_1_.refs_2_.left_here, ...), custom_call_target="tpu_custom_call" | custom-call | flops 1000 | bytes 1000 | tf_op jit(solution)/shard_map/pallas_call | solution.py:53
  31.6 0.1 collective-permute-start.7
  31.7 1.8 %shard_map.83 = (f32[16,128,128]{2,1,0:T(8,128)S(1)}, f32[16,128,128]{2,1,0:T(8,128)S(1)}) custom-call(s32[3]{0:T(128)S(1)} %pad_add_fusion.place, f32[8,128,128]{2,1,0:T(8,128)S(1)} %get-tuple-element.76.refs_0_, f32[256,128]{1,0:T(8,128)S(1)} %get-tuple-element.92.refs_1_), custom_call_target="tpu_custom_call" | custom-call | flops 1000 | bytes 1000 | tf_op jit(solution)/shard_map/pallas_call | solution.py:53
  33.5 0.0 collective-permute-done.7.refs_4_
  33.5 0.0 collective-permute-done.6.refs_0_
  33.5 1.3 %collective-permute-start.10 = (f32[8,128,128]{2,1,0:T(8,128)S(1)}, f32[8,128,128]{2,1,0:T(8,128)S(1)}, u32[]{:S(2)}, u32[]{:S(2)}) collective-permute-start(f32[8,128,128]{2,1,0:T(8,128)S(1)} %collective-permute-done.6.refs_0_), channel_id=1, source_target_pairs={{4,0},{6,2},{8,12},{10,14},{5,1},{7,3},{9,13},{11,15},{20,16},{22,... | collective-permute-start | bytes 1572872 | tf_op jit(solution)/shard_map/ppermute | solution.py:388
  34.8 3.9 %collective-permute-done.9.refs_1_ = f32[8,128,128]{2,1,0:T(8,128)S(1)} collective-permute-done((f32[8,128,128]{2,1,0:T(8,128)S(1)}, f32[8,128,128]{2,1,0:T(8,128)S(1)}, u32[]{:S(2)}, u32[]{:S(2)}) %collective-permute-start.9) | collective-permute-done | bytes 524320 | tf_op jit(solution)/shard_map/ppermute | solution.py:388
  38.7 3.8 %shard_map.84 = (f32[16,8,128]{2,1,0:T(8,128)S(1)}, f32[16,8,128]{2,1,0:T(8,128)S(1)}, f32[256,128]{1,0:T(8,128)S(1)}, f32[8,128,128]{2,1,0:T(8,128)S(1)}, f32[8,128,128]{2,1,0:T(8,128)S(1)}) custom-call(s32[3]{0:T(128)S(1)} %pad_add_fusion.place, f32[8,128,128]{2,1,0:T(8,128)S(1)} %collective-permute-done.6.refs_0_, ...), custom_call_target="tpu_custom_call" | custom-call | flops 1000 | bytes 1000 | tf_op jit(solution)/shard_map/pallas_call | solution.py:53
  42.5 3.4 %collective-permute-start.12 = (f32[8,128,128]{2,1,0:T(8,128)S(1)}, f32[8,128,128]{2,1,0:T(8,128)S(1)}, u32[]{:S(2)}, u32[]{:S(2)}) collective-permute-start(f32[8,128,128]{2,1,0:T(8,128)S(1)} %get-tuple-element.107), channel_id=1, source_target_pairs={{0,4},{2,6},{12,8},{14,10},{1,5},{3,7},{13,9},{15,11},{16,20},{18,... | collective-permute-start | bytes 1572872 | tf_op jit(solution)/shard_map/ppermute | solution.py:388
  45.9 0.7 collective-permute-start.11
  46.7 1.6 %collective-permute-start.13 = (f32[2,2,16,8,128]{4,3,2,1,0:T(8,128)S(1)}, f32[2,2,16,8,128]{4,3,2,1,0:T(8,128)S(1)}, u32[]{:S(2)}, u32[]{:S(2)}) collective-permute-start(f32[2,2,16,8,128]{4,3,2,1,0:T(8,128)S(1)} %pad_maximum_fusion), channel_id=1, source_target_pairs={{0,1},{1,0},{2,3},{3,2},{4,5},{5,4},{6,7},{7,6},{8,9},{9,8},{10,11... | collective-permute-start | bytes 786440 | tf_op jit(solution)/shard_map/ppermute | solution.py:396
  48.2 3.8 %shard_map.85 = (f32[16,128,128]{2,1,0:T(8,128)S(1)}, f32[16,128,128]{2,1,0:T(8,128)S(1)}) custom-call(s32[3]{0:T(128)S(1)} %pad_add_fusion.place, f32[8,128,128]{2,1,0:T(8,128)S(1)} %collective-permute-done.5.refs_0_, f32[8,128,128]{2,1,0:T(8,128)S(1)} %get-tuple-element.96.refs_1_, f32[256,128]{1,0:T(8,128)S(1)} %get-tuple-element.97.refs_2_, ...), custom_call_target="tpu_custom_call" | custom-call | flops 1000 | bytes 1000 | tf_op jit(solution)/shard_map/pallas_call | solution.py:53
  52.0 0.0 collective-permute-done.10.two
  52.0 5.1 %shard_map.86 = (f32[16,8,128]{2,1,0:T(8,128)S(1)}, f32[16,8,128]{2,1,0:T(8,128)}, f32[256,128]{1,0:T(8,128)S(1)}, f32[8,128,128]{2,1,0:T(8,128)S(1)}, f32[8,128...) custom-call(s32[3]{0:T(128)S(1)} %pad_add_fusion.place, f32[8,128,128]{2,1,0:T(8,128)S(1)} %collective-permute-done.8.one, ...), custom_call_target="tpu_custom_call" | custom-call | flops 1000 | bytes 1000 | tf_op jit(solution)/shard_map/pallas_call | solution.py:53
  57.2 0.1 add.12
  57.3 0.1 add.13
  57.3 0.1 collective-permute-start.14
  57.5 2.4 %collective-permute-start.18 = (f32[4,128,128]{2,1,0:T(8,128)S(1)}, f32[4,128,128]{2,1,0:T(8,128)S(1)}, u32[]{:S(2)}, u32[]{:S(2)}) collective-permute-start(f32[4,128,128]{2,1,0:T(8,128)S(1)} %get-tuple-element.145), channel_id=1, source_target_pairs={{0,12},{2,14},{12,0},{14,2},{4,8},{6,10},{8,4},{10,6},{1,13},{3,15... | collective-permute-start | bytes 786440 | tf_op jit(solution)/shard_map/ppermute | solution.py:388
  59.9 1.2 %shard_map.87.kept = f32[16,128,128]{2,1,0:T(8,128)S(1)} custom-call(s32[3]{0:T(128)S(1)} %pad_add_fusion.place, f32[8,128,128]{2,1,0:T(8,128)S(1)} %get-tuple-element.115.right, f32[256,128]{1,0:T(8,128)S(1)} %get-tuple-element.116.d_x, f32[16,128,128]{2,1,0:T(8,128)S(1)} %get-tuple-element.118.here), custom_call_target="tpu_custom_call" | custom-call | flops 1000 | bytes 1000 | tf_op jit(solution)/shard_map/pallas_call | solution.py:53
  61.2 0.7 shard_map.88
  61.8 1.5 %collective-permute-start.15 = (f32[6,128,128]{2,1,0:T(8,128)S(1)}, f32[6,128,128]{2,1,0:T(8,128)S(1)}, u32[]{:S(2)}, u32[]{:S(2)}) collective-permute-start(f32[6,128,128]{2,1,0:T(8,128)S(1)} %get-tuple-element.119), channel_id=1, source_target_pairs={{0,1},{1,0},{2,3},{3,2},{4,5},{5,4},{6,7},{7,6},{8,9},{9,8},{10,11... | collective-permute-start | bytes 1179656 | tf_op jit(solution)/shard_map/ppermute | solution.py:396
  63.4 0.6 collective-permute-start.16
  64.0 2.8 %collective-permute-start.17 = (f32[4,128,128]{2,1,0:T(8,128)S(1)}, f32[4,128,128]{2,1,0:T(8,128)S(1)}, u32[]{:S(2)}, u32[]{:S(2)}) collective-permute-start(f32[4,128,128]{2,1,0:T(8,128)S(1)} %get-tuple-element.143), channel_id=1, source_target_pairs={{0,4},{2,6},{4,0},{6,2},{8,12},{10,14},{12,8},{14,10},{1,5},{3,7},... | collective-permute-start | bytes 786440 | tf_op jit(solution)/shard_map/ppermute | solution.py:388
  66.8 0.1 collective-permute-start.19
  66.8 1.4 %collective-permute-done.18.d_right_across = f32[4,128,128]{2,1,0:T(8,128)S(1)} collective-permute-done((f32[4,128,128]{2,1,0:T(8,128)S(1)}, f32[4,128,128]{2,1,0:T(8,128)S(1)}, u32[]{:S(2)}, u32[]{:S(2)}) %collective-permute-start.18) | collective-permute-done | bytes 262176 | tf_op jit(solution)/shard_map/ppermute | solution.py:388
  68.2 2.4 %collective-permute-start.20 = (f32[4,128,128]{2,1,0:T(8,128)S(1)}, f32[4,128,128]{2,1,0:T(8,128)S(1)}, u32[]{:S(2)}, u32[]{:S(2)}) collective-permute-start(f32[4,128,128]{2,1,0:T(8,128)S(1)} %get-tuple-element.134), channel_id=1, source_target_pairs={{0,12},{2,14},{12,0},{14,2},{4,8},{6,10},{8,4},{10,6},{1,13},{3,15... | collective-permute-start | bytes 786440 | tf_op jit(solution)/shard_map/ppermute | solution.py:388
  70.6 3.2 %collective-permute-done.15.refs_7_.refs_8_ = f32[6,128,128]{2,1,0:T(8,128)S(1)} collective-permute-done((f32[6,128,128]{2,1,0:T(8,128)S(1)}, f32[6,128,128]{2,1,0:T(8,128)S(1)}, u32[]{:S(2)}, u32[]{:S(2)}) %collective-permute-start.15) | collective-permute-done | bytes 393248 | tf_op jit(solution)/shard_map/ppermute | solution.py:396
  73.9 1.1 %shard_map.90.base = f32[4,128,128]{2,1,0:T(8,128)S(1)} custom-call(s32[3]{0:T(128)S(1)} %pad_add_fusion.place, f32[16,8,128]{2,1,0:T(8,128)S(1)} %get-tuple-element.87.refs_0_, f32[16,8,128]{2,1,0:T(8,128)S(1)} %get-tuple-element.89.refs_1_, f32[16,8,128]{2,1,0:T(8,128)S(1)} %get-tuple-element.95.out_next.refs_2_, ...), custom_call_target="tpu_custom_call" | custom-call | flops 1000 | bytes 1000 | tf_op jit(solution)/shard_map/pallas_call | solution.py:53
  75.0 1.0 %shard_map.91.refs_0_ = f32[4,128,128]{2,1,0:T(8,128)S(1)} custom-call(s32[3]{0:T(128)S(1)} %pad_add_fusion.place, f32[8,128,128]{2,1,0:T(8,128)S(1)} %get-tuple-element.72.normed, f32[8,128,128]{2,1,0:T(8,128)S(1)} %get-tuple-element.125.scale, f32[4,128,128]{2,1,0:T(8,128)S(1)} %shard_map.90.base, f32[8,128,128]{2,1,0:T(8,128)S(1)} %get-tuple-element.126.d_right, ...), custom_call_target="tpu_custom_call" | custom-call | flops 1000 | bytes 1000 | tf_op jit(solution)/shard_map/pallas_call | solution.py:53
  76.0 1.5 %collective-permute-start.21 = (f32[4,128,128]{2,1,0:T(8,128)S(1)}, f32[4,128,128]{2,1,0:T(8,128)S(1)}, u32[]{:S(2)}, u32[]{:S(2)}) collective-permute-start(f32[4,128,128]{2,1,0:T(8,128)S(1)} %shard_map.91.refs_0_), channel_id=1, source_target_pairs={{0,1},{1,0},{2,3},{3,2},{4,5},{5,4},{6,7},{7,6},{8,9},{9,8},{10,11... | collective-permute-start | bytes 786440 | tf_op jit(solution)/shard_map/ppermute | solution.py:396
  77.5 4.8 %collective-permute-done.16.refs_8_ = f32[6,128,128]{2,1,0:T(8,128)S(1)} collective-permute-done((f32[6,128,128]{2,1,0:T(8,128)S(1)}, f32[6,128,128]{2,1,0:T(8,128)S(1)}, u32[]{:S(2)}, u32[]{:S(2)}) %collective-permute-start.16) | collective-permute-done | bytes 393248 | tf_op jit(solution)/shard_map/ppermute | solution.py:396
  82.3 1.1 %shard_map.89.base = f32[4,128,128]{2,1,0:T(8,128)S(1)} custom-call(s32[3]{0:T(128)S(1)} %pad_add_fusion.place, f32[16,8,128]{2,1,0:T(8,128)S(1)} %get-tuple-element.87.refs_0_, f32[16,8,128]{2,1,0:T(8,128)S(1)} %get-tuple-element.89.refs_1_, f32[16,8,128]{2,1,0:T(8,128)S(1)} %get-tuple-element.95.out_next.refs_2_, ...), custom_call_target="tpu_custom_call" | custom-call | flops 1000 | bytes 1000 | tf_op jit(solution)/shard_map/pallas_call | solution.py:53
  83.4 2.9 %collective-permute-done.20.d_right_across = f32[4,128,128]{2,1,0:T(8,128)S(1)} collective-permute-done((f32[4,128,128]{2,1,0:T(8,128)S(1)}, f32[4,128,128]{2,1,0:T(8,128)S(1)}, u32[]{:S(2)}, u32[]{:S(2)}) %collective-permute-start.20) | collective-permute-done | bytes 262176 | tf_op jit(solution)/shard_map/ppermute | solution.py:388
  86.2 1.0 %shard_map.92.refs_1_ = f32[4,128,128]{2,1,0:T(8,128)S(1)} custom-call(s32[3]{0:T(128)S(1)} %pad_add_fusion.place, f32[8,128,128]{2,1,0:T(8,128)S(1)} %get-tuple-element.72.normed, f32[8,128,128]{2,1,0:T(8,128)S(1)} %get-tuple-element.125.scale, f32[4,128,128]{2,1,0:T(8,128)S(1)} %shard_map.89.base, f32[8,128,128]{2,1,0:T(8,128)S(1)} %get-tuple-element.126.d_right, ...), custom_call_target="tpu_custom_call" | custom-call | flops 1000 | bytes 1000 | tf_op jit(solution)/shard_map/pallas_call | solution.py:53
  87.3 1.5 %collective-permute-start.22 = (f32[4,128,128]{2,1,0:T(8,128)S(1)}, f32[4,128,128]{2,1,0:T(8,128)S(1)}, u32[]{:S(2)}, u32[]{:S(2)}) collective-permute-start(f32[4,128,128]{2,1,0:T(8,128)S(1)} %shard_map.92.refs_1_), channel_id=1, source_target_pairs={{0,1},{1,0},{2,3},{3,2},{4,5},{5,4},{6,7},{7,6},{8,9},{9,8},{10,11... | collective-permute-start | bytes 786440 | tf_op jit(solution)/shard_map/ppermute | solution.py:396
  88.8 1.8 %shard_map.94 = f32[16,128,128]{2,1,0:T(8,128)} custom-call(s32[3]{0:T(128)S(1)} %pad_add_fusion.place, f32[16,8,128]{2,1,0:T(8,128)S(1)} %get-tuple-element.87.refs_0_, f32[16,8,128]{2,1,0:T(8,128)S(1)} %get-tuple-element.89.refs_1_, f32[16,8,128]{2,1,0:T(8,128)S(1)} %get-tuple-element.95.out_next.refs_2_, ...), custom_call_target="tpu_custom_call" | custom-call | flops 1000 | bytes 1000 | tf_op jit(solution)/shard_map/pallas_call | solution.py:53
  90.6 0.8 shard_map.93.refs_1_
  91.4 0.7 shard_map.95.refs_1_
  92.1 2.1 %collective-permute-done.22.refs_0_ = f32[4,128,128]{2,1,0:T(8,128)S(1)} collective-permute-done((f32[4,128,128]{2,1,0:T(8,128)S(1)}, f32[4,128,128]{2,1,0:T(8,128)S(1)}, u32[]{:S(2)}, u32[]{:S(2)}) %collective-permute-start.22) | collective-permute-done | bytes 262176 | tf_op jit(solution)/shard_map/ppermute | solution.py:396
  94.2 0.7 shard_map.96
  (18 shorter events, 0.1 us)
Async XLA Ops:
  0.6 7.1 %collective-permute-start = (f32[256,128]{1,0:T(8,128)}, f32[256,128]{1,0:T(8,128)S(1)}, u32[]{:S(2)}, u32[]{:S(2)}) collective-permute-start(f32[256,128]{1,0:T(8,128)} %bitcast.25), channel_id=1, source_target_pairs={{0,1},{1,0},{2,3},{3,2},{4,5},{5,4},{6,7},{7,6},{8,9},{9,8},{10,11... | collective-permute-start | bytes 393224 | tf_op jit(solution)/shard_map/ppermute | solution.py:396
  3.6 5.3 %collective-permute-start.1 = (f32[64,128]{1,0:T(8,128)}, f32[64,128]{1,0:T(8,128)S(1)}, u32[]{:S(2)}, u32[]{:S(2)}) collective-permute-start(f32[64,128]{1,0:T(8,128)} %mine_out.1), channel_id=1, source_target_pairs={{0,1},{1,0},{2,3},{3,2},{4,5},{5,4},{6,7},{7,6},{8,9},{9,8},{10,11... | collective-permute-start | bytes 98312 | tf_op jit(solution)/shard_map/ppermute | solution.py:396
  3.8 10.9 %copy-start.3 = (f32[64,128]{1,0:T(8,128)S(1)}, f32[64,128]{1,0:T(8,128)}, u32[]{:S(2)}) copy-start(f32[64,128]{1,0:T(8,128)} %mine_out.1) | copy-start | bytes 98308
  6.0 8.7 %copy-start = (f32[16,128,128]{2,1,0:T(8,128)S(1)}, f32[16,128,128]{2,1,0:T(8,128)}, u32[]{:S(2)}) copy-start(f32[16,128,128]{2,1,0:T(8,128)} %refs_10_.3) | copy-start | bytes 3145732
  6.0 8.7 %copy-start.1 = (f32[16,128,128]{2,1,0:T(8,128)S(1)}, f32[16,128,128]{2,1,0:T(8,128)}, u32[]{:S(2)}) copy-start(f32[16,128,128]{2,1,0:T(8,128)} %pair.3) | copy-start | bytes 3145732
  6.0 8.7 %copy-start.2 = (f32[128,128]{1,0:T(8,128)S(1)}, f32[128,128]{1,0:T(8,128)}, u32[]{:S(2)}) copy-start(f32[128,128]{1,0:T(8,128)} %refs_11_.3) | copy-start | bytes 196612
  6.0 8.7 %collective-permute-start.2 = (f32[8,128,128]{2,1,0:T(8,128)S(1)}, f32[8,128,128]{2,1,0:T(8,128)S(1)}, u32[]{:S(2)}, u32[]{:S(2)}) collective-permute-start(f32[8,128,128]{2,1,0:T(8,128)S(1)} %get-tuple-element.77), channel_id=1, source_target_pairs={{0,2},{2,0},{4,6},{6,4},{8,10},{10,8},{12,14},{14,12},{1,3},{3,1},... | collective-permute-start | bytes 1572872 | tf_op jit(solution)/shard_map/ppermute | solution.py:392
  6.1 8.6 %collective-permute-start.3 = (f32[8,128,128]{2,1,0:T(8,128)S(1)}, f32[8,128,128]{2,1,0:T(8,128)S(1)}, u32[]{:S(2)}, u32[]{:S(2)}) collective-permute-start(f32[8,128,128]{2,1,0:T(8,128)S(1)} %get-tuple-element.78), channel_id=1, source_target_pairs={{0,2},{2,0},{4,6},{6,4},{8,10},{10,8},{12,14},{14,12},{1,3},{3,1},... | collective-permute-start | bytes 1572872 | tf_op jit(solution)/shard_map/ppermute | solution.py:392
  8.9 13.2 %collective-permute-start.5 = (f32[8,128,128]{2,1,0:T(8,128)S(1)}, f32[8,128,128]{2,1,0:T(8,128)S(1)}, u32[]{:S(2)}, u32[]{:S(2)}) collective-permute-start(f32[8,128,128]{2,1,0:T(8,128)S(1)} %get-tuple-element.76.refs_0_), channel_id=1, source_target_pairs={{0,4},{2,6},{4,0},{6,2},{8,12},{10,14},{12,8},{14,10},{1,5},{3,7},... | collective-permute-start | bytes 1572872 | tf_op jit(solution)/shard_map/ppermute | solution.py:388
  10.8 12.0 %collective-permute-start.8 = (f32[8,128,128]{2,1,0:T(8,128)S(1)}, f32[8,128,128]{2,1,0:T(8,128)S(1)}, u32[]{:S(2)}, u32[]{:S(2)}) collective-permute-start(f32[8,128,128]{2,1,0:T(8,128)S(1)} %get-tuple-element.76.refs_0_), channel_id=1, source_target_pairs={{4,8},{6,10},{8,4},{10,6},{5,9},{7,11},{9,5},{11,7},{20,24},{22,26... | collective-permute-start | bytes 1572872 | tf_op jit(solution)/shard_map/ppermute | solution.py:388
  13.0 1.7 %collective-permute-start.4 = (f32[5,16,8,128]{3,2,1,0:T(8,128)S(1)}, f32[5,16,8,128]{3,2,1,0:T(8,128)S(1)}, u32[]{:S(2)}, u32[]{:S(2)}) collective-permute-start(f32[5,16,8,128]{3,2,1,0:T(8,128)S(1)} %shard_map.79), channel_id=1, source_target_pairs={{0,2},{2,0},{4,6},{6,4},{8,10},{10,8},{12,14},{14,12},{1,3},{3,1},... | collective-permute-start | bytes 983048 | tf_op jit(solution)/shard_map/ppermute | solution.py:392
  22.1 11.4 %collective-permute-start.6 = (f32[8,128,128]{2,1,0:T(8,128)S(1)}, f32[8,128,128]{2,1,0:T(8,128)S(1)}, u32[]{:S(2)}, u32[]{:S(2)}) collective-permute-start(f32[8,128,128]{2,1,0:T(8,128)S(1)} %collective-permute-done.5.refs_0_), channel_id=1, source_target_pairs={{4,8},{6,10},{8,4},{10,6},{5,9},{7,11},{9,5},{11,7},{20,24},{22,26... | collective-permute-start | bytes 1572872 | tf_op jit(solution)/shard_map/ppermute | solution.py:388
  22.8 15.9 %collective-permute-start.9 = (f32[8,128,128]{2,1,0:T(8,128)S(1)}, f32[8,128,128]{2,1,0:T(8,128)S(1)}, u32[]{:S(2)}, u32[]{:S(2)}) collective-permute-start(f32[8,128,128]{2,1,0:T(8,128)S(1)} %collective-permute-done.8.one), channel_id=1, source_target_pairs={{4,0},{6,2},{8,12},{10,14},{5,1},{7,3},{9,13},{11,15},{20,16},{22,... | collective-permute-start | bytes 1572872 | tf_op jit(solution)/shard_map/ppermute | solution.py:388
  31.6 1.9 %collective-permute-start.7 = (f32[2,16,8,128]{3,2,1,0:T(8,128)S(1)}, f32[2,16,8,128]{3,2,1,0:T(8,128)S(1)}, u32[]{:S(2)}, u32[]{:S(2)}) collective-permute-start(f32[2,16,8,128]{3,2,1,0:T(8,128)S(1)} %pad_maximum_fusion.1), channel_id=1, source_target_pairs={{0,2},{2,0},{4,6},{6,4},{8,10},{10,8},{12,14},{14,12},{1,3},{3,1},... | collective-permute-start | bytes 393224 | tf_op jit(solution)/shard_map/ppermute | solution.py:392
  33.5 18.5 %collective-permute-start.10 = (f32[8,128,128]{2,1,0:T(8,128)S(1)}, f32[8,128,128]{2,1,0:T(8,128)S(1)}, u32[]{:S(2)}, u32[]{:S(2)}) collective-permute-start(f32[8,128,128]{2,1,0:T(8,128)S(1)} %collective-permute-done.6.refs_0_), channel_id=1, source_target_pairs={{4,0},{6,2},{8,12},{10,14},{5,1},{7,3},{9,13},{11,15},{20,16},{22,... | collective-permute-start | bytes 1572872 | tf_op jit(solution)/shard_map/ppermute | solution.py:388
  42.5 14.7 %collective-permute-start.12 = (f32[8,128,128]{2,1,0:T(8,128)S(1)}, f32[8,128,128]{2,1,0:T(8,128)S(1)}, u32[]{:S(2)}, u32[]{:S(2)}) collective-permute-start(f32[8,128,128]{2,1,0:T(8,128)S(1)} %get-tuple-element.107), channel_id=1, source_target_pairs={{0,4},{2,6},{12,8},{14,10},{1,5},{3,7},{13,9},{15,11},{16,20},{18,... | collective-permute-start | bytes 1572872 | tf_op jit(solution)/shard_map/ppermute | solution.py:388
  45.9 11.3 %collective-permute-start.11 = (f32[8,128,128]{2,1,0:T(8,128)S(1)}, f32[8,128,128]{2,1,0:T(8,128)S(1)}, u32[]{:S(2)}, u32[]{:S(2)}) collective-permute-start(f32[8,128,128]{2,1,0:T(8,128)S(1)} %get-tuple-element.107), channel_id=1, source_target_pairs={{4,8},{6,10},{8,4},{10,6},{5,9},{7,11},{9,5},{11,7},{20,24},{22,26... | collective-permute-start | bytes 1572872 | tf_op jit(solution)/shard_map/ppermute | solution.py:388
  46.7 10.7 %collective-permute-start.13 = (f32[2,2,16,8,128]{4,3,2,1,0:T(8,128)S(1)}, f32[2,2,16,8,128]{4,3,2,1,0:T(8,128)S(1)}, u32[]{:S(2)}, u32[]{:S(2)}) collective-permute-start(f32[2,2,16,8,128]{4,3,2,1,0:T(8,128)S(1)} %pad_maximum_fusion), channel_id=1, source_target_pairs={{0,1},{1,0},{2,3},{3,2},{4,5},{5,4},{6,7},{7,6},{8,9},{9,8},{10,11... | collective-permute-start | bytes 786440 | tf_op jit(solution)/shard_map/ppermute | solution.py:396
  57.3 3.8 %collective-permute-start.14 = (f32[18,128,128]{2,1,0:T(8,128)S(1)}, f32[18,128,128]{2,1,0:T(8,128)S(1)}, u32[]{:S(2)}, u32[]{:S(2)}) collective-permute-start(f32[18,128,128]{2,1,0:T(8,128)S(1)} %get-tuple-element.114), channel_id=1, source_target_pairs={{0,2},{2,0},{4,6},{6,4},{8,10},{10,8},{12,14},{14,12},{1,3},{3,1},... | collective-permute-start | bytes 3538952 | tf_op jit(solution)/shard_map/ppermute | solution.py:392
  57.5 10.8 %collective-permute-start.18 = (f32[4,128,128]{2,1,0:T(8,128)S(1)}, f32[4,128,128]{2,1,0:T(8,128)S(1)}, u32[]{:S(2)}, u32[]{:S(2)}) collective-permute-start(f32[4,128,128]{2,1,0:T(8,128)S(1)} %get-tuple-element.145), channel_id=1, source_target_pairs={{0,12},{2,14},{12,0},{14,2},{4,8},{6,10},{8,4},{10,6},{1,13},{3,15... | collective-permute-start | bytes 786440 | tf_op jit(solution)/shard_map/ppermute | solution.py:388
  61.8 12.0 %collective-permute-start.15 = (f32[6,128,128]{2,1,0:T(8,128)S(1)}, f32[6,128,128]{2,1,0:T(8,128)S(1)}, u32[]{:S(2)}, u32[]{:S(2)}) collective-permute-start(f32[6,128,128]{2,1,0:T(8,128)S(1)} %get-tuple-element.119), channel_id=1, source_target_pairs={{0,1},{1,0},{2,3},{3,2},{4,5},{5,4},{6,7},{7,6},{8,9},{9,8},{10,11... | collective-permute-start | bytes 1179656 | tf_op jit(solution)/shard_map/ppermute | solution.py:396
  63.4 18.9 %collective-permute-start.16 = (f32[6,128,128]{2,1,0:T(8,128)S(1)}, f32[6,128,128]{2,1,0:T(8,128)S(1)}, u32[]{:S(2)}, u32[]{:S(2)}) collective-permute-start(f32[6,128,128]{2,1,0:T(8,128)S(1)} %get-tuple-element.120), channel_id=1, source_target_pairs={{0,1},{1,0},{2,3},{3,2},{4,5},{5,4},{6,7},{7,6},{8,9},{9,8},{10,11... | collective-permute-start | bytes 1179656 | tf_op jit(solution)/shard_map/ppermute | solution.py:396
  64.0 11.0 %collective-permute-start.17 = (f32[4,128,128]{2,1,0:T(8,128)S(1)}, f32[4,128,128]{2,1,0:T(8,128)S(1)}, u32[]{:S(2)}, u32[]{:S(2)}) collective-permute-start(f32[4,128,128]{2,1,0:T(8,128)S(1)} %get-tuple-element.143), channel_id=1, source_target_pairs={{0,4},{2,6},{4,0},{6,2},{8,12},{10,14},{12,8},{14,10},{1,5},{3,7},... | collective-permute-start | bytes 786440 | tf_op jit(solution)/shard_map/ppermute | solution.py:388
  66.8 16.6 %collective-permute-start.19 = (f32[4,128,128]{2,1,0:T(8,128)S(1)}, f32[4,128,128]{2,1,0:T(8,128)S(1)}, u32[]{:S(2)}, u32[]{:S(2)}) collective-permute-start(f32[4,128,128]{2,1,0:T(8,128)S(1)} %get-tuple-element.142), channel_id=1, source_target_pairs={{0,4},{2,6},{4,0},{6,2},{8,12},{10,14},{12,8},{14,10},{1,5},{3,7},... | collective-permute-start | bytes 786440 | tf_op jit(solution)/shard_map/ppermute | solution.py:388
  68.2 18.0 %collective-permute-start.20 = (f32[4,128,128]{2,1,0:T(8,128)S(1)}, f32[4,128,128]{2,1,0:T(8,128)S(1)}, u32[]{:S(2)}, u32[]{:S(2)}) collective-permute-start(f32[4,128,128]{2,1,0:T(8,128)S(1)} %get-tuple-element.134), channel_id=1, source_target_pairs={{0,12},{2,14},{12,0},{14,2},{4,8},{6,10},{8,4},{10,6},{1,13},{3,15... | collective-permute-start | bytes 786440 | tf_op jit(solution)/shard_map/ppermute | solution.py:388
  76.0 15.4 %collective-permute-start.21 = (f32[4,128,128]{2,1,0:T(8,128)S(1)}, f32[4,128,128]{2,1,0:T(8,128)S(1)}, u32[]{:S(2)}, u32[]{:S(2)}) collective-permute-start(f32[4,128,128]{2,1,0:T(8,128)S(1)} %shard_map.91.refs_0_), channel_id=1, source_target_pairs={{0,1},{1,0},{2,3},{3,2},{4,5},{5,4},{6,7},{7,6},{8,9},{9,8},{10,11... | collective-permute-start | bytes 786440 | tf_op jit(solution)/shard_map/ppermute | solution.py:396
  87.3 6.9 %collective-permute-start.22 = (f32[4,128,128]{2,1,0:T(8,128)S(1)}, f32[4,128,128]{2,1,0:T(8,128)S(1)}, u32[]{:S(2)}, u32[]{:S(2)}) collective-permute-start(f32[4,128,128]{2,1,0:T(8,128)S(1)} %shard_map.92.refs_1_), channel_id=1, source_target_pairs={{0,1},{1,0},{2,3},{3,2},{4,5},{5,4},{6,7},{7,6},{8,9},{9,8},{10,11... | collective-permute-start | bytes 786440 | tf_op jit(solution)/shard_map/ppermute | solution.py:396

commit v10 on v9

--- a/solution.py
+++ b/solution.py
@@ -281,14 +281,14 @@
     for first, last, part in zip(cuts, cuts[1:], packed):
         at = slice(half + first, half + last)
         part[: last - first] = kept[at] + received[at]
-    early, late = packed[0], packed[-1]
+    early, late, spare = packed[0], packed[-2], packed[-1]
     for step, out in enumerate((out_next, out_last)):
         at = slice(step * block, (step + 1) * block)
         plane = 2 * half + step
         early[early.shape[0] - 2, at] = flat(out[half:])
         early[early.shape[0] - 1, at] = received[plane, block:]
-        late[late.shape[0] - 2, at] = flat(out[:half])
-        late[late.shape[0] - 1, at] = received[plane, :block]
+        late[late.shape[0] - 1, at] = flat(out[:half])
+        spare[0, at] = received[plane, :block]
 
 
 def gather_out(place, rows, t, count, start, out, here, early_other, early_far, received, far):
@@ -308,7 +308,8 @@
                         value = early_far[far_core, step, at]
                     else:
                         begin = (step - 2) * block + (t % half) * half
-                        value = far[far.shape[0] - 2 + far_core, begin : begin + count * half].reshape(count, half, -1)
+                        ref, plane = far[far_core]
+                        value = ref[plane, begin : begin + count * half].reshape(count, half, -1)
                 elif far_core:
                     if step < 2:
                         value = early_other[step, at]
@@ -320,10 +321,13 @@
 
 
 def update_kernel(rows, place, *refs):
-    here, early_other, early_far, received, far, far_next, gate, update, out = refs[:4], *refs[4:]
+    here, early_other, early_far, received, far, far_next, far_rows, gate, update, out = refs[:4], *refs[4:]
     half = rows // 2
-    gather_out(place, rows, 0, half, 0, out, here, early_other, early_far, received, far)
-    gather_out(place, rows, half, half, half, out, here, early_other, early_far, received, far_next)
+    last = far.shape[0] - 1
+    first_planes = ((far, last - 1), (far, last))
+    second_planes = ((far_next, far_next.shape[0] - 1), (far_rows, far_rows.shape[0] - 1))
+    gather_out(place, rows, 0, half, 0, out, here, early_other, early_far, received, first_planes)
+    gather_out(place, rows, half, half, half, out, here, early_other, early_far, received, second_planes)
     for t in range(0, rows, CHUNK):
         update[pl.ds(source_row(place, t, rows), CHUNK)] = gate[t : t + CHUNK] * out[t : t + CHUNK]
 
@@ -332,7 +336,8 @@
     here, early_other, early_far, received, far, far_rows = refs[:4], *refs[4:9]
     gate, cotangent, w_gate, d_left, open_part, slope, mine, other, base, out = refs[9:]
     count, cols = base.shape[:2]
-    gather_out(place, rows, t, count, 0, out, here, early_other, early_far, received, far)
+    planes = ((far, far.shape[0] - 2), (far, far.shape[0] - 1))
+    gather_out(place, rows, t, count, 0, out, here, early_other, early_far, received, planes)
     w = gated_weights(place, mine, other, 0)
     at = slice(t, t + count)
     opened = gate[at]
@@ -342,8 +347,11 @@
     base[...] = (dot_t(flat(d_gate), w_gate[...]) + dot(both, w)).reshape(count, cols, -1)
 
 
-def pair_kernel(first, place, normed, scale, base, d_right, d_right_near, d_right_across, open_part, slope, mine, other, d_mine):
-    count, cols = d_mine.shape[:2]
+def pair_kernel(first, count, place, normed, scale, base, d_right, d_right_near, d_right_across, open_part, slope, mine, other, *refs):
+    d_mine = refs[-1]
+    cols = d_mine.shape[1]
+    if len(refs) == 2:
+        d_mine[count] = refs[0][0]
     w = gated_weights(place, mine, other, 2)
     at = slice(first, first + count)
     grad = flat(d_right[at] + d_right_near[...] + d_right_across[...])
@@ -352,29 +360,29 @@
     value = flat(normed[at])
     mean_grad = jnp.mean(d_normed, axis=-1, keepdims=True)
     mean_cross = jnp.mean(d_normed * value, axis=-1, keepdims=True)
-    d_mine[...] = ((d_normed - mean_grad - value * mean_cross) * flat(scale[at])).reshape(count, cols, -1)
-
-
-def join_kernel(firsts, sides, *refs):
+    d_mine[:count] = ((d_normed - mean_grad - value * mean_cross) * flat(scale[at])).reshape(count, cols, -1)
+
+
+def join_kernel(firsts, counts, sides, *refs):
     blocks, whole, sems = refs[: len(firsts)], refs[-2], refs[-1]
     side = lax.axis_index("ch")
     half = whole.shape[0] // 2
     copies = []
-    for at, (block, first, mine) in enumerate(zip(blocks, firsts, sides)):
+    for at, (block, first, count, mine) in enumerate(zip(blocks, firsts, counts, sides)):
         start = (side if mine else 1 - side) * half + first
-        copies.append(pltpu.make_async_copy(block, whole.at[pl.ds(start, block.shape[0])], sems.at[at]))
+        copies.append(pltpu.make_async_copy(block.at[:count], whole.at[pl.ds(start, count)], sems.at[at]))
     for copy in copies:
         copy.start()
     for copy in copies:
         copy.wait()
 
 
-def join(blocks, firsts, sides, shape, whole=None):
+def join(blocks, firsts, counts, sides, shape, whole=None):
     anywhere = pl.BlockSpec(memory_space=pl.ANY)
     vmem = pl.BlockSpec(memory_space=pltpu.VMEM)
     given = [] if whole is None else [whole]
     return pl.pallas_call(
-        functools.partial(join_kernel, firsts, sides),
+        functools.partial(join_kernel, firsts, counts, sides),
         out_shape=jax.ShapeDtypeStruct(shape, F32),
         in_specs=[vmem] * len(blocks) + [anywhere] * len(given),
         out_specs=anywhere,
@@ -496,12 +504,14 @@
     (d_left_kept,) = call(last_kept_kernel, [(rows, cols, chans)], (place, rights[3], d_x[3], d_left_here))
     sizes = [last - first for first, last in spans]
     sizes[0] += 2
-    sizes[-1] += 2
+    sizes[-1] += 1
+    sizes.append(1)
     d_left, *packed = call(
         functools.partial(share_kernel, cuts),
         [kept] + [(size, cols, chans) for size in sizes],
         (place, d_left_kept, received, out_here[2], out_here[3]),
     )
+    spare = packed.pop()
     far_parts = [other_half(block) for block in packed]
     for first, last in spans[1:]:
         from_near.append(along(to_near[first:last], NEXT))
@@ -519,9 +529,10 @@
         if at:
             base, mine_parts[-1] = lax.optimization_barrier((base, mine_parts[-1]))
         (rows_done,) = call(
-            functools.partial(pair_kernel, first),
-            [(last - first, cols, width)],
-            (place, normed, scale, base, d_right[0], from_near[at], from_across[at], open_right, slope_right, mine, other),
+            functools.partial(pair_kernel, first, last - first),
+            [(last - first + (at == 0), cols, width)],
+            (place, normed, scale, base, d_right[0], from_near[at], from_across[at], open_right, slope_right, mine, other)
+            + ((spare,) if at == 0 else ()),
         )
         mine_parts.append(rows_done)
         other_parts.append(other_half(rows_done))
@@ -529,14 +540,15 @@
     (update,) = call(
         functools.partial(update_kernel, rows),
         [(rows, cols, width)],
-        (place, *outs, far_parts[0], far_parts[-1], gate_late),
+        (place, *outs, far_parts[0], far_parts[-1], other_parts[0], gate_late),
         scratch=[(rows, cols, width)],
     )
-    d_pair = join(mine_parts, cuts[:-1], (True,) * len(spans), pair.shape)
+    counts = [last - first for first, last in spans]
+    d_pair = join(mine_parts, cuts[:-1], counts, (True,) * len(spans), pair.shape)
     d_pair, update = lax.optimization_barrier((d_pair, update))
-    for first, part in zip(cuts, other_parts):
+    for first, count, part in zip(cuts, counts, other_parts):
         d_pair, part = lax.optimization_barrier((d_pair, part))
-        d_pair = join([part], (first,), (False,), pair.shape, d_pair)
+        d_pair = join([part], (first,), (count,), (False,), pair.shape, d_pair)
     return (update, d_pair)
 
 

time: 95.2 us -> 95.2 us (level)
    ppermute x11, waiting for transfers between devices: 11.6 us -> 12.8 us  [along(): lax.ppermute(block, 'row', [(2 * a + core, 2 * b + core) for a, b in pair...]
where the time goes in v10:
time: 95.2 us; the launch traced here: 94.9 us
  Pallas kernels  40.9 us (43%)
  starting transfers between devices  27.3 us (29%)
  waiting for transfers between devices  25.3 us (27%)
  between operations  1.01 us (1%)
    pallas_call x17, Pallas kernels, call(): pl.pallas_call(kernel, out_shape=[jax.ShapeDtypeStruct(shape, F32) for sh...  38.7 us
    ppermute x11, starting transfers between devices, along(): lax.ppermute(block, 'row', [(2 * a + core, 2 * b + core) for a, b in pair...  17.6 us
    ppermute x11, waiting for transfers between devices, along(): lax.ppermute(block, 'row', [(2 * a + core, 2 * b + core) for a, b in pair...  12.8 us
    ppermute x7, waiting for transfers between devices, other_half(): return lax.ppermute(block, 'ch', [(0, 1), (1, 0)])  10.9 us
    ppermute x7, starting transfers between devices, other_half(): return lax.ppermute(block, 'ch', [(0, 1), (1, 0)])  8.89 us
    pallas_call x3, Pallas kernels, join(): pl.pallas_call(functools.partial(join_kernel, firsts, counts, sides), out...  2.22 us
  transfers between devices with their start and end apart: 23, of which 9 were waited for; matrix products, arithmetic and copies ran while one was open for 0% of the time, Pallas kernels for 42%

profile of v10, /device:TPU:0, one launch (start us, length us, event | category | flops | bytes accessed | tf_op | source)
XLA Modules:
  0.0 94.9 jit_solution(9753066144903306648)
XLA Ops:
  0.6 3.0 %collective-permute-start = (f32[256,128]{1,0:T(8,128)}, f32[256,128]{1,0:T(8,128)S(1)}, u32[]{:S(2)}, u32[]{:S(2)}) collective-permute-start(f32[256,128]{1,0:T(8,128)} %bitcast.25), channel_id=1, source_target_pairs={{0,1},{1,0},{2,3},{3,2},{4,5},{5,4},{6,7},{7,6},{8,9},{9,8},{10,11... | collective-permute-start | bytes 393224 | tf_op jit(solution)/shard_map/ppermute | solution.py:404
  3.6 0.1 collective-permute-start.1
  3.7 0.1 pad_add_fusion.place
  3.8 2.2 %shard_map.77 = (f32[8,128,128]{2,1,0:T(8,128)S(1)}, f32[8,128,128]{2,1,0:T(8,128)S(1)}, f32[16,128]{1,0:T(8,128)S(1)}, f32[4,64,128]{2,1,0:T(8,128)S(1)}, f32[8...) custom-call(s32[3]{0:T(128)S(1)} %pad_add_fusion.place, f32[16,128,128]{2,1,0:T(8,128)} %pair.3, s32[16,128]{1,0:T(8,128)} %mask.1, ...), custom_call_target="tpu_custom_call" | custom-call | flops 1000 | bytes 1000 | tf_op jit(solution)/shard_map/pallas_call | solution.py:53
  6.0 0.0 copy-start
  6.0 0.0 copy-start.1
  6.0 0.0 copy-start.2
  6.0 0.1 collective-permute-start.2
  6.1 0.5 collective-permute-start.3
  6.6 1.1 %collective-permute-done = f32[256,128]{1,0:T(8,128)S(1)} collective-permute-done((f32[256,128]{1,0:T(8,128)}, f32[256,128]{1,0:T(8,128)S(1)}, u32[]{:S(2)}, u32[]{:S(2)}) %collective-permute-start) | collective-permute-done | bytes 131104 | tf_op jit(solution)/shard_map/ppermute | solution.py:404
  7.7 1.2 %shard_map.78 = (f32[8,128,128]{2,1,0:T(8,128)S(1)}, f32[8,128,128]{2,1,0:T(8,128)S(1)}, f32[8,128,128]{2,1,0:T(8,128)S(1)}) custom-call(s32[3]{0:T(128)S(1)} %pad_add_fusion.place, f32[8,128,128]{2,1,0:T(8,128)S(1)} %get-tuple-element.73.normed, f32[16,128]{1,0:T(8,128)S(1)} %get-tuple-element.74.keep, f32[4,64,128]{2,1,0:T(8,128)S(1)} %get-tuple-element.75.mine.refs_15_, ...), custom_call_target="tpu_custom_call" | custom-call | flops 1000 | bytes 1000 | tf_op jit(solution)/shard_map/pallas_call | solution.py:53
  8.9 0.0 collective-permute-done.1.other_out
  8.9 1.9 %collective-permute-start.5 = (f32[8,128,128]{2,1,0:T(8,128)S(1)}, f32[8,128,128]{2,1,0:T(8,128)S(1)}, u32[]{:S(2)}, u32[]{:S(2)}) collective-permute-start(f32[8,128,128]{2,1,0:T(8,128)S(1)} %get-tuple-element.77.refs_0_), channel_id=1, source_target_pairs={{0,4},{2,6},{4,0},{6,2},{8,12},{10,14},{12,8},{14,10},{1,5},{3,7},... | collective-permute-start | bytes 1572872 | tf_op jit(solution)/shard_map/ppermute | solution.py:396
  10.8 0.7 collective-permute-start.8
  11.5 1.5 %shard_map.79 = f32[5,16,8,128]{3,2,1,0:T(8,128)S(1)} custom-call(s32[3]{0:T(128)S(1)} %pad_add_fusion.place, f32[16,128,128]{2,1,0:T(8,128)} %refs_10_.3, f32[16,128]{1,0:T(8,128)S(1)} %get-tuple-element.74.keep), custom_call_target="tpu_custom_call" | custom-call | flops 1000 | bytes 1000 | tf_op jit(solution)/shard_map/pallas_call | solution.py:53
  13.0 0.1 collective-permute-start.4
  13.1 1.6 %collective-permute-done.4.third = f32[5,16,8,128]{3,2,1,0:T(8,128)S(1)} collective-permute-done((f32[5,16,8,128]{3,2,1,0:T(8,128)S(1)}, f32[5,16,8,128]{3,2,1,0:T(8,128)S(1)}, u32[]{:S(2)}, u32[]{:S(2)}) %collective-permute-start.4) | collective-permute-done | bytes 327712 | tf_op jit(solution)/shard_map/ppermute | solution.py:400
  14.8 3.8 %shard_map.80 = (f32[16,128,128]{2,1,0:T(8,128)S(1)}, f32[16,128,128]{2,1,0:T(8,128)S(1)}, f32[8,128,128]{2,1,0:T(8,128)S(1)}, f32[8,128,128]{2,1,0:T(8,128)S(1)...) custom-call(s32[3]{0:T(128)S(1)} %pad_add_fusion.place, ...), custom_call_target="tpu_custom_call" | custom-call | flops 1000 | bytes 1000 | tf_op jit(solution)/shard_map/pallas_call | solution.py:53
  18.6 3.5 %collective-permute-done.5.refs_0_ = f32[8,128,128]{2,1,0:T(8,128)S(1)} collective-permute-done((f32[8,128,128]{2,1,0:T(8,128)S(1)}, f32[8,128,128]{2,1,0:T(8,128)S(1)}, u32[]{:S(2)}, u32[]{:S(2)}) %collective-permute-start.5) | collective-permute-done | bytes 524320 | tf_op jit(solution)/shard_map/ppermute | solution.py:396
  22.1 0.7 collective-permute-start.6
  22.8 0.0 collective-permute-done.8.one
  22.8 1.3 %collective-permute-start.9 = (f32[8,128,128]{2,1,0:T(8,128)S(1)}, f32[8,128,128]{2,1,0:T(8,128)S(1)}, u32[]{:S(2)}, u32[]{:S(2)}) collective-permute-start(f32[8,128,128]{2,1,0:T(8,128)S(1)} %collective-permute-done.8.one), channel_id=1, source_target_pairs={{4,0},{6,2},{8,12},{10,14},{5,1},{7,3},{9,13},{11,15},{20,16},{22,... | collective-permute-start | bytes 1572872 | tf_op jit(solution)/shard_map/ppermute | solution.py:396
  24.1 3.8 %shard_map.81 = (f32[16,8,128]{2,1,0:T(8,128)S(1)}, f32[16,8,128]{2,1,0:T(8,128)S(1)}, f32[256,128]{1,0:T(8,128)S(1)}, f32[8,128,128]{2,1,0:T(8,128)S(1)}) custom-call(s32[3]{0:T(128)S(1)} %pad_add_fusion.place, f32[8,128,128]{2,1,0:T(8,128)S(1)} %get-tuple-element.77.refs_0_, f32[16,128,128]{2,1,0:T(8,128)S(1)} %get-tuple-element.82.refs_1_.refs_2_.left_here, ...), custom_call_target="tpu_custom_call" | custom-call | flops 1000 | bytes 1000 | tf_op jit(solution)/shard_map/pallas_call | solution.py:53
  27.9 3.7 %shard_map.82 = (f32[16,8,128]{2,1,0:T(8,128)S(1)}, f32[16,8,128]{2,1,0:T(8,128)S(1)}, f32[256,128]{1,0:T(8,128)S(1)}, f32[8,128,128]{2,1,0:T(8,128)S(1)}) custom-call(s32[3]{0:T(128)S(1)} %pad_add_fusion.place, f32[8,128,128]{2,1,0:T(8,128)S(1)} %collective-permute-done.5.refs_0_, f32[16,128,128]{2,1,0:T(8,128)S(1)} %get-tuple-element.82.refs_1_.refs_2_.left_here, ...), custom_call_target="tpu_custom_call" | custom-call | flops 1000 | bytes 1000 | tf_op jit(solution)/shard_map/pallas_call | solution.py:53
  31.6 0.1 collective-permute-start.7
  31.7 1.8 %shard_map.83 = (f32[16,128,128]{2,1,0:T(8,128)S(1)}, f32[16,128,128]{2,1,0:T(8,128)S(1)}) custom-call(s32[3]{0:T(128)S(1)} %pad_add_fusion.place, f32[8,128,128]{2,1,0:T(8,128)S(1)} %get-tuple-element.77.refs_0_, f32[256,128]{1,0:T(8,128)S(1)} %get-tuple-element.93.refs_1_), custom_call_target="tpu_custom_call" | custom-call | flops 1000 | bytes 1000 | tf_op jit(solution)/shard_map/pallas_call | solution.py:53
  33.5 0.0 collective-permute-done.6.refs_0_
  33.5 1.3 %collective-permute-start.10 = (f32[8,128,128]{2,1,0:T(8,128)S(1)}, f32[8,128,128]{2,1,0:T(8,128)S(1)}, u32[]{:S(2)}, u32[]{:S(2)}) collective-permute-start(f32[8,128,128]{2,1,0:T(8,128)S(1)} %collective-permute-done.6.refs_0_), channel_id=1, source_target_pairs={{4,0},{6,2},{8,12},{10,14},{5,1},{7,3},{9,13},{11,15},{20,16},{22,... | collective-permute-start | bytes 1572872 | tf_op jit(solution)/shard_map/ppermute | solution.py:396
  34.8 3.9 %collective-permute-done.9.refs_1_ = f32[8,128,128]{2,1,0:T(8,128)S(1)} collective-permute-done((f32[8,128,128]{2,1,0:T(8,128)S(1)}, f32[8,128,128]{2,1,0:T(8,128)S(1)}, u32[]{:S(2)}, u32[]{:S(2)}) %collective-permute-start.9) | collective-permute-done | bytes 524320 | tf_op jit(solution)/shard_map/ppermute | solution.py:396
  38.7 3.8 %shard_map.84 = (f32[16,8,128]{2,1,0:T(8,128)S(1)}, f32[16,8,128]{2,1,0:T(8,128)S(1)}, f32[256,128]{1,0:T(8,128)S(1)}, f32[8,128,128]{2,1,0:T(8,128)S(1)}, f32[8,128,128]{2,1,0:T(8,128)S(1)}) custom-call(s32[3]{0:T(128)S(1)} %pad_add_fusion.place, f32[8,128,128]{2,1,0:T(8,128)S(1)} %collective-permute-done.6.refs_0_, ...), custom_call_target="tpu_custom_call" | custom-call | flops 1000 | bytes 1000 | tf_op jit(solution)/shard_map/pallas_call | solution.py:53
  42.5 3.4 %collective-permute-start.12 = (f32[8,128,128]{2,1,0:T(8,128)S(1)}, f32[8,128,128]{2,1,0:T(8,128)S(1)}, u32[]{:S(2)}, u32[]{:S(2)}) collective-permute-start(f32[8,128,128]{2,1,0:T(8,128)S(1)} %get-tuple-element.108), channel_id=1, source_target_pairs={{0,4},{2,6},{12,8},{14,10},{1,5},{3,7},{13,9},{15,11},{16,20},{18,... | collective-permute-start | bytes 1572872 | tf_op jit(solution)/shard_map/ppermute | solution.py:396
  45.9 0.7 collective-permute-start.11
  46.7 1.6 %collective-permute-start.13 = (f32[2,2,16,8,128]{4,3,2,1,0:T(8,128)S(1)}, f32[2,2,16,8,128]{4,3,2,1,0:T(8,128)S(1)}, u32[]{:S(2)}, u32[]{:S(2)}) collective-permute-start(f32[2,2,16,8,128]{4,3,2,1,0:T(8,128)S(1)} %pad_maximum_fusion), channel_id=1, source_target_pairs={{0,1},{1,0},{2,3},{3,2},{4,5},{5,4},{6,7},{7,6},{8,9},{9,8},{10,11... | collective-permute-start | bytes 786440 | tf_op jit(solution)/shard_map/ppermute | solution.py:404
  48.2 3.8 %shard_map.85 = (f32[16,128,128]{2,1,0:T(8,128)S(1)}, f32[16,128,128]{2,1,0:T(8,128)S(1)}) custom-call(s32[3]{0:T(128)S(1)} %pad_add_fusion.place, f32[8,128,128]{2,1,0:T(8,128)S(1)} %collective-permute-done.5.refs_0_, f32[8,128,128]{2,1,0:T(8,128)S(1)} %get-tuple-element.97.refs_1_, f32[256,128]{1,0:T(8,128)S(1)} %get-tuple-element.98.refs_2_, ...), custom_call_target="tpu_custom_call" | custom-call | flops 1000 | bytes 1000 | tf_op jit(solution)/shard_map/pallas_call | solution.py:53
  52.1 5.1 %shard_map.86 = (f32[16,8,128]{2,1,0:T(8,128)S(1)}, f32[16,8,128]{2,1,0:T(8,128)}, f32[256,128]{1,0:T(8,128)S(1)}, f32[8,128,128]{2,1,0:T(8,128)S(1)}, f32[8,128...) custom-call(s32[3]{0:T(128)S(1)} %pad_add_fusion.place, f32[8,128,128]{2,1,0:T(8,128)S(1)} %collective-permute-done.8.one, ...), custom_call_target="tpu_custom_call" | custom-call | flops 1000 | bytes 1000 | tf_op jit(solution)/shard_map/pallas_call | solution.py:53
  57.2 0.0 collective-permute-done.12
  57.2 0.1 add.12
  57.3 0.0 collective-permute-done.11
  57.3 0.1 add.13
  57.4 0.0 collective-permute-done.13.refs_5_
  57.4 0.1 collective-permute-start.14
  57.5 2.4 %collective-permute-start.18 = (f32[4,128,128]{2,1,0:T(8,128)S(1)}, f32[4,128,128]{2,1,0:T(8,128)S(1)}, u32[]{:S(2)}, u32[]{:S(2)}) collective-permute-start(f32[4,128,128]{2,1,0:T(8,128)S(1)} %get-tuple-element.147), channel_id=1, source_target_pairs={{0,12},{2,14},{12,0},{14,2},{4,8},{6,10},{8,4},{10,6},{1,13},{3,15... | collective-permute-start | bytes 786440 | tf_op jit(solution)/shard_map/ppermute | solution.py:396
  59.9 1.2 %shard_map.87.kept = f32[16,128,128]{2,1,0:T(8,128)S(1)} custom-call(s32[3]{0:T(128)S(1)} %pad_add_fusion.place, f32[8,128,128]{2,1,0:T(8,128)S(1)} %get-tuple-element.116.right, f32[256,128]{1,0:T(8,128)S(1)} %get-tuple-element.117.d_x, f32[16,128,128]{2,1,0:T(8,128)S(1)} %get-tuple-element.119.here), custom_call_target="tpu_custom_call" | custom-call | flops 1000 | bytes 1000 | tf_op jit(solution)/shard_map/pallas_call | solution.py:53
  61.2 0.7 shard_map.88
  61.9 1.5 %collective-permute-start.15 = (f32[6,128,128]{2,1,0:T(8,128)S(1)}, f32[6,128,128]{2,1,0:T(8,128)S(1)}, u32[]{:S(2)}, u32[]{:S(2)}) collective-permute-start(f32[6,128,128]{2,1,0:T(8,128)S(1)} %get-tuple-element.120), channel_id=1, source_target_pairs={{0,1},{1,0},{2,3},{3,2},{4,5},{5,4},{6,7},{7,6},{8,9},{9,8},{10,11... | collective-permute-start | bytes 1179656 | tf_op jit(solution)/shard_map/ppermute | solution.py:404
  63.4 2.8 %collective-permute-start.17 = (f32[4,128,128]{2,1,0:T(8,128)S(1)}, f32[4,128,128]{2,1,0:T(8,128)S(1)}, u32[]{:S(2)}, u32[]{:S(2)}) collective-permute-start(f32[4,128,128]{2,1,0:T(8,128)S(1)} %get-tuple-element.145), channel_id=1, source_target_pairs={{0,4},{2,6},{4,0},{6,2},{8,12},{10,14},{12,8},{14,10},{1,5},{3,7},... | collective-permute-start | bytes 786440 | tf_op jit(solution)/shard_map/ppermute | solution.py:396
  66.2 0.6 collective-permute-start.16
  66.8 0.1 collective-permute-start.19
  66.9 1.4 %collective-permute-done.18.d_right_across = f32[4,128,128]{2,1,0:T(8,128)S(1)} collective-permute-done((f32[4,128,128]{2,1,0:T(8,128)S(1)}, f32[4,128,128]{2,1,0:T(8,128)S(1)}, u32[]{:S(2)}, u32[]{:S(2)}) %collective-permute-start.18) | collective-permute-done | bytes 262176 | tf_op jit(solution)/shard_map/ppermute | solution.py:396
  68.3 2.4 %collective-permute-start.20 = (f32[4,128,128]{2,1,0:T(8,128)S(1)}, f32[4,128,128]{2,1,0:T(8,128)S(1)}, u32[]{:S(2)}, u32[]{:S(2)}) collective-permute-start(f32[4,128,128]{2,1,0:T(8,128)S(1)} %get-tuple-element.136), channel_id=1, source_target_pairs={{0,12},{2,14},{12,0},{14,2},{4,8},{6,10},{8,4},{10,6},{1,13},{3,15... | collective-permute-start | bytes 786440 | tf_op jit(solution)/shard_map/ppermute | solution.py:396
  70.6 3.2 %collective-permute-done.15.refs_7_.refs_8_ = f32[6,128,128]{2,1,0:T(8,128)S(1)} collective-permute-done((f32[6,128,128]{2,1,0:T(8,128)S(1)}, f32[6,128,128]{2,1,0:T(8,128)S(1)}, u32[]{:S(2)}, u32[]{:S(2)}) %collective-permute-start.15) | collective-permute-done | bytes 393248 | tf_op jit(solution)/shard_map/ppermute | solution.py:404
  73.9 1.1 %shard_map.90.base = f32[4,128,128]{2,1,0:T(8,128)S(1)} custom-call(s32[3]{0:T(128)S(1)} %pad_add_fusion.place, f32[16,8,128]{2,1,0:T(8,128)S(1)} %get-tuple-element.88.refs_0_, f32[16,8,128]{2,1,0:T(8,128)S(1)} %get-tuple-element.90.refs_1_, f32[16,8,128]{2,1,0:T(8,128)S(1)} %get-tuple-element.96.out_next.refs_2_, ...), custom_call_target="tpu_custom_call" | custom-call | flops 1000 | bytes 1000 | tf_op jit(solution)/shard_map/pallas_call | solution.py:53
  75.0 1.0 %shard_map.91.refs_0_ = f32[5,128,128]{2,1,0:T(8,128)S(1)} custom-call(s32[3]{0:T(128)S(1)} %pad_add_fusion.place, f32[8,128,128]{2,1,0:T(8,128)S(1)} %get-tuple-element.73.normed, f32[8,128,128]{2,1,0:T(8,128)S(1)} %get-tuple-element.126.scale, f32[4,128,128]{2,1,0:T(8,128)S(1)} %shard_map.90.base, f32[8,128,128]{2,1,0:T(8,128)S(1)} %get-tuple-element.127.d_right, ...), custom_call_target="tpu_custom_call" | custom-call | flops 1000 | bytes 1000 | tf_op jit(solution)/shard_map/pallas_call | solution.py:53
  76.0 1.5 %collective-permute-start.21 = (f32[5,128,128]{2,1,0:T(8,128)S(1)}, f32[5,128,128]{2,1,0:T(8,128)S(1)}, u32[]{:S(2)}, u32[]{:S(2)}) collective-permute-start(f32[5,128,128]{2,1,0:T(8,128)S(1)} %shard_map.91.refs_0_), channel_id=1, source_target_pairs={{0,1},{1,0},{2,3},{3,2},{4,5},{5,4},{6,7},{7,6},{8,9},{9,8},{10,11... | collective-permute-start | bytes 983048 | tf_op jit(solution)/shard_map/ppermute | solution.py:404
  77.6 3.4 %collective-permute-done.16.refs_8_ = f32[5,128,128]{2,1,0:T(8,128)S(1)} collective-permute-done((f32[5,128,128]{2,1,0:T(8,128)S(1)}, f32[5,128,128]{2,1,0:T(8,128)S(1)}, u32[]{:S(2)}, u32[]{:S(2)}) %collective-permute-start.16) | collective-permute-done | bytes 327712 | tf_op jit(solution)/shard_map/ppermute | solution.py:404
  80.9 1.1 %shard_map.89.base = f32[4,128,128]{2,1,0:T(8,128)S(1)} custom-call(s32[3]{0:T(128)S(1)} %pad_add_fusion.place, f32[16,8,128]{2,1,0:T(8,128)S(1)} %get-tuple-element.88.refs_0_, f32[16,8,128]{2,1,0:T(8,128)S(1)} %get-tuple-element.90.refs_1_, f32[16,8,128]{2,1,0:T(8,128)S(1)} %get-tuple-element.96.out_next.refs_2_, ...), custom_call_target="tpu_custom_call" | custom-call | flops 1000 | bytes 1000 | tf_op jit(solution)/shard_map/pallas_call | solution.py:53
  82.0 4.0 %collective-permute-done.20.d_right_across = f32[4,128,128]{2,1,0:T(8,128)S(1)} collective-permute-done((f32[4,128,128]{2,1,0:T(8,128)S(1)}, f32[4,128,128]{2,1,0:T(8,128)S(1)}, u32[]{:S(2)}, u32[]{:S(2)}) %collective-permute-start.20) | collective-permute-done | bytes 262176 | tf_op jit(solution)/shard_map/ppermute | solution.py:396
  86.0 1.0 %shard_map.92.refs_1_ = f32[4,128,128]{2,1,0:T(8,128)S(1)} custom-call(s32[3]{0:T(128)S(1)} %pad_add_fusion.place, f32[8,128,128]{2,1,0:T(8,128)S(1)} %get-tuple-element.73.normed, f32[8,128,128]{2,1,0:T(8,128)S(1)} %get-tuple-element.126.scale, f32[4,128,128]{2,1,0:T(8,128)S(1)} %shard_map.89.base, f32[8,128,128]{2,1,0:T(8,128)S(1)} %get-tuple-element.127.d_right, ...), custom_call_target="tpu_custom_call" | custom-call | flops 1000 | bytes 1000 | tf_op jit(solution)/shard_map/pallas_call | solution.py:53
  87.0 0.6 collective-permute-start.22
  87.6 0.8 shard_map.93.refs_1_
  88.5 1.8 %shard_map.94 = f32[16,128,128]{2,1,0:T(8,128)} custom-call(s32[3]{0:T(128)S(1)} %pad_add_fusion.place, f32[16,8,128]{2,1,0:T(8,128)S(1)} %get-tuple-element.88.refs_0_, f32[16,8,128]{2,1,0:T(8,128)S(1)} %get-tuple-element.90.refs_1_, f32[16,8,128]{2,1,0:T(8,128)S(1)} %get-tuple-element.96.out_next.refs_2_, ...), custom_call_target="tpu_custom_call" | custom-call | flops 1000 | bytes 1000 | tf_op jit(solution)/shard_map/pallas_call | solution.py:53
  90.2 0.7 shard_map.95.refs_1_
  91.0 3.2 %collective-permute-done.22.refs_0_ = f32[4,128,128]{2,1,0:T(8,128)S(1)} collective-permute-done((f32[4,128,128]{2,1,0:T(8,128)S(1)}, f32[4,128,128]{2,1,0:T(8,128)S(1)}, u32[]{:S(2)}, u32[]{:S(2)}) %collective-permute-start.22) | collective-permute-done | bytes 262176 | tf_op jit(solution)/shard_map/ppermute | solution.py:404
  94.2 0.7 shard_map.96
  (18 shorter events, 0.1 us)
Async XLA Ops:
  0.6 7.1 %collective-permute-start = (f32[256,128]{1,0:T(8,128)}, f32[256,128]{1,0:T(8,128)S(1)}, u32[]{:S(2)}, u32[]{:S(2)}) collective-permute-start(f32[256,128]{1,0:T(8,128)} %bitcast.25), channel_id=1, source_target_pairs={{0,1},{1,0},{2,3},{3,2},{4,5},{5,4},{6,7},{7,6},{8,9},{9,8},{10,11... | collective-permute-start | bytes 393224 | tf_op jit(solution)/shard_map/ppermute | solution.py:404
  3.6 5.3 %collective-permute-start.1 = (f32[64,128]{1,0:T(8,128)}, f32[64,128]{1,0:T(8,128)S(1)}, u32[]{:S(2)}, u32[]{:S(2)}) collective-permute-start(f32[64,128]{1,0:T(8,128)} %mine_out.1), channel_id=1, source_target_pairs={{0,1},{1,0},{2,3},{3,2},{4,5},{5,4},{6,7},{7,6},{8,9},{9,8},{10,11... | collective-permute-start | bytes 98312 | tf_op jit(solution)/shard_map/ppermute | solution.py:404
  3.8 10.9 %copy-start.3 = (f32[64,128]{1,0:T(8,128)S(1)}, f32[64,128]{1,0:T(8,128)}, u32[]{:S(2)}) copy-start(f32[64,128]{1,0:T(8,128)} %mine_out.1) | copy-start | bytes 98308
  6.0 8.7 %copy-start = (f32[16,128,128]{2,1,0:T(8,128)S(1)}, f32[16,128,128]{2,1,0:T(8,128)}, u32[]{:S(2)}) copy-start(f32[16,128,128]{2,1,0:T(8,128)} %refs_10_.3) | copy-start | bytes 3145732
  6.0 8.7 %copy-start.1 = (f32[16,128,128]{2,1,0:T(8,128)S(1)}, f32[16,128,128]{2,1,0:T(8,128)}, u32[]{:S(2)}) copy-start(f32[16,128,128]{2,1,0:T(8,128)} %pair.3) | copy-start | bytes 3145732
  6.0 8.7 %copy-start.2 = (f32[128,128]{1,0:T(8,128)S(1)}, f32[128,128]{1,0:T(8,128)}, u32[]{:S(2)}) copy-start(f32[128,128]{1,0:T(8,128)} %refs_11_.3) | copy-start | bytes 196612
  6.0 8.7 %collective-permute-start.2 = (f32[8,128,128]{2,1,0:T(8,128)S(1)}, f32[8,128,128]{2,1,0:T(8,128)S(1)}, u32[]{:S(2)}, u32[]{:S(2)}) collective-permute-start(f32[8,128,128]{2,1,0:T(8,128)S(1)} %get-tuple-element.78), channel_id=1, source_target_pairs={{0,2},{2,0},{4,6},{6,4},{8,10},{10,8},{12,14},{14,12},{1,3},{3,1},... | collective-permute-start | bytes 1572872 | tf_op jit(solution)/shard_map/ppermute | solution.py:400
  6.1 8.6 %collective-permute-start.3 = (f32[8,128,128]{2,1,0:T(8,128)S(1)}, f32[8,128,128]{2,1,0:T(8,128)S(1)}, u32[]{:S(2)}, u32[]{:S(2)}) collective-permute-start(f32[8,128,128]{2,1,0:T(8,128)S(1)} %get-tuple-element.79), channel_id=1, source_target_pairs={{0,2},{2,0},{4,6},{6,4},{8,10},{10,8},{12,14},{14,12},{1,3},{3,1},... | collective-permute-start | bytes 1572872 | tf_op jit(solution)/shard_map/ppermute | solution.py:400
  8.9 13.2 %collective-permute-start.5 = (f32[8,128,128]{2,1,0:T(8,128)S(1)}, f32[8,128,128]{2,1,0:T(8,128)S(1)}, u32[]{:S(2)}, u32[]{:S(2)}) collective-permute-start(f32[8,128,128]{2,1,0:T(8,128)S(1)} %get-tuple-element.77.refs_0_), channel_id=1, source_target_pairs={{0,4},{2,6},{4,0},{6,2},{8,12},{10,14},{12,8},{14,10},{1,5},{3,7},... | collective-permute-start | bytes 1572872 | tf_op jit(solution)/shard_map/ppermute | solution.py:396
  10.8 12.0 %collective-permute-start.8 = (f32[8,128,128]{2,1,0:T(8,128)S(1)}, f32[8,128,128]{2,1,0:T(8,128)S(1)}, u32[]{:S(2)}, u32[]{:S(2)}) collective-permute-start(f32[8,128,128]{2,1,0:T(8,128)S(1)} %get-tuple-element.77.refs_0_), channel_id=1, source_target_pairs={{4,8},{6,10},{8,4},{10,6},{5,9},{7,11},{9,5},{11,7},{20,24},{22,26... | collective-permute-start | bytes 1572872 | tf_op jit(solution)/shard_map/ppermute | solution.py:396
  13.0 1.7 %collective-permute-start.4 = (f32[5,16,8,128]{3,2,1,0:T(8,128)S(1)}, f32[5,16,8,128]{3,2,1,0:T(8,128)S(1)}, u32[]{:S(2)}, u32[]{:S(2)}) collective-permute-start(f32[5,16,8,128]{3,2,1,0:T(8,128)S(1)} %shard_map.79), channel_id=1, source_target_pairs={{0,2},{2,0},{4,6},{6,4},{8,10},{10,8},{12,14},{14,12},{1,3},{3,1},... | collective-permute-start | bytes 983048 | tf_op jit(solution)/shard_map/ppermute | solution.py:400
  22.1 11.4 %collective-permute-start.6 = (f32[8,128,128]{2,1,0:T(8,128)S(1)}, f32[8,128,128]{2,1,0:T(8,128)S(1)}, u32[]{:S(2)}, u32[]{:S(2)}) collective-permute-start(f32[8,128,128]{2,1,0:T(8,128)S(1)} %collective-permute-done.5.refs_0_), channel_id=1, source_target_pairs={{4,8},{6,10},{8,4},{10,6},{5,9},{7,11},{9,5},{11,7},{20,24},{22,26... | collective-permute-start | bytes 1572872 | tf_op jit(solution)/shard_map/ppermute | solution.py:396
  22.8 15.9 %collective-permute-start.9 = (f32[8,128,128]{2,1,0:T(8,128)S(1)}, f32[8,128,128]{2,1,0:T(8,128)S(1)}, u32[]{:S(2)}, u32[]{:S(2)}) collective-permute-start(f32[8,128,128]{2,1,0:T(8,128)S(1)} %collective-permute-done.8.one), channel_id=1, source_target_pairs={{4,0},{6,2},{8,12},{10,14},{5,1},{7,3},{9,13},{11,15},{20,16},{22,... | collective-permute-start | bytes 1572872 | tf_op jit(solution)/shard_map/ppermute | solution.py:396
  31.6 1.9 %collective-permute-start.7 = (f32[2,16,8,128]{3,2,1,0:T(8,128)S(1)}, f32[2,16,8,128]{3,2,1,0:T(8,128)S(1)}, u32[]{:S(2)}, u32[]{:S(2)}) collective-permute-start(f32[2,16,8,128]{3,2,1,0:T(8,128)S(1)} %pad_maximum_fusion.1), channel_id=1, source_target_pairs={{0,2},{2,0},{4,6},{6,4},{8,10},{10,8},{12,14},{14,12},{1,3},{3,1},... | collective-permute-start | bytes 393224 | tf_op jit(solution)/shard_map/ppermute | solution.py:400
  33.5 18.5 %collective-permute-start.10 = (f32[8,128,128]{2,1,0:T(8,128)S(1)}, f32[8,128,128]{2,1,0:T(8,128)S(1)}, u32[]{:S(2)}, u32[]{:S(2)}) collective-permute-start(f32[8,128,128]{2,1,0:T(8,128)S(1)} %collective-permute-done.6.refs_0_), channel_id=1, source_target_pairs={{4,0},{6,2},{8,12},{10,14},{5,1},{7,3},{9,13},{11,15},{20,16},{22,... | collective-permute-start | bytes 1572872 | tf_op jit(solution)/shard_map/ppermute | solution.py:396
  42.5 14.7 %collective-permute-start.12 = (f32[8,128,128]{2,1,0:T(8,128)S(1)}, f32[8,128,128]{2,1,0:T(8,128)S(1)}, u32[]{:S(2)}, u32[]{:S(2)}) collective-permute-start(f32[8,128,128]{2,1,0:T(8,128)S(1)} %get-tuple-element.108), channel_id=1, source_target_pairs={{0,4},{2,6},{12,8},{14,10},{1,5},{3,7},{13,9},{15,11},{16,20},{18,... | collective-permute-start | bytes 1572872 | tf_op jit(solution)/shard_map/ppermute | solution.py:396
  45.9 11.4 %collective-permute-start.11 = (f32[8,128,128]{2,1,0:T(8,128)S(1)}, f32[8,128,128]{2,1,0:T(8,128)S(1)}, u32[]{:S(2)}, u32[]{:S(2)}) collective-permute-start(f32[8,128,128]{2,1,0:T(8,128)S(1)} %get-tuple-element.108), channel_id=1, source_target_pairs={{4,8},{6,10},{8,4},{10,6},{5,9},{7,11},{9,5},{11,7},{20,24},{22,26... | collective-permute-start | bytes 1572872 | tf_op jit(solution)/shard_map/ppermute | solution.py:396
  46.7 10.7 %collective-permute-start.13 = (f32[2,2,16,8,128]{4,3,2,1,0:T(8,128)S(1)}, f32[2,2,16,8,128]{4,3,2,1,0:T(8,128)S(1)}, u32[]{:S(2)}, u32[]{:S(2)}) collective-permute-start(f32[2,2,16,8,128]{4,3,2,1,0:T(8,128)S(1)} %pad_maximum_fusion), channel_id=1, source_target_pairs={{0,1},{1,0},{2,3},{3,2},{4,5},{5,4},{6,7},{7,6},{8,9},{9,8},{10,11... | collective-permute-start | bytes 786440 | tf_op jit(solution)/shard_map/ppermute | solution.py:404
  57.4 3.8 %collective-permute-start.14 = (f32[18,128,128]{2,1,0:T(8,128)S(1)}, f32[18,128,128]{2,1,0:T(8,128)S(1)}, u32[]{:S(2)}, u32[]{:S(2)}) collective-permute-start(f32[18,128,128]{2,1,0:T(8,128)S(1)} %get-tuple-element.115), channel_id=1, source_target_pairs={{0,2},{2,0},{4,6},{6,4},{8,10},{10,8},{12,14},{14,12},{1,3},{3,1},... | collective-permute-start | bytes 3538952 | tf_op jit(solution)/shard_map/ppermute | solution.py:400
  57.5 10.8 %collective-permute-start.18 = (f32[4,128,128]{2,1,0:T(8,128)S(1)}, f32[4,128,128]{2,1,0:T(8,128)S(1)}, u32[]{:S(2)}, u32[]{:S(2)}) collective-permute-start(f32[4,128,128]{2,1,0:T(8,128)S(1)} %get-tuple-element.147), channel_id=1, source_target_pairs={{0,12},{2,14},{12,0},{14,2},{4,8},{6,10},{8,4},{10,6},{1,13},{3,15... | collective-permute-start | bytes 786440 | tf_op jit(solution)/shard_map/ppermute | solution.py:396
  61.9 12.0 %collective-permute-start.15 = (f32[6,128,128]{2,1,0:T(8,128)S(1)}, f32[6,128,128]{2,1,0:T(8,128)S(1)}, u32[]{:S(2)}, u32[]{:S(2)}) collective-permute-start(f32[6,128,128]{2,1,0:T(8,128)S(1)} %get-tuple-element.120), channel_id=1, source_target_pairs={{0,1},{1,0},{2,3},{3,2},{4,5},{5,4},{6,7},{7,6},{8,9},{9,8},{10,11... | collective-permute-start | bytes 1179656 | tf_op jit(solution)/shard_map/ppermute | solution.py:404
  63.4 11.5 %collective-permute-start.17 = (f32[4,128,128]{2,1,0:T(8,128)S(1)}, f32[4,128,128]{2,1,0:T(8,128)S(1)}, u32[]{:S(2)}, u32[]{:S(2)}) collective-permute-start(f32[4,128,128]{2,1,0:T(8,128)S(1)} %get-tuple-element.145), channel_id=1, source_target_pairs={{0,4},{2,6},{4,0},{6,2},{8,12},{10,14},{12,8},{14,10},{1,5},{3,7},... | collective-permute-start | bytes 786440 | tf_op jit(solution)/shard_map/ppermute | solution.py:396
  66.2 14.7 %collective-permute-start.16 = (f32[5,128,128]{2,1,0:T(8,128)S(1)}, f32[5,128,128]{2,1,0:T(8,128)S(1)}, u32[]{:S(2)}, u32[]{:S(2)}) collective-permute-start(f32[5,128,128]{2,1,0:T(8,128)S(1)} %get-tuple-element.121), channel_id=1, source_target_pairs={{0,1},{1,0},{2,3},{3,2},{4,5},{5,4},{6,7},{7,6},{8,9},{9,8},{10,11... | collective-permute-start | bytes 983048 | tf_op jit(solution)/shard_map/ppermute | solution.py:404
  66.8 15.2 %collective-permute-start.19 = (f32[4,128,128]{2,1,0:T(8,128)S(1)}, f32[4,128,128]{2,1,0:T(8,128)S(1)}, u32[]{:S(2)}, u32[]{:S(2)}) collective-permute-start(f32[4,128,128]{2,1,0:T(8,128)S(1)} %get-tuple-element.144), channel_id=1, source_target_pairs={{0,4},{2,6},{4,0},{6,2},{8,12},{10,14},{12,8},{14,10},{1,5},{3,7},... | collective-permute-start | bytes 786440 | tf_op jit(solution)/shard_map/ppermute | solution.py:396
  68.3 17.7 %collective-permute-start.20 = (f32[4,128,128]{2,1,0:T(8,128)S(1)}, f32[4,128,128]{2,1,0:T(8,128)S(1)}, u32[]{:S(2)}, u32[]{:S(2)}) collective-permute-start(f32[4,128,128]{2,1,0:T(8,128)S(1)} %get-tuple-element.136), channel_id=1, source_target_pairs={{0,12},{2,14},{12,0},{14,2},{4,8},{6,10},{8,4},{10,6},{1,13},{3,15... | collective-permute-start | bytes 786440 | tf_op jit(solution)/shard_map/ppermute | solution.py:396
  76.0 12.4 %collective-permute-start.21 = (f32[5,128,128]{2,1,0:T(8,128)S(1)}, f32[5,128,128]{2,1,0:T(8,128)S(1)}, u32[]{:S(2)}, u32[]{:S(2)}) collective-permute-start(f32[5,128,128]{2,1,0:T(8,128)S(1)} %shard_map.91.refs_0_), channel_id=1, source_target_pairs={{0,1},{1,0},{2,3},{3,2},{4,5},{5,4},{6,7},{7,6},{8,9},{9,8},{10,11... | collective-permute-start | bytes 983048 | tf_op jit(solution)/shard_map/ppermute | solution.py:404
  87.0 7.2 %collective-permute-start.22 = (f32[4,128,128]{2,1,0:T(8,128)S(1)}, f32[4,128,128]{2,1,0:T(8,128)S(1)}, u32[]{:S(2)}, u32[]{:S(2)}) collective-permute-start(f32[4,128,128]{2,1,0:T(8,128)S(1)} %shard_map.92.refs_1_), channel_id=1, source_target_pairs={{0,1},{1,0},{2,3},{3,2},{4,5},{5,4},{6,7},{7,6},{8,9},{9,8},{10,11... | collective-permute-start | bytes 786440 | tf_op jit(solution)/shard_map/ppermute | solution.py:404

commit v11 on v9

--- a/solution.py
+++ b/solution.py
@@ -487,9 +487,8 @@
     cuts = [half * eighths // 8 for eighths in CUTS]
     spans = list(zip(cuts, cuts[1:]))
     swapped, to_across = lax.optimization_barrier((swapped, d_right[3] + inward))
-    to_across, to_near, early_far, d_left_sent = lax.optimization_barrier(
-        (to_across, d_right[1] + swapped, early_far, d_left_sent)
-    )
+    to_across, swapped, early_far, d_left_sent = lax.optimization_barrier((to_across, swapped, early_far, d_left_sent))
+    to_near = d_right[1] + swapped
     from_across, from_near = [along(to_across[: cuts[1]], ACROSS)], [along(to_near[: cuts[1]], NEXT)]
     received = other_core(d_left_sent)
     _, d_left_here = lax.optimization_barrier((d_left_sent, d_left_here))

time: 95.2 us -> 95 us (level)
  no operation moved by 1% of the time
where the time goes in v11:
time: 95 us; the launch traced here: 94.8 us
  Pallas kernels  40.9 us (43%)
  starting transfers between devices  28.1 us (30%)
  waiting for transfers between devices  24.4 us (26%)
  between operations  1.01 us (1%)
    pallas_call x17, Pallas kernels, call(): pl.pallas_call(kernel, out_shape=[jax.ShapeDtypeStruct(shape, F32) for sh...  38.7 us
    ppermute x11, starting transfers between devices, along(): lax.ppermute(block, 'row', [(2 * a + core, 2 * b + core) for a, b in pair...  17.5 us
    ppermute x11, waiting for transfers between devices, along(): lax.ppermute(block, 'row', [(2 * a + core, 2 * b + core) for a, b in pair...  11.5 us
    ppermute x7, waiting for transfers between devices, other_half(): return lax.ppermute(block, 'ch', [(0, 1), (1, 0)])  11.3 us
    ppermute x7, starting transfers between devices, other_half(): return lax.ppermute(block, 'ch', [(0, 1), (1, 0)])  9.76 us
    pallas_call x3, Pallas kernels, join(): pl.pallas_call(functools.partial(join_kernel, firsts, sides), out_shape=j...  2.24 us
  transfers between devices with their start and end apart: 23, of which 9 were waited for; matrix products, arithmetic and copies ran while one was open for 0% of the time, Pallas kernels for 42%

profile of v11, /device:TPU:0, one launch (start us, length us, event | category | flops | bytes accessed | tf_op | source)
XLA Modules:
  0.0 94.8 jit_solution(3720399857145506469)
XLA Ops:
  0.6 3.0 %collective-permute-start = (f32[256,128]{1,0:T(8,128)}, f32[256,128]{1,0:T(8,128)S(1)}, u32[]{:S(2)}, u32[]{:S(2)}) collective-permute-start(f32[256,128]{1,0:T(8,128)} %bitcast.25), channel_id=1, source_target_pairs={{0,1},{1,0},{2,3},{3,2},{4,5},{5,4},{6,7},{7,6},{8,9},{9,8},{10,11... | collective-permute-start | bytes 393224 | tf_op jit(solution)/shard_map/ppermute | solution.py:396
  3.6 0.1 collective-permute-start.1
  3.7 0.1 pad_add_fusion.place
  3.8 2.2 %shard_map.77 = (f32[8,128,128]{2,1,0:T(8,128)S(1)}, f32[8,128,128]{2,1,0:T(8,128)S(1)}, f32[16,128]{1,0:T(8,128)S(1)}, f32[4,64,128]{2,1,0:T(8,128)S(1)}, f32[8...) custom-call(s32[3]{0:T(128)S(1)} %pad_add_fusion.place, f32[16,128,128]{2,1,0:T(8,128)} %pair.3, s32[16,128]{1,0:T(8,128)} %mask.1, ...), custom_call_target="tpu_custom_call" | custom-call | flops 1000 | bytes 1000 | tf_op jit(solution)/shard_map/pallas_call | solution.py:53
  6.0 0.0 copy-start
  6.0 0.0 copy-start.1
  6.0 0.0 copy-start.2
  6.0 0.1 collective-permute-start.2
  6.1 0.5 collective-permute-start.3
  6.6 1.1 %collective-permute-done = f32[256,128]{1,0:T(8,128)S(1)} collective-permute-done((f32[256,128]{1,0:T(8,128)}, f32[256,128]{1,0:T(8,128)S(1)}, u32[]{:S(2)}, u32[]{:S(2)}) %collective-permute-start) | collective-permute-done | bytes 131104 | tf_op jit(solution)/shard_map/ppermute | solution.py:396
  7.7 1.2 %shard_map.78 = (f32[8,128,128]{2,1,0:T(8,128)S(1)}, f32[8,128,128]{2,1,0:T(8,128)S(1)}, f32[8,128,128]{2,1,0:T(8,128)S(1)}) custom-call(s32[3]{0:T(128)S(1)} %pad_add_fusion.place, f32[8,128,128]{2,1,0:T(8,128)S(1)} %get-tuple-element.72.normed, f32[16,128]{1,0:T(8,128)S(1)} %get-tuple-element.73.keep, f32[4,64,128]{2,1,0:T(8,128)S(1)} %get-tuple-element.74.mine.refs_15_, ...), custom_call_target="tpu_custom_call" | custom-call | flops 1000 | bytes 1000 | tf_op jit(solution)/shard_map/pallas_call | solution.py:53
  8.9 0.0 collective-permute-done.1.other_out
  8.9 1.9 %collective-permute-start.5 = (f32[8,128,128]{2,1,0:T(8,128)S(1)}, f32[8,128,128]{2,1,0:T(8,128)S(1)}, u32[]{:S(2)}, u32[]{:S(2)}) collective-permute-start(f32[8,128,128]{2,1,0:T(8,128)S(1)} %get-tuple-element.76.refs_0_), channel_id=1, source_target_pairs={{0,4},{2,6},{4,0},{6,2},{8,12},{10,14},{12,8},{14,10},{1,5},{3,7},... | collective-permute-start | bytes 1572872 | tf_op jit(solution)/shard_map/ppermute | solution.py:388
  10.8 0.7 collective-permute-start.8
  11.5 1.5 %shard_map.79 = f32[5,16,8,128]{3,2,1,0:T(8,128)S(1)} custom-call(s32[3]{0:T(128)S(1)} %pad_add_fusion.place, f32[16,128,128]{2,1,0:T(8,128)} %refs_10_.3, f32[16,128]{1,0:T(8,128)S(1)} %get-tuple-element.73.keep), custom_call_target="tpu_custom_call" | custom-call | flops 1000 | bytes 1000 | tf_op jit(solution)/shard_map/pallas_call | solution.py:53
  13.0 0.1 collective-permute-start.4
  13.1 1.6 %collective-permute-done.4.third = f32[5,16,8,128]{3,2,1,0:T(8,128)S(1)} collective-permute-done((f32[5,16,8,128]{3,2,1,0:T(8,128)S(1)}, f32[5,16,8,128]{3,2,1,0:T(8,128)S(1)}, u32[]{:S(2)}, u32[]{:S(2)}) %collective-permute-start.4) | collective-permute-done | bytes 327712 | tf_op jit(solution)/shard_map/ppermute | solution.py:392
  14.7 0.0 collective-permute-done.2.first
  14.7 0.0 collective-permute-done.3.second
  14.8 3.8 %shard_map.80 = (f32[16,128,128]{2,1,0:T(8,128)S(1)}, f32[16,128,128]{2,1,0:T(8,128)S(1)}, f32[8,128,128]{2,1,0:T(8,128)S(1)}, f32[8,128,128]{2,1,0:T(8,128)S(1)...) custom-call(s32[3]{0:T(128)S(1)} %pad_add_fusion.place, ...), custom_call_target="tpu_custom_call" | custom-call | flops 1000 | bytes 1000 | tf_op jit(solution)/shard_map/pallas_call | solution.py:53
  18.6 3.5 %collective-permute-done.5.refs_0_ = f32[8,128,128]{2,1,0:T(8,128)S(1)} collective-permute-done((f32[8,128,128]{2,1,0:T(8,128)S(1)}, f32[8,128,128]{2,1,0:T(8,128)S(1)}, u32[]{:S(2)}, u32[]{:S(2)}) %collective-permute-start.5) | collective-permute-done | bytes 524320 | tf_op jit(solution)/shard_map/ppermute | solution.py:388
  22.1 0.7 collective-permute-start.6
  22.8 1.3 %collective-permute-start.9 = (f32[8,128,128]{2,1,0:T(8,128)S(1)}, f32[8,128,128]{2,1,0:T(8,128)S(1)}, u32[]{:S(2)}, u32[]{:S(2)}) collective-permute-start(f32[8,128,128]{2,1,0:T(8,128)S(1)} %collective-permute-done.8.one), channel_id=1, source_target_pairs={{4,0},{6,2},{8,12},{10,14},{5,1},{7,3},{9,13},{11,15},{20,16},{22,... | collective-permute-start | bytes 1572872 | tf_op jit(solution)/shard_map/ppermute | solution.py:388
  24.1 3.8 %shard_map.81 = (f32[16,8,128]{2,1,0:T(8,128)S(1)}, f32[16,8,128]{2,1,0:T(8,128)S(1)}, f32[256,128]{1,0:T(8,128)S(1)}, f32[8,128,128]{2,1,0:T(8,128)S(1)}) custom-call(s32[3]{0:T(128)S(1)} %pad_add_fusion.place, f32[8,128,128]{2,1,0:T(8,128)S(1)} %get-tuple-element.76.refs_0_, f32[16,128,128]{2,1,0:T(8,128)S(1)} %get-tuple-element.81.refs_1_.refs_2_.left_here, ...), custom_call_target="tpu_custom_call" | custom-call | flops 1000 | bytes 1000 | tf_op jit(solution)/shard_map/pallas_call | solution.py:53
  27.9 3.7 %shard_map.82 = (f32[16,8,128]{2,1,0:T(8,128)S(1)}, f32[16,8,128]{2,1,0:T(8,128)S(1)}, f32[256,128]{1,0:T(8,128)S(1)}, f32[8,128,128]{2,1,0:T(8,128)S(1)}) custom-call(s32[3]{0:T(128)S(1)} %pad_add_fusion.place, f32[8,128,128]{2,1,0:T(8,128)S(1)} %collective-permute-done.5.refs_0_, f32[16,128,128]{2,1,0:T(8,128)S(1)} %get-tuple-element.81.refs_1_.refs_2_.left_here, ...), custom_call_target="tpu_custom_call" | custom-call | flops 1000 | bytes 1000 | tf_op jit(solution)/shard_map/pallas_call | solution.py:53
  31.6 0.1 collective-permute-start.7
  31.7 1.8 %shard_map.83 = (f32[16,128,128]{2,1,0:T(8,128)S(1)}, f32[16,128,128]{2,1,0:T(8,128)S(1)}) custom-call(s32[3]{0:T(128)S(1)} %pad_add_fusion.place, f32[8,128,128]{2,1,0:T(8,128)S(1)} %get-tuple-element.76.refs_0_, f32[256,128]{1,0:T(8,128)S(1)} %get-tuple-element.92.refs_1_), custom_call_target="tpu_custom_call" | custom-call | flops 1000 | bytes 1000 | tf_op jit(solution)/shard_map/pallas_call | solution.py:53
  33.5 0.0 collective-permute-done.7.refs_4_
  33.5 0.0 collective-permute-done.6.refs_0_
  33.5 1.3 %collective-permute-start.10 = (f32[8,128,128]{2,1,0:T(8,128)S(1)}, f32[8,128,128]{2,1,0:T(8,128)S(1)}, u32[]{:S(2)}, u32[]{:S(2)}) collective-permute-start(f32[8,128,128]{2,1,0:T(8,128)S(1)} %collective-permute-done.6.refs_0_), channel_id=1, source_target_pairs={{4,0},{6,2},{8,12},{10,14},{5,1},{7,3},{9,13},{11,15},{20,16},{22,... | collective-permute-start | bytes 1572872 | tf_op jit(solution)/shard_map/ppermute | solution.py:388
  34.8 3.9 %collective-permute-done.9.refs_1_ = f32[8,128,128]{2,1,0:T(8,128)S(1)} collective-permute-done((f32[8,128,128]{2,1,0:T(8,128)S(1)}, f32[8,128,128]{2,1,0:T(8,128)S(1)}, u32[]{:S(2)}, u32[]{:S(2)}) %collective-permute-start.9) | collective-permute-done | bytes 524320 | tf_op jit(solution)/shard_map/ppermute | solution.py:388
  38.7 3.8 %shard_map.84 = (f32[16,8,128]{2,1,0:T(8,128)S(1)}, f32[16,8,128]{2,1,0:T(8,128)S(1)}, f32[256,128]{1,0:T(8,128)S(1)}, f32[8,128,128]{2,1,0:T(8,128)S(1)}, f32[8,128,128]{2,1,0:T(8,128)S(1)}) custom-call(s32[3]{0:T(128)S(1)} %pad_add_fusion.place, f32[8,128,128]{2,1,0:T(8,128)S(1)} %collective-permute-done.6.refs_0_, ...), custom_call_target="tpu_custom_call" | custom-call | flops 1000 | bytes 1000 | tf_op jit(solution)/shard_map/pallas_call | solution.py:53
  42.5 3.4 %collective-permute-start.12 = (f32[8,128,128]{2,1,0:T(8,128)S(1)}, f32[8,128,128]{2,1,0:T(8,128)S(1)}, u32[]{:S(2)}, u32[]{:S(2)}) collective-permute-start(f32[8,128,128]{2,1,0:T(8,128)S(1)} %get-tuple-element.107), channel_id=1, source_target_pairs={{0,4},{2,6},{12,8},{14,10},{1,5},{3,7},{13,9},{15,11},{16,20},{18,... | collective-permute-start | bytes 1572872 | tf_op jit(solution)/shard_map/ppermute | solution.py:388
  45.9 0.7 collective-permute-start.11
  46.7 1.6 %collective-permute-start.13 = (f32[2,2,16,8,128]{4,3,2,1,0:T(8,128)S(1)}, f32[2,2,16,8,128]{4,3,2,1,0:T(8,128)S(1)}, u32[]{:S(2)}, u32[]{:S(2)}) collective-permute-start(f32[2,2,16,8,128]{4,3,2,1,0:T(8,128)S(1)} %pad_maximum_fusion), channel_id=1, source_target_pairs={{0,1},{1,0},{2,3},{3,2},{4,5},{5,4},{6,7},{7,6},{8,9},{9,8},{10,11... | collective-permute-start | bytes 786440 | tf_op jit(solution)/shard_map/ppermute | solution.py:396
  48.2 3.8 %shard_map.85 = (f32[16,128,128]{2,1,0:T(8,128)S(1)}, f32[16,128,128]{2,1,0:T(8,128)S(1)}) custom-call(s32[3]{0:T(128)S(1)} %pad_add_fusion.place, f32[8,128,128]{2,1,0:T(8,128)S(1)} %collective-permute-done.5.refs_0_, f32[8,128,128]{2,1,0:T(8,128)S(1)} %get-tuple-element.96.refs_1_, f32[256,128]{1,0:T(8,128)S(1)} %get-tuple-element.97.refs_2_, ...), custom_call_target="tpu_custom_call" | custom-call | flops 1000 | bytes 1000 | tf_op jit(solution)/shard_map/pallas_call | solution.py:53
  52.0 0.0 collective-permute-done.10.two
  52.0 5.1 %shard_map.86 = (f32[16,8,128]{2,1,0:T(8,128)S(1)}, f32[16,8,128]{2,1,0:T(8,128)}, f32[256,128]{1,0:T(8,128)S(1)}, f32[8,128,128]{2,1,0:T(8,128)S(1)}, f32[8,128...) custom-call(s32[3]{0:T(128)S(1)} %pad_add_fusion.place, f32[8,128,128]{2,1,0:T(8,128)S(1)} %collective-permute-done.8.one, ...), custom_call_target="tpu_custom_call" | custom-call | flops 1000 | bytes 1000 | tf_op jit(solution)/shard_map/pallas_call | solution.py:53
  57.2 0.1 add.12
  57.3 0.1 collective-permute-start.14
  57.4 2.4 %collective-permute-start.18 = (f32[4,128,128]{2,1,0:T(8,128)S(1)}, f32[4,128,128]{2,1,0:T(8,128)S(1)}, u32[]{:S(2)}, u32[]{:S(2)}) collective-permute-start(f32[4,128,128]{2,1,0:T(8,128)S(1)} %get-tuple-element.145), channel_id=1, source_target_pairs={{0,12},{2,14},{12,0},{14,2},{4,8},{6,10},{8,4},{10,6},{1,13},{3,15... | collective-permute-start | bytes 786440 | tf_op jit(solution)/shard_map/ppermute | solution.py:388
  59.9 1.2 %shard_map.87.kept = f32[16,128,128]{2,1,0:T(8,128)S(1)} custom-call(s32[3]{0:T(128)S(1)} %pad_add_fusion.place, f32[8,128,128]{2,1,0:T(8,128)S(1)} %get-tuple-element.114.right, f32[256,128]{1,0:T(8,128)S(1)} %get-tuple-element.115.d_x, f32[16,128,128]{2,1,0:T(8,128)S(1)} %get-tuple-element.117.here), custom_call_target="tpu_custom_call" | custom-call | flops 1000 | bytes 1000 | tf_op jit(solution)/shard_map/pallas_call | solution.py:53
  61.1 0.1 add.13
  61.2 0.7 shard_map.88
  61.9 1.5 %collective-permute-start.15 = (f32[6,128,128]{2,1,0:T(8,128)S(1)}, f32[6,128,128]{2,1,0:T(8,128)S(1)}, u32[]{:S(2)}, u32[]{:S(2)}) collective-permute-start(f32[6,128,128]{2,1,0:T(8,128)S(1)} %get-tuple-element.118), channel_id=1, source_target_pairs={{0,1},{1,0},{2,3},{3,2},{4,5},{5,4},{6,7},{7,6},{8,9},{9,8},{10,11... | collective-permute-start | bytes 1179656 | tf_op jit(solution)/shard_map/ppermute | solution.py:396
  63.4 0.6 collective-permute-start.16
  64.0 2.7 %collective-permute-start.17 = (f32[4,128,128]{2,1,0:T(8,128)S(1)}, f32[4,128,128]{2,1,0:T(8,128)S(1)}, u32[]{:S(2)}, u32[]{:S(2)}) collective-permute-start(f32[4,128,128]{2,1,0:T(8,128)S(1)} %get-tuple-element.143), channel_id=1, source_target_pairs={{0,4},{2,6},{4,0},{6,2},{8,12},{10,14},{12,8},{14,10},{1,5},{3,7},... | collective-permute-start | bytes 786440 | tf_op jit(solution)/shard_map/ppermute | solution.py:388
  66.7 0.1 collective-permute-start.19
  66.8 1.4 %collective-permute-done.18.d_right_across = f32[4,128,128]{2,1,0:T(8,128)S(1)} collective-permute-done((f32[4,128,128]{2,1,0:T(8,128)S(1)}, f32[4,128,128]{2,1,0:T(8,128)S(1)}, u32[]{:S(2)}, u32[]{:S(2)}) %collective-permute-start.18) | collective-permute-done | bytes 262176 | tf_op jit(solution)/shard_map/ppermute | solution.py:388
  68.2 2.4 %collective-permute-start.20 = (f32[4,128,128]{2,1,0:T(8,128)S(1)}, f32[4,128,128]{2,1,0:T(8,128)S(1)}, u32[]{:S(2)}, u32[]{:S(2)}) collective-permute-start(f32[4,128,128]{2,1,0:T(8,128)S(1)} %get-tuple-element.134), channel_id=1, source_target_pairs={{0,12},{2,14},{12,0},{14,2},{4,8},{6,10},{8,4},{10,6},{1,13},{3,15... | collective-permute-start | bytes 786440 | tf_op jit(solution)/shard_map/ppermute | solution.py:388
  70.6 3.3 %collective-permute-done.15.refs_7_.refs_8_ = f32[6,128,128]{2,1,0:T(8,128)S(1)} collective-permute-done((f32[6,128,128]{2,1,0:T(8,128)S(1)}, f32[6,128,128]{2,1,0:T(8,128)S(1)}, u32[]{:S(2)}, u32[]{:S(2)}) %collective-permute-start.15) | collective-permute-done | bytes 393248 | tf_op jit(solution)/shard_map/ppermute | solution.py:396
  73.9 1.1 %shard_map.90.base = f32[4,128,128]{2,1,0:T(8,128)S(1)} custom-call(s32[3]{0:T(128)S(1)} %pad_add_fusion.place, f32[16,8,128]{2,1,0:T(8,128)S(1)} %get-tuple-element.87.refs_0_, f32[16,8,128]{2,1,0:T(8,128)S(1)} %get-tuple-element.89.refs_1_, f32[16,8,128]{2,1,0:T(8,128)S(1)} %get-tuple-element.95.out_next.refs_2_, ...), custom_call_target="tpu_custom_call" | custom-call | flops 1000 | bytes 1000 | tf_op jit(solution)/shard_map/pallas_call | solution.py:53
  75.0 1.0 %shard_map.91.refs_0_ = f32[4,128,128]{2,1,0:T(8,128)S(1)} custom-call(s32[3]{0:T(128)S(1)} %pad_add_fusion.place, f32[8,128,128]{2,1,0:T(8,128)S(1)} %get-tuple-element.72.normed, f32[8,128,128]{2,1,0:T(8,128)S(1)} %get-tuple-element.124.scale, f32[4,128,128]{2,1,0:T(8,128)S(1)} %shard_map.90.base, f32[8,128,128]{2,1,0:T(8,128)S(1)} %get-tuple-element.125.d_right, ...), custom_call_target="tpu_custom_call" | custom-call | flops 1000 | bytes 1000 | tf_op jit(solution)/shard_map/pallas_call | solution.py:53
  76.0 1.5 %collective-permute-start.21 = (f32[4,128,128]{2,1,0:T(8,128)S(1)}, f32[4,128,128]{2,1,0:T(8,128)S(1)}, u32[]{:S(2)}, u32[]{:S(2)}) collective-permute-start(f32[4,128,128]{2,1,0:T(8,128)S(1)} %shard_map.91.refs_0_), channel_id=1, source_target_pairs={{0,1},{1,0},{2,3},{3,2},{4,5},{5,4},{6,7},{7,6},{8,9},{9,8},{10,11... | collective-permute-start | bytes 786440 | tf_op jit(solution)/shard_map/ppermute | solution.py:396
  77.5 4.8 %collective-permute-done.16.refs_8_ = f32[6,128,128]{2,1,0:T(8,128)S(1)} collective-permute-done((f32[6,128,128]{2,1,0:T(8,128)S(1)}, f32[6,128,128]{2,1,0:T(8,128)S(1)}, u32[]{:S(2)}, u32[]{:S(2)}) %collective-permute-start.16) | collective-permute-done | bytes 393248 | tf_op jit(solution)/shard_map/ppermute | solution.py:396
  82.3 1.1 %shard_map.89.base = f32[4,128,128]{2,1,0:T(8,128)S(1)} custom-call(s32[3]{0:T(128)S(1)} %pad_add_fusion.place, f32[16,8,128]{2,1,0:T(8,128)S(1)} %get-tuple-element.87.refs_0_, f32[16,8,128]{2,1,0:T(8,128)S(1)} %get-tuple-element.89.refs_1_, f32[16,8,128]{2,1,0:T(8,128)S(1)} %get-tuple-element.95.out_next.refs_2_, ...), custom_call_target="tpu_custom_call" | custom-call | flops 1000 | bytes 1000 | tf_op jit(solution)/shard_map/pallas_call | solution.py:53
  83.4 2.7 %collective-permute-done.20.d_right_across = f32[4,128,128]{2,1,0:T(8,128)S(1)} collective-permute-done((f32[4,128,128]{2,1,0:T(8,128)S(1)}, f32[4,128,128]{2,1,0:T(8,128)S(1)}, u32[]{:S(2)}, u32[]{:S(2)}) %collective-permute-start.20) | collective-permute-done | bytes 262176 | tf_op jit(solution)/shard_map/ppermute | solution.py:388
  86.1 1.0 %shard_map.92.refs_1_ = f32[4,128,128]{2,1,0:T(8,128)S(1)} custom-call(s32[3]{0:T(128)S(1)} %pad_add_fusion.place, f32[8,128,128]{2,1,0:T(8,128)S(1)} %get-tuple-element.72.normed, f32[8,128,128]{2,1,0:T(8,128)S(1)} %get-tuple-element.124.scale, f32[4,128,128]{2,1,0:T(8,128)S(1)} %shard_map.89.base, f32[8,128,128]{2,1,0:T(8,128)S(1)} %get-tuple-element.125.d_right, ...), custom_call_target="tpu_custom_call" | custom-call | flops 1000 | bytes 1000 | tf_op jit(solution)/shard_map/pallas_call | solution.py:53
  87.2 1.5 %collective-permute-start.22 = (f32[4,128,128]{2,1,0:T(8,128)S(1)}, f32[4,128,128]{2,1,0:T(8,128)S(1)}, u32[]{:S(2)}, u32[]{:S(2)}) collective-permute-start(f32[4,128,128]{2,1,0:T(8,128)S(1)} %shard_map.92.refs_1_), channel_id=1, source_target_pairs={{0,1},{1,0},{2,3},{3,2},{4,5},{5,4},{6,7},{7,6},{8,9},{9,8},{10,11... | collective-permute-start | bytes 786440 | tf_op jit(solution)/shard_map/ppermute | solution.py:396
  88.7 1.8 %shard_map.94 = f32[16,128,128]{2,1,0:T(8,128)} custom-call(s32[3]{0:T(128)S(1)} %pad_add_fusion.place, f32[16,8,128]{2,1,0:T(8,128)S(1)} %get-tuple-element.87.refs_0_, f32[16,8,128]{2,1,0:T(8,128)S(1)} %get-tuple-element.89.refs_1_, f32[16,8,128]{2,1,0:T(8,128)S(1)} %get-tuple-element.95.out_next.refs_2_, ...), custom_call_target="tpu_custom_call" | custom-call | flops 1000 | bytes 1000 | tf_op jit(solution)/shard_map/pallas_call | solution.py:53
  90.4 0.8 shard_map.93.refs_1_
  91.3 0.7 shard_map.95.refs_1_
  92.0 2.1 %collective-permute-done.22.refs_0_ = f32[4,128,128]{2,1,0:T(8,128)S(1)} collective-permute-done((f32[4,128,128]{2,1,0:T(8,128)S(1)}, f32[4,128,128]{2,1,0:T(8,128)S(1)}, u32[]{:S(2)}, u32[]{:S(2)}) %collective-permute-start.22) | collective-permute-done | bytes 262176 | tf_op jit(solution)/shard_map/ppermute | solution.py:396
  94.1 0.7 shard_map.96
  (18 shorter events, 0.1 us)
Async XLA Ops:
  0.6 7.1 %collective-permute-start = (f32[256,128]{1,0:T(8,128)}, f32[256,128]{1,0:T(8,128)S(1)}, u32[]{:S(2)}, u32[]{:S(2)}) collective-permute-start(f32[256,128]{1,0:T(8,128)} %bitcast.25), channel_id=1, source_target_pairs={{0,1},{1,0},{2,3},{3,2},{4,5},{5,4},{6,7},{7,6},{8,9},{9,8},{10,11... | collective-permute-start | bytes 393224 | tf_op jit(solution)/shard_map/ppermute | solution.py:396
  3.6 5.3 %collective-permute-start.1 = (f32[64,128]{1,0:T(8,128)}, f32[64,128]{1,0:T(8,128)S(1)}, u32[]{:S(2)}, u32[]{:S(2)}) collective-permute-start(f32[64,128]{1,0:T(8,128)} %mine_out.1), channel_id=1, source_target_pairs={{0,1},{1,0},{2,3},{3,2},{4,5},{5,4},{6,7},{7,6},{8,9},{9,8},{10,11... | collective-permute-start | bytes 98312 | tf_op jit(solution)/shard_map/ppermute | solution.py:396
  3.8 10.9 %copy-start.3 = (f32[64,128]{1,0:T(8,128)S(1)}, f32[64,128]{1,0:T(8,128)}, u32[]{:S(2)}) copy-start(f32[64,128]{1,0:T(8,128)} %mine_out.1) | copy-start | bytes 98308
  6.0 8.7 %copy-start = (f32[16,128,128]{2,1,0:T(8,128)S(1)}, f32[16,128,128]{2,1,0:T(8,128)}, u32[]{:S(2)}) copy-start(f32[16,128,128]{2,1,0:T(8,128)} %refs_10_.3) | copy-start | bytes 3145732
  6.0 8.7 %copy-start.1 = (f32[16,128,128]{2,1,0:T(8,128)S(1)}, f32[16,128,128]{2,1,0:T(8,128)}, u32[]{:S(2)}) copy-start(f32[16,128,128]{2,1,0:T(8,128)} %pair.3) | copy-start | bytes 3145732
  6.0 8.7 %copy-start.2 = (f32[128,128]{1,0:T(8,128)S(1)}, f32[128,128]{1,0:T(8,128)}, u32[]{:S(2)}) copy-start(f32[128,128]{1,0:T(8,128)} %refs_11_.3) | copy-start | bytes 196612
  6.0 8.7 %collective-permute-start.2 = (f32[8,128,128]{2,1,0:T(8,128)S(1)}, f32[8,128,128]{2,1,0:T(8,128)S(1)}, u32[]{:S(2)}, u32[]{:S(2)}) collective-permute-start(f32[8,128,128]{2,1,0:T(8,128)S(1)} %get-tuple-element.77), channel_id=1, source_target_pairs={{0,2},{2,0},{4,6},{6,4},{8,10},{10,8},{12,14},{14,12},{1,3},{3,1},... | collective-permute-start | bytes 1572872 | tf_op jit(solution)/shard_map/ppermute | solution.py:392
  6.1 8.6 %collective-permute-start.3 = (f32[8,128,128]{2,1,0:T(8,128)S(1)}, f32[8,128,128]{2,1,0:T(8,128)S(1)}, u32[]{:S(2)}, u32[]{:S(2)}) collective-permute-start(f32[8,128,128]{2,1,0:T(8,128)S(1)} %get-tuple-element.78), channel_id=1, source_target_pairs={{0,2},{2,0},{4,6},{6,4},{8,10},{10,8},{12,14},{14,12},{1,3},{3,1},... | collective-permute-start | bytes 1572872 | tf_op jit(solution)/shard_map/ppermute | solution.py:392
  8.9 13.2 %collective-permute-start.5 = (f32[8,128,128]{2,1,0:T(8,128)S(1)}, f32[8,128,128]{2,1,0:T(8,128)S(1)}, u32[]{:S(2)}, u32[]{:S(2)}) collective-permute-start(f32[8,128,128]{2,1,0:T(8,128)S(1)} %get-tuple-element.76.refs_0_), channel_id=1, source_target_pairs={{0,4},{2,6},{4,0},{6,2},{8,12},{10,14},{12,8},{14,10},{1,5},{3,7},... | collective-permute-start | bytes 1572872 | tf_op jit(solution)/shard_map/ppermute | solution.py:388
  10.8 12.0 %collective-permute-start.8 = (f32[8,128,128]{2,1,0:T(8,128)S(1)}, f32[8,128,128]{2,1,0:T(8,128)S(1)}, u32[]{:S(2)}, u32[]{:S(2)}) collective-permute-start(f32[8,128,128]{2,1,0:T(8,128)S(1)} %get-tuple-element.76.refs_0_), channel_id=1, source_target_pairs={{4,8},{6,10},{8,4},{10,6},{5,9},{7,11},{9,5},{11,7},{20,24},{22,26... | collective-permute-start | bytes 1572872 | tf_op jit(solution)/shard_map/ppermute | solution.py:388
  13.0 1.7 %collective-permute-start.4 = (f32[5,16,8,128]{3,2,1,0:T(8,128)S(1)}, f32[5,16,8,128]{3,2,1,0:T(8,128)S(1)}, u32[]{:S(2)}, u32[]{:S(2)}) collective-permute-start(f32[5,16,8,128]{3,2,1,0:T(8,128)S(1)} %shard_map.79), channel_id=1, source_target_pairs={{0,2},{2,0},{4,6},{6,4},{8,10},{10,8},{12,14},{14,12},{1,3},{3,1},... | collective-permute-start | bytes 983048 | tf_op jit(solution)/shard_map/ppermute | solution.py:392
  22.1 11.4 %collective-permute-start.6 = (f32[8,128,128]{2,1,0:T(8,128)S(1)}, f32[8,128,128]{2,1,0:T(8,128)S(1)}, u32[]{:S(2)}, u32[]{:S(2)}) collective-permute-start(f32[8,128,128]{2,1,0:T(8,128)S(1)} %collective-permute-done.5.refs_0_), channel_id=1, source_target_pairs={{4,8},{6,10},{8,4},{10,6},{5,9},{7,11},{9,5},{11,7},{20,24},{22,26... | collective-permute-start | bytes 1572872 | tf_op jit(solution)/shard_map/ppermute | solution.py:388
  22.8 15.9 %collective-permute-start.9 = (f32[8,128,128]{2,1,0:T(8,128)S(1)}, f32[8,128,128]{2,1,0:T(8,128)S(1)}, u32[]{:S(2)}, u32[]{:S(2)}) collective-permute-start(f32[8,128,128]{2,1,0:T(8,128)S(1)} %collective-permute-done.8.one), channel_id=1, source_target_pairs={{4,0},{6,2},{8,12},{10,14},{5,1},{7,3},{9,13},{11,15},{20,16},{22,... | collective-permute-start | bytes 1572872 | tf_op jit(solution)/shard_map/ppermute | solution.py:388
  31.6 1.9 %collective-permute-start.7 = (f32[2,16,8,128]{3,2,1,0:T(8,128)S(1)}, f32[2,16,8,128]{3,2,1,0:T(8,128)S(1)}, u32[]{:S(2)}, u32[]{:S(2)}) collective-permute-start(f32[2,16,8,128]{3,2,1,0:T(8,128)S(1)} %pad_maximum_fusion.1), channel_id=1, source_target_pairs={{0,2},{2,0},{4,6},{6,4},{8,10},{10,8},{12,14},{14,12},{1,3},{3,1},... | collective-permute-start | bytes 393224 | tf_op jit(solution)/shard_map/ppermute | solution.py:392
  33.5 18.5 %collective-permute-start.10 = (f32[8,128,128]{2,1,0:T(8,128)S(1)}, f32[8,128,128]{2,1,0:T(8,128)S(1)}, u32[]{:S(2)}, u32[]{:S(2)}) collective-permute-start(f32[8,128,128]{2,1,0:T(8,128)S(1)} %collective-permute-done.6.refs_0_), channel_id=1, source_target_pairs={{4,0},{6,2},{8,12},{10,14},{5,1},{7,3},{9,13},{11,15},{20,16},{22,... | collective-permute-start | bytes 1572872 | tf_op jit(solution)/shard_map/ppermute | solution.py:388
  42.5 14.7 %collective-permute-start.12 = (f32[8,128,128]{2,1,0:T(8,128)S(1)}, f32[8,128,128]{2,1,0:T(8,128)S(1)}, u32[]{:S(2)}, u32[]{:S(2)}) collective-permute-start(f32[8,128,128]{2,1,0:T(8,128)S(1)} %get-tuple-element.107), channel_id=1, source_target_pairs={{0,4},{2,6},{12,8},{14,10},{1,5},{3,7},{13,9},{15,11},{16,20},{18,... | collective-permute-start | bytes 1572872 | tf_op jit(solution)/shard_map/ppermute | solution.py:388
  45.9 11.4 %collective-permute-start.11 = (f32[8,128,128]{2,1,0:T(8,128)S(1)}, f32[8,128,128]{2,1,0:T(8,128)S(1)}, u32[]{:S(2)}, u32[]{:S(2)}) collective-permute-start(f32[8,128,128]{2,1,0:T(8,128)S(1)} %get-tuple-element.107), channel_id=1, source_target_pairs={{4,8},{6,10},{8,4},{10,6},{5,9},{7,11},{9,5},{11,7},{20,24},{22,26... | collective-permute-start | bytes 1572872 | tf_op jit(solution)/shard_map/ppermute | solution.py:388
  46.7 10.6 %collective-permute-start.13 = (f32[2,2,16,8,128]{4,3,2,1,0:T(8,128)S(1)}, f32[2,2,16,8,128]{4,3,2,1,0:T(8,128)S(1)}, u32[]{:S(2)}, u32[]{:S(2)}) collective-permute-start(f32[2,2,16,8,128]{4,3,2,1,0:T(8,128)S(1)} %pad_maximum_fusion), channel_id=1, source_target_pairs={{0,1},{1,0},{2,3},{3,2},{4,5},{5,4},{6,7},{7,6},{8,9},{9,8},{10,11... | collective-permute-start | bytes 786440 | tf_op jit(solution)/shard_map/ppermute | solution.py:396
  57.3 3.9 %collective-permute-start.14 = (f32[18,128,128]{2,1,0:T(8,128)S(1)}, f32[18,128,128]{2,1,0:T(8,128)S(1)}, u32[]{:S(2)}, u32[]{:S(2)}) collective-permute-start(f32[18,128,128]{2,1,0:T(8,128)S(1)} %get-tuple-element.113), channel_id=1, source_target_pairs={{0,2},{2,0},{4,6},{6,4},{8,10},{10,8},{12,14},{14,12},{1,3},{3,1},... | collective-permute-start | bytes 3538952 | tf_op jit(solution)/shard_map/ppermute | solution.py:392
  57.4 10.8 %collective-permute-start.18 = (f32[4,128,128]{2,1,0:T(8,128)S(1)}, f32[4,128,128]{2,1,0:T(8,128)S(1)}, u32[]{:S(2)}, u32[]{:S(2)}) collective-permute-start(f32[4,128,128]{2,1,0:T(8,128)S(1)} %get-tuple-element.145), channel_id=1, source_target_pairs={{0,12},{2,14},{12,0},{14,2},{4,8},{6,10},{8,4},{10,6},{1,13},{3,15... | collective-permute-start | bytes 786440 | tf_op jit(solution)/shard_map/ppermute | solution.py:388
  61.9 12.0 %collective-permute-start.15 = (f32[6,128,128]{2,1,0:T(8,128)S(1)}, f32[6,128,128]{2,1,0:T(8,128)S(1)}, u32[]{:S(2)}, u32[]{:S(2)}) collective-permute-start(f32[6,128,128]{2,1,0:T(8,128)S(1)} %get-tuple-element.118), channel_id=1, source_target_pairs={{0,1},{1,0},{2,3},{3,2},{4,5},{5,4},{6,7},{7,6},{8,9},{9,8},{10,11... | collective-permute-start | bytes 1179656 | tf_op jit(solution)/shard_map/ppermute | solution.py:396
  63.4 18.9 %collective-permute-start.16 = (f32[6,128,128]{2,1,0:T(8,128)S(1)}, f32[6,128,128]{2,1,0:T(8,128)S(1)}, u32[]{:S(2)}, u32[]{:S(2)}) collective-permute-start(f32[6,128,128]{2,1,0:T(8,128)S(1)} %get-tuple-element.119), channel_id=1, source_target_pairs={{0,1},{1,0},{2,3},{3,2},{4,5},{5,4},{6,7},{7,6},{8,9},{9,8},{10,11... | collective-permute-start | bytes 1179656 | tf_op jit(solution)/shard_map/ppermute | solution.py:396
  64.0 11.0 %collective-permute-start.17 = (f32[4,128,128]{2,1,0:T(8,128)S(1)}, f32[4,128,128]{2,1,0:T(8,128)S(1)}, u32[]{:S(2)}, u32[]{:S(2)}) collective-permute-start(f32[4,128,128]{2,1,0:T(8,128)S(1)} %get-tuple-element.143), channel_id=1, source_target_pairs={{0,4},{2,6},{4,0},{6,2},{8,12},{10,14},{12,8},{14,10},{1,5},{3,7},... | collective-permute-start | bytes 786440 | tf_op jit(solution)/shard_map/ppermute | solution.py:388
  66.7 16.7 %collective-permute-start.19 = (f32[4,128,128]{2,1,0:T(8,128)S(1)}, f32[4,128,128]{2,1,0:T(8,128)S(1)}, u32[]{:S(2)}, u32[]{:S(2)}) collective-permute-start(f32[4,128,128]{2,1,0:T(8,128)S(1)} %get-tuple-element.142), channel_id=1, source_target_pairs={{0,4},{2,6},{4,0},{6,2},{8,12},{10,14},{12,8},{14,10},{1,5},{3,7},... | collective-permute-start | bytes 786440 | tf_op jit(solution)/shard_map/ppermute | solution.py:388
  68.2 17.9 %collective-permute-start.20 = (f32[4,128,128]{2,1,0:T(8,128)S(1)}, f32[4,128,128]{2,1,0:T(8,128)S(1)}, u32[]{:S(2)}, u32[]{:S(2)}) collective-permute-start(f32[4,128,128]{2,1,0:T(8,128)S(1)} %get-tuple-element.134), channel_id=1, source_target_pairs={{0,12},{2,14},{12,0},{14,2},{4,8},{6,10},{8,4},{10,6},{1,13},{3,15... | collective-permute-start | bytes 786440 | tf_op jit(solution)/shard_map/ppermute | solution.py:388
  76.0 15.2 %collective-permute-start.21 = (f32[4,128,128]{2,1,0:T(8,128)S(1)}, f32[4,128,128]{2,1,0:T(8,128)S(1)}, u32[]{:S(2)}, u32[]{:S(2)}) collective-permute-start(f32[4,128,128]{2,1,0:T(8,128)S(1)} %shard_map.91.refs_0_), channel_id=1, source_target_pairs={{0,1},{1,0},{2,3},{3,2},{4,5},{5,4},{6,7},{7,6},{8,9},{9,8},{10,11... | collective-permute-start | bytes 786440 | tf_op jit(solution)/shard_map/ppermute | solution.py:396
  87.2 6.9 %collective-permute-start.22 = (f32[4,128,128]{2,1,0:T(8,128)S(1)}, f32[4,128,128]{2,1,0:T(8,128)S(1)}, u32[]{:S(2)}, u32[]{:S(2)}) collective-permute-start(f32[4,128,128]{2,1,0:T(8,128)S(1)} %shard_map.92.refs_1_), channel_id=1, source_target_pairs={{0,1},{1,0},{2,3},{3,2},{4,5},{5,4},{6,7},{7,6},{8,9},{9,8},{10,11... | collective-permute-start | bytes 786440 | tf_op jit(solution)/shard_map/ppermute | solution.py:396
